TPU v7x, 512 devices: a whole 4x4x16 slice. The times are simulated.
512 devices in a mesh: seq: 4 (over x), tok: 128 (over y, z, core).
Axes of the slice: x: 4, y: 4, z: 16, core: 2. Of those that a mesh axis runs over, the one named last changes fastest.
Arguments:
- tokens: bfloat16 [4, 16384, 768], P('seq', 'tok'), may hold values from -32 to 32
- w_shared: bfloat16 [768, 384], replicated, may hold values from -0.21875 to 0.21875
- w_value: bfloat16 [768, 384], replicated, may hold values from -0.21875 to 0.21875
- cluster_ids: int32 [4, 6, 16384], P('seq', None, 'tok'), may hold values from 0 to 127, as said below
- slot_index: int32 [4, 6, 16384], P('seq', None, 'tok'), may hold values from 0 to 255, as said below
- cotangent: bfloat16 [4, 16384, 384], P('seq', 'tok'), may hold values from -6 to 6
Outputs:
- attention: bfloat16 [4, 16384, 384], P('seq', 'tok')
- grad_tokens: bfloat16 [4, 16384, 768], P('seq', 'tok')
- grad_shared: bfloat16 [768, 384], replicated
- grad_value: bfloat16 [768, 384], replicated
Inputs may be any that keep to these rules, and one draw needn't show every extreme that they name: `cluster_ids`: every cluster of a sequence and head holds at most 256 tokens, and some cluster exactly 256; the 128 tokens of one device hold at most 2 tokens of one cluster of one head, and some exactly 2. `slot_index`: the tokens of a cluster are numbered 0, 1, 2 and so on in order of position.
All inputs are finite; a program needn't handle non-finite values.
Results may differ from a plain program's by a relative error of at most 0.014.
The roundings to bfloat16 on the way count: a program that leaves them out, or rounds other values in their place, can miss the bound.
Values may be sent and summed in bfloat16 or wider, within the bound.
No kernel may reach another device: no remote copies, remote signals or barrier semaphores. Data moves between devices by JAX's collectives and lax.ppermute only.
A program may use at most 64 MiB of HBM per device.

v0:
```python
import jax
import jax.numpy as jnp
from jax import lax
from jax.sharding import PartitionSpec as P


def forward_block(shared_rows, value_rows):
    block_size = shared_rows.shape[0]
    score_scale = shared_rows.shape[1] ** (-0.5)
    ordinal = jnp.arange(block_size)
    allowed = ordinal[None, :] <= ordinal[:, None]
    scores = jnp.dot(shared_rows, shared_rows.T, preferred_element_type=jnp.float32) * score_scale
    scores = jnp.where(allowed, scores, -1e30)
    highest = jnp.max(scores, axis=1, keepdims=True)
    weights = jnp.exp(scores - highest)
    attn_weights = (weights / jnp.sum(weights, axis=1, keepdims=True)).astype(jnp.bfloat16)
    output = jnp.dot(attn_weights, value_rows, preferred_element_type=jnp.float32).astype(
        jnp.bfloat16
    )
    return (output, attn_weights)


def backward_block(shared_rows, value_rows, attn_weights, grad_rows):
    score_scale = shared_rows.shape[1] ** (-0.5)
    d_prob = jnp.dot(grad_rows, value_rows.T, preferred_element_type=jnp.float32)
    wide_weights = attn_weights.astype(jnp.float32)
    row_delta = jnp.sum(wide_weights * d_prob, axis=1, keepdims=True)
    d_score = (wide_weights * (d_prob - row_delta)).astype(jnp.bfloat16)
    both_sides = jnp.dot(d_score, shared_rows, preferred_element_type=jnp.float32) + jnp.dot(
        d_score.T, shared_rows, preferred_element_type=jnp.float32
    )
    d_shared = (both_sides * score_scale).astype(jnp.bfloat16)
    d_value = jnp.dot(attn_weights.T, grad_rows, preferred_element_type=jnp.float32).astype(
        jnp.bfloat16
    )
    return (d_shared, d_value)


def body(tokens, w_shared, w_value, cluster_ids, slot_index, cotangent):
    local_rows = tokens[0]
    local_count = local_rows.shape[0]
    head_count = cluster_ids.shape[1]
    feature_width = w_shared.shape[1]
    head_size = feature_width // head_count
    owners = lax.axis_size("tok")
    capacity = 2 * local_count
    per_peer = capacity // owners
    shared_proj = jnp.dot(local_rows, w_shared, preferred_element_type=jnp.float32).astype(
        jnp.bfloat16
    )
    value_proj = jnp.dot(local_rows, w_value, preferred_element_type=jnp.float32).astype(
        jnp.bfloat16
    )
    cluster_of = cluster_ids[0]
    slot_local = slot_index[0]
    earlier = jnp.arange(local_count)[None, :] < jnp.arange(local_count)[:, None]
    order_within = jnp.sum(
        (cluster_of[:, :, None] == cluster_of[:, None, :]) & earlier[None], axis=2
    )
    destination = cluster_of * per_peer + order_within
    route_mask = destination[:, :, None] == jnp.arange(capacity, dtype=jnp.int32)[None, None, :]
    route = route_mask.astype(jnp.bfloat16)
    route_count = route_mask.astype(jnp.int32)

    def split_heads(matrix):
        return matrix.reshape(local_count, head_count, head_size).transpose(1, 0, 2)

    def send_rows(matrix):
        return jnp.einsum("hls,hlc->hsc", route, matrix, preferred_element_type=jnp.float32).astype(
            jnp.bfloat16
        )

    def take_rows(matrix):
        return jnp.einsum("hls,hsc->hlc", route, matrix, preferred_element_type=jnp.float32).astype(
            jnp.bfloat16
        )

    packed = jnp.concatenate([split_heads(shared_proj), split_heads(value_proj)], axis=-1)
    outgoing = send_rows(packed).reshape(head_count, owners, per_peer, 2 * head_size)
    slot_used = jnp.sum(route_count, axis=1)
    slot_total = jnp.sum(route_count * slot_local[:, :, None], axis=1)
    outgoing_slots = jnp.where(slot_used > 0, slot_total, capacity).reshape(
        head_count, owners, per_peer
    )
    outgoing_grad = send_rows(split_heads(cotangent[0])).reshape(
        head_count, owners, per_peer * head_size
    )

    def slot_mapping(slot_rows):
        return (
            jnp.arange(capacity, dtype=jnp.int32)[:, None] == slot_rows.reshape(-1)[None, :]
        ).astype(jnp.bfloat16)

    def place(row_block, mapping):
        columns = row_block.shape[-1]
        return jnp.dot(
            mapping, row_block.reshape(-1, columns), preferred_element_type=jnp.float32
        ).astype(row_block.dtype)

    def pick(block_rows, mapping, slot_rows):
        picked = jnp.dot(mapping.T, block_rows, preferred_element_type=jnp.float32).astype(
            block_rows.dtype
        )
        return picked.reshape(slot_rows.shape + (block_rows.shape[-1],))

    def single_head(pieces):
        row_block, slot_rows = pieces
        mapping = slot_mapping(slot_rows)
        placed = place(row_block, mapping)
        output, attn_weights = forward_block(placed[:, :head_size], placed[:, head_size:])
        out_rows = pick(output, mapping, slot_rows).reshape(slot_rows.shape[0], -1)
        return (out_rows, placed, attn_weights, slot_rows)

    out_rows, kept_blocks, kept_weights, kept_slots = lax.map(
        single_head,
        (
            lax.all_to_all(outgoing, "tok", split_axis=1, concat_axis=1, tiled=True),
            lax.all_to_all(outgoing_slots, "tok", split_axis=1, concat_axis=1, tiled=True),
        ),
    )
    returned_out = lax.all_to_all(out_rows, "tok", split_axis=1, concat_axis=1, tiled=True)
    grad_in = lax.all_to_all(outgoing_grad, "tok", split_axis=1, concat_axis=1, tiled=True)

    def single_back(pieces):
        placed, attn_weights, slot_rows, grad_flat = pieces
        mapping = slot_mapping(slot_rows)
        shared_block = placed[:, :head_size]
        value_block = placed[:, head_size:]
        grad_block = place(grad_flat.reshape(slot_rows.shape + (head_size,)), mapping)
        d_shared, d_value = backward_block(shared_block, value_block, attn_weights, grad_block)
        return pick(jnp.concatenate([d_shared, d_value], axis=-1), mapping, slot_rows)

    grad_rows = lax.map(single_back, (kept_blocks, kept_weights, kept_slots, grad_in))
    returned_grad = lax.all_to_all(grad_rows, "tok", split_axis=1, concat_axis=1, tiled=True)
    routed_out = take_rows(returned_out.reshape(head_count, capacity, head_size))
    attention = routed_out.transpose(1, 0, 2).reshape(local_count, feature_width)
    routed_grad = take_rows(returned_grad.reshape(head_count, capacity, 2 * head_size))
    d_shared = routed_grad[:, :, :head_size].transpose(1, 0, 2).reshape(local_count, feature_width)
    d_value = routed_grad[:, :, head_size:].transpose(1, 0, 2).reshape(local_count, feature_width)
    grad_tokens = jnp.dot(d_shared, w_shared.T, preferred_element_type=jnp.float32) + jnp.dot(
        d_value, w_value.T, preferred_element_type=jnp.float32
    )
    grad_tokens = grad_tokens.astype(jnp.bfloat16)
    part_shared = jnp.dot(local_rows.T, d_shared, preferred_element_type=jnp.float32)
    part_value = jnp.dot(local_rows.T, d_value, preferred_element_type=jnp.float32)
    total_shared, total_value = lax.psum((part_shared, part_value), ("seq", "tok"))
    grad_shared = total_shared.astype(jnp.bfloat16)
    grad_value = total_value.astype(jnp.bfloat16)
    return (attention[None], grad_tokens[None], grad_shared, grad_value)


def solution(mesh):
    in_specs = (
        P("seq", "tok", None),
        P(),
        P(),
        P("seq", None, "tok"),
        P("seq", None, "tok"),
        P("seq", "tok", None),
    )
    out_specs = (P("seq", "tok", None), P("seq", "tok", None), P(), P())
    return jax.shard_map(body, mesh=mesh, in_specs=in_specs, out_specs=out_specs, check_vma=False)
```

profile of v0, /device:TPU:1, one launch (start us, length us, event | category | flops | bytes accessed | tf_op | source)
XLA Modules:
  0.0 370.8 jit_solution(13206041147293965474)
XLA Ops:
  0.7 0.7 copy.98
  1.4 0.7 copy.99
  2.1 0.3 convert_reduce_fusion.1
  2.4 0.7 multiply_add_fusion
  3.1 0.3 convert_reduce_fusion
  3.4 0.8 copy.61
  4.2 20.6 %all-to-all-start = ((s32[6,128,2]{0,2,1:T(2,128)}), s32[6,128,2]{0,2,1:T(2,128)S(1)}, u32[]{:S(2)}, u32[]{:S(2)}) async-start(s32[6,128,2]{0,2,1:T(2,128)} %bitcast.6), calls=%async_computation | async-start | bytes 262144 | tf_op jit(solution)/shard_map/all_to_all | solution.py:118
  24.8 1.0 copy.73
  25.8 0.3 convolution_convert_fusion.8
  26.6 0.8 copy.75
  27.4 14.7 %all-to-all-done = s32[6,128,2]{0,2,1:T(2,128)S(1)} async-done(((s32[6,128,2]{0,2,1:T(2,128)}), s32[6,128,2]{0,2,1:T(2,128)S(1)}, u32[]{:S(2)}, u32[]{:S(2)}) %all-to-all-start) | async-done | bytes 6176 | tf_op jit(solution)/shard_map/all_to_all | solution.py:118
  42.2 6.9 %all-to-all-start.3 = ((bf16[6,128,128]{2,0,1:T(8,128)(2,1)}), bf16[6,128,128]{2,0,1:T(8,128)(2,1)S(1)}, u32[]{:S(2)}, u32[]{:S(2)}) async-start(bf16[6,128,128]{2,0,1:T(8,128)(2,1)} %copy.75), calls=%async_computation.3 | async-start | bytes 524288 | tf_op jit(solution)/shard_map/all_to_all | solution.py:122
  49.1 0.3 convolution_convert_fusion.11
  49.7 0.3 convolution_convert_fusion.10
  50.3 0.6 convolution_convert_fusion.6
  50.9 1.0 copy.67
  51.9 19.8 %all-to-all-done.3 = bf16[6,128,128]{2,0,1:T(8,128)(2,1)S(1)} async-done(((bf16[6,128,128]{2,0,1:T(8,128)(2,1)}), bf16[6,128,128]{2,0,1:T(8,128)(2,1)S(1)}, u32[]{:S(2)}, u32[]{:S(2)}) %all-to-all-start.3) | async-done | bytes 196640 | tf_op jit(solution)/shard_map/all_to_all | solution.py:122
  71.7 7.3 %all-to-all-start.1 = ((bf16[6,128,2,128]{3,2,0,1:T(2,128)(2,1)}), bf16[6,128,2,128]{3,2,0,1:T(2,128)(2,1)S(1)}, u32[]{:S(2)}, u32[]{:S(2)}) async-start(bf16[6,128,2,128]{3,2,0,1:T(2,128)(2,1)} %copy.67), calls=%async_computation.1 | async-start | bytes 786432 | tf_op jit(solution)/shard_map/all_to_all | solution.py:117
  79.1 1.1 copy.68
  80.2 26.8 %all-to-all-done.1 = bf16[6,128,2,128]{3,2,0,1:T(2,128)(2,1)S(1)} async-done(((bf16[6,128,2,128]{3,2,0,1:T(2,128)(2,1)}), bf16[6,128,2,128]{3,2,0,1:T(2,128)(2,1)S(1)}, u32[]{:S(2)}, u32[]{:S(2)}) %all-to-all-start.1) | async-done | bytes 393248 | tf_op jit(solution)/shard_map/all_to_all | solution.py:117
  107.0 11.7 %while.24 = (s32[]{:T(128)}, bf16[6,128,128]{2,1,0:T(8,128)(2,1)}, bf16[6,256,128]{1,2,0:T(8,128)(2,1)S(1)}, bf16[6,256,256]{1,2,0:T(8,128)(2,1)S(1)}, s32[6,128...) while((s32[]{:T(128)}, bf16[6,128,128]{2,1,0:T(8,128)(2,1)}, ...), condition=%wide.region_6.7_spmd, body=%wide.region_3.6_spmd.sunk | while | flops 42728960 | bytes 1813609 | solution.py:114
  107.8 0.3 convolution_convert_fusion.16
  108.3 0.6 constant_dynamic-update-slice_fusion.4
  109.4 0.3 fusion.84
  109.8 0.3 convolution_convert_fusion.16
  110.3 0.6 constant_dynamic-update-slice_fusion.4
  111.7 0.3 convolution_convert_fusion.16
  112.2 0.6 constant_dynamic-update-slice_fusion.4
  113.7 0.3 convolution_convert_fusion.16
  114.2 0.6 constant_dynamic-update-slice_fusion.4
  115.6 0.3 convolution_convert_fusion.16
  116.2 0.6 constant_dynamic-update-slice_fusion.4
  117.6 0.3 convolution_convert_fusion.16
  118.1 0.6 constant_dynamic-update-slice_fusion.4
  118.7 1.8 copy.70
  120.5 7.4 %all-to-all-start.2 = ((bf16[6,128,128]{2,0,1:T(8,128)(2,1)}), bf16[6,128,128]{2,0,1:T(8,128)(2,1)S(1)}, u32[]{:S(2)}, u32[]{:S(2)}) async-start(bf16[6,128,128]{2,0,1:T(8,128)(2,1)} %copy.70), calls=%async_computation.2 | async-start | bytes 524288 | tf_op jit(solution)/shard_map/all_to_all | solution.py:121
  127.9 14.7 %while.25 = (s32[]{:T(128)}, bf16[6,128,2,128]{3,2,0,1:T(2,128)(2,1)}, s32[6,128,2]{2,1,0:T(8,128)S(1)}, bf16[6,256,256]{1,2,0:T(8,128)(2,1)S(1)}, bf16[6,128,12...) while((s32[]{:T(128)}, bf16[6,128,2,128]{3,2,0,1:T(2,128)(2,1)}, ...), condition=%wide.region_9.10_spmd, body=%wide.region_7.9_spmd.sunk | while | flops 59621120 | bytes 2498673 | solution.py:133
  128.7 0.3 fusion.96
  129.7 0.7 constant_dynamic-update-slice_fusion.5
  131.1 0.3 fusion.96
  132.1 0.7 constant_dynamic-update-slice_fusion.5
  133.6 0.3 fusion.96
  134.6 0.7 constant_dynamic-update-slice_fusion.5
  136.0 0.3 fusion.96
  137.0 0.7 constant_dynamic-update-slice_fusion.5
  138.4 0.3 fusion.96
  139.4 0.7 constant_dynamic-update-slice_fusion.5
  140.9 0.3 fusion.96
  141.9 0.7 constant_dynamic-update-slice_fusion.5
  142.6 7.9 %all-to-all-done.2 = bf16[6,128,128]{2,0,1:T(8,128)(2,1)S(1)} async-done(((bf16[6,128,128]{2,0,1:T(8,128)(2,1)}), bf16[6,128,128]{2,0,1:T(8,128)(2,1)S(1)}, u32[]{:S(2)}, u32[]{:S(2)}) %all-to-all-start.2) | async-done | bytes 196640 | tf_op jit(solution)/shard_map/all_to_all | solution.py:121
  150.5 8.4 %all-to-all-start.4 = ((bf16[6,128,2,128]{3,2,0,1:T(2,128)(2,1)}), bf16[6,128,2,128]{3,2,0,1:T(2,128)(2,1)S(1)}, u32[]{:S(2)}, u32[]{:S(2)}) async-start(bf16[6,128,2,128]{3,2,0,1:T(2,128)(2,1)} %get-tuple-element.73), calls=%async_computation.4 | async-start | bytes 786432 | tf_op jit(solution)/shard_map/all_to_all | solution.py:134
  159.1 0.4 convolution_convert_fusion.9
  159.5 0.8 copy.82
  160.3 26.5 %all-to-all-done.4 = bf16[6,128,2,128]{3,2,0,1:T(2,128)(2,1)S(1)} async-done(((bf16[6,128,2,128]{3,2,0,1:T(2,128)(2,1)}), bf16[6,128,2,128]{3,2,0,1:T(2,128)(2,1)S(1)}, u32[]{:S(2)}, u32[]{:S(2)}) %all-to-all-start.4) | async-done | bytes 393248 | tf_op jit(solution)/shard_map/all_to_all | solution.py:134
  186.7 0.3 copy.80
  187.0 0.4 convolution_convert_fusion.7
  187.5 0.3 fusion.43
  187.8 0.3 convolution_bitcast_fusion.1
  188.1 0.3 convolution_bitcast_fusion
  188.4 0.5 copy-done.3
  188.9 1.0 fusion.28
  189.9 177.7 %all-reduce.2 = (bf16[768,384]{0,1:T(8,128)(2,1)}, bf16[768,384]{0,1:T(8,128)(2,1)S(1)}) all-reduce(f32[768,384]{0,1:T(8,128)S(1)} %convolution_bitcast_fusion.1, f32[768,384]{0,1:T(8,128)S(1)} %convolution_bitcast_fusion), channel_id=1, replica_groups=mesh['seq'=4,'tok'=128] {'seq','tok'}, use_global_device_ids=true, to_apply=%region_10.11 | all-reduce | flops 589824 | bytes 3538944 | tf_op jit(solution)/shard_map/psum | solution.py:146
  367.6 2.1 copy.83
  369.7 1.1 copy.84
  (148 shorter events, 15.5 us)
Async XLA Ops:
  0.6 48.5 %copy-start = (bf16[768,384]{1,0:T(8,128)(2,1)S(1)}, bf16[768,384]{1,0:T(8,128)(2,1)}, u32[]{:S(2)}) copy-start(bf16[768,384]{1,0:T(8,128)(2,1)} %param.11) | copy-start | bytes 1769476
  4.2 38.0 %all-to-all-start = ((s32[6,128,2]{0,2,1:T(2,128)}), s32[6,128,2]{0,2,1:T(2,128)S(1)}, u32[]{:S(2)}, u32[]{:S(2)}) async-start(s32[6,128,2]{0,2,1:T(2,128)} %bitcast.6), calls=%async_computation | async-start | bytes 262144 | tf_op jit(solution)/shard_map/all_to_all | solution.py:118
  26.1 23.0 %copy-start.1 = (bf16[1,128,768]{2,1,0:T(8,128)(2,1)S(1)}, bf16[1,128,768]{2,1,0:T(8,128)(2,1)}, u32[]{:S(2)}) copy-start(bf16[1,128,768]{2,1,0:T(8,128)(2,1)} %param.10) | copy-start | bytes 589828
  26.6 23.1 %copy-start.2 = (bf16[768,384]{1,0:T(8,128)(2,1)S(1)}, bf16[768,384]{1,0:T(8,128)(2,1)}, u32[]{:S(2)}) copy-start(bf16[768,384]{1,0:T(8,128)(2,1)} %param.12) | copy-start | bytes 1769476
  42.2 29.5 %all-to-all-start.3 = ((bf16[6,128,128]{2,0,1:T(8,128)(2,1)}), bf16[6,128,128]{2,0,1:T(8,128)(2,1)S(1)}, u32[]{:S(2)}, u32[]{:S(2)}) async-start(bf16[6,128,128]{2,0,1:T(8,128)(2,1)} %copy.75), calls=%async_computation.3 | async-start | bytes 524288 | tf_op jit(solution)/shard_map/all_to_all | solution.py:122
  71.7 35.3 %all-to-all-start.1 = ((bf16[6,128,2,128]{3,2,0,1:T(2,128)(2,1)}), bf16[6,128,2,128]{3,2,0,1:T(2,128)(2,1)S(1)}, u32[]{:S(2)}, u32[]{:S(2)}) async-start(bf16[6,128,2,128]{3,2,0,1:T(2,128)(2,1)} %copy.67), calls=%async_computation.1 | async-start | bytes 786432 | tf_op jit(solution)/shard_map/all_to_all | solution.py:117
  120.5 30.0 %all-to-all-start.2 = ((bf16[6,128,128]{2,0,1:T(8,128)(2,1)}), bf16[6,128,128]{2,0,1:T(8,128)(2,1)S(1)}, u32[]{:S(2)}, u32[]{:S(2)}) async-start(bf16[6,128,128]{2,0,1:T(8,128)(2,1)} %copy.70), calls=%async_computation.2 | async-start | bytes 524288 | tf_op jit(solution)/shard_map/all_to_all | solution.py:121
  150.5 36.2 %all-to-all-start.4 = ((bf16[6,128,2,128]{3,2,0,1:T(2,128)(2,1)}), bf16[6,128,2,128]{3,2,0,1:T(2,128)(2,1)S(1)}, u32[]{:S(2)}, u32[]{:S(2)}) async-start(bf16[6,128,2,128]{3,2,0,1:T(2,128)(2,1)} %get-tuple-element.73), calls=%async_computation.4 | async-start | bytes 786432 | tf_op jit(solution)/shard_map/all_to_all | solution.py:134
  187.8 1.1 copy-start.3
where the time goes:
time: 372 us; the launch traced here: 371 us
  blocking collectives  178 us (48%)
  waiting for transfers between devices  95.7 us (26%)
  starting transfers between devices  50.5 us (14%)
  local copies, waits for them, and re-layouts  26.4 us (7%)
  matrix products  16.4 us (4%)
    psum x1, blocking collectives, body(): lax.psum((part_shared, part_value), ('seq', 'tok'))  178 us
    all_to_all x1, waiting for transfers between devices, body(): lax.all_to_all(outgoing, 'tok', split_axis=1, concat_axis=1, tiled=True)  26.8 us
    all_to_all x1, waiting for transfers between devices, body(): lax.all_to_all(grad_rows, 'tok', split_axis=1, concat_axis=1, tiled=True)  26.5 us
    all_to_all x1, starting transfers between devices, body(): lax.all_to_all(outgoing_slots, 'tok', split_axis=1, concat_axis=1, tiled=...  20.6 us
    all_to_all x1, waiting for transfers between devices, body(): lax.all_to_all(outgoing_grad, 'tok', split_axis=1, concat_axis=1, tiled=T...  19.8 us
    all_to_all x1, waiting for transfers between devices, body(): lax.all_to_all(outgoing_slots, 'tok', split_axis=1, concat_axis=1, tiled=...  14.7 us
    all_to_all x1, starting transfers between devices, body(): lax.all_to_all(grad_rows, 'tok', split_axis=1, concat_axis=1, tiled=True)  8.37 us
    all_to_all x1, waiting for transfers between devices, body(): lax.all_to_all(out_rows, 'tok', split_axis=1, concat_axis=1, tiled=True)  7.93 us
  transfers between devices with their start and end apart: 5, of which 5 were waited for; matrix products, arithmetic and copies ran while one was open for 6% of the time, Pallas kernels for 0%

commit v1 on v0

v1 whole, which is shorter than its diff:
```python
import jax
import jax.numpy as jnp
from jax import lax
from jax.experimental import pallas as pl
from jax.experimental.pallas import tpu as pltpu
from jax.sharding import Mesh
from jax.sharding import PartitionSpec as P

F32 = jnp.float32
BF16 = jnp.bfloat16
HEADS = 6
HEAD = 64
ROWS = 256
LOCAL = 128
WIDTH = 768
PROJ = 384
UNUSED = 65536.0
PLANE = ("y", "c")
TOK = ("y", "z", "c")


def iota(shape, dim):
    return lax.broadcasted_iota(jnp.int32, shape, dim)


def dot(a, b, dims=((1,), (0,))):
    return lax.dot_general(a, b, (dims, ((), ())), preferred_element_type=F32)


def send_kernel(tok_ref, ws_ref, wv_ref, cluster_ref, cot_ref, out_ref, dest_ref):
    tokens = tok_ref[...]
    shared = dot(tokens, ws_ref[...]).astype(BF16)
    value = dot(tokens, wv_ref[...]).astype(BF16)
    cot = cot_ref[...]
    sub = iota((LOCAL, LOCAL), 0)
    lane = iota((LOCAL, LOCAL), 1)
    sub_rows = iota((ROWS, LOCAL), 0)
    lane_rows = iota((ROWS, LOCAL), 1)
    blank = jnp.zeros((LOCAL, HEAD), BF16)
    pending = None
    for h in range(HEADS):
        cluster = cluster_ref[h : h + 1, :]
        member = (sub == cluster).astype(BF16)
        same = dot(member, member, ((0,), (0,)))
        order = jnp.sum(jnp.where(sub < lane, same, 0.0), axis=0, keepdims=True)
        dest = cluster * 2 + order.astype(jnp.int32)
        dest_ref[h : h + 1, :] = dest
        hit = sub_rows == dest
        used = jnp.sum(jnp.where(hit, 1.0, 0.0), axis=1, keepdims=True)
        cols = slice(h * HEAD, (h + 1) * HEAD)
        tail = [cot[:, cols], blank] if h % 2 == 0 else [blank, cot[:, cols]]
        packed = jnp.concatenate([shared[:, cols], value[:, cols]] + tail, axis=1)
        moved = dot(hit.astype(BF16), packed)
        mark = (lane_rows == 0) & (used < 0.5)
        out_ref[h] = jnp.where(mark, UNUSED, moved[:, :LOCAL]).astype(BF16)
        if h % 2 == 0:
            pending = moved[:, LOCAL:]
        else:
            out_ref[HEADS + h // 2] = (pending + moved[:, LOCAL:]).astype(BF16)


def attend_kernel(in_ref, out_ref):
    lane_rows = iota((ROWS, LOCAL), 1)
    causal = iota((ROWS, ROWS), 1) <= iota((ROWS, ROWS), 0)
    pending = None
    for h in range(HEADS):
        block = in_ref[h]
        empty = block[:, :1].astype(F32) > 32768.0
        first = lane_rows == 0
        block = jnp.where(empty & first, 0.0, block.astype(F32)).astype(BF16)
        shared = block[:, :HEAD]
        value = block[:, HEAD:]
        pair = in_ref[HEADS + h // 2]
        cot = pair[:, :HEAD] if h % 2 == 0 else pair[:, HEAD:]
        bias_lane = lane_rows == HEAD
        head_lanes = lane_rows < HEAD
        wide = block.astype(F32)
        query = jnp.where(head_lanes, wide, jnp.where(bias_lane, 1.0, 0.0)).astype(BF16)
        key = jnp.where(
            head_lanes, wide, jnp.where(bias_lane & empty, -1e30, 0.0)
        ).astype(BF16)
        scores = dot(query, key, ((1,), (1,))) * 0.125
        scores = jnp.where(causal, scores, -1e30)
        highest = jnp.max(scores, axis=1, keepdims=True)
        weights = jnp.exp(scores - highest)
        probs = (weights / jnp.sum(weights, axis=1, keepdims=True)).astype(BF16)
        out = dot(probs, value)
        d_prob = dot(cot, value, ((1,), (1,)))
        wide_probs = probs.astype(F32)
        delta = jnp.sum(wide_probs * d_prob, axis=1, keepdims=True)
        d_score = (wide_probs * (d_prob - delta)).astype(BF16)
        both = dot(d_score, shared) + dot(d_score, shared, ((0,), (0,)))
        d_shared = (both * 0.125).astype(BF16)
        d_value = dot(probs, cot, ((0,), (0,))).astype(BF16)
        out_ref[h] = jnp.concatenate([d_shared, d_value], axis=1)
        if h % 2 == 0:
            pending = out.astype(BF16)
        else:
            out_ref[HEADS + h // 2] = jnp.concatenate([pending, out.astype(BF16)], axis=1)


def return_kernel(in_ref, dest_ref, ws_ref, wv_ref, att_ref, grad_ref, dt_ref):
    sub_rows = iota((ROWS, LOCAL), 0)
    lane = iota((LOCAL, LOCAL), 1)
    d_shared = []
    d_value = []
    pending = None
    for h in range(HEADS):
        route = (sub_rows == dest_ref[h : h + 1, :]).astype(BF16)
        block = in_ref[h]
        turned = dot(block, route, ((0,), (0,))).astype(BF16)
        dt_ref[h * HEAD : (h + 1) * HEAD, :] = turned[:HEAD]
        dt_ref[PROJ + h * HEAD : PROJ + (h + 1) * HEAD, :] = turned[HEAD:]
        rows = dot(route, block, ((0,), (0,))).astype(BF16)
        d_shared.append(rows[:, :HEAD])
        d_value.append(rows[:, HEAD:])
        pair = dot(route, in_ref[HEADS + h // 2], ((0,), (0,)))
        if h % 2 == 0:
            pending = pair
        else:
            k = h // 2
            att_ref[:, k * LOCAL : (k + 1) * LOCAL] = jnp.where(
                lane < HEAD, pending, pair
            ).astype(BF16)
    left = jnp.concatenate(d_shared, axis=1)
    right = jnp.concatenate(d_value, axis=1)
    total = dot(left, ws_ref[...], ((1,), (1,))) + dot(right, wv_ref[...], ((1,), (1,)))
    grad_ref[...] = total.astype(BF16)


def partial_kernel(dt_ref, tok_ref, out_ref):
    total = dot(dt_ref[0], tok_ref[0])
    for s in range(1, dt_ref.shape[0]):
        total = total + dot(dt_ref[s], tok_ref[s])
    part = total.astype(BF16)
    columns = part.shape[0]
    for k in range(WIDTH // LOCAL):
        out_ref[k * columns : (k + 1) * columns, :] = part[:, k * LOCAL : (k + 1) * LOCAL]


def call(kernel, out, *args):
    return pl.pallas_call(
        kernel,
        out_shape=out,
        compiler_params=pltpu.CompilerParams(vmem_limit_bytes=48 * 1024 * 1024),
    )(*args)


def shape(*dims):
    return jax.ShapeDtypeStruct(dims, BF16)


def swap(rows, axes):
    return lax.all_to_all(rows, axes, split_axis=0, concat_axis=0, tiled=True)


def body(tokens, w_shared, w_value, cluster_ids, slot_index, cotangent):
    rows = tokens[0]
    plane_rows = lax.all_gather(rows, PLANE, axis=0, tiled=False)
    sent, dest = call(
        send_kernel,
        (shape(9, ROWS, LOCAL), jax.ShapeDtypeStruct((HEADS, LOCAL), jnp.int32)),
        rows,
        w_shared,
        w_value,
        cluster_ids[0],
        cotangent[0],
    )

    def route(blocks):
        split = blocks.reshape(9, LOCAL, 2, LOCAL)
        moved = lax.all_to_all(split, TOK, split_axis=1, concat_axis=1, tiled=True)
        return moved.reshape(9, ROWS, LOCAL)

    worked = call(attend_kernel, shape(9, ROWS, LOCAL), route(sent))
    attention, grad_tokens, turned = call(
        return_kernel,
        (shape(LOCAL, PROJ), shape(LOCAL, WIDTH), shape(WIDTH, LOCAL)),
        route(worked),
        dest,
        w_shared,
        w_value,
    )
    columns = WIDTH // 8
    mixed = swap(turned.reshape(8, columns, LOCAL), PLANE)
    part = call(partial_kernel, shape(6 * columns, LOCAL), mixed, plane_rows)
    pieces = swap(part.reshape(64, 9, LOCAL), ("x", "z"))
    piece = jnp.sum(pieces.astype(F32), axis=0).astype(BF16)
    block = swap(jnp.broadcast_to(piece[None], (64, 9, LOCAL)), ("x", "z"))
    block = block.reshape(1, 6 * columns, LOCAL)
    whole = swap(jnp.broadcast_to(block, (8, 6 * columns, LOCAL)), PLANE)
    whole = whole.reshape(8, 6, columns, LOCAL).transpose(1, 3, 0, 2).reshape(WIDTH, WIDTH)
    return (attention[None], grad_tokens[None], whole[:, :PROJ], whole[:, PROJ:])


def solution(mesh):
    fine = Mesh(mesh.devices.reshape(4, 4, 16, 2), ("x", "y", "z", "c"))
    in_specs = (
        P("x", TOK, None),
        P(),
        P(),
        P("x", None, TOK),
        P("x", None, TOK),
        P("x", TOK, None),
    )
    out_specs = (P("x", TOK, None), P("x", TOK, None), P(), P())
    return jax.shard_map(body, mesh=fine, in_specs=in_specs, out_specs=out_specs, check_vma=False)
```

time: 372 us -> 219 us (0.59)
  blocking collectives: 178 us -> 117 us
  waiting for transfers between devices: 95.7 us -> 41.5 us
  starting transfers between devices: 50.5 us -> 26.3 us
  matrix products: 16.4 us -> 0 us
  local copies, waits for them, and re-layouts: 26.4 us -> 12.3 us
  between operations: 0.91 us -> 14.2 us
  Pallas kernels: 0 us -> 7.09 us
    psum x1 -> x0, blocking collectives: 178 us -> none  [body(): lax.psum((part_shared, part_value), ('seq', 'tok'))]
    all_to_all x0 -> x4, blocking collectives: none -> 117 us  [the longest x3 73.4 us: swap(): return lax.all_to_all(rows, axes, split_axis=0, concat_axis=0, tiled=True)]
    all_to_all x5 -> x2, waiting for transfers between devices: 95.7 us -> 40.8 us  [the longest x1 34.9 us: route(): moved = lax.all_to_all(split, TOK, split_axis=1, concat_axis=1, tiled=True)]
    all_to_all x5 -> x2, starting transfers between devices: 50.5 us -> 26.2 us  [the longest x1 20.6 us: route(): moved = lax.all_to_all(split, TOK, split_axis=1, concat_axis=1, tiled=True)]
    dot_general x64 -> x0, matrix products: 16.4 us -> none  [the longest x12 2.97 us: pick(): jnp.dot(mapping.T, block_rows, preferred_element_type=jnp.float32)]
    dynamic_update_slice x12 -> x0, local copies, waits for them, and re-layouts: 7.83 us -> none  [the longest x6 4.09 us: body(): lax.map(single_back, (kept_blocks, kept_weights, kept_slots, grad_in))]
    pallas_call x0 -> x4, Pallas kernels: none -> 7.09 us  [call(): pl.pallas_call(kernel, out_shape=out, compiler_params=pltpu.CompilerParam...]
  transfers between devices with their start and end apart: 5 -> 3, of which waited for: 5 -> 2; matrix products, arithmetic and copies ran while one was open for 6% -> 1% of each run, Pallas kernels for 0% -> 3%
where the time goes in v1:
time: 219 us; the launch traced here: 218 us
  blocking collectives  117 us (53%)
  waiting for transfers between devices  41.5 us (19%)
  starting transfers between devices  26.3 us (12%)
  between operations  14.2 us (6%)
  local copies, waits for them, and re-layouts  12.3 us (6%)
  Pallas kernels  7.09 us (3%)
    all_to_all x3, blocking collectives, swap(): return lax.all_to_all(rows, axes, split_axis=0, concat_axis=0, tiled=True)  73.4 us
    all_to_all x1, blocking collectives, route(): moved = lax.all_to_all(split, TOK, split_axis=1, concat_axis=1, tiled=True)  43.1 us
    all_to_all x1, waiting for transfers between devices, route(): moved = lax.all_to_all(split, TOK, split_axis=1, concat_axis=1, tiled=True)  34.9 us
    all_to_all x1, starting transfers between devices, route(): moved = lax.all_to_all(split, TOK, split_axis=1, concat_axis=1, tiled=True)  20.6 us
    pallas_call x4, Pallas kernels, call(): pl.pallas_call(kernel, out_shape=out, compiler_params=pltpu.CompilerParam...  7.09 us
    unnamed x15, local copies, waits for them, and re-layouts  6.05 us
    all_to_all x1, waiting for transfers between devices, swap(): return lax.all_to_all(rows, axes, split_axis=0, concat_axis=0, tiled=True)  5.89 us
    all_to_all x1, starting transfers between devices, swap(): return lax.all_to_all(rows, axes, split_axis=0, concat_axis=0, tiled=True)  5.65 us
  transfers between devices with their start and end apart: 3, of which 2 were waited for; matrix products, arithmetic and copies ran while one was open for 1% of the time, Pallas kernels for 3%

profile of v1, /device:TPU:1, one launch (start us, length us, event | category | flops | bytes accessed | tf_op | source)
XLA Modules:
  0.0 218.0 jit_solution(14018825209064010633)
XLA Ops:
  7.2 0.7 copy.17
  7.9 0.0 copy-start
  7.9 1.1 copy-done
  8.9 0.0 copy-start.2
  8.9 1.1 copy-done.2
  10.0 0.0 copy-start.5
  10.0 0.9 copy-done.5
  10.9 0.0 copy-start.6
  10.9 0.9 copy-done.6
  11.8 1.1 shard_map.84
  12.9 1.2 copy.10
  14.1 20.6 %all-to-all-start = ((bf16[9,128,2,128]{3,2,0,1:T(2,128)(2,1)}), bf16[9,128,2,128]{3,2,0,1:T(2,128)(2,1)S(1)}, u32[]{:S(2)}, u32[]{:S(2)}) async-start(bf16[9,128,2,128]{3,2,0,1:T(2,128)(2,1)} %copy.10), calls=%async_computation | async-start | bytes 1179648 | tf_op jit(solution)/shard_map/all_to_all | solution.py:172
  34.7 0.0 all-gather.2.cloned.1.call-start
  34.7 0.7 all-gather.2.cloned.1.call-update
  35.4 34.9 %all-to-all-done = bf16[9,128,2,128]{3,2,0,1:T(2,128)(2,1)S(1)} async-done(((bf16[9,128,2,128]{3,2,0,1:T(2,128)(2,1)}), bf16[9,128,2,128]{3,2,0,1:T(2,128)(2,1)S(1)}, u32[]{:S(2)}, u32[]{:S(2)}) %all-to-all-start) | async-done | bytes 589856 | tf_op jit(solution)/shard_map/all_to_all | solution.py:172
  70.3 0.5 copy.11
  70.8 3.8 %shard_map.85 = bf16[9,256,128]{2,1,0:T(8,128)(2,1)S(1)} custom-call(bf16[9,256,128]{2,1,0:T(8,128)(2,1)S(1)} %bitcast.18), custom_call_target="tpu_custom_call" | custom-call | tf_op jit(solution)/shard_map/pallas_call | solution.py:142
  74.6 0.4 copy.12
  75.0 0.0 copy-start.1
  75.0 0.0 copy-start.3
  75.0 43.1 %all_to_all.30 = bf16[9,128,2,128]{3,2,0,1:T(2,128)(2,1)S(1)} all-to-all(bf16[9,128,2,128]{3,2,0,1:T(2,128)(2,1)S(1)} %copy.12), channel_id=1, replica_groups=mesh['x'=4,'y'=4,'z'=16,'c'=2] {'y','z','c'}, dimensions={1} | all-to-all | bytes 1179648 | tf_op jit(solution)/shard_map/all_to_all | solution.py:172
  118.2 0.5 copy.13
  118.6 0.0 copy-done.1
  118.6 0.0 copy-done.3
  118.6 1.8 shard_map.86
  120.4 5.6 %all-to-all-start.2 = ((bf16[8,96,128]{2,1,0:T(8,128)(2,1)}), bf16[8,96,128]{2,1,0:T(8,128)(2,1)S(1)}, u32[]{:S(2)}, u32[]{:S(2)}) async-start(bf16[8,96,128]{2,1,0:T(8,128)(2,1)} %bitcast.8), calls=%async_computation.2 | async-start | bytes 393216 | tf_op jit(solution)/shard_map/all_to_all | solution.py:154
  126.0 0.0 all-gather.2.cloned.1.call-done.tok_ref
  126.0 5.9 %all-to-all-done.2.dt_ref = bf16[8,96,128]{2,1,0:T(8,128)(2,1)S(1)} async-done(((bf16[8,96,128]{2,1,0:T(8,128)(2,1)}), bf16[8,96,128]{2,1,0:T(8,128)(2,1)S(1)}, u32[]{:S(2)}, u32[]{:S(2)}) %all-to-all-start.2) | async-done | bytes 196640 | tf_op jit(solution)/shard_map/all_to_all | solution.py:154
  131.9 0.0 copy-start.4
  131.9 1.4 copy-done.4
  133.3 0.5 shard_map.87
  133.8 0.1 reshape.40
  133.9 24.5 %all_to_all.31 = bf16[64,9,128]{2,1,0:T(8,128)(2,1)S(1)} all-to-all(bf16[64,9,128]{2,1,0:T(8,128)(2,1)S(1)} %reshape.40), channel_id=1, replica_groups=mesh['x'=4,'y'=4,'z'=16,'c'=2] {'x','z'}, dimensions={0} | all-to-all | bytes 294912 | tf_op jit(solution)/shard_map/all_to_all | solution.py:154
  158.4 0.1 reduce_sum.12
  158.6 26.2 %all_to_all.32 = bf16[64,9,128]{2,1,0:T(8,128)(2,1)S(1)} all-to-all(bf16[64,9,128]{2,1,0:T(8,128)(2,1)S(1)} %broadcast_in_dim.21), channel_id=1, replica_groups=mesh['x'=4,'y'=4,'z'=16,'c'=2] {'x','z'}, dimensions={0} | all-to-all | bytes 294912 | tf_op jit(solution)/shard_map/all_to_all | solution.py:154
  184.7 0.1 broadcast_in_dim.22
  184.8 0.2 broadcast_in_dim.23
  184.9 22.7 %all_to_all.33 = bf16[8,576,128]{2,1,0:T(8,128)(2,1)S(1)} all-to-all(bf16[8,576,128]{2,1,0:T(8,128)(2,1)S(1)} %broadcast_in_dim.23), channel_id=1, replica_groups=mesh['x'=4,'y'=4,'z'=16,'c'=2] {'y','c'}, dimensions={0} | all-to-all | bytes 2359296 | tf_op jit(solution)/shard_map/all_to_all | solution.py:154
  207.7 1.0 copy.14
  208.7 1.3 reshape.42
  210.0 1.1 fusion
  (1 shorter events, 0.0 us)
Async XLA Ops:
  7.9 1.1 copy-start
  8.9 1.1 copy-start.2
  10.0 0.9 copy-start.5
  10.9 0.9 copy-start.6
  14.1 56.2 %all-to-all-start = ((bf16[9,128,2,128]{3,2,0,1:T(2,128)(2,1)}), bf16[9,128,2,128]{3,2,0,1:T(2,128)(2,1)S(1)}, u32[]{:S(2)}, u32[]{:S(2)}) async-start(bf16[9,128,2,128]{3,2,0,1:T(2,128)(2,1)} %copy.10), calls=%async_computation | async-start | bytes 1179648 | tf_op jit(solution)/shard_map/all_to_all | solution.py:172
  34.7 91.4 %all-gather.2.cloned.1.call-start = ((), (), s32[]{:S(2)}) async-start(), calls=%async_computation.6 | async-start | bytes 1769472 | tf_op jit(solution)/shard_map/all_gather | solution.py:159
  75.0 43.6 %copy-start.1 = (bf16[768,384]{1,0:T(8,128)(2,1)S(1)}, bf16[768,384]{1,0:T(8,128)(2,1)}, u32[]{:S(2)}) copy-start(bf16[768,384]{1,0:T(8,128)(2,1)} %ws_ref.3) | copy-start | bytes 1769476
  75.0 43.6 %copy-start.3 = (bf16[768,384]{1,0:T(8,128)(2,1)S(1)}, bf16[768,384]{1,0:T(8,128)(2,1)}, u32[]{:S(2)}) copy-start(bf16[768,384]{1,0:T(8,128)(2,1)} %wv_ref.3) | copy-start | bytes 1769476
  120.4 11.5 %all-to-all-start.2 = ((bf16[8,96,128]{2,1,0:T(8,128)(2,1)}), bf16[8,96,128]{2,1,0:T(8,128)(2,1)S(1)}, u32[]{:S(2)}, u32[]{:S(2)}) async-start(bf16[8,96,128]{2,1,0:T(8,128)(2,1)} %bitcast.8), calls=%async_computation.2 | async-start | bytes 393216 | tf_op jit(solution)/shard_map/all_to_all | solution.py:154
  131.9 1.4 copy-start.4
Sparse Core Ops, SparseCore 0:
  37.6 34.2 all-gather.1

commit v2 on v1

--- a/solution.py
+++ b/solution.py
@@ -16,7 +16,11 @@
 PROJ = 384
 UNUSED = 65536.0
 PLANE = ("y", "c")
-TOK = ("y", "z", "c")
+TOK = ("y", "zh", "zl", "c")
+STEPS = [(dy, dc) for dy in range(4) for dc in range(2)]
+COLUMNS = 96
+PIECE = 36
+SLOT = 40
 
 
 def iota(shape, dim):
@@ -27,7 +31,17 @@
     return lax.dot_general(a, b, (dims, ((), ())), preferred_element_type=F32)
 
 
-def send_kernel(tok_ref, ws_ref, wv_ref, cluster_ref, cot_ref, out_ref, dest_ref):
+def send_kernel(*refs):
+    sources, (out_ref, dest_ref), targets, sems = refs[:5], refs[5:7], refs[7:12], refs[12]
+    copies = [
+        pltpu.make_async_copy(source, target, sems.at[n])
+        for n, (source, target) in enumerate(zip(sources, targets))
+    ]
+    for copy in copies:
+        copy.start()
+    tok_ref, ws_ref, wv_ref, cluster_ref, cot_ref = targets
+    for copy in copies:
+        copy.wait()
     tokens = tok_ref[...]
     shared = dot(tokens, ws_ref[...]).astype(BF16)
     value = dot(tokens, wv_ref[...]).astype(BF16)
@@ -39,7 +53,7 @@
     blank = jnp.zeros((LOCAL, HEAD), BF16)
     pending = None
     for h in range(HEADS):
-        cluster = cluster_ref[h : h + 1, :]
+        cluster = cluster_ref[h]
         member = (sub == cluster).astype(BF16)
         same = dot(member, member, ((0,), (0,)))
         order = jnp.sum(jnp.where(sub < lane, same, 0.0), axis=0, keepdims=True)
@@ -108,9 +122,7 @@
     for h in range(HEADS):
         route = (sub_rows == dest_ref[h : h + 1, :]).astype(BF16)
         block = in_ref[h]
-        turned = dot(block, route, ((0,), (0,))).astype(BF16)
-        dt_ref[h * HEAD : (h + 1) * HEAD, :] = turned[:HEAD]
-        dt_ref[PROJ + h * HEAD : PROJ + (h + 1) * HEAD, :] = turned[HEAD:]
+        dt_ref[h * LOCAL : (h + 1) * LOCAL, :] = dot(block, route, ((0,), (0,))).astype(BF16)
         rows = dot(route, block, ((0,), (0,))).astype(BF16)
         d_shared.append(rows[:, :HEAD])
         d_value.append(rows[:, HEAD:])
@@ -128,21 +140,59 @@
     grad_ref[...] = total.astype(BF16)
 
 
-def partial_kernel(dt_ref, tok_ref, out_ref):
-    total = dot(dt_ref[0], tok_ref[0])
-    for s in range(1, dt_ref.shape[0]):
-        total = total + dot(dt_ref[s], tok_ref[s])
-    part = total.astype(BF16)
-    columns = part.shape[0]
+def partial_kernel(place_ref, dt_ref, *refs):
+    tok_refs, out_ref, scratch = refs[:8], refs[8], refs[9]
+    total = None
+    for n, (dy, dc) in enumerate(STEPS):
+        source = lax.rem(place_ref[0] + 4 - dy, 4) * 2 + lax.rem(place_ref[1] + dc, 2)
+        term = dot(dt_ref[source], tok_refs[n][...])
+        total = term if total is None else total + term
     for k in range(WIDTH // LOCAL):
-        out_ref[k * columns : (k + 1) * columns, :] = part[:, k * LOCAL : (k + 1) * LOCAL]
-
-
-def call(kernel, out, *args):
+        scratch[k * COLUMNS : (k + 1) * COLUMNS, :] = total[:, k * LOCAL : (k + 1) * LOCAL]
+    scratch[16 * PIECE :, :] = jnp.zeros((8, LOCAL), F32)
+    for i in range(16):
+        out_ref[i] = scratch[i * PIECE : i * PIECE + SLOT, :].astype(BF16)
+
+
+def sum_kernel(in_ref, out_ref):
+    total = in_ref[0].astype(F32)
+    for i in range(1, in_ref.shape[0]):
+        total = total + in_ref[i].astype(F32)
+    total = total.astype(BF16)
+    for i in range(out_ref.shape[0]):
+        out_ref[i] = total
+
+
+def finish_kernel(place_ref, mine_ref, other_ref, shared_ref, value_ref, scratch):
+    here = place_ref[1]
+    for y in range(4):
+        for i in range(16):
+            rows = slice(i * PIECE, (i + 1) * PIECE)
+            scratch[here, y, rows, :] = mine_ref[y * 16 + i].astype(F32)[:PIECE]
+            scratch[1 - here, y, rows, :] = other_ref[y * 16 + i].astype(F32)[:PIECE]
+    for k in range(WIDTH // LOCAL):
+        first = k * COLUMNS
+        strip = [scratch[j % 2, j // 2, first : first + COLUMNS, :] for j in range(8)]
+        strip = jnp.concatenate(strip, axis=0)
+        for half, ref in enumerate((shared_ref, value_ref)):
+            heads = [
+                strip[h * LOCAL + half * HEAD : h * LOCAL + (half + 1) * HEAD]
+                for h in range(HEADS)
+            ]
+            ref[k * LOCAL : (k + 1) * LOCAL, :] = jnp.concatenate(heads, axis=0).T.astype(BF16)
+
+
+def call(kernel, out, *args, scratch=(), scalars=0, held=False):
+    space = pl.ANY if held else pltpu.VMEM
+    limit = (60 if held else 48) * 1024 * 1024
+    specs = [pl.BlockSpec(memory_space=pltpu.SMEM)] * scalars
+    specs += [pl.BlockSpec(memory_space=space)] * (len(args) - scalars)
     return pl.pallas_call(
         kernel,
         out_shape=out,
-        compiler_params=pltpu.CompilerParams(vmem_limit_bytes=48 * 1024 * 1024),
+        in_specs=specs,
+        scratch_shapes=scratch,
+        compiler_params=pltpu.CompilerParams(vmem_limit_bytes=limit),
     )(*args)
 
 
@@ -156,15 +206,24 @@
 
 def body(tokens, w_shared, w_value, cluster_ids, slot_index, cotangent):
     rows = tokens[0]
-    plane_rows = lax.all_gather(rows, PLANE, axis=0, tiled=False)
+    place = jnp.stack([lax.axis_index("y"), lax.axis_index("c")]).astype(jnp.int32)
     sent, dest = call(
         send_kernel,
         (shape(9, ROWS, LOCAL), jax.ShapeDtypeStruct((HEADS, LOCAL), jnp.int32)),
         rows,
         w_shared,
         w_value,
-        cluster_ids[0],
+        cluster_ids.transpose(1, 0, 2),
         cotangent[0],
+        scratch=[
+            pltpu.VMEM((LOCAL, WIDTH), BF16),
+            pltpu.VMEM((WIDTH, PROJ), BF16),
+            pltpu.VMEM((WIDTH, PROJ), BF16),
+            pltpu.VMEM((HEADS, 1, LOCAL), jnp.int32),
+            pltpu.VMEM((LOCAL, PROJ), BF16),
+            pltpu.SemaphoreType.DMA((5,)),
+        ],
+        held=True,
     )
 
     def route(blocks):
@@ -172,6 +231,12 @@
         moved = lax.all_to_all(split, TOK, split_axis=1, concat_axis=1, tiled=True)
         return moved.reshape(9, ROWS, LOCAL)
 
+    plane_rows = []
+    for dy, dc in STEPS[1:]:
+        pairs = [
+            (y * 2 + c, (y + dy) % 4 * 2 + (c + dc) % 2) for y in range(4) for c in range(2)
+        ]
+        plane_rows.append(lax.ppermute(rows, PLANE, pairs))
     worked = call(attend_kernel, shape(9, ROWS, LOCAL), route(sent))
     attention, grad_tokens, turned = call(
         return_kernel,
@@ -181,20 +246,35 @@
         w_shared,
         w_value,
     )
-    columns = WIDTH // 8
-    mixed = swap(turned.reshape(8, columns, LOCAL), PLANE)
-    part = call(partial_kernel, shape(6 * columns, LOCAL), mixed, plane_rows)
-    pieces = swap(part.reshape(64, 9, LOCAL), ("x", "z"))
-    piece = jnp.sum(pieces.astype(F32), axis=0).astype(BF16)
-    block = swap(jnp.broadcast_to(piece[None], (64, 9, LOCAL)), ("x", "z"))
-    block = block.reshape(1, 6 * columns, LOCAL)
-    whole = swap(jnp.broadcast_to(block, (8, 6 * columns, LOCAL)), PLANE)
-    whole = whole.reshape(8, 6, columns, LOCAL).transpose(1, 3, 0, 2).reshape(WIDTH, WIDTH)
-    return (attention[None], grad_tokens[None], whole[:, :PROJ], whole[:, PROJ:])
+    mixed = swap(turned.reshape(8, COLUMNS, LOCAL), PLANE)
+    part = call(
+        partial_kernel,
+        shape(16, SLOT, LOCAL),
+        place,
+        mixed,
+        rows,
+        *plane_rows,
+        scratch=[pltpu.VMEM((16 * PIECE + 8, LOCAL), F32)],
+        scalars=1,
+    )
+    part = call(sum_kernel, shape(4, SLOT, LOCAL), swap(part, ("x", "zl")))
+    block = call(sum_kernel, shape(64, SLOT, LOCAL), swap(part, "zh"))
+    block = swap(block, ("y", "x", "zl"))
+    other = lax.ppermute(block, "c", [(0, 1), (1, 0)])
+    grad_shared, grad_value = call(
+        finish_kernel,
+        (shape(WIDTH, PROJ), shape(WIDTH, PROJ)),
+        place,
+        block,
+        other,
+        scratch=[pltpu.VMEM((2, 4, 16 * PIECE, LOCAL), F32)],
+        scalars=1,
+    )
+    return (attention[None], grad_tokens[None], grad_shared, grad_value)
 
 
 def solution(mesh):
-    fine = Mesh(mesh.devices.reshape(4, 4, 16, 2), ("x", "y", "z", "c"))
+    fine = Mesh(mesh.devices.reshape(4, 4, 4, 4, 2), ("x", "y", "zh", "zl", "c"))
     in_specs = (
         P("x", TOK, None),
         P(),

time: 219 us -> 186 us (0.85)
  waiting for transfers between devices: 41.5 us -> 20.4 us
  starting transfers between devices: 26.3 us -> 40.6 us
  between operations: 14.2 us -> 0.83 us
  blocking collectives: 117 us -> 108 us
  local copies, waits for them, and re-layouts: 12.3 us -> 3.62 us
  Pallas kernels: 7.09 us -> 12.1 us
    all_to_all x1, waiting for transfers between devices: 34.9 us -> 5.68 us  [route(): moved = lax.all_to_all(split, TOK, split_axis=1, concat_axis=1, tiled=True)]
    ppermute x0 -> x8, starting transfers between devices: none -> 27.3 us  [the longest x7 22.6 us: body(): plane_rows.append(lax.ppermute(rows, PLANE, pairs))]
    all_to_all x3, blocking collectives: 73.4 us -> 52.1 us  [swap(): return lax.all_to_all(rows, axes, split_axis=0, concat_axis=0, tiled=True)]
    all_to_all x1, starting transfers between devices: 20.6 us -> 7.69 us  [route(): moved = lax.all_to_all(split, TOK, split_axis=1, concat_axis=1, tiled=True)]
    all_to_all x1, blocking collectives: 43.1 us -> 56 us  [route(): moved = lax.all_to_all(split, TOK, split_axis=1, concat_axis=1, tiled=True)]
    ppermute x0 -> x8, waiting for transfers between devices: none -> 8.98 us  [the longest x7 7.28 us: body(): plane_rows.append(lax.ppermute(rows, PLANE, pairs))]
    unnamed x15 -> x8, local copies, waits for them, and re-layouts: 6.05 us -> 0.02 us
    pallas_call x4 -> x7, Pallas kernels: 7.09 us -> 12.1 us  [call(): pl.pallas_call(kernel, out_shape=out, in_specs=specs, scratch_shapes=scra...]
  transfers between devices with their start and end apart: 3 -> 10, of which waited for: 2 -> 4; matrix products, arithmetic and copies ran while one was open for 1% -> 0% of each run, Pallas kernels for 3% -> 1%
where the time goes in v2:
time: 186 us
  blocking collectives  108 us (58%)
  starting transfers between devices  40.6 us (22%)
  waiting for transfers between devices  20.4 us (11%)
  Pallas kernels  12.1 us (7%)
  local copies, waits for them, and re-layouts  3.62 us (2%)
    all_to_all x1, blocking collectives, route(): moved = lax.all_to_all(split, TOK, split_axis=1, concat_axis=1, tiled=True)  56 us
    all_to_all x3, blocking collectives, swap(): return lax.all_to_all(rows, axes, split_axis=0, concat_axis=0, tiled=True)  52.1 us
    ppermute x7, starting transfers between devices, body(): plane_rows.append(lax.ppermute(rows, PLANE, pairs))  22.6 us
    pallas_call x7, Pallas kernels, call(): pl.pallas_call(kernel, out_shape=out, in_specs=specs, scratch_shapes=scra...  12.1 us
    all_to_all x1, starting transfers between devices, route(): moved = lax.all_to_all(split, TOK, split_axis=1, concat_axis=1, tiled=True)  7.69 us
    ppermute x7, waiting for transfers between devices, body(): plane_rows.append(lax.ppermute(rows, PLANE, pairs))  7.28 us
    all_to_all x1, waiting for transfers between devices, swap(): return lax.all_to_all(rows, axes, split_axis=0, concat_axis=0, tiled=True)  5.78 us
    all_to_all x1, waiting for transfers between devices, route(): moved = lax.all_to_all(split, TOK, split_axis=1, concat_axis=1, tiled=True)  5.68 us
  transfers between devices with their start and end apart: 10, of which 4 were waited for; matrix products, arithmetic and copies ran while one was open for 0% of the time, Pallas kernels for 1%

profile of v2, /device:TPU:1, one launch (start us, length us, event | category | flops | bytes accessed | tf_op | source)
XLA Modules:
  0.0 185.8 jit_solution(11763630918754423315)
XLA Ops:
  0.6 3.3 %shard_map.84 = (bf16[9,256,128]{2,1,0:T(8,128)(2,1)}, s32[6,128]{1,0:T(8,128)}) custom-call(bf16[128,768]{1,0:T(8,128)(2,1)} %bitcast.15, bf16[768,384]{1,0:T(8,128)(2,1)} %ws_ref.1, bf16[768,384]{1,0:T(8,128)(2,1)} %wv_ref.1, s32[6,1,128]{2,1,0:T(1,128)} %bitcast.26, bf16[128,384]{1,0:T(8,128)(2,1)} %bitcast.25), custom_call_target="tpu_custom_call" | custom-call | tf_op jit(solution)/shard_map/pallas_call | solution.py:190
  4.0 1.5 copy.9
  5.4 56.0 %all_to_all.30 = bf16[9,128,2,128]{3,2,0,1:T(2,128)(2,1)S(1)} all-to-all(bf16[9,128,2,128]{3,2,0,1:T(2,128)(2,1)S(1)} %copy.9), channel_id=1, replica_groups=mesh['x'=4,'y'=4,'zh'=4,'zl'=4,'c'=2] {'y','zh','zl','c'}, dimensions={1} | all-to-all | bytes 1179648 | tf_op jit(solution)/shard_map/all_to_all | solution.py:231
  61.5 0.5 copy.10
  61.9 3.8 %shard_map.85 = bf16[9,256,128]{2,1,0:T(8,128)(2,1)S(1)} custom-call(bf16[9,256,128]{2,1,0:T(8,128)(2,1)S(1)} %bitcast.13), custom_call_target="tpu_custom_call" | custom-call | tf_op jit(solution)/shard_map/pallas_call | solution.py:190
  65.7 1.2 copy.11
  66.9 0.0 copy-start.2
  66.9 0.0 copy-start.3
  66.9 7.7 %all-to-all-start.1 = ((bf16[9,128,2,128]{3,2,0,1:T(2,128)(2,1)}), bf16[9,128,2,128]{3,2,0,1:T(2,128)(2,1)S(1)}, u32[]{:S(2)}, u32[]{:S(2)}) async-start(bf16[9,128,2,128]{3,2,0,1:T(2,128)(2,1)} %copy.11), calls=%async_computation.1 | async-start | bytes 1179648 | tf_op jit(solution)/shard_map/all_to_all | solution.py:231
  74.6 0.0 copy-done.2
  74.6 0.0 copy-start
  74.6 0.0 copy-start.1
  74.7 5.4 %collective-permute-start.6 = (bf16[128,768]{1,0:T(8,128)(2,1)S(1)}, bf16[128,768]{1,0:T(8,128)(2,1)S(1)}, u32[]{:S(2)}, u32[]{:S(2)}) collective-permute-start(bf16[128,768]{1,0:T(8,128)(2,1)S(1)} %bitcast.16), channel_id=1, source_target_pairs={{0,97},{1,96},{32,1},{33,0},{64,33},{65,32},{96,65},{97,64},{2,99}... | collective-permute-start | bytes 589832 | tf_op jit(solution)/shard_map/ppermute | solution.py:239
  80.1 2.3 %collective-permute-start.5 = (bf16[128,768]{1,0:T(8,128)(2,1)S(1)}, bf16[128,768]{1,0:T(8,128)(2,1)S(1)}, u32[]{:S(2)}, u32[]{:S(2)}) collective-permute-start(bf16[128,768]{1,0:T(8,128)(2,1)S(1)} %bitcast.17), channel_id=1, source_target_pairs={{0,96},{1,97},{32,0},{33,1},{64,32},{65,33},{96,64},{97,65},{2,98}... | collective-permute-start | bytes 589832 | tf_op jit(solution)/shard_map/ppermute | solution.py:239
  82.4 2.0 %collective-permute-start.4 = (bf16[128,768]{1,0:T(8,128)(2,1)S(1)}, bf16[128,768]{1,0:T(8,128)(2,1)S(1)}, u32[]{:S(2)}, u32[]{:S(2)}) collective-permute-start(bf16[128,768]{1,0:T(8,128)(2,1)S(1)} %bitcast.18), channel_id=1, source_target_pairs={{0,65},{1,64},{32,97},{33,96},{64,1},{65,0},{96,33},{97,32},{2,67}... | collective-permute-start | bytes 589832 | tf_op jit(solution)/shard_map/ppermute | solution.py:239
  84.3 5.1 %collective-permute-start.3 = (bf16[128,768]{1,0:T(8,128)(2,1)S(1)}, bf16[128,768]{1,0:T(8,128)(2,1)S(1)}, u32[]{:S(2)}, u32[]{:S(2)}) collective-permute-start(bf16[128,768]{1,0:T(8,128)(2,1)S(1)} %bitcast.19), channel_id=1, source_target_pairs={{0,64},{1,65},{32,96},{33,97},{64,0},{65,1},{96,32},{97,33},{2,66}... | collective-permute-start | bytes 589832 | tf_op jit(solution)/shard_map/ppermute | solution.py:239
  89.5 3.2 %collective-permute-start.2 = (bf16[128,768]{1,0:T(8,128)(2,1)S(1)}, bf16[128,768]{1,0:T(8,128)(2,1)S(1)}, u32[]{:S(2)}, u32[]{:S(2)}) collective-permute-start(bf16[128,768]{1,0:T(8,128)(2,1)S(1)} %bitcast.20), channel_id=1, source_target_pairs={{0,33},{1,32},{32,65},{33,64},{64,97},{65,96},{96,1},{97,0},{2,35}... | collective-permute-start | bytes 589832 | tf_op jit(solution)/shard_map/ppermute | solution.py:239
  92.7 0.0 collective-permute-done.6.refs_7_
  92.8 1.9 %collective-permute-start.1 = (bf16[128,768]{1,0:T(8,128)(2,1)S(1)}, bf16[128,768]{1,0:T(8,128)(2,1)S(1)}, u32[]{:S(2)}, u32[]{:S(2)}) collective-permute-start(bf16[128,768]{1,0:T(8,128)(2,1)S(1)} %bitcast.21), channel_id=1, source_target_pairs={{0,32},{1,33},{32,64},{33,65},{64,96},{65,97},{96,0},{97,1},{2,34}... | collective-permute-start | bytes 589832 | tf_op jit(solution)/shard_map/ppermute | solution.py:239
  94.7 7.3 %collective-permute-done.5.refs_6_ = bf16[128,768]{1,0:T(8,128)(2,1)S(1)} collective-permute-done((bf16[128,768]{1,0:T(8,128)(2,1)S(1)}, bf16[128,768]{1,0:T(8,128)(2,1)S(1)}, u32[]{:S(2)}, u32[]{:S(2)}) %collective-permute-start.5) | collective-permute-done | bytes 196640 | tf_op jit(solution)/shard_map/ppermute | solution.py:239
  101.9 2.6 %collective-permute-start = (bf16[128,768]{1,0:T(8,128)(2,1)S(1)}, bf16[128,768]{1,0:T(8,128)(2,1)S(1)}, u32[]{:S(2)}, u32[]{:S(2)}) collective-permute-start(bf16[128,768]{1,0:T(8,128)(2,1)S(1)} %bitcast.22), channel_id=1, source_target_pairs={{0,1},{1,0},{32,33},{33,32},{64,65},{65,64},{96,97},{97,96},{2,3},... | collective-permute-start | bytes 589832 | tf_op jit(solution)/shard_map/ppermute | solution.py:239
  104.6 5.7 %all-to-all-done.1 = bf16[9,128,2,128]{3,2,0,1:T(2,128)(2,1)S(1)} async-done(((bf16[9,128,2,128]{3,2,0,1:T(2,128)(2,1)}), bf16[9,128,2,128]{3,2,0,1:T(2,128)(2,1)S(1)}, u32[]{:S(2)}, u32[]{:S(2)}) %all-to-all-start.1) | async-done | bytes 589856 | tf_op jit(solution)/shard_map/all_to_all | solution.py:231
  110.3 0.5 copy.12
  110.7 0.0 copy-done.3
  110.7 0.0 copy-done
  110.7 0.0 copy-done.1
  110.8 1.8 shard_map.86
  112.5 5.6 %all-to-all-start.2 = ((bf16[8,96,128]{2,1,0:T(8,128)(2,1)}), bf16[8,96,128]{2,1,0:T(8,128)(2,1)S(1)}, u32[]{:S(2)}, u32[]{:S(2)}) async-start(bf16[8,96,128]{2,1,0:T(8,128)(2,1)} %bitcast.11), calls=%async_computation.2 | async-start | bytes 393216 | tf_op jit(solution)/shard_map/all_to_all | solution.py:204
  118.2 0.1 pad_add_fusion.place_ref
  118.2 0.0 collective-permute-done.4.refs_5_
  118.2 0.0 collective-permute-done.3.refs_4_
  118.2 0.0 collective-permute-done.2.refs_3_
  118.2 0.0 collective-permute-done.1.refs_2_
  118.3 0.0 collective-permute-done.refs_1_
  118.3 5.8 %all-to-all-done.2.dt_ref = bf16[8,96,128]{2,1,0:T(8,128)(2,1)S(1)} async-done(((bf16[8,96,128]{2,1,0:T(8,128)(2,1)}), bf16[8,96,128]{2,1,0:T(8,128)(2,1)S(1)}, u32[]{:S(2)}, u32[]{:S(2)}) %all-to-all-start.2) | async-done | bytes 196640 | tf_op jit(solution)/shard_map/all_to_all | solution.py:204
  124.0 1.0 shard_map.87
  125.1 12.0 %all_to_all.31.in_ref = bf16[16,40,128]{2,1,0:T(8,128)(2,1)S(1)} all-to-all(bf16[16,40,128]{2,1,0:T(8,128)(2,1)S(1)} %shard_map.87), channel_id=1, replica_groups=mesh['x'=4,'y'=4,'zh'=4,'zl'=4,'c'=2] {'x','zl'}, dimensions={0} | all-to-all | bytes 327680 | tf_op jit(solution)/shard_map/all_to_all | solution.py:204
  137.1 16.0 %all_to_all.32.in_ref = bf16[4,40,128]{2,1,0:T(8,128)(2,1)S(1)} all-to-all(bf16[4,40,128]{2,1,0:T(8,128)(2,1)S(1)} %shard_map.88), channel_id=1, replica_groups=mesh['x'=4,'y'=4,'zh'=4,'zl'=4,'c'=2] {'zh'}, dimensions={0} | all-to-all | bytes 81920 | tf_op jit(solution)/shard_map/all_to_all | solution.py:204
  153.2 24.0 %all_to_all.33.mine_ref = bf16[64,40,128]{2,1,0:T(8,128)(2,1)S(1)} all-to-all(bf16[64,40,128]{2,1,0:T(8,128)(2,1)S(1)} %shard_map.89), channel_id=1, replica_groups=mesh['x'=4,'y'=4,'zh'=4,'zl'=4,'c'=2] {'y','x','zl'}, dimensions={0} | all-to-all | bytes 1310720 | tf_op jit(solution)/shard_map/all_to_all | solution.py:204
  177.3 4.7 %collective-permute-start.7 = (bf16[64,40,128]{2,1,0:T(8,128)(2,1)S(1)}, bf16[64,40,128]{2,1,0:T(8,128)(2,1)S(1)}, u32[]{:S(2)}, u32[]{:S(2)}) collective-permute-start(bf16[64,40,128]{2,1,0:T(8,128)(2,1)S(1)} %all_to_all.33.mine_ref), channel_id=1, source_target_pairs={{0,1},{1,0},{2,3},{3,2},{4,5},{5,4},{6,7},{7,6},{8,9},{9,8},{10,11... | collective-permute-start | bytes 1966088 | tf_op jit(solution)/shard_map/ppermute | solution.py:263
  181.9 1.7 collective-permute-done.7.other_ref
  183.6 2.1 %shard_map.90 = (bf16[768,384]{1,0:T(8,128)(2,1)}, bf16[768,384]{1,0:T(8,128)(2,1)}) custom-call(s32[2]{0:T(128)S(1)} %pad_add_fusion.place_ref, bf16[64,40,128]{2,1,0:T(8,128)(2,1)S(1)} %all_to_all.33.mine_ref, bf16[64,40,128]{2,1,0:T(8,128)(2,1)S(1)} %collective-permute-done.7.other_ref), custom_call_target="tpu_custom_call" | custom-call | tf_op jit(solution)/shard_map/pallas_call | solution.py:190
  (2 shorter events, 0.1 us)
Async XLA Ops:
  66.9 7.7 %copy-start.2 = (bf16[1,128,768]{2,1,0:T(8,128)(2,1)S(1)}, bf16[1,128,768]{2,1,0:T(8,128)(2,1)}, u32[]{:S(2)}) copy-start(bf16[1,128,768]{2,1,0:T(8,128)(2,1)} %param.6) | copy-start | bytes 589828
  66.9 43.8 %copy-start.3 = (s32[6,128]{1,0:T(8,128)S(1)}, s32[6,128]{1,0:T(8,128)}, u32[]{:S(2)}) copy-start(s32[6,128]{1,0:T(8,128)} %get-tuple-element.12.dest_ref) | copy-start | bytes 9220
  66.9 43.3 %all-to-all-start.1 = ((bf16[9,128,2,128]{3,2,0,1:T(2,128)(2,1)}), bf16[9,128,2,128]{3,2,0,1:T(2,128)(2,1)S(1)}, u32[]{:S(2)}, u32[]{:S(2)}) async-start(bf16[9,128,2,128]{3,2,0,1:T(2,128)(2,1)} %copy.11), calls=%async_computation.1 | async-start | bytes 1179648 | tf_op jit(solution)/shard_map/all_to_all | solution.py:231
  74.6 36.1 %copy-start = (bf16[768,384]{1,0:T(8,128)(2,1)S(1)}, bf16[768,384]{1,0:T(8,128)(2,1)}, u32[]{:S(2)}) copy-start(bf16[768,384]{1,0:T(8,128)(2,1)} %ws_ref.1) | copy-start | bytes 1769476
  74.6 36.1 %copy-start.1 = (bf16[768,384]{1,0:T(8,128)(2,1)S(1)}, bf16[768,384]{1,0:T(8,128)(2,1)}, u32[]{:S(2)}) copy-start(bf16[768,384]{1,0:T(8,128)(2,1)} %wv_ref.1) | copy-start | bytes 1769476
  74.7 18.1 %collective-permute-start.6 = (bf16[128,768]{1,0:T(8,128)(2,1)S(1)}, bf16[128,768]{1,0:T(8,128)(2,1)S(1)}, u32[]{:S(2)}, u32[]{:S(2)}) collective-permute-start(bf16[128,768]{1,0:T(8,128)(2,1)S(1)} %bitcast.16), channel_id=1, source_target_pairs={{0,97},{1,96},{32,1},{33,0},{64,33},{65,32},{96,65},{97,64},{2,99}... | collective-permute-start | bytes 589832 | tf_op jit(solution)/shard_map/ppermute | solution.py:239
  80.1 21.9 %collective-permute-start.5 = (bf16[128,768]{1,0:T(8,128)(2,1)S(1)}, bf16[128,768]{1,0:T(8,128)(2,1)S(1)}, u32[]{:S(2)}, u32[]{:S(2)}) collective-permute-start(bf16[128,768]{1,0:T(8,128)(2,1)S(1)} %bitcast.17), channel_id=1, source_target_pairs={{0,96},{1,97},{32,0},{33,1},{64,32},{65,33},{96,64},{97,65},{2,98}... | collective-permute-start | bytes 589832 | tf_op jit(solution)/shard_map/ppermute | solution.py:239
  82.4 35.9 %collective-permute-start.4 = (bf16[128,768]{1,0:T(8,128)(2,1)S(1)}, bf16[128,768]{1,0:T(8,128)(2,1)S(1)}, u32[]{:S(2)}, u32[]{:S(2)}) collective-permute-start(bf16[128,768]{1,0:T(8,128)(2,1)S(1)} %bitcast.18), channel_id=1, source_target_pairs={{0,65},{1,64},{32,97},{33,96},{64,1},{65,0},{96,33},{97,32},{2,67}... | collective-permute-start | bytes 589832 | tf_op jit(solution)/shard_map/ppermute | solution.py:239
  84.3 33.9 %collective-permute-start.3 = (bf16[128,768]{1,0:T(8,128)(2,1)S(1)}, bf16[128,768]{1,0:T(8,128)(2,1)S(1)}, u32[]{:S(2)}, u32[]{:S(2)}) collective-permute-start(bf16[128,768]{1,0:T(8,128)(2,1)S(1)} %bitcast.19), channel_id=1, source_target_pairs={{0,64},{1,65},{32,96},{33,97},{64,0},{65,1},{96,32},{97,33},{2,66}... | collective-permute-start | bytes 589832 | tf_op jit(solution)/shard_map/ppermute | solution.py:239
  89.5 28.8 %collective-permute-start.2 = (bf16[128,768]{1,0:T(8,128)(2,1)S(1)}, bf16[128,768]{1,0:T(8,128)(2,1)S(1)}, u32[]{:S(2)}, u32[]{:S(2)}) collective-permute-start(bf16[128,768]{1,0:T(8,128)(2,1)S(1)} %bitcast.20), channel_id=1, source_target_pairs={{0,33},{1,32},{32,65},{33,64},{64,97},{65,96},{96,1},{97,0},{2,35}... | collective-permute-start | bytes 589832 | tf_op jit(solution)/shard_map/ppermute | solution.py:239
  92.8 25.5 %collective-permute-start.1 = (bf16[128,768]{1,0:T(8,128)(2,1)S(1)}, bf16[128,768]{1,0:T(8,128)(2,1)S(1)}, u32[]{:S(2)}, u32[]{:S(2)}) collective-permute-start(bf16[128,768]{1,0:T(8,128)(2,1)S(1)} %bitcast.21), channel_id=1, source_target_pairs={{0,32},{1,33},{32,64},{33,65},{64,96},{65,97},{96,0},{97,1},{2,34}... | collective-permute-start | bytes 589832 | tf_op jit(solution)/shard_map/ppermute | solution.py:239
  101.9 16.3 %collective-permute-start = (bf16[128,768]{1,0:T(8,128)(2,1)S(1)}, bf16[128,768]{1,0:T(8,128)(2,1)S(1)}, u32[]{:S(2)}, u32[]{:S(2)}) collective-permute-start(bf16[128,768]{1,0:T(8,128)(2,1)S(1)} %bitcast.22), channel_id=1, source_target_pairs={{0,1},{1,0},{32,33},{33,32},{64,65},{65,64},{96,97},{97,96},{2,3},... | collective-permute-start | bytes 589832 | tf_op jit(solution)/shard_map/ppermute | solution.py:239
  112.5 11.5 %all-to-all-start.2 = ((bf16[8,96,128]{2,1,0:T(8,128)(2,1)}), bf16[8,96,128]{2,1,0:T(8,128)(2,1)S(1)}, u32[]{:S(2)}, u32[]{:S(2)}) async-start(bf16[8,96,128]{2,1,0:T(8,128)(2,1)} %bitcast.11), calls=%async_computation.2 | async-start | bytes 393216 | tf_op jit(solution)/shard_map/all_to_all | solution.py:204
  177.3 6.4 %collective-permute-start.7 = (bf16[64,40,128]{2,1,0:T(8,128)(2,1)S(1)}, bf16[64,40,128]{2,1,0:T(8,128)(2,1)S(1)}, u32[]{:S(2)}, u32[]{:S(2)}) collective-permute-start(bf16[64,40,128]{2,1,0:T(8,128)(2,1)S(1)} %all_to_all.33.mine_ref), channel_id=1, source_target_pairs={{0,1},{1,0},{2,3},{3,2},{4,5},{5,4},{6,7},{7,6},{8,9},{9,8},{10,11... | collective-permute-start | bytes 1966088 | tf_op jit(solution)/shard_map/ppermute | solution.py:263

commit v3 on v2

--- a/solution.py
+++ b/solution.py
@@ -17,10 +17,12 @@
 UNUSED = 65536.0
 PLANE = ("y", "c")
 TOK = ("y", "zh", "zl", "c")
+OWNERS = ("y", "c", "zh", "zl")
 STEPS = [(dy, dc) for dy in range(4) for dc in range(2)]
 COLUMNS = 96
 PIECE = 36
 SLOT = 40
+BLOCK = 16
 
 
 def iota(shape, dim):
@@ -32,7 +34,7 @@
 
 
 def send_kernel(*refs):
-    sources, (out_ref, dest_ref), targets, sems = refs[:5], refs[5:7], refs[7:12], refs[12]
+    sources, (out_ref, ext_ref), targets, sems = refs[:5], refs[5:7], refs[7:12], refs[12]
     copies = [
         pltpu.make_async_copy(source, target, sems.at[n])
         for n, (source, target) in enumerate(zip(sources, targets))
@@ -43,6 +45,7 @@
     for copy in copies:
         copy.wait()
     tokens = tok_ref[...]
+    ext_ref[:LOCAL, :] = tokens
     shared = dot(tokens, ws_ref[...]).astype(BF16)
     value = dot(tokens, wv_ref[...]).astype(BF16)
     cot = cot_ref[...]
@@ -57,8 +60,11 @@
         member = (sub == cluster).astype(BF16)
         same = dot(member, member, ((0,), (0,)))
         order = jnp.sum(jnp.where(sub < lane, same, 0.0), axis=0, keepdims=True)
-        dest = cluster * 2 + order.astype(jnp.int32)
-        dest_ref[h : h + 1, :] = dest
+        owner = (cluster & 96) + (cluster & 1) * 16 + ((cluster >> 1) & 15)
+        dest = owner * 2 + order.astype(jnp.int32)
+        ext_ref[LOCAL:, h * LOCAL : (h + 1) * LOCAL] = jnp.broadcast_to(
+            dest.astype(F32), (16, LOCAL)
+        ).astype(BF16)
         hit = sub_rows == dest
         used = jnp.sum(jnp.where(hit, 1.0, 0.0), axis=1, keepdims=True)
         cols = slice(h * HEAD, (h + 1) * HEAD)
@@ -73,9 +79,28 @@
             out_ref[HEADS + h // 2] = (pending + moved[:, LOCAL:]).astype(BF16)
 
 
+def position(row):
+    return (row & 192) + ((row >> 1) & 15) * 4 + ((row >> 5) & 1) * 2 + (row & 1)
+
+
+def spread(block, slot):
+    rows = block.shape[0] // 8
+    turned = [block[:rows]]
+    for p in range(1, 8):
+        turned.append(pltpu.roll(block[p * rows : (p + 1) * rows], BLOCK * p, 1))
+    parts = []
+    for m in range(8):
+        part = turned[-m % 8]
+        for q in range(1, 8):
+            part = jnp.where(slot == q, turned[(q - m) % 8], part)
+        parts.append(part)
+    return parts
+
+
 def attend_kernel(in_ref, out_ref):
     lane_rows = iota((ROWS, LOCAL), 1)
-    causal = iota((ROWS, ROWS), 1) <= iota((ROWS, ROWS), 0)
+    causal = position(iota((ROWS, ROWS), 1)) <= position(iota((ROWS, ROWS), 0))
+    slot = iota((ROWS // 8, LOCAL), 1) >> 4
     pending = None
     for h in range(HEADS):
         block = in_ref[h]
@@ -104,54 +129,92 @@
         delta = jnp.sum(wide_probs * d_prob, axis=1, keepdims=True)
         d_score = (wide_probs * (d_prob - delta)).astype(BF16)
         both = dot(d_score, shared) + dot(d_score, shared, ((0,), (0,)))
-        d_shared = (both * 0.125).astype(BF16)
-        d_value = dot(probs, cot, ((0,), (0,))).astype(BF16)
-        out_ref[h] = jnp.concatenate([d_shared, d_value], axis=1)
+        d_value = dot(probs, cot, ((0,), (0,)))
+        for m, part in enumerate(spread(jnp.concatenate([both * 0.125, d_value], axis=1), slot)):
+            n = h * 8 + m
+            out_ref[n // 6 * 9 + n % 6] = part.astype(BF16)
         if h % 2 == 0:
-            pending = out.astype(BF16)
+            pending = out
         else:
-            out_ref[HEADS + h // 2] = jnp.concatenate([pending, out.astype(BF16)], axis=1)
-
-
-def return_kernel(in_ref, dest_ref, ws_ref, wv_ref, att_ref, grad_ref, dt_ref):
-    sub_rows = iota((ROWS, LOCAL), 0)
-    lane = iota((LOCAL, LOCAL), 1)
-    d_shared = []
-    d_value = []
-    pending = None
-    for h in range(HEADS):
-        route = (sub_rows == dest_ref[h : h + 1, :]).astype(BF16)
-        block = in_ref[h]
-        dt_ref[h * LOCAL : (h + 1) * LOCAL, :] = dot(block, route, ((0,), (0,))).astype(BF16)
-        rows = dot(route, block, ((0,), (0,))).astype(BF16)
-        d_shared.append(rows[:, :HEAD])
-        d_value.append(rows[:, HEAD:])
-        pair = dot(route, in_ref[HEADS + h // 2], ((0,), (0,)))
-        if h % 2 == 0:
-            pending = pair
-        else:
-            k = h // 2
-            att_ref[:, k * LOCAL : (k + 1) * LOCAL] = jnp.where(
-                lane < HEAD, pending, pair
-            ).astype(BF16)
-    left = jnp.concatenate(d_shared, axis=1)
-    right = jnp.concatenate(d_value, axis=1)
-    total = dot(left, ws_ref[...], ((1,), (1,))) + dot(right, wv_ref[...], ((1,), (1,)))
-    grad_ref[...] = total.astype(BF16)
-
-
-def partial_kernel(place_ref, dt_ref, *refs):
-    tok_refs, out_ref, scratch = refs[:8], refs[8], refs[9]
+            for m, part in enumerate(spread(jnp.concatenate([pending, out], axis=1), slot)):
+                n = h // 2 * 8 + m
+                out_ref[n // 3 * 9 + 6 + n % 3] = part.astype(BF16)
+
+
+def index_of(place_ref, dy, dc):
+    return lax.rem(place_ref[0] + dy, 4) * 2 + lax.rem(place_ref[1] + dc, 2)
+
+
+def gather_columns(place_ref, in_ref, base, count, turn, exts, dests, out_ref, first):
+    j = place_ref[0] * 2 + place_ref[1]
+    head = (j * 3 // 4, (j * 6 + 5) // 8)
+    lane_slot = iota((ROWS, LOCAL), 1) >> 4
+    sub_rows = iota((ROWS, LOCAL), 0).astype(F32)
+    for n, (dy, dc) in enumerate(STEPS):
+        source = index_of(place_ref, 4 - dy, dc)
+        for i in range(2):
+            lanes = pl.ds(pl.multiple_of(head[i] * LOCAL, LOCAL), LOCAL)
+            dests[i, source] = exts[n][LOCAL:, lanes].astype(F32)[:8]
+    shift = lax.rem(j * turn, 8) * BLOCK
+    turned = [pltpu.roll(in_ref[base + b].astype(F32), shift, 1) for b in range(count)]
+    limit = lax.rem(j, 4)
+    limit = jnp.where(limit == 1, 1, jnp.where(limit == 2, 2, 3)) * count
+    for p in range(8):
+        rows = turned[0]
+        for b in range(1, count):
+            rows = jnp.where(lane_slot == (b + p) % 8, turned[b], rows)
+        rows = rows.astype(BF16)
+        found = [
+            dot(rows, (sub_rows == dests[i, p, :1]).astype(BF16), ((0,), (0,))) for i in range(2)
+        ]
+        blocks = []
+        for b in range(count):
+            cut = slice((b + p) % 8 * BLOCK, ((b + p) % 8 + 1) * BLOCK)
+            blocks.append(jnp.where(b * 3 < limit, found[0][cut], found[1][cut]))
+        out_ref[p, first : first + count * BLOCK, :] = jnp.concatenate(blocks, axis=0).astype(BF16)
+
+
+def partial_kernel(place_ref, in_ref, *refs):
+    exts, (out_ref, cols_ref), (dests, scratch) = refs[:8], refs[8:10], refs[10:]
+    gather_columns(place_ref, in_ref, 0, 6, 2, exts, dests, cols_ref, 0)
     total = None
     for n, (dy, dc) in enumerate(STEPS):
-        source = lax.rem(place_ref[0] + 4 - dy, 4) * 2 + lax.rem(place_ref[1] + dc, 2)
-        term = dot(dt_ref[source], tok_refs[n][...])
+        source = index_of(place_ref, 4 - dy, dc)
+        term = dot(cols_ref[source], exts[n][:LOCAL, :])
         total = term if total is None else total + term
     for k in range(WIDTH // LOCAL):
         scratch[k * COLUMNS : (k + 1) * COLUMNS, :] = total[:, k * LOCAL : (k + 1) * LOCAL]
     scratch[16 * PIECE :, :] = jnp.zeros((8, LOCAL), F32)
     for i in range(16):
         out_ref[i] = scratch[i * PIECE : i * PIECE + SLOT, :].astype(BF16)
+
+
+def forward_kernel(place_ref, in_ref, cols_ref, *refs):
+    exts, outs, (dests, scratch) = refs[:8], refs[8:16], refs[16:]
+    gather_columns(place_ref, in_ref, 6, 3, 5, exts, dests, scratch, 0)
+    for n, (dy, dc) in enumerate(STEPS):
+        target = index_of(place_ref, dy, dc)
+        outs[n][:COLUMNS, :] = cols_ref[target]
+        outs[n][COLUMNS:, :] = scratch[target]
+
+
+def return_kernel(place_ref, *refs):
+    parts, (ws_ref, wv_ref), (att_ref, grad_ref), held = refs[:8], refs[8:10], refs[10:12], refs[12]
+    for n, (dy, dc) in enumerate(STEPS):
+        held[index_of(place_ref, 4 - dy, dc)] = parts[n][...]
+
+    def columns(blocks, per, first):
+        rows = [
+            held[n // per, first + n % per * BLOCK : first + (n % per + 1) * BLOCK, :]
+            for n in blocks
+        ]
+        return jnp.concatenate(rows, axis=0).astype(F32).T.astype(BF16)
+
+    left = columns([h * 8 + m for h in range(HEADS) for m in range(4)], 6, 0)
+    right = columns([h * 8 + 4 + m for h in range(HEADS) for m in range(4)], 6, 0)
+    att_ref[...] = columns(range(24), 3, COLUMNS)
+    total = dot(left, ws_ref[...], ((1,), (1,))) + dot(right, wv_ref[...], ((1,), (1,)))
+    grad_ref[...] = total.astype(BF16)
 
 
 def sum_kernel(in_ref, out_ref):
@@ -207,9 +270,9 @@
 def body(tokens, w_shared, w_value, cluster_ids, slot_index, cotangent):
     rows = tokens[0]
     place = jnp.stack([lax.axis_index("y"), lax.axis_index("c")]).astype(jnp.int32)
-    sent, dest = call(
+    sent, ext = call(
         send_kernel,
-        (shape(9, ROWS, LOCAL), jax.ShapeDtypeStruct((HEADS, LOCAL), jnp.int32)),
+        (shape(9, ROWS, LOCAL), shape(LOCAL + 16, WIDTH)),
         rows,
         w_shared,
         w_value,
@@ -226,40 +289,57 @@
         held=True,
     )
 
-    def route(blocks):
-        split = blocks.reshape(9, LOCAL, 2, LOCAL)
-        moved = lax.all_to_all(split, TOK, split_axis=1, concat_axis=1, tiled=True)
-        return moved.reshape(9, ROWS, LOCAL)
-
-    plane_rows = []
-    for dy, dc in STEPS[1:]:
-        pairs = [
-            (y * 2 + c, (y + dy) % 4 * 2 + (c + dc) % 2) for y in range(4) for c in range(2)
-        ]
-        plane_rows.append(lax.ppermute(rows, PLANE, pairs))
-    worked = call(attend_kernel, shape(9, ROWS, LOCAL), route(sent))
-    attention, grad_tokens, turned = call(
+    def exchange(mine):
+        parts = []
+        for part, (dy, dc) in zip(mine, STEPS):
+            pairs = [
+                (y * 2 + c, (y + dy) % 4 * 2 + (c + dc) % 2) for y in range(4) for c in range(2)
+            ]
+            parts.append(lax.ppermute(part, PLANE, pairs) if dy or dc else part)
+        return parts
+
+    arrived = swap(sent.reshape(9, LOCAL, 2, LOCAL).transpose(1, 0, 2, 3), OWNERS)
+    arrived = arrived.transpose(1, 0, 2, 3)
+    worked = call(attend_kernel, shape(72, 32, LOCAL), arrived.reshape(9, ROWS, LOCAL))
+    worked = worked.reshape(8, 9, 16, 2, LOCAL).transpose(0, 2, 1, 3, 4)
+    back = swap(worked.reshape(LOCAL, 9, 2, LOCAL), OWNERS)
+    back = back.transpose(1, 0, 2, 3).reshape(9, ROWS, LOCAL)
+    exts = exchange([ext] * 8)
+    part, cols = call(
+        partial_kernel,
+        (shape(16, SLOT, LOCAL), shape(8, COLUMNS, LOCAL)),
+        place,
+        back,
+        *exts,
+        scratch=[pltpu.VMEM((2, 8, 8, LOCAL), F32), pltpu.VMEM((16 * PIECE + 8, LOCAL), F32)],
+        scalars=1,
+    )
+    parts = call(
+        forward_kernel,
+        tuple(shape(COLUMNS * 3 // 2, LOCAL) for _ in STEPS),
+        place,
+        back,
+        cols,
+        *exts,
+        scratch=[pltpu.VMEM((2, 8, 8, LOCAL), F32), pltpu.VMEM((8, COLUMNS // 2, LOCAL), BF16)],
+        scalars=1,
+    )
+    part = call(sum_kernel, shape(4, SLOT, LOCAL), swap(part, ("x", "zl")))
+    part, parts = lax.optimization_barrier((part, parts))
+    block = call(sum_kernel, shape(64, SLOT, LOCAL), swap(part, "zh"))
+    block, parts = lax.optimization_barrier((block, exchange(parts)))
+    attention, grad_tokens = call(
         return_kernel,
-        (shape(LOCAL, PROJ), shape(LOCAL, WIDTH), shape(WIDTH, LOCAL)),
-        route(worked),
-        dest,
+        (shape(LOCAL, PROJ), shape(LOCAL, WIDTH)),
+        place,
+        *parts,
         w_shared,
         w_value,
-    )
-    mixed = swap(turned.reshape(8, COLUMNS, LOCAL), PLANE)
-    part = call(
-        partial_kernel,
-        shape(16, SLOT, LOCAL),
-        place,
-        mixed,
-        rows,
-        *plane_rows,
-        scratch=[pltpu.VMEM((16 * PIECE + 8, LOCAL), F32)],
+        scratch=[pltpu.VMEM((8, COLUMNS * 3 // 2, LOCAL), BF16)],
         scalars=1,
     )
-    part = call(sum_kernel, shape(4, SLOT, LOCAL), swap(part, ("x", "zl")))
-    block = call(sum_kernel, shape(64, SLOT, LOCAL), swap(part, "zh"))
     block = swap(block, ("y", "x", "zl"))
+    block, attention, grad_tokens = lax.optimization_barrier((block, attention, grad_tokens))
     other = lax.ppermute(block, "c", [(0, 1), (1, 0)])
     grad_shared, grad_value = call(
         finish_kernel,

time: 186 us -> 199 us (1.070)
  blocking collectives: 108 us -> 54.9 us
  starting transfers between devices: 40.6 us -> 78.2 us
  waiting for transfers between devices: 20.4 us -> 42.9 us
  Pallas kernels: 12.1 us -> 17.1 us
    all_to_all x1 -> x0, blocking collectives: 56 us -> none  [route(): moved = lax.all_to_all(split, TOK, split_axis=1, concat_axis=1, tiled=True)]
    all_to_all x1 -> x4, waiting for transfers between devices: 5.78 us -> 37 us  [swap(): return lax.all_to_all(rows, axes, split_axis=0, concat_axis=0, tiled=True)]
    ppermute x7 -> x14, starting transfers between devices: 22.6 us -> 46.8 us  [exchange(): parts.append(lax.ppermute(part, PLANE, pairs) if dy or dc else part)]
    all_to_all x1 -> x4, starting transfers between devices: 5.64 us -> 27.9 us  [swap(): return lax.all_to_all(rows, axes, split_axis=0, concat_axis=0, tiled=True)]
    all_to_all x1 -> x0, starting transfers between devices: 7.69 us -> none  [route(): moved = lax.all_to_all(split, TOK, split_axis=1, concat_axis=1, tiled=True)]
    all_to_all x1 -> x0, waiting for transfers between devices: 5.68 us -> none  [route(): moved = lax.all_to_all(split, TOK, split_axis=1, concat_axis=1, tiled=True)]
    pallas_call x7 -> x8, Pallas kernels: 12.1 us -> 17.1 us  [call(): pl.pallas_call(kernel, out_shape=out, in_specs=specs, scratch_shapes=scra...]
    ppermute x7 -> x14, waiting for transfers between devices: 7.28 us -> 4.25 us  [exchange(): parts.append(lax.ppermute(part, PLANE, pairs) if dy or dc else part)]
  transfers between devices with their start and end apart: 10 -> 19, of which waited for: 4 -> 6; matrix products, arithmetic and copies ran while one was open for 0% -> 0% of each run, Pallas kernels for 1% -> 2%
where the time goes in v3:
time: 199 us; the launch traced here: 198 us
  starting transfers between devices  78.2 us (39%)
  blocking collectives  54.9 us (28%)
  waiting for transfers between devices  42.9 us (22%)
  Pallas kernels  17.1 us (9%)
  local copies, waits for them, and re-layouts  3.61 us (2%)
    all_to_all x1, blocking collectives, swap(): return lax.all_to_all(rows, axes, split_axis=0, concat_axis=0, tiled=True)  54.9 us
    ppermute x14, starting transfers between devices, exchange(): parts.append(lax.ppermute(part, PLANE, pairs) if dy or dc else part)  46.8 us
    all_to_all x4, waiting for transfers between devices, swap(): return lax.all_to_all(rows, axes, split_axis=0, concat_axis=0, tiled=True)  37 us
    all_to_all x4, starting transfers between devices, swap(): return lax.all_to_all(rows, axes, split_axis=0, concat_axis=0, tiled=True)  27.9 us
    pallas_call x8, Pallas kernels, call(): pl.pallas_call(kernel, out_shape=out, in_specs=specs, scratch_shapes=scra...  17.1 us
    ppermute x14, waiting for transfers between devices, exchange(): parts.append(lax.ppermute(part, PLANE, pairs) if dy or dc else part)  4.25 us
  transfers between devices with their start and end apart: 19, of which 6 were waited for; matrix products, arithmetic and copies ran while one was open for 0% of the time, Pallas kernels for 2%

profile of v3, /device:TPU:1, one launch (start us, length us, event | category | flops | bytes accessed | tf_op | source)
XLA Modules:
  0.0 197.7 jit_solution(14946055891528046741)
XLA Ops:
  0.6 3.3 %shard_map.84 = (bf16[9,256,128]{2,1,0:T(8,128)(2,1)}, bf16[144,768]{1,0:T(8,128)(2,1)}) custom-call(bf16[128,768]{1,0:T(8,128)(2,1)} %bitcast.27, bf16[768,384]{1,0:T(8,128)(2,1)} %refs_8_.1, bf16[768,384]{1,0:T(8,128)(2,1)} %refs_9_.1, s32[6,1,128]{2,1,0:T(1,128)} %bitcast.29, bf16[128,384]{1,0:T(8,128)(2,1)} %bitcast.28), custom_call_target="tpu_custom_call" | custom-call | tf_op jit(solution)/shard_map/pallas_call | solution.py:253
  4.0 1.5 copy.15
  5.4 54.9 %all_to_all.25 = bf16[128,9,2,128]{3,2,1,0:T(2,128)(2,1)S(1)} all-to-all(bf16[128,9,2,128]{3,2,1,0:T(2,128)(2,1)S(1)} %bitcast.24), channel_id=1, replica_groups=mesh['x'=4,'y'=4,'zh'=4,'zl'=4,'c'=2] {'y','c','zh','zl'}, dimensions={0} | all-to-all | bytes 1179648 | tf_op jit(solution)/shard_map/all_to_all | solution.py:267
  60.3 0.5 copy.11
  60.8 4.4 %shard_map.85 = bf16[72,32,128]{2,1,0:T(8,128)(2,1)S(1)} custom-call(bf16[9,256,128]{2,1,0:T(8,128)(2,1)S(1)} %bitcast.21), custom_call_target="tpu_custom_call" | custom-call | tf_op jit(solution)/shard_map/pallas_call | solution.py:253
  65.2 1.2 copy.12
  66.4 0.0 copy-start.2
  66.4 8.3 %all-to-all-start.1 = ((bf16[128,9,2,128]{3,2,1,0:T(2,128)(2,1)}), bf16[128,9,2,128]{3,2,1,0:T(2,128)(2,1)S(1)}, u32[]{:S(2)}, u32[]{:S(2)}) async-start(bf16[128,9,2,128]{3,2,1,0:T(2,128)(2,1)} %bitcast.11), calls=%async_computation.1 | async-start | bytes 1179648 | tf_op jit(solution)/shard_map/all_to_all | solution.py:267
  74.7 0.0 copy-done.2
  74.7 2.8 %collective-permute-start = (bf16[144,768]{1,0:T(8,128)(2,1)S(1)}, bf16[144,768]{1,0:T(8,128)(2,1)S(1)}, u32[]{:S(2)}, u32[]{:S(2)}) collective-permute-start(bf16[144,768]{1,0:T(8,128)(2,1)S(1)} %copy-done.2), channel_id=1, source_target_pairs={{0,1},{1,0},{32,33},{33,32},{64,65},{65,64},{96,97},{97,96},{2,3},... | collective-permute-start | bytes 663560 | tf_op jit(solution)/shard_map/ppermute | solution.py:298
  77.5 2.9 %collective-permute-start.1 = (bf16[144,768]{1,0:T(8,128)(2,1)S(1)}, bf16[144,768]{1,0:T(8,128)(2,1)S(1)}, u32[]{:S(2)}, u32[]{:S(2)}) collective-permute-start(bf16[144,768]{1,0:T(8,128)(2,1)S(1)} %copy-done.2), channel_id=1, source_target_pairs={{0,32},{1,33},{32,64},{33,65},{64,96},{65,97},{96,0},{97,1},{2,34}... | collective-permute-start | bytes 663560 | tf_op jit(solution)/shard_map/ppermute | solution.py:298
  80.4 3.7 %collective-permute-start.2 = (bf16[144,768]{1,0:T(8,128)(2,1)S(1)}, bf16[144,768]{1,0:T(8,128)(2,1)S(1)}, u32[]{:S(2)}, u32[]{:S(2)}) collective-permute-start(bf16[144,768]{1,0:T(8,128)(2,1)S(1)} %copy-done.2), channel_id=1, source_target_pairs={{0,33},{1,32},{32,65},{33,64},{64,97},{65,96},{96,1},{97,0},{2,35}... | collective-permute-start | bytes 663560 | tf_op jit(solution)/shard_map/ppermute | solution.py:298
  84.1 3.2 %collective-permute-start.3 = (bf16[144,768]{1,0:T(8,128)(2,1)S(1)}, bf16[144,768]{1,0:T(8,128)(2,1)S(1)}, u32[]{:S(2)}, u32[]{:S(2)}) collective-permute-start(bf16[144,768]{1,0:T(8,128)(2,1)S(1)} %copy-done.2), channel_id=1, source_target_pairs={{0,64},{1,65},{32,96},{33,97},{64,0},{65,1},{96,32},{97,33},{2,66}... | collective-permute-start | bytes 663560 | tf_op jit(solution)/shard_map/ppermute | solution.py:298
  87.3 3.8 %collective-permute-start.4 = (bf16[144,768]{1,0:T(8,128)(2,1)S(1)}, bf16[144,768]{1,0:T(8,128)(2,1)S(1)}, u32[]{:S(2)}, u32[]{:S(2)}) collective-permute-start(bf16[144,768]{1,0:T(8,128)(2,1)S(1)} %copy-done.2), channel_id=1, source_target_pairs={{0,65},{1,64},{32,97},{33,96},{64,1},{65,0},{96,33},{97,32},{2,67}... | collective-permute-start | bytes 663560 | tf_op jit(solution)/shard_map/ppermute | solution.py:298
  91.1 0.0 collective-permute-done.refs_1_
  91.1 3.2 %collective-permute-start.5 = (bf16[144,768]{1,0:T(8,128)(2,1)S(1)}, bf16[144,768]{1,0:T(8,128)(2,1)S(1)}, u32[]{:S(2)}, u32[]{:S(2)}) collective-permute-start(bf16[144,768]{1,0:T(8,128)(2,1)S(1)} %copy-done.2), channel_id=1, source_target_pairs={{0,96},{1,97},{32,0},{33,1},{64,32},{65,33},{96,64},{97,65},{2,98}... | collective-permute-start | bytes 663560 | tf_op jit(solution)/shard_map/ppermute | solution.py:298
  94.3 0.0 collective-permute-done.1.refs_2_
  94.3 2.8 %collective-permute-start.6 = (bf16[144,768]{1,0:T(8,128)(2,1)S(1)}, bf16[144,768]{1,0:T(8,128)(2,1)S(1)}, u32[]{:S(2)}, u32[]{:S(2)}) collective-permute-start(bf16[144,768]{1,0:T(8,128)(2,1)S(1)} %copy-done.2), channel_id=1, source_target_pairs={{0,97},{1,96},{32,1},{33,0},{64,33},{65,32},{96,65},{97,64},{2,99}... | collective-permute-start | bytes 663560 | tf_op jit(solution)/shard_map/ppermute | solution.py:298
  97.1 0.1 pad_add_fusion.place_ref
  97.2 12.1 %all-to-all-done.1 = bf16[128,9,2,128]{3,2,1,0:T(2,128)(2,1)S(1)} async-done(((bf16[128,9,2,128]{3,2,1,0:T(2,128)(2,1)}), bf16[128,9,2,128]{3,2,1,0:T(2,128)(2,1)S(1)}, u32[]{:S(2)}, u32[]{:S(2)}) %all-to-all-start.1) | async-done | bytes 589856 | tf_op jit(solution)/shard_map/all_to_all | solution.py:267
  109.2 0.5 copy.13
  109.7 0.0 collective-permute-done.2.refs_3_
  109.7 0.0 collective-permute-done.3.refs_4_
  109.7 0.0 collective-permute-done.4.refs_5_
  109.7 0.0 collective-permute-done.5.refs_6_
  109.8 1.8 collective-permute-done.6.refs_7_
  111.6 2.7 %shard_map.86 = (bf16[16,40,128]{2,1,0:T(8,128)(2,1)}, bf16[8,96,128]{2,1,0:T(8,128)(2,1)S(1)}) custom-call(s32[2]{0:T(128)S(1)} %pad_add_fusion.place_ref, bf16[9,256,128]{2,1,0:T(8,128)(2,1)S(1)} %bitcast.19, bf16[144,768]{1,0:T(8,128)(2,1)S(1)} %copy-done.2, bf16[144,768]{1,0:T(8,128)(2,1)S(1)} %collective-permute-done.refs_1_, ...), custom_call_target="tpu_custom_call" | custom-call | tf_op jit(solution)/shard_map/pallas_call | solution.py:253
  114.3 6.5 %all-to-all-start.2 = ((bf16[16,40,128]{2,1,0:T(8,128)(2,1)}), bf16[16,40,128]{2,1,0:T(8,128)(2,1)S(1)}, u32[]{:S(2)}, u32[]{:S(2)}) async-start(bf16[16,40,128]{2,1,0:T(8,128)(2,1)} %get-tuple-element.43), calls=%async_computation.2 | async-start | bytes 327680 | tf_op jit(solution)/shard_map/all_to_all | solution.py:267
  120.8 1.2 shard_map.88
  122.0 6.2 %all-to-all-done.2.in_ref = bf16[16,40,128]{2,1,0:T(8,128)(2,1)S(1)} async-done(((bf16[16,40,128]{2,1,0:T(8,128)(2,1)}), bf16[16,40,128]{2,1,0:T(8,128)(2,1)S(1)}, u32[]{:S(2)}, u32[]{:S(2)}) %all-to-all-start.2) | async-done | bytes 163872 | tf_op jit(solution)/shard_map/all_to_all | solution.py:267
  128.2 0.6 shard_map.87
  128.8 8.2 %all-to-all-start.3 = ((bf16[4,40,128]{2,1,0:T(8,128)(2,1)}), bf16[4,40,128]{2,1,0:T(8,128)(2,1)S(1)}, u32[]{:S(2)}, u32[]{:S(2)}) async-start(bf16[4,40,128]{2,1,0:T(8,128)(2,1)} %shard_map.87), calls=%async_computation.3 | async-start | bytes 81920 | tf_op jit(solution)/shard_map/all_to_all | solution.py:267
  137.0 4.4 %collective-permute-start.7 = (bf16[144,128]{1,0:T(8,128)(2,1)S(1)}, bf16[144,128]{1,0:T(8,128)(2,1)S(1)}, u32[]{:S(2)}, u32[]{:S(2)}) collective-permute-start(bf16[144,128]{1,0:T(8,128)(2,1)S(1)} %get-tuple-element.55), channel_id=1, source_target_pairs={{0,1},{1,0},{32,33},{33,32},{64,65},{65,64},{96,97},{97,96},{2,3},... | collective-permute-start | bytes 110600 | tf_op jit(solution)/shard_map/ppermute | solution.py:298
  141.5 4.4 %collective-permute-start.8 = (bf16[144,128]{1,0:T(8,128)(2,1)S(1)}, bf16[144,128]{1,0:T(8,128)(2,1)S(1)}, u32[]{:S(2)}, u32[]{:S(2)}) collective-permute-start(bf16[144,128]{1,0:T(8,128)(2,1)S(1)} %get-tuple-element.56), channel_id=1, source_target_pairs={{0,32},{1,33},{32,64},{33,65},{64,96},{65,97},{96,0},{97,1},{2,34}... | collective-permute-start | bytes 110600 | tf_op jit(solution)/shard_map/ppermute | solution.py:298
  145.9 2.2 %collective-permute-start.9 = (bf16[144,128]{1,0:T(8,128)(2,1)S(1)}, bf16[144,128]{1,0:T(8,128)(2,1)S(1)}, u32[]{:S(2)}, u32[]{:S(2)}) collective-permute-start(bf16[144,128]{1,0:T(8,128)(2,1)S(1)} %get-tuple-element.57), channel_id=1, source_target_pairs={{0,33},{1,32},{32,65},{33,64},{64,97},{65,96},{96,1},{97,0},{2,35}... | collective-permute-start | bytes 110600 | tf_op jit(solution)/shard_map/ppermute | solution.py:298
  148.0 3.2 %collective-permute-start.10 = (bf16[144,128]{1,0:T(8,128)(2,1)S(1)}, bf16[144,128]{1,0:T(8,128)(2,1)S(1)}, u32[]{:S(2)}, u32[]{:S(2)}) collective-permute-start(bf16[144,128]{1,0:T(8,128)(2,1)S(1)} %get-tuple-element.58), channel_id=1, source_target_pairs={{0,64},{1,65},{32,96},{33,97},{64,0},{65,1},{96,32},{97,33},{2,66}... | collective-permute-start | bytes 110600 | tf_op jit(solution)/shard_map/ppermute | solution.py:298
  151.3 4.0 %collective-permute-start.11 = (bf16[144,128]{1,0:T(8,128)(2,1)S(1)}, bf16[144,128]{1,0:T(8,128)(2,1)S(1)}, u32[]{:S(2)}, u32[]{:S(2)}) collective-permute-start(bf16[144,128]{1,0:T(8,128)(2,1)S(1)} %get-tuple-element.59), channel_id=1, source_target_pairs={{0,65},{1,64},{32,97},{33,96},{64,1},{65,0},{96,33},{97,32},{2,67}... | collective-permute-start | bytes 110600 | tf_op jit(solution)/shard_map/ppermute | solution.py:298
  155.2 0.0 collective-permute-done.7.refs_1_
  155.2 4.5 %collective-permute-start.12 = (bf16[144,128]{1,0:T(8,128)(2,1)S(1)}, bf16[144,128]{1,0:T(8,128)(2,1)S(1)}, u32[]{:S(2)}, u32[]{:S(2)}) collective-permute-start(bf16[144,128]{1,0:T(8,128)(2,1)S(1)} %get-tuple-element.60), channel_id=1, source_target_pairs={{0,96},{1,97},{32,0},{33,1},{64,32},{65,33},{96,64},{97,65},{2,98}... | collective-permute-start | bytes 110600 | tf_op jit(solution)/shard_map/ppermute | solution.py:298
  159.7 0.0 collective-permute-done.8.refs_2_
  159.7 1.9 collective-permute-start.13
  161.7 0.0 all-to-all-done.3.in_ref
  161.7 0.9 shard_map.89
  162.6 0.0 copy-start
  162.6 0.0 copy-start.1
  162.6 0.0 collective-permute-done.9.refs_3_
  162.6 0.0 collective-permute-done.10.refs_4_
  162.6 0.0 collective-permute-done.11.refs_5_
  162.6 0.0 collective-permute-done.12.refs_6_
  162.6 2.4 %collective-permute-done.13.refs_7_ = bf16[144,128]{1,0:T(8,128)(2,1)S(1)} collective-permute-done((bf16[144,128]{1,0:T(8,128)(2,1)S(1)}, bf16[144,128]{1,0:T(8,128)(2,1)S(1)}, u32[]{:S(2)}, u32[]{:S(2)}) %collective-permute-start.13) | collective-permute-done | bytes 36896 | tf_op jit(solution)/shard_map/ppermute | solution.py:298
  165.0 4.8 %all-to-all-start.4 = ((bf16[64,40,128]{2,1,0:T(8,128)(2,1)}), bf16[64,40,128]{2,1,0:T(8,128)(2,1)S(1)}, u32[]{:S(2)}, u32[]{:S(2)}) async-start(bf16[64,40,128]{2,1,0:T(8,128)(2,1)} %shard_map.89), calls=%async_computation.4 | async-start | bytes 1310720 | tf_op jit(solution)/shard_map/all_to_all | solution.py:267
  169.9 0.0 copy-done
  169.9 0.0 copy-done.1
  169.9 1.8 shard_map.90
  171.7 18.7 %all-to-all-done.4.mine_ref = bf16[64,40,128]{2,1,0:T(8,128)(2,1)S(1)} async-done(((bf16[64,40,128]{2,1,0:T(8,128)(2,1)}), bf16[64,40,128]{2,1,0:T(8,128)(2,1)S(1)}, u32[]{:S(2)}, u32[]{:S(2)}) %all-to-all-start.4) | async-done | bytes 655392 | tf_op jit(solution)/shard_map/all_to_all | solution.py:267
  190.4 3.5 %collective-permute-start.14 = (bf16[64,40,128]{2,1,0:T(8,128)(2,1)S(1)}, bf16[64,40,128]{2,1,0:T(8,128)(2,1)S(1)}, u32[]{:S(2)}, u32[]{:S(2)}) collective-permute-start(bf16[64,40,128]{2,1,0:T(8,128)(2,1)S(1)} %all-to-all-done.4.mine_ref), channel_id=1, source_target_pairs={{0,1},{1,0},{2,3},{3,2},{4,5},{5,4},{6,7},{7,6},{8,9},{9,8},{10,11... | collective-permute-start | bytes 1966088 | tf_op jit(solution)/shard_map/ppermute | solution.py:343
  193.9 1.7 collective-permute-done.14.other_ref
  195.6 2.2 %shard_map.91 = (bf16[768,384]{1,0:T(8,128)(2,1)}, bf16[768,384]{1,0:T(8,128)(2,1)}) custom-call(s32[2]{0:T(128)S(1)} %pad_add_fusion.place_ref, bf16[64,40,128]{2,1,0:T(8,128)(2,1)S(1)} %all-to-all-done.4.mine_ref, bf16[64,40,128]{2,1,0:T(8,128)(2,1)S(1)} %collective-permute-done.14.other_ref), custom_call_target="tpu_custom_call" | custom-call | tf_op jit(solution)/shard_map/pallas_call | solution.py:253
Async XLA Ops:
  66.4 8.3 %copy-start.2 = (bf16[144,768]{1,0:T(8,128)(2,1)S(1)}, bf16[144,768]{1,0:T(8,128)(2,1)}, u32[]{:S(2)}) copy-start(bf16[144,768]{1,0:T(8,128)(2,1)} %get-tuple-element.42.refs_0_) | copy-start | bytes 663556
  66.4 42.9 %all-to-all-start.1 = ((bf16[128,9,2,128]{3,2,1,0:T(2,128)(2,1)}), bf16[128,9,2,128]{3,2,1,0:T(2,128)(2,1)S(1)}, u32[]{:S(2)}, u32[]{:S(2)}) async-start(bf16[128,9,2,128]{3,2,1,0:T(2,128)(2,1)} %bitcast.11), calls=%async_computation.1 | async-start | bytes 1179648 | tf_op jit(solution)/shard_map/all_to_all | solution.py:267
  74.7 16.4 %collective-permute-start = (bf16[144,768]{1,0:T(8,128)(2,1)S(1)}, bf16[144,768]{1,0:T(8,128)(2,1)S(1)}, u32[]{:S(2)}, u32[]{:S(2)}) collective-permute-start(bf16[144,768]{1,0:T(8,128)(2,1)S(1)} %copy-done.2), channel_id=1, source_target_pairs={{0,1},{1,0},{32,33},{33,32},{64,65},{65,64},{96,97},{97,96},{2,3},... | collective-permute-start | bytes 663560 | tf_op jit(solution)/shard_map/ppermute | solution.py:298
  77.5 16.8 %collective-permute-start.1 = (bf16[144,768]{1,0:T(8,128)(2,1)S(1)}, bf16[144,768]{1,0:T(8,128)(2,1)S(1)}, u32[]{:S(2)}, u32[]{:S(2)}) collective-permute-start(bf16[144,768]{1,0:T(8,128)(2,1)S(1)} %copy-done.2), channel_id=1, source_target_pairs={{0,32},{1,33},{32,64},{33,65},{64,96},{65,97},{96,0},{97,1},{2,34}... | collective-permute-start | bytes 663560 | tf_op jit(solution)/shard_map/ppermute | solution.py:298
  80.4 29.3 %collective-permute-start.2 = (bf16[144,768]{1,0:T(8,128)(2,1)S(1)}, bf16[144,768]{1,0:T(8,128)(2,1)S(1)}, u32[]{:S(2)}, u32[]{:S(2)}) collective-permute-start(bf16[144,768]{1,0:T(8,128)(2,1)S(1)} %copy-done.2), channel_id=1, source_target_pairs={{0,33},{1,32},{32,65},{33,64},{64,97},{65,96},{96,1},{97,0},{2,35}... | collective-permute-start | bytes 663560 | tf_op jit(solution)/shard_map/ppermute | solution.py:298
  84.1 25.6 %collective-permute-start.3 = (bf16[144,768]{1,0:T(8,128)(2,1)S(1)}, bf16[144,768]{1,0:T(8,128)(2,1)S(1)}, u32[]{:S(2)}, u32[]{:S(2)}) collective-permute-start(bf16[144,768]{1,0:T(8,128)(2,1)S(1)} %copy-done.2), channel_id=1, source_target_pairs={{0,64},{1,65},{32,96},{33,97},{64,0},{65,1},{96,32},{97,33},{2,66}... | collective-permute-start | bytes 663560 | tf_op jit(solution)/shard_map/ppermute | solution.py:298
  87.3 22.4 %collective-permute-start.4 = (bf16[144,768]{1,0:T(8,128)(2,1)S(1)}, bf16[144,768]{1,0:T(8,128)(2,1)S(1)}, u32[]{:S(2)}, u32[]{:S(2)}) collective-permute-start(bf16[144,768]{1,0:T(8,128)(2,1)S(1)} %copy-done.2), channel_id=1, source_target_pairs={{0,65},{1,64},{32,97},{33,96},{64,1},{65,0},{96,33},{97,32},{2,67}... | collective-permute-start | bytes 663560 | tf_op jit(solution)/shard_map/ppermute | solution.py:298
  91.1 18.7 %collective-permute-start.5 = (bf16[144,768]{1,0:T(8,128)(2,1)S(1)}, bf16[144,768]{1,0:T(8,128)(2,1)S(1)}, u32[]{:S(2)}, u32[]{:S(2)}) collective-permute-start(bf16[144,768]{1,0:T(8,128)(2,1)S(1)} %copy-done.2), channel_id=1, source_target_pairs={{0,96},{1,97},{32,0},{33,1},{64,32},{65,33},{96,64},{97,65},{2,98}... | collective-permute-start | bytes 663560 | tf_op jit(solution)/shard_map/ppermute | solution.py:298
  94.3 17.3 %collective-permute-start.6 = (bf16[144,768]{1,0:T(8,128)(2,1)S(1)}, bf16[144,768]{1,0:T(8,128)(2,1)S(1)}, u32[]{:S(2)}, u32[]{:S(2)}) collective-permute-start(bf16[144,768]{1,0:T(8,128)(2,1)S(1)} %copy-done.2), channel_id=1, source_target_pairs={{0,97},{1,96},{32,1},{33,0},{64,33},{65,32},{96,65},{97,64},{2,99}... | collective-permute-start | bytes 663560 | tf_op jit(solution)/shard_map/ppermute | solution.py:298
  114.3 13.9 %all-to-all-start.2 = ((bf16[16,40,128]{2,1,0:T(8,128)(2,1)}), bf16[16,40,128]{2,1,0:T(8,128)(2,1)S(1)}, u32[]{:S(2)}, u32[]{:S(2)}) async-start(bf16[16,40,128]{2,1,0:T(8,128)(2,1)} %get-tuple-element.43), calls=%async_computation.2 | async-start | bytes 327680 | tf_op jit(solution)/shard_map/all_to_all | solution.py:267
  128.8 32.9 %all-to-all-start.3 = ((bf16[4,40,128]{2,1,0:T(8,128)(2,1)}), bf16[4,40,128]{2,1,0:T(8,128)(2,1)S(1)}, u32[]{:S(2)}, u32[]{:S(2)}) async-start(bf16[4,40,128]{2,1,0:T(8,128)(2,1)} %shard_map.87), calls=%async_computation.3 | async-start | bytes 81920 | tf_op jit(solution)/shard_map/all_to_all | solution.py:267
  137.0 18.2 %collective-permute-start.7 = (bf16[144,128]{1,0:T(8,128)(2,1)S(1)}, bf16[144,128]{1,0:T(8,128)(2,1)S(1)}, u32[]{:S(2)}, u32[]{:S(2)}) collective-permute-start(bf16[144,128]{1,0:T(8,128)(2,1)S(1)} %get-tuple-element.55), channel_id=1, source_target_pairs={{0,1},{1,0},{32,33},{33,32},{64,65},{65,64},{96,97},{97,96},{2,3},... | collective-permute-start | bytes 110600 | tf_op jit(solution)/shard_map/ppermute | solution.py:298
  141.5 18.3 %collective-permute-start.8 = (bf16[144,128]{1,0:T(8,128)(2,1)S(1)}, bf16[144,128]{1,0:T(8,128)(2,1)S(1)}, u32[]{:S(2)}, u32[]{:S(2)}) collective-permute-start(bf16[144,128]{1,0:T(8,128)(2,1)S(1)} %get-tuple-element.56), channel_id=1, source_target_pairs={{0,32},{1,33},{32,64},{33,65},{64,96},{65,97},{96,0},{97,1},{2,34}... | collective-permute-start | bytes 110600 | tf_op jit(solution)/shard_map/ppermute | solution.py:298
  145.9 16.7 %collective-permute-start.9 = (bf16[144,128]{1,0:T(8,128)(2,1)S(1)}, bf16[144,128]{1,0:T(8,128)(2,1)S(1)}, u32[]{:S(2)}, u32[]{:S(2)}) collective-permute-start(bf16[144,128]{1,0:T(8,128)(2,1)S(1)} %get-tuple-element.57), channel_id=1, source_target_pairs={{0,33},{1,32},{32,65},{33,64},{64,97},{65,96},{96,1},{97,0},{2,35}... | collective-permute-start | bytes 110600 | tf_op jit(solution)/shard_map/ppermute | solution.py:298
  148.0 14.5 %collective-permute-start.10 = (bf16[144,128]{1,0:T(8,128)(2,1)S(1)}, bf16[144,128]{1,0:T(8,128)(2,1)S(1)}, u32[]{:S(2)}, u32[]{:S(2)}) collective-permute-start(bf16[144,128]{1,0:T(8,128)(2,1)S(1)} %get-tuple-element.58), channel_id=1, source_target_pairs={{0,64},{1,65},{32,96},{33,97},{64,0},{65,1},{96,32},{97,33},{2,66}... | collective-permute-start | bytes 110600 | tf_op jit(solution)/shard_map/ppermute | solution.py:298
  151.3 11.3 %collective-permute-start.11 = (bf16[144,128]{1,0:T(8,128)(2,1)S(1)}, bf16[144,128]{1,0:T(8,128)(2,1)S(1)}, u32[]{:S(2)}, u32[]{:S(2)}) collective-permute-start(bf16[144,128]{1,0:T(8,128)(2,1)S(1)} %get-tuple-element.59), channel_id=1, source_target_pairs={{0,65},{1,64},{32,97},{33,96},{64,1},{65,0},{96,33},{97,32},{2,67}... | collective-permute-start | bytes 110600 | tf_op jit(solution)/shard_map/ppermute | solution.py:298
  155.2 7.4 %collective-permute-start.12 = (bf16[144,128]{1,0:T(8,128)(2,1)S(1)}, bf16[144,128]{1,0:T(8,128)(2,1)S(1)}, u32[]{:S(2)}, u32[]{:S(2)}) collective-permute-start(bf16[144,128]{1,0:T(8,128)(2,1)S(1)} %get-tuple-element.60), channel_id=1, source_target_pairs={{0,96},{1,97},{32,0},{33,1},{64,32},{65,33},{96,64},{97,65},{2,98}... | collective-permute-start | bytes 110600 | tf_op jit(solution)/shard_map/ppermute | solution.py:298
  159.7 5.3 %collective-permute-start.13 = (bf16[144,128]{1,0:T(8,128)(2,1)S(1)}, bf16[144,128]{1,0:T(8,128)(2,1)S(1)}, u32[]{:S(2)}, u32[]{:S(2)}) collective-permute-start(bf16[144,128]{1,0:T(8,128)(2,1)S(1)} %get-tuple-element.61), channel_id=1, source_target_pairs={{0,97},{1,96},{32,1},{33,0},{64,33},{65,32},{96,65},{97,64},{2,99}... | collective-permute-start | bytes 110600 | tf_op jit(solution)/shard_map/ppermute | solution.py:298
  162.6 7.3 %copy-start = (bf16[768,384]{1,0:T(8,128)(2,1)S(1)}, bf16[768,384]{1,0:T(8,128)(2,1)}, u32[]{:S(2)}) copy-start(bf16[768,384]{1,0:T(8,128)(2,1)} %refs_8_.1) | copy-start | bytes 1769476
  162.6 7.3 %copy-start.1 = (bf16[768,384]{1,0:T(8,128)(2,1)S(1)}, bf16[768,384]{1,0:T(8,128)(2,1)}, u32[]{:S(2)}) copy-start(bf16[768,384]{1,0:T(8,128)(2,1)} %refs_9_.1) | copy-start | bytes 1769476
  165.0 25.3 %all-to-all-start.4 = ((bf16[64,40,128]{2,1,0:T(8,128)(2,1)}), bf16[64,40,128]{2,1,0:T(8,128)(2,1)S(1)}, u32[]{:S(2)}, u32[]{:S(2)}) async-start(bf16[64,40,128]{2,1,0:T(8,128)(2,1)} %shard_map.89), calls=%async_computation.4 | async-start | bytes 1310720 | tf_op jit(solution)/shard_map/all_to_all | solution.py:267
  190.4 5.2 %collective-permute-start.14 = (bf16[64,40,128]{2,1,0:T(8,128)(2,1)S(1)}, bf16[64,40,128]{2,1,0:T(8,128)(2,1)S(1)}, u32[]{:S(2)}, u32[]{:S(2)}) collective-permute-start(bf16[64,40,128]{2,1,0:T(8,128)(2,1)S(1)} %all-to-all-done.4.mine_ref), channel_id=1, source_target_pairs={{0,1},{1,0},{2,3},{3,2},{4,5},{5,4},{6,7},{7,6},{8,9},{9,8},{10,11... | collective-permute-start | bytes 1966088 | tf_op jit(solution)/shard_map/ppermute | solution.py:343

commit v4 on v3

--- a/solution.py
+++ b/solution.py
@@ -23,6 +23,8 @@
 PIECE = 36
 SLOT = 40
 BLOCK = 16
+WHOLE = 576
+MESSAGE = 144
 
 
 def iota(shape, dim):
@@ -190,18 +192,30 @@
 
 
 def forward_kernel(place_ref, in_ref, cols_ref, *refs):
-    exts, outs, (dests, scratch) = refs[:8], refs[8:16], refs[16:]
+    exts, (keep_ref, give_ref), (dests, scratch) = refs[:8], refs[8:10], refs[10:]
     gather_columns(place_ref, in_ref, 6, 3, 5, exts, dests, scratch, 0)
-    for n, (dy, dc) in enumerate(STEPS):
-        target = index_of(place_ref, dy, dc)
-        outs[n][:COLUMNS, :] = cols_ref[target]
-        outs[n][COLUMNS:, :] = scratch[target]
-
-
-def return_kernel(place_ref, *refs):
-    parts, (ws_ref, wv_ref), (att_ref, grad_ref), held = refs[:8], refs[8:10], refs[10:12], refs[12]
-    for n, (dy, dc) in enumerate(STEPS):
-        held[index_of(place_ref, 4 - dy, dc)] = parts[n][...]
+    here = place_ref[1]
+    for y in range(4):
+        for ref, c in ((keep_ref, here), (give_ref, 1 - here)):
+            ref[y, :COLUMNS, :] = cols_ref[y * 2 + c]
+            ref[y, COLUMNS:, :] = scratch[y * 2 + c]
+
+
+def pack_kernel(block_ref, keep_ref, got_ref, out_ref, scratch):
+    for i in range(16):
+        scratch[i * PIECE : (i + 1) * PIECE, :] = block_ref[i].astype(F32)[:PIECE]
+    block = scratch[...].astype(BF16)
+    for y in range(4):
+        out_ref[y, :WHOLE, :] = block
+        out_ref[y, WHOLE : WHOLE + MESSAGE, :] = keep_ref[y]
+        out_ref[y, WHOLE + MESSAGE :, :] = got_ref[y]
+
+
+def return_kernel(place_ref, all_ref, ws_ref, wv_ref, att_ref, grad_ref, held):
+    here = place_ref[1]
+    for y in range(4):
+        held[y * 2 + here] = all_ref[y, WHOLE : WHOLE + MESSAGE, :]
+        held[y * 2 + 1 - here] = all_ref[y, WHOLE + MESSAGE :, :]
 
     def columns(blocks, per, first):
         rows = [
@@ -226,16 +240,15 @@
         out_ref[i] = total
 
 
-def finish_kernel(place_ref, mine_ref, other_ref, shared_ref, value_ref, scratch):
-    here = place_ref[1]
-    for y in range(4):
-        for i in range(16):
-            rows = slice(i * PIECE, (i + 1) * PIECE)
-            scratch[here, y, rows, :] = mine_ref[y * 16 + i].astype(F32)[:PIECE]
-            scratch[1 - here, y, rows, :] = other_ref[y * 16 + i].astype(F32)[:PIECE]
+def finish_kernel(place_ref, mine_ref, other_ref, shared_ref, value_ref):
+    first = place_ref[1] == 0
     for k in range(WIDTH // LOCAL):
-        first = k * COLUMNS
-        strip = [scratch[j % 2, j // 2, first : first + COLUMNS, :] for j in range(8)]
+        rows = slice(k * COLUMNS, (k + 1) * COLUMNS)
+        strip = []
+        for y in range(4):
+            mine = mine_ref[y, rows, :].astype(F32)
+            other = other_ref[y, rows, :].astype(F32)
+            strip += [jnp.where(first, mine, other), jnp.where(first, other, mine)]
         strip = jnp.concatenate(strip, axis=0)
         for half, ref in enumerate((shared_ref, value_ref)):
             heads = [
@@ -289,22 +302,19 @@
         held=True,
     )
 
-    def exchange(mine):
-        parts = []
-        for part, (dy, dc) in zip(mine, STEPS):
-            pairs = [
-                (y * 2 + c, (y + dy) % 4 * 2 + (c + dc) % 2) for y in range(4) for c in range(2)
-            ]
-            parts.append(lax.ppermute(part, PLANE, pairs) if dy or dc else part)
-        return parts
+    def shift(part, dy, dc):
+        pairs = [(y * 2 + c, (y + dy) % 4 * 2 + (c + dc) % 2) for y in range(4) for c in range(2)]
+        return lax.ppermute(part, PLANE, pairs) if dy or dc else part
 
     arrived = swap(sent.reshape(9, LOCAL, 2, LOCAL).transpose(1, 0, 2, 3), OWNERS)
+    early = [shift(ext, dy, dc) for dy, dc in STEPS[:5]]
+    arrived, ext, early = lax.optimization_barrier((arrived, ext, early))
+    exts = early + [shift(ext, dy, dc) for dy, dc in STEPS[5:]]
     arrived = arrived.transpose(1, 0, 2, 3)
     worked = call(attend_kernel, shape(72, 32, LOCAL), arrived.reshape(9, ROWS, LOCAL))
     worked = worked.reshape(8, 9, 16, 2, LOCAL).transpose(0, 2, 1, 3, 4)
     back = swap(worked.reshape(LOCAL, 9, 2, LOCAL), OWNERS)
     back = back.transpose(1, 0, 2, 3).reshape(9, ROWS, LOCAL)
-    exts = exchange([ext] * 8)
     part, cols = call(
         partial_kernel,
         (shape(16, SLOT, LOCAL), shape(8, COLUMNS, LOCAL)),
@@ -314,9 +324,9 @@
         scratch=[pltpu.VMEM((2, 8, 8, LOCAL), F32), pltpu.VMEM((16 * PIECE + 8, LOCAL), F32)],
         scalars=1,
     )
-    parts = call(
+    keep, give = call(
         forward_kernel,
-        tuple(shape(COLUMNS * 3 // 2, LOCAL) for _ in STEPS),
+        (shape(4, MESSAGE, LOCAL), shape(4, MESSAGE, LOCAL)),
         place,
         back,
         cols,
@@ -324,30 +334,38 @@
         scratch=[pltpu.VMEM((2, 8, 8, LOCAL), F32), pltpu.VMEM((8, COLUMNS // 2, LOCAL), BF16)],
         scalars=1,
     )
-    part = call(sum_kernel, shape(4, SLOT, LOCAL), swap(part, ("x", "zl")))
-    part, parts = lax.optimization_barrier((part, parts))
-    block = call(sum_kernel, shape(64, SLOT, LOCAL), swap(part, "zh"))
-    block, parts = lax.optimization_barrier((block, exchange(parts)))
+    got = lax.ppermute(give, "c", [(0, 1), (1, 0)])
+    part = swap(part, ("x", "zl"))
+    part, keep, got = lax.optimization_barrier((part, keep, got))
+    part = call(sum_kernel, shape(4, SLOT, LOCAL), part)
+    block = call(sum_kernel, shape(16, SLOT, LOCAL), swap(part, "zh"))
+    block = swap(block, ("x", "zl"))
+    block = call(
+        pack_kernel,
+        shape(4, WHOLE + 2 * MESSAGE, LOCAL),
+        block,
+        keep,
+        got,
+        scratch=[pltpu.VMEM((WHOLE, LOCAL), F32)],
+    )
+    block = swap(block, "y")
+    other = lax.ppermute(block, "c", [(0, 1), (1, 0)])
     attention, grad_tokens = call(
         return_kernel,
         (shape(LOCAL, PROJ), shape(LOCAL, WIDTH)),
         place,
-        *parts,
+        block,
         w_shared,
         w_value,
-        scratch=[pltpu.VMEM((8, COLUMNS * 3 // 2, LOCAL), BF16)],
+        scratch=[pltpu.VMEM((8, MESSAGE, LOCAL), BF16)],
         scalars=1,
     )
-    block = swap(block, ("y", "x", "zl"))
-    block, attention, grad_tokens = lax.optimization_barrier((block, attention, grad_tokens))
-    other = lax.ppermute(block, "c", [(0, 1), (1, 0)])
     grad_shared, grad_value = call(
         finish_kernel,
         (shape(WIDTH, PROJ), shape(WIDTH, PROJ)),
         place,
         block,
         other,
-        scratch=[pltpu.VMEM((2, 4, 16 * PIECE, LOCAL), F32)],
         scalars=1,
     )
     return (attention[None], grad_tokens[None], grad_shared, grad_value)

time: 199 us -> 180 us (0.905)
  blocking collectives: 54.9 us -> 39.9 us
  starting transfers between devices: 78.2 us -> 68.1 us
  waiting for transfers between devices: 42.9 us -> 50.2 us
    ppermute x14 -> x8, starting transfers between devices: 46.8 us -> 25.1 us  [the longest x7 22.7 us: shift(): return lax.ppermute(part, PLANE, pairs) if dy or dc else part]
    all_to_all x1 -> x3, blocking collectives: 54.9 us -> 39.9 us  [swap(): return lax.all_to_all(rows, axes, split_axis=0, concat_axis=0, tiled=True)]
    ppermute x14 -> x8, waiting for transfers between devices: 4.25 us -> 16.1 us  [the longest x7 15.1 us: shift(): return lax.ppermute(part, PLANE, pairs) if dy or dc else part]
    all_to_all x4 -> x3, starting transfers between devices: 27.9 us -> 36.6 us  [swap(): return lax.all_to_all(rows, axes, split_axis=0, concat_axis=0, tiled=True)]
    all_to_all x4 -> x3, waiting for transfers between devices: 37 us -> 33.8 us  [swap(): return lax.all_to_all(rows, axes, split_axis=0, concat_axis=0, tiled=True)]
    ppermute x1, starting transfers between devices: 3.49 us -> 6.3 us  [body(): other = lax.ppermute(block, 'c', [(0, 1), (1, 0)])]
    pallas_call x8 -> x9, Pallas kernels: 17.1 us -> 15.5 us  [call(): pl.pallas_call(kernel, out_shape=out, in_specs=specs, scratch_shapes=scra...]
  transfers between devices with their start and end apart: 19 -> 12, of which waited for: 6 -> 8; matrix products, arithmetic and copies ran while one was open for 0% -> 0% of each run, Pallas kernels for 2% -> 2%
where the time goes in v4:
time: 180 us; the launch traced here: 179 us
  starting transfers between devices  68.1 us (38%)
  waiting for transfers between devices  50.2 us (28%)
  blocking collectives  39.9 us (22%)
  Pallas kernels  15.5 us (9%)
  local copies, waits for them, and re-layouts  4.43 us (2%)
    all_to_all x3, blocking collectives, swap(): return lax.all_to_all(rows, axes, split_axis=0, concat_axis=0, tiled=True)  39.9 us
    all_to_all x3, starting transfers between devices, swap(): return lax.all_to_all(rows, axes, split_axis=0, concat_axis=0, tiled=True)  36.6 us
    all_to_all x3, waiting for transfers between devices, swap(): return lax.all_to_all(rows, axes, split_axis=0, concat_axis=0, tiled=True)  33.8 us
    ppermute x7, starting transfers between devices, shift(): return lax.ppermute(part, PLANE, pairs) if dy or dc else part  22.7 us
    pallas_call x9, Pallas kernels, call(): pl.pallas_call(kernel, out_shape=out, in_specs=specs, scratch_shapes=scra...  15.5 us
    ppermute x7, waiting for transfers between devices, shift(): return lax.ppermute(part, PLANE, pairs) if dy or dc else part  15.1 us
    ppermute x1, starting transfers between devices, body(): other = lax.ppermute(block, 'c', [(0, 1), (1, 0)])  6.3 us
  transfers between devices with their start and end apart: 12, of which 8 were waited for; matrix products, arithmetic and copies ran while one was open for 0% of the time, Pallas kernels for 2%

profile of v4, /device:TPU:1, one launch (start us, length us, event | category | flops | bytes accessed | tf_op | source)
XLA Modules:
  0.0 179.0 jit_solution(2335315514526431436)
XLA Ops:
  0.6 3.3 %shard_map.84 = (bf16[9,256,128]{2,1,0:T(8,128)(2,1)}, bf16[144,768]{1,0:T(8,128)(2,1)}) custom-call(bf16[128,768]{1,0:T(8,128)(2,1)} %bitcast.26, bf16[768,384]{1,0:T(8,128)(2,1)} %ws_ref.1, bf16[768,384]{1,0:T(8,128)(2,1)} %wv_ref.1, s32[6,1,128]{2,1,0:T(1,128)} %bitcast.28, bf16[128,384]{1,0:T(8,128)(2,1)} %bitcast.27), custom_call_target="tpu_custom_call" | custom-call | tf_op jit(solution)/shard_map/pallas_call | solution.py:266
  4.0 2.3 %copy.15 = bf16[9,128,2,128]{3,2,0,1:T(2,128)(2,1)} copy(bf16[9,128,2,128]{3,2,1,0:T(2,128)(2,1)} %bitcast.25) | data formatting | bytes 1179648 | tf_op jit(solution)/shard_map/reshape | solution.py:309
  6.2 0.0 copy-start.2
  6.2 20.7 %all-to-all-start = ((bf16[128,9,2,128]{3,2,1,0:T(2,128)(2,1)}), bf16[128,9,2,128]{3,2,1,0:T(2,128)(2,1)S(1)}, u32[]{:S(2)}, u32[]{:S(2)}) async-start(bf16[128,9,2,128]{3,2,1,0:T(2,128)(2,1)} %bitcast.18), calls=%async_computation | async-start | bytes 1179648 | tf_op jit(solution)/shard_map/all_to_all | solution.py:280
  27.0 0.0 copy-done.2
  27.0 2.8 %collective-permute-start = (bf16[144,768]{1,0:T(8,128)(2,1)S(1)}, bf16[144,768]{1,0:T(8,128)(2,1)S(1)}, u32[]{:S(2)}, u32[]{:S(2)}) collective-permute-start(bf16[144,768]{1,0:T(8,128)(2,1)S(1)} %copy-done.2), channel_id=1, source_target_pairs={{0,1},{1,0},{32,33},{33,32},{64,65},{65,64},{96,97},{97,96},{2,3},... | collective-permute-start | bytes 663560 | tf_op jit(solution)/shard_map/ppermute | solution.py:307
  29.8 2.9 %collective-permute-start.1 = (bf16[144,768]{1,0:T(8,128)(2,1)S(1)}, bf16[144,768]{1,0:T(8,128)(2,1)S(1)}, u32[]{:S(2)}, u32[]{:S(2)}) collective-permute-start(bf16[144,768]{1,0:T(8,128)(2,1)S(1)} %copy-done.2), channel_id=1, source_target_pairs={{0,32},{1,33},{32,64},{33,65},{64,96},{65,97},{96,0},{97,1},{2,34}... | collective-permute-start | bytes 663560 | tf_op jit(solution)/shard_map/ppermute | solution.py:307
  32.6 3.7 %collective-permute-start.2 = (bf16[144,768]{1,0:T(8,128)(2,1)S(1)}, bf16[144,768]{1,0:T(8,128)(2,1)S(1)}, u32[]{:S(2)}, u32[]{:S(2)}) collective-permute-start(bf16[144,768]{1,0:T(8,128)(2,1)S(1)} %copy-done.2), channel_id=1, source_target_pairs={{0,33},{1,32},{32,65},{33,64},{64,97},{65,96},{96,1},{97,0},{2,35}... | collective-permute-start | bytes 663560 | tf_op jit(solution)/shard_map/ppermute | solution.py:307
  36.3 3.2 %collective-permute-start.3 = (bf16[144,768]{1,0:T(8,128)(2,1)S(1)}, bf16[144,768]{1,0:T(8,128)(2,1)S(1)}, u32[]{:S(2)}, u32[]{:S(2)}) collective-permute-start(bf16[144,768]{1,0:T(8,128)(2,1)S(1)} %copy-done.2), channel_id=1, source_target_pairs={{0,64},{1,65},{32,96},{33,97},{64,0},{65,1},{96,32},{97,33},{2,66}... | collective-permute-start | bytes 663560 | tf_op jit(solution)/shard_map/ppermute | solution.py:307
  39.6 0.0 collective-permute-done.refs_1_
  39.6 1.6 collective-permute-done.1.refs_2_
  41.2 6.7 %collective-permute-done.2.refs_3_ = bf16[144,768]{1,0:T(8,128)(2,1)S(1)} collective-permute-done((bf16[144,768]{1,0:T(8,128)(2,1)S(1)}, bf16[144,768]{1,0:T(8,128)(2,1)S(1)}, u32[]{:S(2)}, u32[]{:S(2)}) %collective-permute-start.2) | collective-permute-done | bytes 221216 | tf_op jit(solution)/shard_map/ppermute | solution.py:307
  47.9 6.8 %collective-permute-done.3.refs_4_ = bf16[144,768]{1,0:T(8,128)(2,1)S(1)} collective-permute-done((bf16[144,768]{1,0:T(8,128)(2,1)S(1)}, bf16[144,768]{1,0:T(8,128)(2,1)S(1)}, u32[]{:S(2)}, u32[]{:S(2)}) %collective-permute-start.3) | collective-permute-done | bytes 221216 | tf_op jit(solution)/shard_map/ppermute | solution.py:307
  54.7 6.8 %all-to-all-done = bf16[128,9,2,128]{3,2,1,0:T(2,128)(2,1)S(1)} async-done(((bf16[128,9,2,128]{3,2,1,0:T(2,128)(2,1)}), bf16[128,9,2,128]{3,2,1,0:T(2,128)(2,1)S(1)}, u32[]{:S(2)}, u32[]{:S(2)}) %all-to-all-start) | async-done | bytes 589856 | tf_op jit(solution)/shard_map/all_to_all | solution.py:280
  61.5 0.5 copy.11
  62.0 4.4 %shard_map.85 = bf16[72,32,128]{2,1,0:T(8,128)(2,1)S(1)} custom-call(bf16[9,256,128]{2,1,0:T(8,128)(2,1)S(1)} %bitcast.21), custom_call_target="tpu_custom_call" | custom-call | tf_op jit(solution)/shard_map/pallas_call | solution.py:266
  66.3 1.2 copy.12
  67.5 8.2 %all-to-all-start.1 = ((bf16[128,9,2,128]{3,2,1,0:T(2,128)(2,1)}), bf16[128,9,2,128]{3,2,1,0:T(2,128)(2,1)S(1)}, u32[]{:S(2)}, u32[]{:S(2)}) async-start(bf16[128,9,2,128]{3,2,1,0:T(2,128)(2,1)} %bitcast.11), calls=%async_computation.1 | async-start | bytes 1179648 | tf_op jit(solution)/shard_map/all_to_all | solution.py:280
  75.7 5.4 %collective-permute-start.4 = (bf16[144,768]{1,0:T(8,128)(2,1)S(1)}, bf16[144,768]{1,0:T(8,128)(2,1)S(1)}, u32[]{:S(2)}, u32[]{:S(2)}) collective-permute-start(bf16[144,768]{1,0:T(8,128)(2,1)S(1)} %copy-done.2), channel_id=1, source_target_pairs={{0,65},{1,64},{32,97},{33,96},{64,1},{65,0},{96,33},{97,32},{2,67}... | collective-permute-start | bytes 663560 | tf_op jit(solution)/shard_map/ppermute | solution.py:307
  81.1 2.6 %collective-permute-start.5 = (bf16[144,768]{1,0:T(8,128)(2,1)S(1)}, bf16[144,768]{1,0:T(8,128)(2,1)S(1)}, u32[]{:S(2)}, u32[]{:S(2)}) collective-permute-start(bf16[144,768]{1,0:T(8,128)(2,1)S(1)} %copy-done.2), channel_id=1, source_target_pairs={{0,96},{1,97},{32,0},{33,1},{64,32},{65,33},{96,64},{97,65},{2,98}... | collective-permute-start | bytes 663560 | tf_op jit(solution)/shard_map/ppermute | solution.py:307
  83.7 2.2 %collective-permute-start.6 = (bf16[144,768]{1,0:T(8,128)(2,1)S(1)}, bf16[144,768]{1,0:T(8,128)(2,1)S(1)}, u32[]{:S(2)}, u32[]{:S(2)}) collective-permute-start(bf16[144,768]{1,0:T(8,128)(2,1)S(1)} %copy-done.2), channel_id=1, source_target_pairs={{0,97},{1,96},{32,1},{33,0},{64,33},{65,32},{96,65},{97,64},{2,99}... | collective-permute-start | bytes 663560 | tf_op jit(solution)/shard_map/ppermute | solution.py:307
  85.9 0.1 pad_add_fusion.place_ref
  86.0 24.3 %all-to-all-done.1 = bf16[128,9,2,128]{3,2,1,0:T(2,128)(2,1)S(1)} async-done(((bf16[128,9,2,128]{3,2,1,0:T(2,128)(2,1)}), bf16[128,9,2,128]{3,2,1,0:T(2,128)(2,1)S(1)}, u32[]{:S(2)}, u32[]{:S(2)}) %all-to-all-start.1) | async-done | bytes 589856 | tf_op jit(solution)/shard_map/all_to_all | solution.py:280
  110.3 0.5 copy.13
  110.7 0.0 collective-permute-done.4.refs_5_
  110.7 0.0 collective-permute-done.5.refs_6_
  110.8 0.0 collective-permute-done.6.refs_7_
  110.8 2.7 %shard_map.86 = (bf16[16,40,128]{2,1,0:T(8,128)(2,1)}, bf16[8,96,128]{2,1,0:T(8,128)(2,1)S(1)}) custom-call(s32[2]{0:T(128)S(1)} %pad_add_fusion.place_ref, bf16[9,256,128]{2,1,0:T(8,128)(2,1)S(1)} %bitcast.19, bf16[144,768]{1,0:T(8,128)(2,1)S(1)} %copy-done.2, bf16[144,768]{1,0:T(8,128)(2,1)S(1)} %collective-permute-done.refs_1_, ...), custom_call_target="tpu_custom_call" | custom-call | tf_op jit(solution)/shard_map/pallas_call | solution.py:266
  113.5 7.7 %all-to-all-start.2 = ((bf16[16,40,128]{2,1,0:T(8,128)(2,1)}), bf16[16,40,128]{2,1,0:T(8,128)(2,1)S(1)}, u32[]{:S(2)}, u32[]{:S(2)}) async-start(bf16[16,40,128]{2,1,0:T(8,128)(2,1)} %get-tuple-element.33), calls=%async_computation.2 | async-start | bytes 327680 | tf_op jit(solution)/shard_map/all_to_all | solution.py:280
  121.2 1.2 shard_map.87
  122.4 2.4 %collective-permute-start.7 = (bf16[4,144,128]{2,1,0:T(8,128)(2,1)S(1)}, bf16[4,144,128]{2,1,0:T(8,128)(2,1)S(1)}, u32[]{:S(2)}, u32[]{:S(2)}) collective-permute-start(bf16[4,144,128]{2,1,0:T(8,128)(2,1)S(1)} %get-tuple-element.36), channel_id=1, source_target_pairs={{0,1},{1,0},{2,3},{3,2},{4,5},{5,4},{6,7},{7,6},{8,9},{9,8},{10,11... | collective-permute-start | bytes 442376 | tf_op jit(solution)/shard_map/ppermute | solution.py:337
  124.9 1.0 collective-permute-done.7.got_ref
  125.9 2.7 %all-to-all-done.2.in_ref = bf16[16,40,128]{2,1,0:T(8,128)(2,1)S(1)} async-done(((bf16[16,40,128]{2,1,0:T(8,128)(2,1)}), bf16[16,40,128]{2,1,0:T(8,128)(2,1)S(1)}, u32[]{:S(2)}, u32[]{:S(2)}) %all-to-all-start.2) | async-done | bytes 163872 | tf_op jit(solution)/shard_map/all_to_all | solution.py:280
  128.6 16.0 %all_to_all.30.in_ref = bf16[4,40,128]{2,1,0:T(8,128)(2,1)S(1)} all-to-all(bf16[4,40,128]{2,1,0:T(8,128)(2,1)S(1)} %shard_map.88), channel_id=1, replica_groups=mesh['x'=4,'y'=4,'zh'=4,'zl'=4,'c'=2] {'zh'}, dimensions={0} | all-to-all | bytes 81920 | tf_op jit(solution)/shard_map/all_to_all | solution.py:280
  144.7 11.4 %all_to_all.31.block_ref = bf16[16,40,128]{2,1,0:T(8,128)(2,1)S(1)} all-to-all(bf16[16,40,128]{2,1,0:T(8,128)(2,1)S(1)} %shard_map.89), channel_id=1, replica_groups=mesh['x'=4,'y'=4,'zh'=4,'zl'=4,'c'=2] {'x','zl'}, dimensions={0} | all-to-all | bytes 327680 | tf_op jit(solution)/shard_map/all_to_all | solution.py:280
  156.0 0.1 shard_map.90
  156.1 0.0 copy-start
  156.1 0.0 copy-start.1
  156.1 12.5 %all_to_all.32.all_ref.mine_ref = bf16[4,864,128]{2,1,0:T(8,128)(2,1)S(1)} all-to-all(bf16[4,864,128]{2,1,0:T(8,128)(2,1)S(1)} %shard_map.90), channel_id=1, replica_groups=mesh['x'=4,'y'=4,'zh'=4,'zl'=4,'c'=2] {'y'}, dimensions={0} | all-to-all | bytes 1769472 | tf_op jit(solution)/shard_map/all_to_all | solution.py:280
  168.7 6.3 %collective-permute-start.8 = (bf16[4,864,128]{2,1,0:T(8,128)(2,1)S(1)}, bf16[4,864,128]{2,1,0:T(8,128)(2,1)S(1)}, u32[]{:S(2)}, u32[]{:S(2)}) collective-permute-start(bf16[4,864,128]{2,1,0:T(8,128)(2,1)S(1)} %all_to_all.32.all_ref.mine_ref), channel_id=1, source_target_pairs={{0,1},{1,0},{2,3},{3,2},{4,5},{5,4},{6,7},{7,6},{8,9},{9,8},{10,11... | collective-permute-start | bytes 2654216 | tf_op jit(solution)/shard_map/ppermute | solution.py:352
  175.0 0.0 copy-done
  175.0 0.0 copy-done.1
  175.0 1.8 shard_map.91
  176.8 0.2 collective-permute-done.8.other_ref
  177.0 2.0 %shard_map.92 = (bf16[768,384]{1,0:T(8,128)(2,1)}, bf16[768,384]{1,0:T(8,128)(2,1)}) custom-call(s32[2]{0:T(128)S(1)} %pad_add_fusion.place_ref, bf16[4,864,128]{2,1,0:T(8,128)(2,1)S(1)} %all_to_all.32.all_ref.mine_ref, bf16[4,864,128]{2,1,0:T(8,128)(2,1)S(1)} %collective-permute-done.8.other_ref), custom_call_target="tpu_custom_call" | custom-call | tf_op jit(solution)/shard_map/pallas_call | solution.py:266
  (2 shorter events, 0.0 us)
Async XLA Ops:
  6.2 20.7 %copy-start.2 = (bf16[144,768]{1,0:T(8,128)(2,1)S(1)}, bf16[144,768]{1,0:T(8,128)(2,1)}, u32[]{:S(2)}) copy-start(bf16[144,768]{1,0:T(8,128)(2,1)} %get-tuple-element.32.refs_0_) | copy-start | bytes 663556
  6.2 55.2 %all-to-all-start = ((bf16[128,9,2,128]{3,2,1,0:T(2,128)(2,1)}), bf16[128,9,2,128]{3,2,1,0:T(2,128)(2,1)S(1)}, u32[]{:S(2)}, u32[]{:S(2)}) async-start(bf16[128,9,2,128]{3,2,1,0:T(2,128)(2,1)} %bitcast.18), calls=%async_computation | async-start | bytes 1179648 | tf_op jit(solution)/shard_map/all_to_all | solution.py:280
  27.0 12.6 %collective-permute-start = (bf16[144,768]{1,0:T(8,128)(2,1)S(1)}, bf16[144,768]{1,0:T(8,128)(2,1)S(1)}, u32[]{:S(2)}, u32[]{:S(2)}) collective-permute-start(bf16[144,768]{1,0:T(8,128)(2,1)S(1)} %copy-done.2), channel_id=1, source_target_pairs={{0,1},{1,0},{32,33},{33,32},{64,65},{65,64},{96,97},{97,96},{2,3},... | collective-permute-start | bytes 663560 | tf_op jit(solution)/shard_map/ppermute | solution.py:307
  29.8 11.4 %collective-permute-start.1 = (bf16[144,768]{1,0:T(8,128)(2,1)S(1)}, bf16[144,768]{1,0:T(8,128)(2,1)S(1)}, u32[]{:S(2)}, u32[]{:S(2)}) collective-permute-start(bf16[144,768]{1,0:T(8,128)(2,1)S(1)} %copy-done.2), channel_id=1, source_target_pairs={{0,32},{1,33},{32,64},{33,65},{64,96},{65,97},{96,0},{97,1},{2,34}... | collective-permute-start | bytes 663560 | tf_op jit(solution)/shard_map/ppermute | solution.py:307
  32.6 15.2 %collective-permute-start.2 = (bf16[144,768]{1,0:T(8,128)(2,1)S(1)}, bf16[144,768]{1,0:T(8,128)(2,1)S(1)}, u32[]{:S(2)}, u32[]{:S(2)}) collective-permute-start(bf16[144,768]{1,0:T(8,128)(2,1)S(1)} %copy-done.2), channel_id=1, source_target_pairs={{0,33},{1,32},{32,65},{33,64},{64,97},{65,96},{96,1},{97,0},{2,35}... | collective-permute-start | bytes 663560 | tf_op jit(solution)/shard_map/ppermute | solution.py:307
  36.3 18.3 %collective-permute-start.3 = (bf16[144,768]{1,0:T(8,128)(2,1)S(1)}, bf16[144,768]{1,0:T(8,128)(2,1)S(1)}, u32[]{:S(2)}, u32[]{:S(2)}) collective-permute-start(bf16[144,768]{1,0:T(8,128)(2,1)S(1)} %copy-done.2), channel_id=1, source_target_pairs={{0,64},{1,65},{32,96},{33,97},{64,0},{65,1},{96,32},{97,33},{2,66}... | collective-permute-start | bytes 663560 | tf_op jit(solution)/shard_map/ppermute | solution.py:307
  67.5 42.7 %all-to-all-start.1 = ((bf16[128,9,2,128]{3,2,1,0:T(2,128)(2,1)}), bf16[128,9,2,128]{3,2,1,0:T(2,128)(2,1)S(1)}, u32[]{:S(2)}, u32[]{:S(2)}) async-start(bf16[128,9,2,128]{3,2,1,0:T(2,128)(2,1)} %bitcast.11), calls=%async_computation.1 | async-start | bytes 1179648 | tf_op jit(solution)/shard_map/all_to_all | solution.py:280
  75.7 35.0 %collective-permute-start.4 = (bf16[144,768]{1,0:T(8,128)(2,1)S(1)}, bf16[144,768]{1,0:T(8,128)(2,1)S(1)}, u32[]{:S(2)}, u32[]{:S(2)}) collective-permute-start(bf16[144,768]{1,0:T(8,128)(2,1)S(1)} %copy-done.2), channel_id=1, source_target_pairs={{0,65},{1,64},{32,97},{33,96},{64,1},{65,0},{96,33},{97,32},{2,67}... | collective-permute-start | bytes 663560 | tf_op jit(solution)/shard_map/ppermute | solution.py:307
  81.1 29.6 %collective-permute-start.5 = (bf16[144,768]{1,0:T(8,128)(2,1)S(1)}, bf16[144,768]{1,0:T(8,128)(2,1)S(1)}, u32[]{:S(2)}, u32[]{:S(2)}) collective-permute-start(bf16[144,768]{1,0:T(8,128)(2,1)S(1)} %copy-done.2), channel_id=1, source_target_pairs={{0,96},{1,97},{32,0},{33,1},{64,32},{65,33},{96,64},{97,65},{2,98}... | collective-permute-start | bytes 663560 | tf_op jit(solution)/shard_map/ppermute | solution.py:307
  83.7 27.1 %collective-permute-start.6 = (bf16[144,768]{1,0:T(8,128)(2,1)S(1)}, bf16[144,768]{1,0:T(8,128)(2,1)S(1)}, u32[]{:S(2)}, u32[]{:S(2)}) collective-permute-start(bf16[144,768]{1,0:T(8,128)(2,1)S(1)} %copy-done.2), channel_id=1, source_target_pairs={{0,97},{1,96},{32,1},{33,0},{64,33},{65,32},{96,65},{97,64},{2,99}... | collective-permute-start | bytes 663560 | tf_op jit(solution)/shard_map/ppermute | solution.py:307
  113.5 15.1 %all-to-all-start.2 = ((bf16[16,40,128]{2,1,0:T(8,128)(2,1)}), bf16[16,40,128]{2,1,0:T(8,128)(2,1)S(1)}, u32[]{:S(2)}, u32[]{:S(2)}) async-start(bf16[16,40,128]{2,1,0:T(8,128)(2,1)} %get-tuple-element.33), calls=%async_computation.2 | async-start | bytes 327680 | tf_op jit(solution)/shard_map/all_to_all | solution.py:280
  122.4 3.4 %collective-permute-start.7 = (bf16[4,144,128]{2,1,0:T(8,128)(2,1)S(1)}, bf16[4,144,128]{2,1,0:T(8,128)(2,1)S(1)}, u32[]{:S(2)}, u32[]{:S(2)}) collective-permute-start(bf16[4,144,128]{2,1,0:T(8,128)(2,1)S(1)} %get-tuple-element.36), channel_id=1, source_target_pairs={{0,1},{1,0},{2,3},{3,2},{4,5},{5,4},{6,7},{7,6},{8,9},{9,8},{10,11... | collective-permute-start | bytes 442376 | tf_op jit(solution)/shard_map/ppermute | solution.py:337
  156.1 18.8 %copy-start = (bf16[768,384]{1,0:T(8,128)(2,1)S(1)}, bf16[768,384]{1,0:T(8,128)(2,1)}, u32[]{:S(2)}) copy-start(bf16[768,384]{1,0:T(8,128)(2,1)} %ws_ref.1) | copy-start | bytes 1769476
  156.1 18.8 %copy-start.1 = (bf16[768,384]{1,0:T(8,128)(2,1)S(1)}, bf16[768,384]{1,0:T(8,128)(2,1)}, u32[]{:S(2)}) copy-start(bf16[768,384]{1,0:T(8,128)(2,1)} %wv_ref.1) | copy-start | bytes 1769476
  168.7 8.3 %collective-permute-start.8 = (bf16[4,864,128]{2,1,0:T(8,128)(2,1)S(1)}, bf16[4,864,128]{2,1,0:T(8,128)(2,1)S(1)}, u32[]{:S(2)}, u32[]{:S(2)}) collective-permute-start(bf16[4,864,128]{2,1,0:T(8,128)(2,1)S(1)} %all_to_all.32.all_ref.mine_ref), channel_id=1, source_target_pairs={{0,1},{1,0},{2,3},{3,2},{4,5},{5,4},{6,7},{7,6},{8,9},{9,8},{10,11... | collective-permute-start | bytes 2654216 | tf_op jit(solution)/shard_map/ppermute | solution.py:352

commit v5 on v4

--- a/solution.py
+++ b/solution.py
@@ -23,7 +23,6 @@
 PIECE = 36
 SLOT = 40
 BLOCK = 16
-WHOLE = 576
 MESSAGE = 144
 
 
@@ -43,20 +42,14 @@
     ]
     for copy in copies:
         copy.start()
-    tok_ref, ws_ref, wv_ref, cluster_ref, cot_ref = targets
-    for copy in copies:
-        copy.wait()
-    tokens = tok_ref[...]
-    ext_ref[:LOCAL, :] = tokens
-    shared = dot(tokens, ws_ref[...]).astype(BF16)
-    value = dot(tokens, wv_ref[...]).astype(BF16)
-    cot = cot_ref[...]
+    cluster_ref, tok_ref, ws_ref, wv_ref, cot_ref = targets
     sub = iota((LOCAL, LOCAL), 0)
     lane = iota((LOCAL, LOCAL), 1)
     sub_rows = iota((ROWS, LOCAL), 0)
     lane_rows = iota((ROWS, LOCAL), 1)
-    blank = jnp.zeros((LOCAL, HEAD), BF16)
-    pending = None
+    copies[0].wait()
+    hits = []
+    marks = []
     for h in range(HEADS):
         cluster = cluster_ref[h]
         member = (sub == cluster).astype(BF16)
@@ -69,12 +62,23 @@
         ).astype(BF16)
         hit = sub_rows == dest
         used = jnp.sum(jnp.where(hit, 1.0, 0.0), axis=1, keepdims=True)
+        hits.append(hit.astype(BF16))
+        marks.append(jnp.where((lane_rows == 0) & (used < 0.5), UNUSED, 0.0))
+    for copy in copies[1:]:
+        copy.wait()
+    tokens = tok_ref[...]
+    ext_ref[:LOCAL, :] = tokens
+    shared = dot(tokens, ws_ref[...]).astype(BF16)
+    value = dot(tokens, wv_ref[...]).astype(BF16)
+    cot = cot_ref[...]
+    blank = jnp.zeros((LOCAL, HEAD), BF16)
+    pending = None
+    for h in range(HEADS):
         cols = slice(h * HEAD, (h + 1) * HEAD)
         tail = [cot[:, cols], blank] if h % 2 == 0 else [blank, cot[:, cols]]
         packed = jnp.concatenate([shared[:, cols], value[:, cols]] + tail, axis=1)
-        moved = dot(hit.astype(BF16), packed)
-        mark = (lane_rows == 0) & (used < 0.5)
-        out_ref[h] = jnp.where(mark, UNUSED, moved[:, :LOCAL]).astype(BF16)
+        moved = dot(hits[h], packed)
+        out_ref[h] = (moved[:, :LOCAL] + marks[h]).astype(BF16)
         if h % 2 == 0:
             pending = moved[:, LOCAL:]
         else:
@@ -156,7 +160,7 @@
         source = index_of(place_ref, 4 - dy, dc)
         for i in range(2):
             lanes = pl.ds(pl.multiple_of(head[i] * LOCAL, LOCAL), LOCAL)
-            dests[i, source] = exts[n][LOCAL:, lanes].astype(F32)[:8]
+            dests[i, source] = exts[n // 2][n % 2, LOCAL:, lanes].astype(F32)[:8]
     shift = lax.rem(j * turn, 8) * BLOCK
     turned = [pltpu.roll(in_ref[base + b].astype(F32), shift, 1) for b in range(count)]
     limit = lax.rem(j, 4)
@@ -177,12 +181,12 @@
 
 
 def partial_kernel(place_ref, in_ref, *refs):
-    exts, (out_ref, cols_ref), (dests, scratch) = refs[:8], refs[8:10], refs[10:]
+    exts, (out_ref, cols_ref), (dests, scratch) = refs[:4], refs[4:6], refs[6:]
     gather_columns(place_ref, in_ref, 0, 6, 2, exts, dests, cols_ref, 0)
     total = None
     for n, (dy, dc) in enumerate(STEPS):
         source = index_of(place_ref, 4 - dy, dc)
-        term = dot(cols_ref[source], exts[n][:LOCAL, :])
+        term = dot(cols_ref[source], exts[n // 2][n % 2, :LOCAL, :])
         total = term if total is None else total + term
     for k in range(WIDTH // LOCAL):
         scratch[k * COLUMNS : (k + 1) * COLUMNS, :] = total[:, k * LOCAL : (k + 1) * LOCAL]
@@ -192,7 +196,7 @@
 
 
 def forward_kernel(place_ref, in_ref, cols_ref, *refs):
-    exts, (keep_ref, give_ref), (dests, scratch) = refs[:8], refs[8:10], refs[10:]
+    exts, (keep_ref, give_ref), (dests, scratch) = refs[:4], refs[4:6], refs[6:]
     gather_columns(place_ref, in_ref, 6, 3, 5, exts, dests, scratch, 0)
     here = place_ref[1]
     for y in range(4):
@@ -201,21 +205,33 @@
             ref[y, COLUMNS:, :] = scratch[y * 2 + c]
 
 
-def pack_kernel(block_ref, keep_ref, got_ref, out_ref, scratch):
+def pack_kernel(in_ref, keep_ref, give_ref, out_ref):
+    total = in_ref[0].astype(F32)
+    for i in range(1, 4):
+        total = total + in_ref[i].astype(F32)
+    total = jnp.concatenate([total, jnp.zeros((8, LOCAL), F32)], axis=0).astype(BF16)
+    for y in range(4):
+        out_ref[y, :MESSAGE, :] = keep_ref[y]
+        out_ref[y, MESSAGE : 2 * MESSAGE, :] = give_ref[y]
+        out_ref[y, 2 * MESSAGE :, :] = total
+
+
+def repeat_kernel(all_ref, out_ref, keep_ref, give_ref, scratch):
+    for y in range(4):
+        keep_ref[y] = all_ref[y, :MESSAGE, :]
+        give_ref[y] = all_ref[y, MESSAGE : 2 * MESSAGE, :]
+        piece = all_ref[y, 2 * MESSAGE :, :].astype(F32)
+        scratch[y * PIECE : (y + 1) * PIECE, :] = piece[:PIECE]
+    block = scratch[...].astype(BF16)
     for i in range(16):
-        scratch[i * PIECE : (i + 1) * PIECE, :] = block_ref[i].astype(F32)[:PIECE]
-    block = scratch[...].astype(BF16)
-    for y in range(4):
-        out_ref[y, :WHOLE, :] = block
-        out_ref[y, WHOLE : WHOLE + MESSAGE, :] = keep_ref[y]
-        out_ref[y, WHOLE + MESSAGE :, :] = got_ref[y]
-
-
-def return_kernel(place_ref, all_ref, ws_ref, wv_ref, att_ref, grad_ref, held):
+        out_ref[i] = block
+
+
+def return_kernel(place_ref, keep_ref, got_ref, ws_ref, wv_ref, att_ref, grad_ref, held):
     here = place_ref[1]
     for y in range(4):
-        held[y * 2 + here] = all_ref[y, WHOLE : WHOLE + MESSAGE, :]
-        held[y * 2 + 1 - here] = all_ref[y, WHOLE + MESSAGE :, :]
+        held[y * 2 + here] = keep_ref[y]
+        held[y * 2 + 1 - here] = got_ref[y]
 
     def columns(blocks, per, first):
         rows = [
@@ -240,15 +256,19 @@
         out_ref[i] = total
 
 
-def finish_kernel(place_ref, mine_ref, other_ref, shared_ref, value_ref):
-    first = place_ref[1] == 0
+def finish_kernel(place_ref, mine_ref, other_ref, shared_ref, value_ref, wide, scratch):
+    here = place_ref[1]
+    for i in range(16):
+        wide[0, i] = mine_ref[i].astype(F32)
+        wide[1, i] = other_ref[i].astype(F32)
+    for y in range(4):
+        for i in range(16):
+            rows = slice(i * PIECE, (i + 1) * PIECE)
+            scratch[here, y, rows, :] = wide[0, i, y * PIECE : (y + 1) * PIECE, :]
+            scratch[1 - here, y, rows, :] = wide[1, i, y * PIECE : (y + 1) * PIECE, :]
     for k in range(WIDTH // LOCAL):
-        rows = slice(k * COLUMNS, (k + 1) * COLUMNS)
-        strip = []
-        for y in range(4):
-            mine = mine_ref[y, rows, :].astype(F32)
-            other = other_ref[y, rows, :].astype(F32)
-            strip += [jnp.where(first, mine, other), jnp.where(first, other, mine)]
+        first = k * COLUMNS
+        strip = [scratch[j % 2, j // 2, first : first + COLUMNS, :] for j in range(8)]
         strip = jnp.concatenate(strip, axis=0)
         for half, ref in enumerate((shared_ref, value_ref)):
             heads = [
@@ -260,7 +280,8 @@
 
 def call(kernel, out, *args, scratch=(), scalars=0, held=False):
     space = pl.ANY if held else pltpu.VMEM
-    limit = (60 if held else 48) * 1024 * 1024
+    if held:
+        args = [pltpu.with_memory_space_constraint(arg, pltpu.HBM) for arg in args]
     specs = [pl.BlockSpec(memory_space=pltpu.SMEM)] * scalars
     specs += [pl.BlockSpec(memory_space=space)] * (len(args) - scalars)
     return pl.pallas_call(
@@ -268,7 +289,7 @@
         out_shape=out,
         in_specs=specs,
         scratch_shapes=scratch,
-        compiler_params=pltpu.CompilerParams(vmem_limit_bytes=limit),
+        compiler_params=pltpu.CompilerParams(vmem_limit_bytes=48 * 1024 * 1024),
     )(*args)
 
 
@@ -286,30 +307,32 @@
     sent, ext = call(
         send_kernel,
         (shape(9, ROWS, LOCAL), shape(LOCAL + 16, WIDTH)),
+        cluster_ids.transpose(1, 0, 2),
         rows,
         w_shared,
         w_value,
-        cluster_ids.transpose(1, 0, 2),
         cotangent[0],
         scratch=[
+            pltpu.VMEM((HEADS, 1, LOCAL), jnp.int32),
             pltpu.VMEM((LOCAL, WIDTH), BF16),
             pltpu.VMEM((WIDTH, PROJ), BF16),
             pltpu.VMEM((WIDTH, PROJ), BF16),
-            pltpu.VMEM((HEADS, 1, LOCAL), jnp.int32),
             pltpu.VMEM((LOCAL, PROJ), BF16),
             pltpu.SemaphoreType.DMA((5,)),
         ],
         held=True,
     )
 
-    def shift(part, dy, dc):
-        pairs = [(y * 2 + c, (y + dy) % 4 * 2 + (c + dc) % 2) for y in range(4) for c in range(2)]
-        return lax.ppermute(part, PLANE, pairs) if dy or dc else part
+    def shift(pair, dy):
+        return lax.ppermute(pair, "y", [(y, (y + dy) % 4) for y in range(4)])
+
+    def flip(part):
+        return lax.ppermute(part, "c", [(0, 1), (1, 0)])
 
     arrived = swap(sent.reshape(9, LOCAL, 2, LOCAL).transpose(1, 0, 2, 3), OWNERS)
-    early = [shift(ext, dy, dc) for dy, dc in STEPS[:5]]
-    arrived, ext, early = lax.optimization_barrier((arrived, ext, early))
-    exts = early + [shift(ext, dy, dc) for dy, dc in STEPS[5:]]
+    pair = jnp.stack([ext, flip(ext)])
+    exts = [pair] + [shift(pair, dy) for dy in range(1, 4)]
+    arrived, exts, place = lax.optimization_barrier((arrived, exts, place))
     arrived = arrived.transpose(1, 0, 2, 3)
     worked = call(attend_kernel, shape(72, 32, LOCAL), arrived.reshape(9, ROWS, LOCAL))
     worked = worked.reshape(8, 9, 16, 2, LOCAL).transpose(0, 2, 1, 3, 4)
@@ -334,38 +357,38 @@
         scratch=[pltpu.VMEM((2, 8, 8, LOCAL), F32), pltpu.VMEM((8, COLUMNS // 2, LOCAL), BF16)],
         scalars=1,
     )
-    got = lax.ppermute(give, "c", [(0, 1), (1, 0)])
-    part = swap(part, ("x", "zl"))
-    part, keep, got = lax.optimization_barrier((part, keep, got))
-    part = call(sum_kernel, shape(4, SLOT, LOCAL), part)
-    block = call(sum_kernel, shape(16, SLOT, LOCAL), swap(part, "zh"))
-    block = swap(block, ("x", "zl"))
-    block = call(
-        pack_kernel,
-        shape(4, WHOLE + 2 * MESSAGE, LOCAL),
+    part, keep, give = lax.optimization_barrier((swap(part, ("x", "zl")), keep, give))
+    part = swap(call(sum_kernel, shape(4, SLOT, LOCAL), part), "zh")
+    block = swap(call(pack_kernel, shape(4, 2 * MESSAGE + 48, LOCAL), part, keep, give), "y")
+    pieces, keep, give = call(
+        repeat_kernel,
+        (shape(16, 4 * PIECE, LOCAL), shape(4, MESSAGE, LOCAL), shape(4, MESSAGE, LOCAL)),
         block,
-        keep,
-        got,
-        scratch=[pltpu.VMEM((WHOLE, LOCAL), F32)],
-    )
-    block = swap(block, "y")
-    other = lax.ppermute(block, "c", [(0, 1), (1, 0)])
+        scratch=[pltpu.VMEM((4 * PIECE, LOCAL), F32)],
+    )
     attention, grad_tokens = call(
         return_kernel,
         (shape(LOCAL, PROJ), shape(LOCAL, WIDTH)),
         place,
-        block,
+        keep,
+        flip(give),
         w_shared,
         w_value,
         scratch=[pltpu.VMEM((8, MESSAGE, LOCAL), BF16)],
         scalars=1,
     )
+    pieces = swap(pieces, ("x", "zl"))
+    pieces, attention, grad_tokens = lax.optimization_barrier((pieces, attention, grad_tokens))
     grad_shared, grad_value = call(
         finish_kernel,
         (shape(WIDTH, PROJ), shape(WIDTH, PROJ)),
         place,
-        block,
-        other,
+        pieces,
+        flip(pieces),
+        scratch=[
+            pltpu.VMEM((2, 16, 4 * PIECE, LOCAL), F32),
+            pltpu.VMEM((2, 4, 16 * PIECE, LOCAL), F32),
+        ],
         scalars=1,
     )
     return (attention[None], grad_tokens[None], grad_shared, grad_value)

time: 180 us -> 188 us (1.044)
  blocking collectives: 39.9 us -> 74.7 us
  waiting for transfers between devices: 50.2 us -> 37.7 us
  starting transfers between devices: 68.1 us -> 55.7 us
  local copies, waits for them, and re-layouts: 4.43 us -> 2.54 us
    all_to_all x3, blocking collectives: 39.9 us -> 74.7 us  [swap(): return lax.all_to_all(rows, axes, split_axis=0, concat_axis=0, tiled=True)]
    all_to_all x3, waiting for transfers between devices: 33.8 us -> 13.8 us  [swap(): return lax.all_to_all(rows, axes, split_axis=0, concat_axis=0, tiled=True)]
    ppermute x9 -> x6, starting transfers between devices: 31.4 us -> 23.7 us  [the longest x3 13.1 us: flip(): return lax.ppermute(part, 'c', [(0, 1), (1, 0)])]
    ppermute x9 -> x6, waiting for transfers between devices: 16.3 us -> 23.9 us  [the longest x3 20.2 us: shift(): return lax.ppermute(pair, 'y', [(y, (y + dy) % 4) for y in range(4)])]
    all_to_all x3, starting transfers between devices: 36.6 us -> 32 us  [swap(): return lax.all_to_all(rows, axes, split_axis=0, concat_axis=0, tiled=True)]
  transfers between devices with their start and end apart: 12 -> 9, of which waited for: 8 -> 8; matrix products, arithmetic and copies ran while one was open for 0% -> 0% of each run, Pallas kernels for 2% -> 2%
where the time goes in v5:
time: 188 us; the launch traced here: 187 us
  blocking collectives  74.7 us (40%)
  starting transfers between devices  55.7 us (30%)
  waiting for transfers between devices  37.7 us (20%)
  Pallas kernels  15.4 us (8%)
  local copies, waits for them, and re-layouts  2.54 us (1%)
    all_to_all x3, blocking collectives, swap(): return lax.all_to_all(rows, axes, split_axis=0, concat_axis=0, tiled=True)  74.7 us
    all_to_all x3, starting transfers between devices, swap(): return lax.all_to_all(rows, axes, split_axis=0, concat_axis=0, tiled=True)  32 us
    ppermute x3, waiting for transfers between devices, shift(): return lax.ppermute(pair, 'y', [(y, (y + dy) % 4) for y in range(4)])  20.2 us
    pallas_call x9, Pallas kernels, call(): pl.pallas_call(kernel, out_shape=out, in_specs=specs, scratch_shapes=scra...  15.4 us
    all_to_all x3, waiting for transfers between devices, swap(): return lax.all_to_all(rows, axes, split_axis=0, concat_axis=0, tiled=True)  13.8 us
    ppermute x3, starting transfers between devices, flip(): return lax.ppermute(part, 'c', [(0, 1), (1, 0)])  13.1 us
    ppermute x3, starting transfers between devices, shift(): return lax.ppermute(pair, 'y', [(y, (y + dy) % 4) for y in range(4)])  10.6 us
  transfers between devices with their start and end apart: 9, of which 8 were waited for; matrix products, arithmetic and copies ran while one was open for 0% of the time, Pallas kernels for 2%

profile of v5, /device:TPU:1, one launch (start us, length us, event | category | flops | bytes accessed | tf_op | source)
XLA Modules:
  0.0 187.0 jit_solution(10604856343631298239)
XLA Ops:
  0.6 2.2 %shard_map.84 = (bf16[9,256,128]{2,1,0:T(8,128)(2,1)S(1)}, bf16[144,768]{1,0:T(8,128)(2,1)S(1)}) custom-call(s32[6,1,128]{2,1,0:T(1,128)} %bitcast.33, bf16[128,768]{1,0:T(8,128)(2,1)} %bitcast.31, bf16[768,384]{1,0:T(8,128)(2,1)} %ws_ref.1, bf16[768,384]{1,0:T(8,128)(2,1)} %wv_ref.1, bf16[128,384]{1,0:T(8,128)(2,1)} %bitcast.32), custom_call_target="tpu_custom_call" | custom-call | tf_op jit(solution)/shard_map/pallas_call | solution.py:287
  2.8 1.2 copy.15
  4.0 20.6 %all-to-all-start = ((bf16[128,9,2,128]{3,2,1,0:T(2,128)(2,1)}), bf16[128,9,2,128]{3,2,1,0:T(2,128)(2,1)S(1)}, u32[]{:S(2)}, u32[]{:S(2)}) async-start(bf16[128,9,2,128]{3,2,1,0:T(2,128)(2,1)} %bitcast.20), calls=%async_computation | async-start | bytes 1179648 | tf_op jit(solution)/shard_map/all_to_all | solution.py:301
  24.6 2.8 %collective-permute-start = (bf16[144,768]{1,0:T(8,128)(2,1)S(1)}, bf16[144,768]{1,0:T(8,128)(2,1)S(1)}, u32[]{:S(2)}, u32[]{:S(2)}) collective-permute-start(bf16[144,768]{1,0:T(8,128)(2,1)S(1)} %get-tuple-element.30), channel_id=1, source_target_pairs={{0,1},{1,0},{2,3},{3,2},{4,5},{5,4},{6,7},{7,6},{8,9},{9,8},{10,11... | collective-permute-start | bytes 663560 | tf_op jit(solution)/shard_map/ppermute | solution.py:330
  27.4 1.1 collective-permute-done
  28.5 2.9 %collective-permute-start.1 = (bf16[2,144,768]{2,1,0:T(8,128)(2,1)S(1)}, bf16[2,144,768]{2,1,0:T(8,128)(2,1)S(1)}, u32[]{:S(2)}, u32[]{:S(2)}) collective-permute-start(bf16[2,144,768]{2,1,0:T(8,128)(2,1)S(1)} %pad_maximum_fusion.refs_0_), channel_id=1, source_target_pairs={{0,32},{32,64},{64,96},{96,0},{1,33},{33,65},{65,97},{97,1},{2,34}... | collective-permute-start | bytes 1327112 | tf_op jit(solution)/shard_map/ppermute | solution.py:327
  31.5 4.7 %collective-permute-start.2 = (bf16[2,144,768]{2,1,0:T(8,128)(2,1)S(1)}, bf16[2,144,768]{2,1,0:T(8,128)(2,1)S(1)}, u32[]{:S(2)}, u32[]{:S(2)}) collective-permute-start(bf16[2,144,768]{2,1,0:T(8,128)(2,1)S(1)} %pad_maximum_fusion.refs_0_), channel_id=1, source_target_pairs={{0,64},{32,96},{64,0},{96,32},{1,65},{33,97},{65,1},{97,33},{2,66}... | collective-permute-start | bytes 1327112 | tf_op jit(solution)/shard_map/ppermute | solution.py:327
  36.2 2.9 %collective-permute-start.3 = (bf16[2,144,768]{2,1,0:T(8,128)(2,1)S(1)}, bf16[2,144,768]{2,1,0:T(8,128)(2,1)S(1)}, u32[]{:S(2)}, u32[]{:S(2)}) collective-permute-start(bf16[2,144,768]{2,1,0:T(8,128)(2,1)S(1)} %pad_maximum_fusion.refs_0_), channel_id=1, source_target_pairs={{0,96},{32,0},{64,32},{96,64},{1,97},{33,1},{65,33},{97,65},{2,98}... | collective-permute-start | bytes 1327112 | tf_op jit(solution)/shard_map/ppermute | solution.py:327
  39.1 0.1 pad_add_fusion.place_ref
  39.2 6.7 %collective-permute-done.1.refs_1_ = bf16[2,144,768]{2,1,0:T(8,128)(2,1)S(1)} collective-permute-done((bf16[2,144,768]{2,1,0:T(8,128)(2,1)S(1)}, bf16[2,144,768]{2,1,0:T(8,128)(2,1)S(1)}, u32[]{:S(2)}, u32[]{:S(2)}) %collective-permute-start.1) | collective-permute-done | bytes 442400 | tf_op jit(solution)/shard_map/ppermute | solution.py:327
  45.9 12.9 %collective-permute-done.2.refs_2_ = bf16[2,144,768]{2,1,0:T(8,128)(2,1)S(1)} collective-permute-done((bf16[2,144,768]{2,1,0:T(8,128)(2,1)S(1)}, bf16[2,144,768]{2,1,0:T(8,128)(2,1)S(1)}, u32[]{:S(2)}, u32[]{:S(2)}) %collective-permute-start.2) | collective-permute-done | bytes 442400 | tf_op jit(solution)/shard_map/ppermute | solution.py:327
  58.8 0.6 collective-permute-done.3.refs_3_
  59.4 0.0 all-to-all-done
  59.4 0.5 copy.11
  59.9 4.4 %shard_map.85 = bf16[72,32,128]{2,1,0:T(8,128)(2,1)S(1)} custom-call(bf16[9,256,128]{2,1,0:T(8,128)(2,1)S(1)} %bitcast.23), custom_call_target="tpu_custom_call" | custom-call | tf_op jit(solution)/shard_map/pallas_call | solution.py:287
  64.3 0.4 copy.12
  64.7 49.9 %all_to_all.30 = bf16[128,9,2,128]{3,2,1,0:T(2,128)(2,1)S(1)} all-to-all(bf16[128,9,2,128]{3,2,1,0:T(2,128)(2,1)S(1)} %bitcast.28), channel_id=1, replica_groups=mesh['x'=4,'y'=4,'zh'=4,'zl'=4,'c'=2] {'y','c','zh','zl'}, dimensions={0} | all-to-all | bytes 1179648 | tf_op jit(solution)/shard_map/all_to_all | solution.py:301
  114.6 0.5 copy.13
  115.1 2.7 %shard_map.86 = (bf16[16,40,128]{2,1,0:T(8,128)(2,1)}, bf16[8,96,128]{2,1,0:T(8,128)(2,1)S(1)}) custom-call(s32[2]{0:T(128)S(1)} %pad_add_fusion.place_ref, bf16[9,256,128]{2,1,0:T(8,128)(2,1)S(1)} %bitcast.21, bf16[2,144,768]{2,1,0:T(8,128)(2,1)S(1)} %pad_maximum_fusion.refs_0_, bf16[2,144,768]{2,1,0:T(8,128)(2,1)S(1)} %collective-permute-done.1.refs_1_, ...), custom_call_target="tpu_custom_call" | custom-call | tf_op jit(solution)/shard_map/pallas_call | solution.py:287
  117.8 7.7 %all-to-all-start.2 = ((bf16[16,40,128]{2,1,0:T(8,128)(2,1)}), bf16[16,40,128]{2,1,0:T(8,128)(2,1)S(1)}, u32[]{:S(2)}, u32[]{:S(2)}) async-start(bf16[16,40,128]{2,1,0:T(8,128)(2,1)} %get-tuple-element.37), calls=%async_computation.2 | async-start | bytes 327680 | tf_op jit(solution)/shard_map/all_to_all | solution.py:301
  125.5 1.2 shard_map.87
  126.7 6.2 %all-to-all-done.2.in_ref = bf16[16,40,128]{2,1,0:T(8,128)(2,1)S(1)} async-done(((bf16[16,40,128]{2,1,0:T(8,128)(2,1)}), bf16[16,40,128]{2,1,0:T(8,128)(2,1)S(1)}, u32[]{:S(2)}, u32[]{:S(2)}) %all-to-all-start.2) | async-done | bytes 163872 | tf_op jit(solution)/shard_map/all_to_all | solution.py:301
  132.9 16.0 %all_to_all.31.in_ref = bf16[4,40,128]{2,1,0:T(8,128)(2,1)S(1)} all-to-all(bf16[4,40,128]{2,1,0:T(8,128)(2,1)S(1)} %shard_map.88), channel_id=1, replica_groups=mesh['x'=4,'y'=4,'zh'=4,'zl'=4,'c'=2] {'zh'}, dimensions={0} | all-to-all | bytes 81920 | tf_op jit(solution)/shard_map/all_to_all | solution.py:301
  149.0 8.7 %all_to_all.32.all_ref = bf16[4,336,128]{2,1,0:T(8,128)(2,1)S(1)} all-to-all(bf16[4,336,128]{2,1,0:T(8,128)(2,1)S(1)} %shard_map.89), channel_id=1, replica_groups=mesh['x'=4,'y'=4,'zh'=4,'zl'=4,'c'=2] {'y'}, dimensions={0} | all-to-all | bytes 688128 | tf_op jit(solution)/shard_map/all_to_all | solution.py:301
  157.7 0.9 shard_map.90
  158.6 0.0 copy-start
  158.6 0.0 copy-start.1
  158.6 3.7 %all-to-all-start.5 = ((bf16[16,144,128]{2,1,0:T(8,128)(2,1)}), bf16[16,144,128]{2,1,0:T(8,128)(2,1)S(1)}, u32[]{:S(2)}, u32[]{:S(2)}) async-start(bf16[16,144,128]{2,1,0:T(8,128)(2,1)} %get-tuple-element.44), calls=%async_computation.5 | async-start | bytes 1179648 | tf_op jit(solution)/shard_map/all_to_all | solution.py:301
  162.3 5.7 %collective-permute-start.4 = (bf16[4,144,128]{2,1,0:T(8,128)(2,1)S(1)}, bf16[4,144,128]{2,1,0:T(8,128)(2,1)S(1)}, u32[]{:S(2)}, u32[]{:S(2)}) collective-permute-start(bf16[4,144,128]{2,1,0:T(8,128)(2,1)S(1)} %get-tuple-element.46), channel_id=1, source_target_pairs={{0,1},{1,0},{2,3},{3,2},{4,5},{5,4},{6,7},{7,6},{8,9},{9,8},{10,11... | collective-permute-start | bytes 442376 | tf_op jit(solution)/shard_map/ppermute | solution.py:330
  168.1 1.0 collective-permute-done.4.got_ref
  169.1 0.0 copy-done
  169.1 0.0 copy-done.1
  169.1 1.8 shard_map.91
  170.9 7.6 %all-to-all-done.5.mine_ref = bf16[16,144,128]{2,1,0:T(8,128)(2,1)S(1)} async-done(((bf16[16,144,128]{2,1,0:T(8,128)(2,1)}), bf16[16,144,128]{2,1,0:T(8,128)(2,1)S(1)}, u32[]{:S(2)}, u32[]{:S(2)}) %all-to-all-start.5) | async-done | bytes 589856 | tf_op jit(solution)/shard_map/all_to_all | solution.py:301
  178.5 4.6 %collective-permute-start.5 = (bf16[16,144,128]{2,1,0:T(8,128)(2,1)S(1)}, bf16[16,144,128]{2,1,0:T(8,128)(2,1)S(1)}, u32[]{:S(2)}, u32[]{:S(2)}) collective-permute-start(bf16[16,144,128]{2,1,0:T(8,128)(2,1)S(1)} %all-to-all-done.5.mine_ref), channel_id=1, source_target_pairs={{0,1},{1,0},{2,3},{3,2},{4,5},{5,4},{6,7},{7,6},{8,9},{9,8},{10,11... | collective-permute-start | bytes 1769480 | tf_op jit(solution)/shard_map/ppermute | solution.py:330
  183.1 1.6 collective-permute-done.5.other_ref
  184.7 2.3 %shard_map.92 = (bf16[768,384]{1,0:T(8,128)(2,1)}, bf16[768,384]{1,0:T(8,128)(2,1)}) custom-call(s32[2]{0:T(128)S(1)} %pad_add_fusion.place_ref, bf16[16,144,128]{2,1,0:T(8,128)(2,1)S(1)} %all-to-all-done.5.mine_ref, bf16[16,144,128]{2,1,0:T(8,128)(2,1)S(1)} %collective-permute-done.5.other_ref), custom_call_target="tpu_custom_call" | custom-call | tf_op jit(solution)/shard_map/pallas_call | solution.py:287
  (3 shorter events, 0.1 us)
Async XLA Ops:
  4.0 55.4 %all-to-all-start = ((bf16[128,9,2,128]{3,2,1,0:T(2,128)(2,1)}), bf16[128,9,2,128]{3,2,1,0:T(2,128)(2,1)S(1)}, u32[]{:S(2)}, u32[]{:S(2)}) async-start(bf16[128,9,2,128]{3,2,1,0:T(2,128)(2,1)} %bitcast.20), calls=%async_computation | async-start | bytes 1179648 | tf_op jit(solution)/shard_map/all_to_all | solution.py:301
  24.6 3.9 %collective-permute-start = (bf16[144,768]{1,0:T(8,128)(2,1)S(1)}, bf16[144,768]{1,0:T(8,128)(2,1)S(1)}, u32[]{:S(2)}, u32[]{:S(2)}) collective-permute-start(bf16[144,768]{1,0:T(8,128)(2,1)S(1)} %get-tuple-element.30), channel_id=1, source_target_pairs={{0,1},{1,0},{2,3},{3,2},{4,5},{5,4},{6,7},{7,6},{8,9},{9,8},{10,11... | collective-permute-start | bytes 663560 | tf_op jit(solution)/shard_map/ppermute | solution.py:330
  28.5 17.4 %collective-permute-start.1 = (bf16[2,144,768]{2,1,0:T(8,128)(2,1)S(1)}, bf16[2,144,768]{2,1,0:T(8,128)(2,1)S(1)}, u32[]{:S(2)}, u32[]{:S(2)}) collective-permute-start(bf16[2,144,768]{2,1,0:T(8,128)(2,1)S(1)} %pad_maximum_fusion.refs_0_), channel_id=1, source_target_pairs={{0,32},{32,64},{64,96},{96,0},{1,33},{33,65},{65,97},{97,1},{2,34}... | collective-permute-start | bytes 1327112 | tf_op jit(solution)/shard_map/ppermute | solution.py:327
  31.5 27.4 %collective-permute-start.2 = (bf16[2,144,768]{2,1,0:T(8,128)(2,1)S(1)}, bf16[2,144,768]{2,1,0:T(8,128)(2,1)S(1)}, u32[]{:S(2)}, u32[]{:S(2)}) collective-permute-start(bf16[2,144,768]{2,1,0:T(8,128)(2,1)S(1)} %pad_maximum_fusion.refs_0_), channel_id=1, source_target_pairs={{0,64},{32,96},{64,0},{96,32},{1,65},{33,97},{65,1},{97,33},{2,66}... | collective-permute-start | bytes 1327112 | tf_op jit(solution)/shard_map/ppermute | solution.py:327
  36.2 23.2 %collective-permute-start.3 = (bf16[2,144,768]{2,1,0:T(8,128)(2,1)S(1)}, bf16[2,144,768]{2,1,0:T(8,128)(2,1)S(1)}, u32[]{:S(2)}, u32[]{:S(2)}) collective-permute-start(bf16[2,144,768]{2,1,0:T(8,128)(2,1)S(1)} %pad_maximum_fusion.refs_0_), channel_id=1, source_target_pairs={{0,96},{32,0},{64,32},{96,64},{1,97},{33,1},{65,33},{97,65},{2,98}... | collective-permute-start | bytes 1327112 | tf_op jit(solution)/shard_map/ppermute | solution.py:327
  117.8 15.1 %all-to-all-start.2 = ((bf16[16,40,128]{2,1,0:T(8,128)(2,1)}), bf16[16,40,128]{2,1,0:T(8,128)(2,1)S(1)}, u32[]{:S(2)}, u32[]{:S(2)}) async-start(bf16[16,40,128]{2,1,0:T(8,128)(2,1)} %get-tuple-element.37), calls=%async_computation.2 | async-start | bytes 327680 | tf_op jit(solution)/shard_map/all_to_all | solution.py:301
  158.6 10.5 %copy-start = (bf16[768,384]{1,0:T(8,128)(2,1)S(1)}, bf16[768,384]{1,0:T(8,128)(2,1)}, u32[]{:S(2)}) copy-start(bf16[768,384]{1,0:T(8,128)(2,1)} %ws_ref.1) | copy-start | bytes 1769476
  158.6 10.5 %copy-start.1 = (bf16[768,384]{1,0:T(8,128)(2,1)S(1)}, bf16[768,384]{1,0:T(8,128)(2,1)}, u32[]{:S(2)}) copy-start(bf16[768,384]{1,0:T(8,128)(2,1)} %wv_ref.1) | copy-start | bytes 1769476
  158.6 19.9 %all-to-all-start.5 = ((bf16[16,144,128]{2,1,0:T(8,128)(2,1)}), bf16[16,144,128]{2,1,0:T(8,128)(2,1)S(1)}, u32[]{:S(2)}, u32[]{:S(2)}) async-start(bf16[16,144,128]{2,1,0:T(8,128)(2,1)} %get-tuple-element.44), calls=%async_computation.5 | async-start | bytes 1179648 | tf_op jit(solution)/shard_map/all_to_all | solution.py:301
  162.3 6.7 %collective-permute-start.4 = (bf16[4,144,128]{2,1,0:T(8,128)(2,1)S(1)}, bf16[4,144,128]{2,1,0:T(8,128)(2,1)S(1)}, u32[]{:S(2)}, u32[]{:S(2)}) collective-permute-start(bf16[4,144,128]{2,1,0:T(8,128)(2,1)S(1)} %get-tuple-element.46), channel_id=1, source_target_pairs={{0,1},{1,0},{2,3},{3,2},{4,5},{5,4},{6,7},{7,6},{8,9},{9,8},{10,11... | collective-permute-start | bytes 442376 | tf_op jit(solution)/shard_map/ppermute | solution.py:330
  178.5 6.2 %collective-permute-start.5 = (bf16[16,144,128]{2,1,0:T(8,128)(2,1)S(1)}, bf16[16,144,128]{2,1,0:T(8,128)(2,1)S(1)}, u32[]{:S(2)}, u32[]{:S(2)}) collective-permute-start(bf16[16,144,128]{2,1,0:T(8,128)(2,1)S(1)} %all-to-all-done.5.mine_ref), channel_id=1, source_target_pairs={{0,1},{1,0},{2,3},{3,2},{4,5},{5,4},{6,7},{7,6},{8,9},{9,8},{10,11... | collective-permute-start | bytes 1769480 | tf_op jit(solution)/shard_map/ppermute | solution.py:330

commit v6 on v4

--- a/solution.py
+++ b/solution.py
@@ -43,20 +43,14 @@
     ]
     for copy in copies:
         copy.start()
-    tok_ref, ws_ref, wv_ref, cluster_ref, cot_ref = targets
-    for copy in copies:
-        copy.wait()
-    tokens = tok_ref[...]
-    ext_ref[:LOCAL, :] = tokens
-    shared = dot(tokens, ws_ref[...]).astype(BF16)
-    value = dot(tokens, wv_ref[...]).astype(BF16)
-    cot = cot_ref[...]
+    cluster_ref, tok_ref, ws_ref, wv_ref, cot_ref = targets
     sub = iota((LOCAL, LOCAL), 0)
     lane = iota((LOCAL, LOCAL), 1)
     sub_rows = iota((ROWS, LOCAL), 0)
     lane_rows = iota((ROWS, LOCAL), 1)
-    blank = jnp.zeros((LOCAL, HEAD), BF16)
-    pending = None
+    copies[0].wait()
+    hits = []
+    marks = []
     for h in range(HEADS):
         cluster = cluster_ref[h]
         member = (sub == cluster).astype(BF16)
@@ -69,12 +63,23 @@
         ).astype(BF16)
         hit = sub_rows == dest
         used = jnp.sum(jnp.where(hit, 1.0, 0.0), axis=1, keepdims=True)
+        hits.append(hit.astype(BF16))
+        marks.append(jnp.where((lane_rows == 0) & (used < 0.5), UNUSED, 0.0))
+    for copy in copies[1:]:
+        copy.wait()
+    tokens = tok_ref[...]
+    ext_ref[:LOCAL, :] = tokens
+    shared = dot(tokens, ws_ref[...]).astype(BF16)
+    value = dot(tokens, wv_ref[...]).astype(BF16)
+    cot = cot_ref[...]
+    blank = jnp.zeros((LOCAL, HEAD), BF16)
+    pending = None
+    for h in range(HEADS):
         cols = slice(h * HEAD, (h + 1) * HEAD)
         tail = [cot[:, cols], blank] if h % 2 == 0 else [blank, cot[:, cols]]
         packed = jnp.concatenate([shared[:, cols], value[:, cols]] + tail, axis=1)
-        moved = dot(hit.astype(BF16), packed)
-        mark = (lane_rows == 0) & (used < 0.5)
-        out_ref[h] = jnp.where(mark, UNUSED, moved[:, :LOCAL]).astype(BF16)
+        moved = dot(hits[h], packed)
+        out_ref[h] = (moved[:, :LOCAL] + marks[h]).astype(BF16)
         if h % 2 == 0:
             pending = moved[:, LOCAL:]
         else:
@@ -156,7 +161,7 @@
         source = index_of(place_ref, 4 - dy, dc)
         for i in range(2):
             lanes = pl.ds(pl.multiple_of(head[i] * LOCAL, LOCAL), LOCAL)
-            dests[i, source] = exts[n][LOCAL:, lanes].astype(F32)[:8]
+            dests[i, source] = exts[n // 2][n % 2, LOCAL:, lanes].astype(F32)[:8]
     shift = lax.rem(j * turn, 8) * BLOCK
     turned = [pltpu.roll(in_ref[base + b].astype(F32), shift, 1) for b in range(count)]
     limit = lax.rem(j, 4)
@@ -177,12 +182,12 @@
 
 
 def partial_kernel(place_ref, in_ref, *refs):
-    exts, (out_ref, cols_ref), (dests, scratch) = refs[:8], refs[8:10], refs[10:]
+    exts, (out_ref, cols_ref), (dests, scratch) = refs[:4], refs[4:6], refs[6:]
     gather_columns(place_ref, in_ref, 0, 6, 2, exts, dests, cols_ref, 0)
     total = None
     for n, (dy, dc) in enumerate(STEPS):
         source = index_of(place_ref, 4 - dy, dc)
-        term = dot(cols_ref[source], exts[n][:LOCAL, :])
+        term = dot(cols_ref[source], exts[n // 2][n % 2, :LOCAL, :])
         total = term if total is None else total + term
     for k in range(WIDTH // LOCAL):
         scratch[k * COLUMNS : (k + 1) * COLUMNS, :] = total[:, k * LOCAL : (k + 1) * LOCAL]
@@ -192,7 +197,7 @@
 
 
 def forward_kernel(place_ref, in_ref, cols_ref, *refs):
-    exts, (keep_ref, give_ref), (dests, scratch) = refs[:8], refs[8:10], refs[10:]
+    exts, (keep_ref, give_ref), (dests, scratch) = refs[:4], refs[4:6], refs[6:]
     gather_columns(place_ref, in_ref, 6, 3, 5, exts, dests, scratch, 0)
     here = place_ref[1]
     for y in range(4):
@@ -260,7 +265,8 @@
 
 def call(kernel, out, *args, scratch=(), scalars=0, held=False):
     space = pl.ANY if held else pltpu.VMEM
-    limit = (60 if held else 48) * 1024 * 1024
+    if held:
+        args = [pltpu.with_memory_space_constraint(arg, pltpu.HBM) for arg in args]
     specs = [pl.BlockSpec(memory_space=pltpu.SMEM)] * scalars
     specs += [pl.BlockSpec(memory_space=space)] * (len(args) - scalars)
     return pl.pallas_call(
@@ -268,7 +274,7 @@
         out_shape=out,
         in_specs=specs,
         scratch_shapes=scratch,
-        compiler_params=pltpu.CompilerParams(vmem_limit_bytes=limit),
+        compiler_params=pltpu.CompilerParams(vmem_limit_bytes=48 * 1024 * 1024),
     )(*args)
 
 
@@ -286,30 +292,33 @@
     sent, ext = call(
         send_kernel,
         (shape(9, ROWS, LOCAL), shape(LOCAL + 16, WIDTH)),
+        cluster_ids.transpose(1, 0, 2),
         rows,
         w_shared,
         w_value,
-        cluster_ids.transpose(1, 0, 2),
         cotangent[0],
         scratch=[
+            pltpu.VMEM((HEADS, 1, LOCAL), jnp.int32),
             pltpu.VMEM((LOCAL, WIDTH), BF16),
             pltpu.VMEM((WIDTH, PROJ), BF16),
             pltpu.VMEM((WIDTH, PROJ), BF16),
-            pltpu.VMEM((HEADS, 1, LOCAL), jnp.int32),
             pltpu.VMEM((LOCAL, PROJ), BF16),
             pltpu.SemaphoreType.DMA((5,)),
         ],
         held=True,
     )
 
-    def shift(part, dy, dc):
-        pairs = [(y * 2 + c, (y + dy) % 4 * 2 + (c + dc) % 2) for y in range(4) for c in range(2)]
-        return lax.ppermute(part, PLANE, pairs) if dy or dc else part
+    def shift(pair, dy):
+        return lax.ppermute(pair, "y", [(y, (y + dy) % 4) for y in range(4)])
+
+    def flip(part):
+        return lax.ppermute(part, "c", [(0, 1), (1, 0)])
 
     arrived = swap(sent.reshape(9, LOCAL, 2, LOCAL).transpose(1, 0, 2, 3), OWNERS)
-    early = [shift(ext, dy, dc) for dy, dc in STEPS[:5]]
-    arrived, ext, early = lax.optimization_barrier((arrived, ext, early))
-    exts = early + [shift(ext, dy, dc) for dy, dc in STEPS[5:]]
+    pair = jnp.stack([ext, flip(ext)])
+    near = (shift(pair, 1), shift(pair, 3))
+    arrived, pair, near, place = lax.optimization_barrier((arrived, pair, near, place))
+    exts = [pair, near[0], shift(pair, 2), near[1]]
     arrived = arrived.transpose(1, 0, 2, 3)
     worked = call(attend_kernel, shape(72, 32, LOCAL), arrived.reshape(9, ROWS, LOCAL))
     worked = worked.reshape(8, 9, 16, 2, LOCAL).transpose(0, 2, 1, 3, 4)
@@ -334,7 +343,7 @@
         scratch=[pltpu.VMEM((2, 8, 8, LOCAL), F32), pltpu.VMEM((8, COLUMNS // 2, LOCAL), BF16)],
         scalars=1,
     )
-    got = lax.ppermute(give, "c", [(0, 1), (1, 0)])
+    got = flip(give)
     part = swap(part, ("x", "zl"))
     part, keep, got = lax.optimization_barrier((part, keep, got))
     part = call(sum_kernel, shape(4, SLOT, LOCAL), part)
@@ -349,7 +358,7 @@
         scratch=[pltpu.VMEM((WHOLE, LOCAL), F32)],
     )
     block = swap(block, "y")
-    other = lax.ppermute(block, "c", [(0, 1), (1, 0)])
+    other = flip(block)
     attention, grad_tokens = call(
         return_kernel,
         (shape(LOCAL, PROJ), shape(LOCAL, WIDTH)),

time: 180 us -> 177 us (0.983)
  starting transfers between devices: 68.1 us -> 59.9 us
  waiting for transfers between devices: 50.2 us -> 58.2 us
    all_to_all x3, waiting for transfers between devices: 33.8 us -> 43.8 us  [swap(): return lax.all_to_all(rows, axes, split_axis=0, concat_axis=0, tiled=True)]
    ppermute x9 -> x6, starting transfers between devices: 31.4 us -> 23.4 us  [the longest x3 11.9 us: shift(): return lax.ppermute(pair, 'y', [(y, (y + dy) % 4) for y in range(4)])]
    ppermute x9 -> x6, waiting for transfers between devices: 16.3 us -> 14.4 us  [the longest x3 12.1 us: shift(): return lax.ppermute(pair, 'y', [(y, (y + dy) % 4) for y in range(4)])]
  transfers between devices with their start and end apart: 12 -> 9, of which waited for: 8 -> 8; matrix products, arithmetic and copies ran while one was open for 0% -> 0% of each run, Pallas kernels for 2% -> 2%
where the time goes in v6:
time: 177 us
  starting transfers between devices  59.9 us (34%)
  waiting for transfers between devices  58.2 us (33%)
  blocking collectives  39.9 us (23%)
  Pallas kernels  14.3 us (8%)
  local copies, waits for them, and re-layouts  3.36 us (2%)
    all_to_all x3, waiting for transfers between devices, swap(): return lax.all_to_all(rows, axes, split_axis=0, concat_axis=0, tiled=True)  43.8 us
    all_to_all x3, blocking collectives, swap(): return lax.all_to_all(rows, axes, split_axis=0, concat_axis=0, tiled=True)  39.9 us
    all_to_all x3, starting transfers between devices, swap(): return lax.all_to_all(rows, axes, split_axis=0, concat_axis=0, tiled=True)  36.5 us
    pallas_call x9, Pallas kernels, call(): pl.pallas_call(kernel, out_shape=out, in_specs=specs, scratch_shapes=scra...  14.3 us
    ppermute x3, waiting for transfers between devices, shift(): return lax.ppermute(pair, 'y', [(y, (y + dy) % 4) for y in range(4)])  12.1 us
    ppermute x3, starting transfers between devices, shift(): return lax.ppermute(pair, 'y', [(y, (y + dy) % 4) for y in range(4)])  11.9 us
    ppermute x3, starting transfers between devices, flip(): return lax.ppermute(part, 'c', [(0, 1), (1, 0)])  11.5 us
  transfers between devices with their start and end apart: 9, of which 8 were waited for; matrix products, arithmetic and copies ran while one was open for 0% of the time, Pallas kernels for 2%

profile of v6, /device:TPU:1, one launch (start us, length us, event | category | flops | bytes accessed | tf_op | source)
XLA Modules:
  0.0 176.6 jit_solution(17487528181216427702)
XLA Ops:
  0.6 2.2 %shard_map.84 = (bf16[9,256,128]{2,1,0:T(8,128)(2,1)S(1)}, bf16[144,768]{1,0:T(8,128)(2,1)S(1)}) custom-call(s32[6,1,128]{2,1,0:T(1,128)} %bitcast.32, bf16[128,768]{1,0:T(8,128)(2,1)} %bitcast.30, bf16[768,384]{1,0:T(8,128)(2,1)} %ws_ref.1, bf16[768,384]{1,0:T(8,128)(2,1)} %wv_ref.1, bf16[128,384]{1,0:T(8,128)(2,1)} %bitcast.31), custom_call_target="tpu_custom_call" | custom-call | tf_op jit(solution)/shard_map/pallas_call | solution.py:272
  2.8 1.2 copy.15
  4.0 20.6 %all-to-all-start = ((bf16[128,9,2,128]{3,2,1,0:T(2,128)(2,1)}), bf16[128,9,2,128]{3,2,1,0:T(2,128)(2,1)S(1)}, u32[]{:S(2)}, u32[]{:S(2)}) async-start(bf16[128,9,2,128]{3,2,1,0:T(2,128)(2,1)} %bitcast.20), calls=%async_computation | async-start | bytes 1179648 | tf_op jit(solution)/shard_map/all_to_all | solution.py:286
  24.6 2.8 %collective-permute-start = (bf16[144,768]{1,0:T(8,128)(2,1)S(1)}, bf16[144,768]{1,0:T(8,128)(2,1)S(1)}, u32[]{:S(2)}, u32[]{:S(2)}) collective-permute-start(bf16[144,768]{1,0:T(8,128)(2,1)S(1)} %get-tuple-element.23), channel_id=1, source_target_pairs={{0,1},{1,0},{2,3},{3,2},{4,5},{5,4},{6,7},{7,6},{8,9},{9,8},{10,11... | collective-permute-start | bytes 663560 | tf_op jit(solution)/shard_map/ppermute | solution.py:315
  27.4 1.1 collective-permute-done
  28.5 2.9 %collective-permute-start.1 = (bf16[2,144,768]{2,1,0:T(8,128)(2,1)S(1)}, bf16[2,144,768]{2,1,0:T(8,128)(2,1)S(1)}, u32[]{:S(2)}, u32[]{:S(2)}) collective-permute-start(bf16[2,144,768]{2,1,0:T(8,128)(2,1)S(1)} %pad_maximum_fusion.refs_0_), channel_id=1, source_target_pairs={{0,32},{32,64},{64,96},{96,0},{1,33},{33,65},{65,97},{97,1},{2,34}... | collective-permute-start | bytes 1327112 | tf_op jit(solution)/shard_map/ppermute | solution.py:312
  31.5 3.6 %collective-permute-start.2 = (bf16[2,144,768]{2,1,0:T(8,128)(2,1)S(1)}, bf16[2,144,768]{2,1,0:T(8,128)(2,1)S(1)}, u32[]{:S(2)}, u32[]{:S(2)}) collective-permute-start(bf16[2,144,768]{2,1,0:T(8,128)(2,1)S(1)} %pad_maximum_fusion.refs_0_), channel_id=1, source_target_pairs={{0,96},{32,0},{64,32},{96,64},{1,97},{33,1},{65,33},{97,65},{2,98}... | collective-permute-start | bytes 1327112 | tf_op jit(solution)/shard_map/ppermute | solution.py:312
  35.1 0.1 pad_add_fusion.place_ref
  35.1 10.8 %collective-permute-done.1.refs_1_ = bf16[2,144,768]{2,1,0:T(8,128)(2,1)S(1)} collective-permute-done((bf16[2,144,768]{2,1,0:T(8,128)(2,1)S(1)}, bf16[2,144,768]{2,1,0:T(8,128)(2,1)S(1)}, u32[]{:S(2)}, u32[]{:S(2)}) %collective-permute-start.1) | collective-permute-done | bytes 442400 | tf_op jit(solution)/shard_map/ppermute | solution.py:312
  45.9 1.3 collective-permute-done.2.refs_3_
  47.2 11.9 %all-to-all-done = bf16[128,9,2,128]{3,2,1,0:T(2,128)(2,1)S(1)} async-done(((bf16[128,9,2,128]{3,2,1,0:T(2,128)(2,1)}), bf16[128,9,2,128]{3,2,1,0:T(2,128)(2,1)S(1)}, u32[]{:S(2)}, u32[]{:S(2)}) %all-to-all-start) | async-done | bytes 589856 | tf_op jit(solution)/shard_map/all_to_all | solution.py:286
  59.1 0.5 copy.11
  59.6 4.4 %shard_map.85 = bf16[72,32,128]{2,1,0:T(8,128)(2,1)S(1)} custom-call(bf16[9,256,128]{2,1,0:T(8,128)(2,1)S(1)} %bitcast.23), custom_call_target="tpu_custom_call" | custom-call | tf_op jit(solution)/shard_map/pallas_call | solution.py:272
  64.0 1.2 copy.12
  65.2 8.2 %all-to-all-start.1 = ((bf16[128,9,2,128]{3,2,1,0:T(2,128)(2,1)}), bf16[128,9,2,128]{3,2,1,0:T(2,128)(2,1)S(1)}, u32[]{:S(2)}, u32[]{:S(2)}) async-start(bf16[128,9,2,128]{3,2,1,0:T(2,128)(2,1)} %bitcast.13), calls=%async_computation.1 | async-start | bytes 1179648 | tf_op jit(solution)/shard_map/all_to_all | solution.py:286
  73.4 5.4 %collective-permute-start.3 = (bf16[2,144,768]{2,1,0:T(8,128)(2,1)S(1)}, bf16[2,144,768]{2,1,0:T(8,128)(2,1)S(1)}, u32[]{:S(2)}, u32[]{:S(2)}) collective-permute-start(bf16[2,144,768]{2,1,0:T(8,128)(2,1)S(1)} %pad_maximum_fusion.refs_0_), channel_id=1, source_target_pairs={{0,64},{32,96},{64,0},{96,32},{1,65},{33,97},{65,1},{97,33},{2,66}... | collective-permute-start | bytes 1327112 | tf_op jit(solution)/shard_map/ppermute | solution.py:312
  78.7 29.2 %all-to-all-done.1 = bf16[128,9,2,128]{3,2,1,0:T(2,128)(2,1)S(1)} async-done(((bf16[128,9,2,128]{3,2,1,0:T(2,128)(2,1)}), bf16[128,9,2,128]{3,2,1,0:T(2,128)(2,1)S(1)}, u32[]{:S(2)}, u32[]{:S(2)}) %all-to-all-start.1) | async-done | bytes 589856 | tf_op jit(solution)/shard_map/all_to_all | solution.py:286
  107.9 0.5 copy.13
  108.4 0.0 collective-permute-done.3.refs_2_
  108.4 2.7 %shard_map.86 = (bf16[16,40,128]{2,1,0:T(8,128)(2,1)}, bf16[8,96,128]{2,1,0:T(8,128)(2,1)S(1)}) custom-call(s32[2]{0:T(128)S(1)} %pad_add_fusion.place_ref, bf16[9,256,128]{2,1,0:T(8,128)(2,1)S(1)} %bitcast.21, bf16[2,144,768]{2,1,0:T(8,128)(2,1)S(1)} %pad_maximum_fusion.refs_0_, bf16[2,144,768]{2,1,0:T(8,128)(2,1)S(1)} %collective-permute-done.1.refs_1_, ...), custom_call_target="tpu_custom_call" | custom-call | tf_op jit(solution)/shard_map/pallas_call | solution.py:272
  111.1 7.8 %all-to-all-start.2 = ((bf16[16,40,128]{2,1,0:T(8,128)(2,1)}), bf16[16,40,128]{2,1,0:T(8,128)(2,1)S(1)}, u32[]{:S(2)}, u32[]{:S(2)}) async-start(bf16[16,40,128]{2,1,0:T(8,128)(2,1)} %get-tuple-element.29), calls=%async_computation.2 | async-start | bytes 327680 | tf_op jit(solution)/shard_map/all_to_all | solution.py:286
  118.8 1.2 shard_map.87
  120.1 2.4 %collective-permute-start.4 = (bf16[4,144,128]{2,1,0:T(8,128)(2,1)S(1)}, bf16[4,144,128]{2,1,0:T(8,128)(2,1)S(1)}, u32[]{:S(2)}, u32[]{:S(2)}) collective-permute-start(bf16[4,144,128]{2,1,0:T(8,128)(2,1)S(1)} %get-tuple-element.32), channel_id=1, source_target_pairs={{0,1},{1,0},{2,3},{3,2},{4,5},{5,4},{6,7},{7,6},{8,9},{9,8},{10,11... | collective-permute-start | bytes 442376 | tf_op jit(solution)/shard_map/ppermute | solution.py:315
  122.5 1.0 collective-permute-done.4.got_ref
  123.5 2.7 %all-to-all-done.2.in_ref = bf16[16,40,128]{2,1,0:T(8,128)(2,1)S(1)} async-done(((bf16[16,40,128]{2,1,0:T(8,128)(2,1)}), bf16[16,40,128]{2,1,0:T(8,128)(2,1)S(1)}, u32[]{:S(2)}, u32[]{:S(2)}) %all-to-all-start.2) | async-done | bytes 163872 | tf_op jit(solution)/shard_map/all_to_all | solution.py:286
  126.3 16.0 %all_to_all.30.in_ref = bf16[4,40,128]{2,1,0:T(8,128)(2,1)S(1)} all-to-all(bf16[4,40,128]{2,1,0:T(8,128)(2,1)S(1)} %shard_map.88), channel_id=1, replica_groups=mesh['x'=4,'y'=4,'zh'=4,'zl'=4,'c'=2] {'zh'}, dimensions={0} | all-to-all | bytes 81920 | tf_op jit(solution)/shard_map/all_to_all | solution.py:286
  142.3 11.4 %all_to_all.31.block_ref = bf16[16,40,128]{2,1,0:T(8,128)(2,1)S(1)} all-to-all(bf16[16,40,128]{2,1,0:T(8,128)(2,1)S(1)} %shard_map.89), channel_id=1, replica_groups=mesh['x'=4,'y'=4,'zh'=4,'zl'=4,'c'=2] {'x','zl'}, dimensions={0} | all-to-all | bytes 327680 | tf_op jit(solution)/shard_map/all_to_all | solution.py:286
  153.7 0.1 shard_map.90
  153.7 0.0 copy-start
  153.8 0.0 copy-start.1
  153.8 12.5 %all_to_all.32.all_ref.mine_ref = bf16[4,864,128]{2,1,0:T(8,128)(2,1)S(1)} all-to-all(bf16[4,864,128]{2,1,0:T(8,128)(2,1)S(1)} %shard_map.90), channel_id=1, replica_groups=mesh['x'=4,'y'=4,'zh'=4,'zl'=4,'c'=2] {'y'}, dimensions={0} | all-to-all | bytes 1769472 | tf_op jit(solution)/shard_map/all_to_all | solution.py:286
  166.3 6.3 %collective-permute-start.5 = (bf16[4,864,128]{2,1,0:T(8,128)(2,1)S(1)}, bf16[4,864,128]{2,1,0:T(8,128)(2,1)S(1)}, u32[]{:S(2)}, u32[]{:S(2)}) collective-permute-start(bf16[4,864,128]{2,1,0:T(8,128)(2,1)S(1)} %all_to_all.32.all_ref.mine_ref), channel_id=1, source_target_pairs={{0,1},{1,0},{2,3},{3,2},{4,5},{5,4},{6,7},{7,6},{8,9},{9,8},{10,11... | collective-permute-start | bytes 2654216 | tf_op jit(solution)/shard_map/ppermute | solution.py:315
  172.6 0.0 copy-done
  172.6 0.0 copy-done.1
  172.6 1.8 %shard_map.91 = (bf16[128,384]{1,0:T(8,128)(2,1)}, bf16[128,768]{1,0:T(8,128)(2,1)}) custom-call(s32[2]{0:T(128)S(1)} %pad_add_fusion.place_ref, bf16[4,864,128]{2,1,0:T(8,128)(2,1)S(1)} %all_to_all.32.all_ref.mine_ref, bf16[768,384]{1,0:T(8,128)(2,1)S(1)} %copy-done, bf16[768,384]{1,0:T(8,128)(2,1)S(1)} %copy-done.1), custom_call_target="tpu_custom_call" | custom-call | tf_op jit(solution)/shard_map/pallas_call | solution.py:272
  174.4 0.2 collective-permute-done.5.other_ref
  174.6 2.0 %shard_map.92 = (bf16[768,384]{1,0:T(8,128)(2,1)}, bf16[768,384]{1,0:T(8,128)(2,1)}) custom-call(s32[2]{0:T(128)S(1)} %pad_add_fusion.place_ref, bf16[4,864,128]{2,1,0:T(8,128)(2,1)S(1)} %all_to_all.32.all_ref.mine_ref, bf16[4,864,128]{2,1,0:T(8,128)(2,1)S(1)} %collective-permute-done.5.other_ref), custom_call_target="tpu_custom_call" | custom-call | tf_op jit(solution)/shard_map/pallas_call | solution.py:272
  (3 shorter events, 0.1 us)
Async XLA Ops:
  4.0 55.1 %all-to-all-start = ((bf16[128,9,2,128]{3,2,1,0:T(2,128)(2,1)}), bf16[128,9,2,128]{3,2,1,0:T(2,128)(2,1)S(1)}, u32[]{:S(2)}, u32[]{:S(2)}) async-start(bf16[128,9,2,128]{3,2,1,0:T(2,128)(2,1)} %bitcast.20), calls=%async_computation | async-start | bytes 1179648 | tf_op jit(solution)/shard_map/all_to_all | solution.py:286
  24.6 3.9 %collective-permute-start = (bf16[144,768]{1,0:T(8,128)(2,1)S(1)}, bf16[144,768]{1,0:T(8,128)(2,1)S(1)}, u32[]{:S(2)}, u32[]{:S(2)}) collective-permute-start(bf16[144,768]{1,0:T(8,128)(2,1)S(1)} %get-tuple-element.23), channel_id=1, source_target_pairs={{0,1},{1,0},{2,3},{3,2},{4,5},{5,4},{6,7},{7,6},{8,9},{9,8},{10,11... | collective-permute-start | bytes 663560 | tf_op jit(solution)/shard_map/ppermute | solution.py:315
  28.5 17.4 %collective-permute-start.1 = (bf16[2,144,768]{2,1,0:T(8,128)(2,1)S(1)}, bf16[2,144,768]{2,1,0:T(8,128)(2,1)S(1)}, u32[]{:S(2)}, u32[]{:S(2)}) collective-permute-start(bf16[2,144,768]{2,1,0:T(8,128)(2,1)S(1)} %pad_maximum_fusion.refs_0_), channel_id=1, source_target_pairs={{0,32},{32,64},{64,96},{96,0},{1,33},{33,65},{65,97},{97,1},{2,34}... | collective-permute-start | bytes 1327112 | tf_op jit(solution)/shard_map/ppermute | solution.py:312
  31.5 15.7 %collective-permute-start.2 = (bf16[2,144,768]{2,1,0:T(8,128)(2,1)S(1)}, bf16[2,144,768]{2,1,0:T(8,128)(2,1)S(1)}, u32[]{:S(2)}, u32[]{:S(2)}) collective-permute-start(bf16[2,144,768]{2,1,0:T(8,128)(2,1)S(1)} %pad_maximum_fusion.refs_0_), channel_id=1, source_target_pairs={{0,96},{32,0},{64,32},{96,64},{1,97},{33,1},{65,33},{97,65},{2,98}... | collective-permute-start | bytes 1327112 | tf_op jit(solution)/shard_map/ppermute | solution.py:312
  65.2 42.7 %all-to-all-start.1 = ((bf16[128,9,2,128]{3,2,1,0:T(2,128)(2,1)}), bf16[128,9,2,128]{3,2,1,0:T(2,128)(2,1)S(1)}, u32[]{:S(2)}, u32[]{:S(2)}) async-start(bf16[128,9,2,128]{3,2,1,0:T(2,128)(2,1)} %bitcast.13), calls=%async_computation.1 | async-start | bytes 1179648 | tf_op jit(solution)/shard_map/all_to_all | solution.py:286
  73.4 35.0 %collective-permute-start.3 = (bf16[2,144,768]{2,1,0:T(8,128)(2,1)S(1)}, bf16[2,144,768]{2,1,0:T(8,128)(2,1)S(1)}, u32[]{:S(2)}, u32[]{:S(2)}) collective-permute-start(bf16[2,144,768]{2,1,0:T(8,128)(2,1)S(1)} %pad_maximum_fusion.refs_0_), channel_id=1, source_target_pairs={{0,64},{32,96},{64,0},{96,32},{1,65},{33,97},{65,1},{97,33},{2,66}... | collective-permute-start | bytes 1327112 | tf_op jit(solution)/shard_map/ppermute | solution.py:312
  111.1 15.1 %all-to-all-start.2 = ((bf16[16,40,128]{2,1,0:T(8,128)(2,1)}), bf16[16,40,128]{2,1,0:T(8,128)(2,1)S(1)}, u32[]{:S(2)}, u32[]{:S(2)}) async-start(bf16[16,40,128]{2,1,0:T(8,128)(2,1)} %get-tuple-element.29), calls=%async_computation.2 | async-start | bytes 327680 | tf_op jit(solution)/shard_map/all_to_all | solution.py:286
  120.1 3.4 %collective-permute-start.4 = (bf16[4,144,128]{2,1,0:T(8,128)(2,1)S(1)}, bf16[4,144,128]{2,1,0:T(8,128)(2,1)S(1)}, u32[]{:S(2)}, u32[]{:S(2)}) collective-permute-start(bf16[4,144,128]{2,1,0:T(8,128)(2,1)S(1)} %get-tuple-element.32), channel_id=1, source_target_pairs={{0,1},{1,0},{2,3},{3,2},{4,5},{5,4},{6,7},{7,6},{8,9},{9,8},{10,11... | collective-permute-start | bytes 442376 | tf_op jit(solution)/shard_map/ppermute | solution.py:315
  153.7 18.8 %copy-start = (bf16[768,384]{1,0:T(8,128)(2,1)S(1)}, bf16[768,384]{1,0:T(8,128)(2,1)}, u32[]{:S(2)}) copy-start(bf16[768,384]{1,0:T(8,128)(2,1)} %ws_ref.1) | copy-start | bytes 1769476
  153.8 18.8 %copy-start.1 = (bf16[768,384]{1,0:T(8,128)(2,1)S(1)}, bf16[768,384]{1,0:T(8,128)(2,1)}, u32[]{:S(2)}) copy-start(bf16[768,384]{1,0:T(8,128)(2,1)} %wv_ref.1) | copy-start | bytes 1769476
  166.3 8.3 %collective-permute-start.5 = (bf16[4,864,128]{2,1,0:T(8,128)(2,1)S(1)}, bf16[4,864,128]{2,1,0:T(8,128)(2,1)S(1)}, u32[]{:S(2)}, u32[]{:S(2)}) collective-permute-start(bf16[4,864,128]{2,1,0:T(8,128)(2,1)S(1)} %all_to_all.32.all_ref.mine_ref), channel_id=1, source_target_pairs={{0,1},{1,0},{2,3},{3,2},{4,5},{5,4},{6,7},{7,6},{8,9},{9,8},{10,11... | collective-permute-start | bytes 2654216 | tf_op jit(solution)/shard_map/ppermute | solution.py:315

commit v7 on v6

--- a/solution.py
+++ b/solution.py
@@ -16,8 +16,11 @@
 PROJ = 384
 UNUSED = 65536.0
 PLANE = ("y", "c")
-TOK = ("y", "zh", "zl", "c")
-OWNERS = ("y", "c", "zh", "zl")
+TOK = ("y", "z", "c")
+OWNERS = ("y", "c", "z")
+RING = [(3, 4, 9, 14), (2, 7, 8, 13), (1, 6, 11, 12), (0, 5, 10, 15)]
+FAR = [list(group) for group in RING]
+NEAR = [[x * 16 + RING[n][b] for x in range(4) for n in range(4)] for b in range(4)]
 STEPS = [(dy, dc) for dy in range(4) for dc in range(2)]
 COLUMNS = 96
 PIECE = 36
@@ -92,58 +95,78 @@
 
 def spread(block, slot):
     rows = block.shape[0] // 8
-    turned = [block[:rows]]
-    for p in range(1, 8):
-        turned.append(pltpu.roll(block[p * rows : (p + 1) * rows], BLOCK * p, 1))
-    parts = []
-    for m in range(8):
-        part = turned[-m % 8]
-        for q in range(1, 8):
-            part = jnp.where(slot == q, turned[(q - m) % 8], part)
-        parts.append(part)
+    parts = [block[p * rows : (p + 1) * rows] for p in range(8)]
+    for bit in (1, 2, 4):
+        odd = (slot & bit) != 0
+        after = list(parts)
+        for p in range(8):
+            if p & bit == 0:
+                low, high = parts[p], parts[p + bit]
+                after[p] = jnp.where(odd, pltpu.roll(high, BLOCK * bit, 1), low)
+                after[p + bit] = jnp.where(odd, high, pltpu.roll(low, LOCAL - BLOCK * bit, 1))
+        parts = after
     return parts
 
 
 def attend_kernel(in_ref, out_ref):
+    half = ROWS // 2
     lane_rows = iota((ROWS, LOCAL), 1)
-    causal = position(iota((ROWS, ROWS), 1)) <= position(iota((ROWS, ROWS), 0))
+    first = lane_rows == 0
+    bias_lane = lane_rows == HEAD
+    head_lanes = lane_rows < HEAD
+    left_causal = position(iota((half, half), 0)) <= position(iota((half, half), 1))
+    right_causal = position(iota((ROWS, half), 0)) <= position(iota((ROWS, half), 1) + half)
     slot = iota((ROWS // 8, LOCAL), 1) >> 4
+    hidden = jnp.zeros((half, half), BF16)
     pending = None
     for h in range(HEADS):
-        block = in_ref[h]
-        empty = block[:, :1].astype(F32) > 32768.0
-        first = lane_rows == 0
-        block = jnp.where(empty & first, 0.0, block.astype(F32)).astype(BF16)
+        block = in_ref[h].astype(F32)
+        empty = block[:, :1] > 32768.0
+        block = jnp.where(empty & first, 0.0, block)
+        query = jnp.where(head_lanes, block * 0.125, jnp.where(bias_lane, 1.0, 0.0)).astype(BF16)
+        key = jnp.where(
+            head_lanes, block, jnp.where(bias_lane & empty, -1e30, 0.0)
+        ).astype(BF16)
+        block = block.astype(BF16)
         shared = block[:, :HEAD]
         value = block[:, HEAD:]
         pair = in_ref[HEADS + h // 2]
         cot = pair[:, :HEAD] if h % 2 == 0 else pair[:, HEAD:]
-        bias_lane = lane_rows == HEAD
-        head_lanes = lane_rows < HEAD
-        wide = block.astype(F32)
-        query = jnp.where(head_lanes, wide, jnp.where(bias_lane, 1.0, 0.0)).astype(BF16)
-        key = jnp.where(
-            head_lanes, wide, jnp.where(bias_lane & empty, -1e30, 0.0)
-        ).astype(BF16)
-        scores = dot(query, key, ((1,), (1,))) * 0.125
-        scores = jnp.where(causal, scores, -1e30)
-        highest = jnp.max(scores, axis=1, keepdims=True)
-        weights = jnp.exp(scores - highest)
-        probs = (weights / jnp.sum(weights, axis=1, keepdims=True)).astype(BF16)
-        out = dot(probs, value)
-        d_prob = dot(cot, value, ((1,), (1,)))
-        wide_probs = probs.astype(F32)
-        delta = jnp.sum(wide_probs * d_prob, axis=1, keepdims=True)
-        d_score = (wide_probs * (d_prob - delta)).astype(BF16)
-        both = dot(d_score, shared) + dot(d_score, shared, ((0,), (0,)))
-        d_value = dot(probs, cot, ((0,), (0,)))
-        for m, part in enumerate(spread(jnp.concatenate([both * 0.125, d_value], axis=1), slot)):
+        probs = []
+        d_scores = []
+        for rows, cols, causal in (
+            (slice(0, half), slice(0, half), left_causal),
+            (slice(0, ROWS), slice(half, ROWS), right_causal),
+        ):
+            scores = dot(key[rows], query[cols], ((1,), (1,)))
+            scores = jnp.where(causal, scores, -1e30)
+            weights = jnp.exp(scores - jnp.max(scores, axis=0, keepdims=True))
+            scale = 1.0 / jnp.sum(weights, axis=0, keepdims=True)
+            prob = (weights * scale).astype(BF16)
+            d_prob = dot(value[rows], cot[cols], ((1,), (1,)))
+            wide = prob.astype(F32)
+            delta = jnp.sum(wide * d_prob, axis=0, keepdims=True)
+            probs.append(prob)
+            d_scores.append((wide * (d_prob - delta)).astype(BF16))
+        probs = jnp.concatenate([jnp.concatenate([probs[0], hidden], axis=0), probs[1]], axis=1)
+        d_scores = jnp.concatenate(
+            [jnp.concatenate([d_scores[0], hidden], axis=0), d_scores[1]], axis=1
+        )
+        turned = block.T
+        above = dot(turned[:HEAD], d_scores)
+        out = dot(turned[HEAD:], probs)
+        both = jnp.concatenate([above, out], axis=0).T
+        d_shared = (dot(d_scores, shared) + both[:, :HEAD]) * 0.125
+        d_value = dot(probs, cot)
+        for m, part in enumerate(spread(jnp.concatenate([d_shared, d_value], axis=1), slot)):
             n = h * 8 + m
             out_ref[n // 6 * 9 + n % 6] = part.astype(BF16)
         if h % 2 == 0:
-            pending = out
+            pending = both
         else:
-            for m, part in enumerate(spread(jnp.concatenate([pending, out], axis=1), slot)):
+            lane = iota((ROWS, LOCAL), 1) < HEAD
+            joined = jnp.where(lane, pltpu.roll(pending, HEAD, 1), both)
+            for m, part in enumerate(spread(joined, slot)):
                 n = h // 2 * 8 + m
                 out_ref[n // 3 * 9 + 6 + n % 3] = part.astype(BF16)
 
@@ -152,7 +175,7 @@
     return lax.rem(place_ref[0] + dy, 4) * 2 + lax.rem(place_ref[1] + dc, 2)
 
 
-def gather_columns(place_ref, in_ref, base, count, turn, exts, dests, out_ref, first):
+def gather_columns(place_ref, in_ref, base, count, exts, dests, out_ref, first):
     j = place_ref[0] * 2 + place_ref[1]
     head = (j * 3 // 4, (j * 6 + 5) // 8)
     lane_slot = iota((ROWS, LOCAL), 1) >> 4
@@ -162,8 +185,8 @@
         for i in range(2):
             lanes = pl.ds(pl.multiple_of(head[i] * LOCAL, LOCAL), LOCAL)
             dests[i, source] = exts[n // 2][n % 2, LOCAL:, lanes].astype(F32)[:8]
-    shift = lax.rem(j * turn, 8) * BLOCK
-    turned = [pltpu.roll(in_ref[base + b].astype(F32), shift, 1) for b in range(count)]
+    turned = [in_ref[base + b].astype(F32) for b in range(count)]
+    turned = [pltpu.roll(rows, BLOCK * b, 1) if b else rows for b, rows in enumerate(turned)]
     limit = lax.rem(j, 4)
     limit = jnp.where(limit == 1, 1, jnp.where(limit == 2, 2, 3)) * count
     for p in range(8):
@@ -171,9 +194,9 @@
         for b in range(1, count):
             rows = jnp.where(lane_slot == (b + p) % 8, turned[b], rows)
         rows = rows.astype(BF16)
-        found = [
-            dot(rows, (sub_rows == dests[i, p, :1]).astype(BF16), ((0,), (0,))) for i in range(2)
-        ]
+        routes = [(sub_rows == dests[i, p, :1]).astype(BF16) for i in range(2)]
+        found = dot(rows, jnp.concatenate(routes, axis=1), ((0,), (0,)))
+        found = [found[:, :LOCAL], found[:, LOCAL:]]
         blocks = []
         for b in range(count):
             cut = slice((b + p) % 8 * BLOCK, ((b + p) % 8 + 1) * BLOCK)
@@ -183,7 +206,7 @@
 
 def partial_kernel(place_ref, in_ref, *refs):
     exts, (out_ref, cols_ref), (dests, scratch) = refs[:4], refs[4:6], refs[6:]
-    gather_columns(place_ref, in_ref, 0, 6, 2, exts, dests, cols_ref, 0)
+    gather_columns(place_ref, in_ref, 0, 6, exts, dests, cols_ref, 0)
     total = None
     for n, (dy, dc) in enumerate(STEPS):
         source = index_of(place_ref, 4 - dy, dc)
@@ -198,7 +221,7 @@
 
 def forward_kernel(place_ref, in_ref, cols_ref, *refs):
     exts, (keep_ref, give_ref), (dests, scratch) = refs[:4], refs[4:6], refs[6:]
-    gather_columns(place_ref, in_ref, 6, 3, 5, exts, dests, scratch, 0)
+    gather_columns(place_ref, in_ref, 6, 3, exts, dests, scratch, 0)
     here = place_ref[1]
     for y in range(4):
         for ref, c in ((keep_ref, here), (give_ref, 1 - here)):
@@ -245,8 +268,9 @@
         out_ref[i] = total
 
 
-def finish_kernel(place_ref, mine_ref, other_ref, shared_ref, value_ref):
+def finish_kernel(place_ref, mine_ref, other_ref, shared_ref, value_ref, held, sems):
     first = place_ref[1] == 0
+    copies = []
     for k in range(WIDTH // LOCAL):
         rows = slice(k * COLUMNS, (k + 1) * COLUMNS)
         strip = []
@@ -255,15 +279,22 @@
             other = other_ref[y, rows, :].astype(F32)
             strip += [jnp.where(first, mine, other), jnp.where(first, other, mine)]
         strip = jnp.concatenate(strip, axis=0)
+        lines = slice(k * LOCAL, (k + 1) * LOCAL)
         for half, ref in enumerate((shared_ref, value_ref)):
             heads = [
                 strip[h * LOCAL + half * HEAD : h * LOCAL + (half + 1) * HEAD]
                 for h in range(HEADS)
             ]
-            ref[k * LOCAL : (k + 1) * LOCAL, :] = jnp.concatenate(heads, axis=0).T.astype(BF16)
-
-
-def call(kernel, out, *args, scratch=(), scalars=0, held=False):
+            held[half, lines, :] = jnp.concatenate(heads, axis=0).T.astype(BF16)
+            copies.append(
+                pltpu.make_async_copy(held.at[half, lines], ref.at[lines], sems.at[half, k])
+            )
+            copies[-1].start()
+    for copy in copies:
+        copy.wait()
+
+
+def call(kernel, out, *args, scratch=(), scalars=0, held=False, far=False):
     space = pl.ANY if held else pltpu.VMEM
     if held:
         args = [pltpu.with_memory_space_constraint(arg, pltpu.HBM) for arg in args]
@@ -273,6 +304,7 @@
         kernel,
         out_shape=out,
         in_specs=specs,
+        out_specs=jax.tree.map(lambda _: pl.BlockSpec(memory_space=pl.ANY if far else pltpu.VMEM), out),
         scratch_shapes=scratch,
         compiler_params=pltpu.CompilerParams(vmem_limit_bytes=48 * 1024 * 1024),
     )(*args)
@@ -282,8 +314,10 @@
     return jax.ShapeDtypeStruct(dims, BF16)
 
 
-def swap(rows, axes):
-    return lax.all_to_all(rows, axes, split_axis=0, concat_axis=0, tiled=True)
+def swap(rows, axes, groups=None):
+    return lax.all_to_all(
+        rows, axes, split_axis=0, concat_axis=0, tiled=True, axis_index_groups=groups
+    )
 
 
 def body(tokens, w_shared, w_value, cluster_ids, slot_index, cotangent):
@@ -344,11 +378,11 @@
         scalars=1,
     )
     got = flip(give)
-    part = swap(part, ("x", "zl"))
+    part = swap(part, ("x", "z"), NEAR)
     part, keep, got = lax.optimization_barrier((part, keep, got))
     part = call(sum_kernel, shape(4, SLOT, LOCAL), part)
-    block = call(sum_kernel, shape(16, SLOT, LOCAL), swap(part, "zh"))
-    block = swap(block, ("x", "zl"))
+    block = call(sum_kernel, shape(16, SLOT, LOCAL), swap(part, "z", FAR))
+    block = swap(block, ("x", "z"), NEAR)
     block = call(
         pack_kernel,
         shape(4, WHOLE + 2 * MESSAGE, LOCAL),
@@ -375,13 +409,18 @@
         place,
         block,
         other,
+        scratch=[
+            pltpu.VMEM((2, WIDTH, PROJ), BF16),
+            pltpu.SemaphoreType.DMA((2, WIDTH // LOCAL)),
+        ],
         scalars=1,
+        far=True,
     )
     return (attention[None], grad_tokens[None], grad_shared, grad_value)
 
 
 def solution(mesh):
-    fine = Mesh(mesh.devices.reshape(4, 4, 4, 4, 2), ("x", "y", "zh", "zl", "c"))
+    fine = Mesh(mesh.devices.reshape(4, 4, 16, 2), ("x", "y", "z", "c"))
     in_specs = (
         P("x", TOK, None),
         P(),

time: 177 us -> 171 us (0.966)
  blocking collectives: 39.9 us -> 35.4 us
  waiting for transfers between devices: 58.2 us -> 55.8 us
  starting transfers between devices: 59.9 us -> 62 us
    all_to_all x3, blocking collectives: 39.9 us -> 35.4 us  [swap(): lax.all_to_all(rows, axes, split_axis=0, concat_axis=0, tiled=True, axis_...]
    all_to_all x3, waiting for transfers between devices: 43.8 us -> 41.4 us  [swap(): lax.all_to_all(rows, axes, split_axis=0, concat_axis=0, tiled=True, axis_...]
where the time goes in v7:
time: 171 us; the launch traced here: 170 us
  starting transfers between devices  62 us (36%)
  waiting for transfers between devices  55.8 us (33%)
  blocking collectives  35.4 us (21%)
  Pallas kernels  12.7 us (7%)
  local copies, waits for them, and re-layouts  3.36 us (2%)
    all_to_all x3, waiting for transfers between devices, swap(): lax.all_to_all(rows, axes, split_axis=0, concat_axis=0, tiled=True, axis_...  41.4 us
    all_to_all x3, starting transfers between devices, swap(): lax.all_to_all(rows, axes, split_axis=0, concat_axis=0, tiled=True, axis_...  37.6 us
    all_to_all x3, blocking collectives, swap(): lax.all_to_all(rows, axes, split_axis=0, concat_axis=0, tiled=True, axis_...  35.4 us
    ppermute x3, starting transfers between devices, flip(): return lax.ppermute(part, 'c', [(0, 1), (1, 0)])  12.7 us
    pallas_call x9, Pallas kernels, call(): pl.pallas_call(kernel, out_shape=out, in_specs=specs, out_specs=jax.tree....  12.7 us
    ppermute x3, waiting for transfers between devices, shift(): return lax.ppermute(pair, 'y', [(y, (y + dy) % 4) for y in range(4)])  12.1 us
    ppermute x3, starting transfers between devices, shift(): return lax.ppermute(pair, 'y', [(y, (y + dy) % 4) for y in range(4)])  11.7 us
  transfers between devices with their start and end apart: 9, of which 8 were waited for; matrix products, arithmetic and copies ran while one was open for 0% of the time, Pallas kernels for 2%

profile of v7, /device:TPU:1, one launch (start us, length us, event | category | flops | bytes accessed | tf_op | source)
XLA Modules:
  0.0 170.2 jit_solution(5352064056749443742)
XLA Ops:
  0.6 2.2 %shard_map.84 = (bf16[9,256,128]{2,1,0:T(8,128)(2,1)S(1)}, bf16[144,768]{1,0:T(8,128)(2,1)S(1)}) custom-call(s32[6,1,128]{2,1,0:T(1,128)} %bitcast.32, bf16[128,768]{1,0:T(8,128)(2,1)} %bitcast.30, bf16[768,384]{1,0:T(8,128)(2,1)} %ws_ref.1, bf16[768,384]{1,0:T(8,128)(2,1)} %wv_ref.1, bf16[128,384]{1,0:T(8,128)(2,1)} %bitcast.31), custom_call_target="tpu_custom_call" | custom-call | tf_op jit(solution)/shard_map/pallas_call | solution.py:303
  2.8 1.2 copy.15
  4.0 20.6 %all-to-all-start = ((bf16[128,9,2,128]{3,2,1,0:T(2,128)(2,1)}), bf16[128,9,2,128]{3,2,1,0:T(2,128)(2,1)S(1)}, u32[]{:S(2)}, u32[]{:S(2)}) async-start(bf16[128,9,2,128]{3,2,1,0:T(2,128)(2,1)} %bitcast.20), calls=%async_computation | async-start | bytes 1179648 | tf_op jit(solution)/shard_map/all_to_all | solution.py:318
  24.6 2.8 %collective-permute-start = (bf16[144,768]{1,0:T(8,128)(2,1)S(1)}, bf16[144,768]{1,0:T(8,128)(2,1)S(1)}, u32[]{:S(2)}, u32[]{:S(2)}) collective-permute-start(bf16[144,768]{1,0:T(8,128)(2,1)S(1)} %get-tuple-element.23), channel_id=1, source_target_pairs={{0,1},{1,0},{2,3},{3,2},{4,5},{5,4},{6,7},{7,6},{8,9},{9,8},{10,11... | collective-permute-start | bytes 663560 | tf_op jit(solution)/shard_map/ppermute | solution.py:349
  27.4 1.1 collective-permute-done
  28.5 2.9 %collective-permute-start.1 = (bf16[2,144,768]{2,1,0:T(8,128)(2,1)S(1)}, bf16[2,144,768]{2,1,0:T(8,128)(2,1)S(1)}, u32[]{:S(2)}, u32[]{:S(2)}) collective-permute-start(bf16[2,144,768]{2,1,0:T(8,128)(2,1)S(1)} %pad_maximum_fusion.refs_0_), channel_id=1, source_target_pairs={{0,32},{32,64},{64,96},{96,0},{1,33},{33,65},{65,97},{97,1},{2,34}... | collective-permute-start | bytes 1327112 | tf_op jit(solution)/shard_map/ppermute | solution.py:346
  31.5 3.6 %collective-permute-start.2 = (bf16[2,144,768]{2,1,0:T(8,128)(2,1)S(1)}, bf16[2,144,768]{2,1,0:T(8,128)(2,1)S(1)}, u32[]{:S(2)}, u32[]{:S(2)}) collective-permute-start(bf16[2,144,768]{2,1,0:T(8,128)(2,1)S(1)} %pad_maximum_fusion.refs_0_), channel_id=1, source_target_pairs={{0,96},{32,0},{64,32},{96,64},{1,97},{33,1},{65,33},{97,65},{2,98}... | collective-permute-start | bytes 1327112 | tf_op jit(solution)/shard_map/ppermute | solution.py:346
  35.1 0.1 pad_add_fusion.place_ref
  35.1 10.8 %collective-permute-done.1.refs_1_ = bf16[2,144,768]{2,1,0:T(8,128)(2,1)S(1)} collective-permute-done((bf16[2,144,768]{2,1,0:T(8,128)(2,1)S(1)}, bf16[2,144,768]{2,1,0:T(8,128)(2,1)S(1)}, u32[]{:S(2)}, u32[]{:S(2)}) %collective-permute-start.1) | collective-permute-done | bytes 442400 | tf_op jit(solution)/shard_map/ppermute | solution.py:346
  45.9 1.3 collective-permute-done.2.refs_3_
  47.2 11.9 %all-to-all-done = bf16[128,9,2,128]{3,2,1,0:T(2,128)(2,1)S(1)} async-done(((bf16[128,9,2,128]{3,2,1,0:T(2,128)(2,1)}), bf16[128,9,2,128]{3,2,1,0:T(2,128)(2,1)S(1)}, u32[]{:S(2)}, u32[]{:S(2)}) %all-to-all-start) | async-done | bytes 589856 | tf_op jit(solution)/shard_map/all_to_all | solution.py:318
  59.1 0.5 copy.11
  59.6 3.3 %shard_map.85 = bf16[72,32,128]{2,1,0:T(8,128)(2,1)S(1)} custom-call(bf16[9,256,128]{2,1,0:T(8,128)(2,1)S(1)} %bitcast.23), custom_call_target="tpu_custom_call" | custom-call | tf_op jit(solution)/shard_map/pallas_call | solution.py:303
  62.9 1.2 copy.12
  64.1 8.2 %all-to-all-start.1 = ((bf16[128,9,2,128]{3,2,1,0:T(2,128)(2,1)}), bf16[128,9,2,128]{3,2,1,0:T(2,128)(2,1)S(1)}, u32[]{:S(2)}, u32[]{:S(2)}) async-start(bf16[128,9,2,128]{3,2,1,0:T(2,128)(2,1)} %bitcast.13), calls=%async_computation.1 | async-start | bytes 1179648 | tf_op jit(solution)/shard_map/all_to_all | solution.py:318
  72.3 5.2 %collective-permute-start.3 = (bf16[2,144,768]{2,1,0:T(8,128)(2,1)S(1)}, bf16[2,144,768]{2,1,0:T(8,128)(2,1)S(1)}, u32[]{:S(2)}, u32[]{:S(2)}) collective-permute-start(bf16[2,144,768]{2,1,0:T(8,128)(2,1)S(1)} %pad_maximum_fusion.refs_0_), channel_id=1, source_target_pairs={{0,64},{32,96},{64,0},{96,32},{1,65},{33,97},{65,1},{97,33},{2,66}... | collective-permute-start | bytes 1327112 | tf_op jit(solution)/shard_map/ppermute | solution.py:346
  77.5 29.3 %all-to-all-done.1 = bf16[128,9,2,128]{3,2,1,0:T(2,128)(2,1)S(1)} async-done(((bf16[128,9,2,128]{3,2,1,0:T(2,128)(2,1)}), bf16[128,9,2,128]{3,2,1,0:T(2,128)(2,1)S(1)}, u32[]{:S(2)}, u32[]{:S(2)}) %all-to-all-start.1) | async-done | bytes 589856 | tf_op jit(solution)/shard_map/all_to_all | solution.py:318
  106.9 0.5 copy.13
  107.3 0.0 collective-permute-done.3.refs_2_
  107.3 2.5 %shard_map.86 = (bf16[16,40,128]{2,1,0:T(8,128)(2,1)}, bf16[8,96,128]{2,1,0:T(8,128)(2,1)S(1)}) custom-call(s32[2]{0:T(128)S(1)} %pad_add_fusion.place_ref, bf16[9,256,128]{2,1,0:T(8,128)(2,1)S(1)} %bitcast.21, bf16[2,144,768]{2,1,0:T(8,128)(2,1)S(1)} %pad_maximum_fusion.refs_0_, bf16[2,144,768]{2,1,0:T(8,128)(2,1)S(1)} %collective-permute-done.1.refs_1_, ...), custom_call_target="tpu_custom_call" | custom-call | tf_op jit(solution)/shard_map/pallas_call | solution.py:303
  109.8 8.8 %all-to-all-start.2 = ((bf16[16,40,128]{2,1,0:T(8,128)(2,1)}), bf16[16,40,128]{2,1,0:T(8,128)(2,1)S(1)}, u32[]{:S(2)}, u32[]{:S(2)}) async-start(bf16[16,40,128]{2,1,0:T(8,128)(2,1)} %get-tuple-element.29), calls=%async_computation.2 | async-start | bytes 327680 | tf_op jit(solution)/shard_map/all_to_all | solution.py:318
  118.6 1.1 shard_map.87
  119.7 2.7 %collective-permute-start.4 = (bf16[4,144,128]{2,1,0:T(8,128)(2,1)S(1)}, bf16[4,144,128]{2,1,0:T(8,128)(2,1)S(1)}, u32[]{:S(2)}, u32[]{:S(2)}) collective-permute-start(bf16[4,144,128]{2,1,0:T(8,128)(2,1)S(1)} %get-tuple-element.32), channel_id=1, source_target_pairs={{0,1},{1,0},{2,3},{3,2},{4,5},{5,4},{6,7},{7,6},{8,9},{9,8},{10,11... | collective-permute-start | bytes 442376 | tf_op jit(solution)/shard_map/ppermute | solution.py:349
  122.4 1.0 collective-permute-done.4.got_ref
  123.4 0.1 all-to-all-done.2.in_ref
  123.6 12.6 %all_to_all.30.in_ref = bf16[4,40,128]{2,1,0:T(8,128)(2,1)S(1)} all-to-all(bf16[4,40,128]{2,1,0:T(8,128)(2,1)S(1)} %shard_map.88), channel_id=1, replica_groups={{6,8,18,28},{4,14,16,26},{2,12,22,24},{0,10,20,30},{7,9,19,29},{5,15,17..., dimensions={0} | all-to-all | bytes 81920 | tf_op jit(solution)/shard_map/all_to_all | solution.py:318
  136.2 11.3 %all_to_all.31.block_ref = bf16[16,40,128]{2,1,0:T(8,128)(2,1)S(1)} all-to-all(bf16[16,40,128]{2,1,0:T(8,128)(2,1)S(1)} %shard_map.89), channel_id=1, replica_groups={{6,4,2,0,134,132,130,128,262,260,258,256,390,388,386,384},{8,14,12,10,1..., dimensions={0} | all-to-all | bytes 327680 | tf_op jit(solution)/shard_map/all_to_all | solution.py:318
  147.5 0.1 shard_map.90
  147.6 0.0 copy-start
  147.6 0.0 copy-start.1
  147.6 11.5 %all_to_all.32.all_ref.mine_ref = bf16[4,864,128]{2,1,0:T(8,128)(2,1)S(1)} all-to-all(bf16[4,864,128]{2,1,0:T(8,128)(2,1)S(1)} %shard_map.90), channel_id=1, replica_groups=mesh['x'=4,'y'=4,'z'=16,'c'=2] {'y'}, dimensions={0} | all-to-all | bytes 1769472 | tf_op jit(solution)/shard_map/all_to_all | solution.py:318
  159.1 7.2 %collective-permute-start.5 = (bf16[4,864,128]{2,1,0:T(8,128)(2,1)S(1)}, bf16[4,864,128]{2,1,0:T(8,128)(2,1)S(1)}, u32[]{:S(2)}, u32[]{:S(2)}) collective-permute-start(bf16[4,864,128]{2,1,0:T(8,128)(2,1)S(1)} %all_to_all.32.all_ref.mine_ref), channel_id=1, source_target_pairs={{0,1},{1,0},{2,3},{3,2},{4,5},{5,4},{6,7},{7,6},{8,9},{9,8},{10,11... | collective-permute-start | bytes 2654216 | tf_op jit(solution)/shard_map/ppermute | solution.py:349
  166.3 0.0 copy-done
  166.4 0.0 copy-done.1
  166.4 1.8 %shard_map.91 = (bf16[128,384]{1,0:T(8,128)(2,1)}, bf16[128,768]{1,0:T(8,128)(2,1)}) custom-call(s32[2]{0:T(128)S(1)} %pad_add_fusion.place_ref, bf16[4,864,128]{2,1,0:T(8,128)(2,1)S(1)} %all_to_all.32.all_ref.mine_ref, bf16[768,384]{1,0:T(8,128)(2,1)S(1)} %copy-done, bf16[768,384]{1,0:T(8,128)(2,1)S(1)} %copy-done.1), custom_call_target="tpu_custom_call" | custom-call | tf_op jit(solution)/shard_map/pallas_call | solution.py:303
  168.1 0.2 collective-permute-done.5.other_ref
  168.4 1.8 %shard_map.92 = (bf16[768,384]{1,0:T(8,128)(2,1)}, bf16[768,384]{1,0:T(8,128)(2,1)}) custom-call(s32[2]{0:T(128)S(1)} %pad_add_fusion.place_ref, bf16[4,864,128]{2,1,0:T(8,128)(2,1)S(1)} %all_to_all.32.all_ref.mine_ref, bf16[4,864,128]{2,1,0:T(8,128)(2,1)S(1)} %collective-permute-done.5.other_ref), custom_call_target="tpu_custom_call" | custom-call | tf_op jit(solution)/shard_map/pallas_call | solution.py:303
  (3 shorter events, 0.1 us)
Async XLA Ops:
  4.0 55.1 %all-to-all-start = ((bf16[128,9,2,128]{3,2,1,0:T(2,128)(2,1)}), bf16[128,9,2,128]{3,2,1,0:T(2,128)(2,1)S(1)}, u32[]{:S(2)}, u32[]{:S(2)}) async-start(bf16[128,9,2,128]{3,2,1,0:T(2,128)(2,1)} %bitcast.20), calls=%async_computation | async-start | bytes 1179648 | tf_op jit(solution)/shard_map/all_to_all | solution.py:318
  24.6 3.9 %collective-permute-start = (bf16[144,768]{1,0:T(8,128)(2,1)S(1)}, bf16[144,768]{1,0:T(8,128)(2,1)S(1)}, u32[]{:S(2)}, u32[]{:S(2)}) collective-permute-start(bf16[144,768]{1,0:T(8,128)(2,1)S(1)} %get-tuple-element.23), channel_id=1, source_target_pairs={{0,1},{1,0},{2,3},{3,2},{4,5},{5,4},{6,7},{7,6},{8,9},{9,8},{10,11... | collective-permute-start | bytes 663560 | tf_op jit(solution)/shard_map/ppermute | solution.py:349
  28.5 17.4 %collective-permute-start.1 = (bf16[2,144,768]{2,1,0:T(8,128)(2,1)S(1)}, bf16[2,144,768]{2,1,0:T(8,128)(2,1)S(1)}, u32[]{:S(2)}, u32[]{:S(2)}) collective-permute-start(bf16[2,144,768]{2,1,0:T(8,128)(2,1)S(1)} %pad_maximum_fusion.refs_0_), channel_id=1, source_target_pairs={{0,32},{32,64},{64,96},{96,0},{1,33},{33,65},{65,97},{97,1},{2,34}... | collective-permute-start | bytes 1327112 | tf_op jit(solution)/shard_map/ppermute | solution.py:346
  31.5 15.7 %collective-permute-start.2 = (bf16[2,144,768]{2,1,0:T(8,128)(2,1)S(1)}, bf16[2,144,768]{2,1,0:T(8,128)(2,1)S(1)}, u32[]{:S(2)}, u32[]{:S(2)}) collective-permute-start(bf16[2,144,768]{2,1,0:T(8,128)(2,1)S(1)} %pad_maximum_fusion.refs_0_), channel_id=1, source_target_pairs={{0,96},{32,0},{64,32},{96,64},{1,97},{33,1},{65,33},{97,65},{2,98}... | collective-permute-start | bytes 1327112 | tf_op jit(solution)/shard_map/ppermute | solution.py:346
  64.1 42.7 %all-to-all-start.1 = ((bf16[128,9,2,128]{3,2,1,0:T(2,128)(2,1)}), bf16[128,9,2,128]{3,2,1,0:T(2,128)(2,1)S(1)}, u32[]{:S(2)}, u32[]{:S(2)}) async-start(bf16[128,9,2,128]{3,2,1,0:T(2,128)(2,1)} %bitcast.13), calls=%async_computation.1 | async-start | bytes 1179648 | tf_op jit(solution)/shard_map/all_to_all | solution.py:318
  72.3 35.0 %collective-permute-start.3 = (bf16[2,144,768]{2,1,0:T(8,128)(2,1)S(1)}, bf16[2,144,768]{2,1,0:T(8,128)(2,1)S(1)}, u32[]{:S(2)}, u32[]{:S(2)}) collective-permute-start(bf16[2,144,768]{2,1,0:T(8,128)(2,1)S(1)} %pad_maximum_fusion.refs_0_), channel_id=1, source_target_pairs={{0,64},{32,96},{64,0},{96,32},{1,65},{33,97},{65,1},{97,33},{2,66}... | collective-permute-start | bytes 1327112 | tf_op jit(solution)/shard_map/ppermute | solution.py:346
  109.8 13.8 %all-to-all-start.2 = ((bf16[16,40,128]{2,1,0:T(8,128)(2,1)}), bf16[16,40,128]{2,1,0:T(8,128)(2,1)S(1)}, u32[]{:S(2)}, u32[]{:S(2)}) async-start(bf16[16,40,128]{2,1,0:T(8,128)(2,1)} %get-tuple-element.29), calls=%async_computation.2 | async-start | bytes 327680 | tf_op jit(solution)/shard_map/all_to_all | solution.py:318
  119.7 3.7 %collective-permute-start.4 = (bf16[4,144,128]{2,1,0:T(8,128)(2,1)S(1)}, bf16[4,144,128]{2,1,0:T(8,128)(2,1)S(1)}, u32[]{:S(2)}, u32[]{:S(2)}) collective-permute-start(bf16[4,144,128]{2,1,0:T(8,128)(2,1)S(1)} %get-tuple-element.32), channel_id=1, source_target_pairs={{0,1},{1,0},{2,3},{3,2},{4,5},{5,4},{6,7},{7,6},{8,9},{9,8},{10,11... | collective-permute-start | bytes 442376 | tf_op jit(solution)/shard_map/ppermute | solution.py:349
  147.6 18.8 %copy-start = (bf16[768,384]{1,0:T(8,128)(2,1)S(1)}, bf16[768,384]{1,0:T(8,128)(2,1)}, u32[]{:S(2)}) copy-start(bf16[768,384]{1,0:T(8,128)(2,1)} %ws_ref.1) | copy-start | bytes 1769476
  147.6 18.8 %copy-start.1 = (bf16[768,384]{1,0:T(8,128)(2,1)S(1)}, bf16[768,384]{1,0:T(8,128)(2,1)}, u32[]{:S(2)}) copy-start(bf16[768,384]{1,0:T(8,128)(2,1)} %wv_ref.1) | copy-start | bytes 1769476
  159.1 9.3 %collective-permute-start.5 = (bf16[4,864,128]{2,1,0:T(8,128)(2,1)S(1)}, bf16[4,864,128]{2,1,0:T(8,128)(2,1)S(1)}, u32[]{:S(2)}, u32[]{:S(2)}) collective-permute-start(bf16[4,864,128]{2,1,0:T(8,128)(2,1)S(1)} %all_to_all.32.all_ref.mine_ref), channel_id=1, source_target_pairs={{0,1},{1,0},{2,3},{3,2},{4,5},{5,4},{6,7},{7,6},{8,9},{9,8},{10,11... | collective-permute-start | bytes 2654216 | tf_op jit(solution)/shard_map/ppermute | solution.py:349

commit v8 on v7

--- a/solution.py
+++ b/solution.py
@@ -82,11 +82,12 @@
         tail = [cot[:, cols], blank] if h % 2 == 0 else [blank, cot[:, cols]]
         packed = jnp.concatenate([shared[:, cols], value[:, cols]] + tail, axis=1)
         moved = dot(hits[h], packed)
-        out_ref[h] = (moved[:, :LOCAL] + marks[h]).astype(BF16)
+        out_ref[:, h] = (moved[:, :LOCAL] + marks[h]).astype(BF16).reshape(LOCAL, 2, LOCAL)
         if h % 2 == 0:
             pending = moved[:, LOCAL:]
         else:
-            out_ref[HEADS + h // 2] = (pending + moved[:, LOCAL:]).astype(BF16)
+            packed = (pending + moved[:, LOCAL:]).astype(BF16)
+            out_ref[:, HEADS + h // 2] = packed.reshape(LOCAL, 2, LOCAL)
 
 
 def position(row):
@@ -160,7 +161,7 @@
         d_value = dot(probs, cot)
         for m, part in enumerate(spread(jnp.concatenate([d_shared, d_value], axis=1), slot)):
             n = h * 8 + m
-            out_ref[n // 6 * 9 + n % 6] = part.astype(BF16)
+            out_ref[n // 6 * 16 : (n // 6 + 1) * 16, n % 6] = part.astype(BF16).reshape(16, 2, LOCAL)
         if h % 2 == 0:
             pending = both
         else:
@@ -168,7 +169,7 @@
             joined = jnp.where(lane, pltpu.roll(pending, HEAD, 1), both)
             for m, part in enumerate(spread(joined, slot)):
                 n = h // 2 * 8 + m
-                out_ref[n // 3 * 9 + 6 + n % 3] = part.astype(BF16)
+                out_ref[n // 3 * 16 : (n // 3 + 1) * 16, 6 + n % 3] = part.astype(BF16).reshape(16, 2, LOCAL)
 
 
 def index_of(place_ref, dy, dc):
@@ -185,7 +186,7 @@
         for i in range(2):
             lanes = pl.ds(pl.multiple_of(head[i] * LOCAL, LOCAL), LOCAL)
             dests[i, source] = exts[n // 2][n % 2, LOCAL:, lanes].astype(F32)[:8]
-    turned = [in_ref[base + b].astype(F32) for b in range(count)]
+    turned = [in_ref[:, base + b].reshape(ROWS, LOCAL).astype(F32) for b in range(count)]
     turned = [pltpu.roll(rows, BLOCK * b, 1) if b else rows for b, rows in enumerate(turned)]
     limit = lax.rem(j, 4)
     limit = jnp.where(limit == 1, 1, jnp.where(limit == 2, 2, 3)) * count
@@ -275,8 +276,8 @@
         rows = slice(k * COLUMNS, (k + 1) * COLUMNS)
         strip = []
         for y in range(4):
-            mine = mine_ref[y, rows, :].astype(F32)
-            other = other_ref[y, rows, :].astype(F32)
+            mine = mine_ref[y, rows, :]
+            other = other_ref[y, rows, :]
             strip += [jnp.where(first, mine, other), jnp.where(first, other, mine)]
         strip = jnp.concatenate(strip, axis=0)
         lines = slice(k * LOCAL, (k + 1) * LOCAL)
@@ -285,7 +286,7 @@
                 strip[h * LOCAL + half * HEAD : h * LOCAL + (half + 1) * HEAD]
                 for h in range(HEADS)
             ]
-            held[half, lines, :] = jnp.concatenate(heads, axis=0).T.astype(BF16)
+            held[half, lines, :] = jnp.concatenate(heads, axis=0).T
             copies.append(
                 pltpu.make_async_copy(held.at[half, lines], ref.at[lines], sems.at[half, k])
             )
@@ -325,7 +326,7 @@
     place = jnp.stack([lax.axis_index("y"), lax.axis_index("c")]).astype(jnp.int32)
     sent, ext = call(
         send_kernel,
-        (shape(9, ROWS, LOCAL), shape(LOCAL + 16, WIDTH)),
+        (shape(LOCAL, 9, 2, LOCAL), shape(LOCAL + 16, WIDTH)),
         cluster_ids.transpose(1, 0, 2),
         rows,
         w_shared,
@@ -348,16 +349,14 @@
     def flip(part):
         return lax.ppermute(part, "c", [(0, 1), (1, 0)])
 
-    arrived = swap(sent.reshape(9, LOCAL, 2, LOCAL).transpose(1, 0, 2, 3), OWNERS)
+    arrived = swap(sent, OWNERS)
     pair = jnp.stack([ext, flip(ext)])
     near = (shift(pair, 1), shift(pair, 3))
     arrived, pair, near, place = lax.optimization_barrier((arrived, pair, near, place))
     exts = [pair, near[0], shift(pair, 2), near[1]]
-    arrived = arrived.transpose(1, 0, 2, 3)
-    worked = call(attend_kernel, shape(72, 32, LOCAL), arrived.reshape(9, ROWS, LOCAL))
-    worked = worked.reshape(8, 9, 16, 2, LOCAL).transpose(0, 2, 1, 3, 4)
-    back = swap(worked.reshape(LOCAL, 9, 2, LOCAL), OWNERS)
-    back = back.transpose(1, 0, 2, 3).reshape(9, ROWS, LOCAL)
+    arrived = arrived.transpose(1, 0, 2, 3).reshape(9, ROWS, LOCAL)
+    worked = call(attend_kernel, shape(LOCAL, 9, 2, LOCAL), arrived)
+    back = swap(worked, OWNERS)
     part, cols = call(
         partial_kernel,
         (shape(16, SLOT, LOCAL), shape(8, COLUMNS, LOCAL)),

time: 171 us -> 170 us (level)
  local copies, waits for them, and re-layouts: 3.36 us -> 0.46 us
  Pallas kernels: 12.7 us -> 14.7 us
    all_to_all x3, waiting for transfers between devices: 41.4 us -> 29.3 us  [swap(): lax.all_to_all(rows, axes, split_axis=0, concat_axis=0, tiled=True, axis_...]
    ppermute x3, waiting for transfers between devices: 12.1 us -> 24.1 us  [shift(): return lax.ppermute(pair, 'y', [(y, (y + dy) % 4) for y in range(4)])]
    pallas_call x9, Pallas kernels: 12.7 us -> 14.7 us  [call(): pl.pallas_call(kernel, out_shape=out, in_specs=specs, out_specs=jax.tree....]
  transfers between devices with their start and end apart: 9 -> 9, of which waited for: 8 -> 9; matrix products, arithmetic and copies ran while one was open for 0% -> 0% of each run, Pallas kernels for 2% -> 2%
where the time goes in v8:
time: 170 us; the launch traced here: 169 us
  starting transfers between devices  62 us (36%)
  waiting for transfers between devices  55.7 us (33%)
  blocking collectives  35.5 us (21%)
  Pallas kernels  14.7 us (9%)
    all_to_all x3, starting transfers between devices, swap(): lax.all_to_all(rows, axes, split_axis=0, concat_axis=0, tiled=True, axis_...  37.6 us
    all_to_all x3, blocking collectives, swap(): lax.all_to_all(rows, axes, split_axis=0, concat_axis=0, tiled=True, axis_...  35.5 us
    all_to_all x3, waiting for transfers between devices, swap(): lax.all_to_all(rows, axes, split_axis=0, concat_axis=0, tiled=True, axis_...  29.3 us
    ppermute x3, waiting for transfers between devices, shift(): return lax.ppermute(pair, 'y', [(y, (y + dy) % 4) for y in range(4)])  24.1 us
    pallas_call x9, Pallas kernels, call(): pl.pallas_call(kernel, out_shape=out, in_specs=specs, out_specs=jax.tree....  14.7 us
    ppermute x3, starting transfers between devices, flip(): return lax.ppermute(part, 'c', [(0, 1), (1, 0)])  12.7 us
    ppermute x3, starting transfers between devices, shift(): return lax.ppermute(pair, 'y', [(y, (y + dy) % 4) for y in range(4)])  11.7 us
  transfers between devices with their start and end apart: 9, of which 9 were waited for; matrix products, arithmetic and copies ran while one was open for 0% of the time, Pallas kernels for 2%

profile of v8, /device:TPU:1, one launch (start us, length us, event | category | flops | bytes accessed | tf_op | source)
XLA Modules:
  0.0 169.3 jit_solution(2555702920113404359)
XLA Ops:
  0.6 3.2 %shard_map.84 = (bf16[128,9,2,128]{3,2,1,0:T(2,128)(2,1)}, bf16[144,768]{1,0:T(8,128)(2,1)S(1)}) custom-call(s32[6,1,128]{2,1,0:T(1,128)} %bitcast.17, bf16[128,768]{1,0:T(8,128)(2,1)} %bitcast.15, bf16[768,384]{1,0:T(8,128)(2,1)} %ws_ref.1, bf16[768,384]{1,0:T(8,128)(2,1)} %wv_ref.1, bf16[128,384]{1,0:T(8,128)(2,1)} %bitcast.16), custom_call_target="tpu_custom_call" | custom-call | tf_op jit(solution)/shard_map/pallas_call | solution.py:304
  3.8 20.6 %all-to-all-start = ((bf16[128,9,2,128]{3,2,1,0:T(2,128)(2,1)}), bf16[128,9,2,128]{3,2,1,0:T(2,128)(2,1)S(1)}, u32[]{:S(2)}, u32[]{:S(2)}) async-start(bf16[128,9,2,128]{3,2,1,0:T(2,128)(2,1)} %get-tuple-element.22), calls=%async_computation | async-start | bytes 1179648 | tf_op jit(solution)/shard_map/all_to_all | solution.py:319
  24.4 2.8 %collective-permute-start = (bf16[144,768]{1,0:T(8,128)(2,1)S(1)}, bf16[144,768]{1,0:T(8,128)(2,1)S(1)}, u32[]{:S(2)}, u32[]{:S(2)}) collective-permute-start(bf16[144,768]{1,0:T(8,128)(2,1)S(1)} %get-tuple-element.23), channel_id=1, source_target_pairs={{0,1},{1,0},{2,3},{3,2},{4,5},{5,4},{6,7},{7,6},{8,9},{9,8},{10,11... | collective-permute-start | bytes 663560 | tf_op jit(solution)/shard_map/ppermute | solution.py:350
  27.2 1.1 collective-permute-done
  28.3 2.9 %collective-permute-start.1 = (bf16[2,144,768]{2,1,0:T(8,128)(2,1)S(1)}, bf16[2,144,768]{2,1,0:T(8,128)(2,1)S(1)}, u32[]{:S(2)}, u32[]{:S(2)}) collective-permute-start(bf16[2,144,768]{2,1,0:T(8,128)(2,1)S(1)} %pad_maximum_fusion.refs_0_), channel_id=1, source_target_pairs={{0,32},{32,64},{64,96},{96,0},{1,33},{33,65},{65,97},{97,1},{2,34}... | collective-permute-start | bytes 1327112 | tf_op jit(solution)/shard_map/ppermute | solution.py:347
  31.3 3.6 %collective-permute-start.2 = (bf16[2,144,768]{2,1,0:T(8,128)(2,1)S(1)}, bf16[2,144,768]{2,1,0:T(8,128)(2,1)S(1)}, u32[]{:S(2)}, u32[]{:S(2)}) collective-permute-start(bf16[2,144,768]{2,1,0:T(8,128)(2,1)S(1)} %pad_maximum_fusion.refs_0_), channel_id=1, source_target_pairs={{0,96},{32,0},{64,32},{96,64},{1,97},{33,1},{65,33},{97,65},{2,98}... | collective-permute-start | bytes 1327112 | tf_op jit(solution)/shard_map/ppermute | solution.py:347
  34.9 0.1 pad_add_fusion.place_ref
  35.0 10.8 %collective-permute-done.1.refs_1_ = bf16[2,144,768]{2,1,0:T(8,128)(2,1)S(1)} collective-permute-done((bf16[2,144,768]{2,1,0:T(8,128)(2,1)S(1)}, bf16[2,144,768]{2,1,0:T(8,128)(2,1)S(1)}, u32[]{:S(2)}, u32[]{:S(2)}) %collective-permute-start.1) | collective-permute-done | bytes 442400 | tf_op jit(solution)/shard_map/ppermute | solution.py:347
  45.7 1.3 collective-permute-done.2.refs_3_
  47.0 11.9 %all-to-all-done = bf16[128,9,2,128]{3,2,1,0:T(2,128)(2,1)S(1)} async-done(((bf16[128,9,2,128]{3,2,1,0:T(2,128)(2,1)}), bf16[128,9,2,128]{3,2,1,0:T(2,128)(2,1)S(1)}, u32[]{:S(2)}, u32[]{:S(2)}) %all-to-all-start) | async-done | bytes 589856 | tf_op jit(solution)/shard_map/all_to_all | solution.py:319
  58.9 0.5 copy.9
  59.4 4.2 %shard_map.85 = bf16[128,9,2,128]{3,2,1,0:T(2,128)(2,1)} custom-call(bf16[9,256,128]{2,1,0:T(8,128)(2,1)S(1)} %bitcast.11), custom_call_target="tpu_custom_call" | custom-call | tf_op jit(solution)/shard_map/pallas_call | solution.py:304
  63.6 8.2 %all-to-all-start.1 = ((bf16[128,9,2,128]{3,2,1,0:T(2,128)(2,1)}), bf16[128,9,2,128]{3,2,1,0:T(2,128)(2,1)S(1)}, u32[]{:S(2)}, u32[]{:S(2)}) async-start(bf16[128,9,2,128]{3,2,1,0:T(2,128)(2,1)} %shard_map.85), calls=%async_computation.1 | async-start | bytes 1179648 | tf_op jit(solution)/shard_map/all_to_all | solution.py:319
  71.8 5.2 %collective-permute-start.3 = (bf16[2,144,768]{2,1,0:T(8,128)(2,1)S(1)}, bf16[2,144,768]{2,1,0:T(8,128)(2,1)S(1)}, u32[]{:S(2)}, u32[]{:S(2)}) collective-permute-start(bf16[2,144,768]{2,1,0:T(8,128)(2,1)S(1)} %pad_maximum_fusion.refs_0_), channel_id=1, source_target_pairs={{0,64},{32,96},{64,0},{96,32},{1,65},{33,97},{65,1},{97,33},{2,66}... | collective-permute-start | bytes 1327112 | tf_op jit(solution)/shard_map/ppermute | solution.py:347
  77.0 12.1 %collective-permute-done.3.refs_2_ = bf16[2,144,768]{2,1,0:T(8,128)(2,1)S(1)} collective-permute-done((bf16[2,144,768]{2,1,0:T(8,128)(2,1)S(1)}, bf16[2,144,768]{2,1,0:T(8,128)(2,1)S(1)}, u32[]{:S(2)}, u32[]{:S(2)}) %collective-permute-start.3) | collective-permute-done | bytes 442400 | tf_op jit(solution)/shard_map/ppermute | solution.py:347
  89.0 17.3 %all-to-all-done.1.in_ref = bf16[128,9,2,128]{3,2,1,0:T(2,128)(2,1)S(1)} async-done(((bf16[128,9,2,128]{3,2,1,0:T(2,128)(2,1)}), bf16[128,9,2,128]{3,2,1,0:T(2,128)(2,1)S(1)}, u32[]{:S(2)}, u32[]{:S(2)}) %all-to-all-start.1) | async-done | bytes 589856 | tf_op jit(solution)/shard_map/all_to_all | solution.py:319
  106.3 2.6 %shard_map.86 = (bf16[16,40,128]{2,1,0:T(8,128)(2,1)}, bf16[8,96,128]{2,1,0:T(8,128)(2,1)S(1)}) custom-call(s32[2]{0:T(128)S(1)} %pad_add_fusion.place_ref, bf16[128,9,2,128]{3,2,1,0:T(2,128)(2,1)S(1)} %all-to-all-done.1.in_ref, bf16[2,144,768]{2,1,0:T(8,128)(2,1)S(1)} %pad_maximum_fusion.refs_0_, bf16[2,144,768]{2,1,0:T(8,128)(2,1)S(1)} %collective-permute-done.1.refs_1_, ...), custom_call_target="tpu_custom_call" | custom-call | tf_op jit(solution)/shard_map/pallas_call | solution.py:304
  108.9 8.8 %all-to-all-start.2 = ((bf16[16,40,128]{2,1,0:T(8,128)(2,1)}), bf16[16,40,128]{2,1,0:T(8,128)(2,1)S(1)}, u32[]{:S(2)}, u32[]{:S(2)}) async-start(bf16[16,40,128]{2,1,0:T(8,128)(2,1)} %get-tuple-element.29), calls=%async_computation.2 | async-start | bytes 327680 | tf_op jit(solution)/shard_map/all_to_all | solution.py:319
  117.8 1.1 shard_map.87
  118.9 2.7 %collective-permute-start.4 = (bf16[4,144,128]{2,1,0:T(8,128)(2,1)S(1)}, bf16[4,144,128]{2,1,0:T(8,128)(2,1)S(1)}, u32[]{:S(2)}, u32[]{:S(2)}) collective-permute-start(bf16[4,144,128]{2,1,0:T(8,128)(2,1)S(1)} %get-tuple-element.32), channel_id=1, source_target_pairs={{0,1},{1,0},{2,3},{3,2},{4,5},{5,4},{6,7},{7,6},{8,9},{9,8},{10,11... | collective-permute-start | bytes 442376 | tf_op jit(solution)/shard_map/ppermute | solution.py:350
  121.6 1.0 collective-permute-done.4.got_ref
  122.6 0.1 all-to-all-done.2.in_ref
  122.7 12.6 %all_to_all.30.in_ref = bf16[4,40,128]{2,1,0:T(8,128)(2,1)S(1)} all-to-all(bf16[4,40,128]{2,1,0:T(8,128)(2,1)S(1)} %shard_map.88), channel_id=1, replica_groups={{6,8,18,28},{4,14,16,26},{2,12,22,24},{0,10,20,30},{7,9,19,29},{5,15,17..., dimensions={0} | all-to-all | bytes 81920 | tf_op jit(solution)/shard_map/all_to_all | solution.py:319
  135.4 11.3 %all_to_all.31.block_ref = bf16[16,40,128]{2,1,0:T(8,128)(2,1)S(1)} all-to-all(bf16[16,40,128]{2,1,0:T(8,128)(2,1)S(1)} %shard_map.89), channel_id=1, replica_groups={{6,4,2,0,134,132,130,128,262,260,258,256,390,388,386,384},{8,14,12,10,1..., dimensions={0} | all-to-all | bytes 327680 | tf_op jit(solution)/shard_map/all_to_all | solution.py:319
  146.7 0.1 shard_map.90
  146.8 0.0 copy-start
  146.8 0.0 copy-start.1
  146.8 11.6 %all_to_all.32.all_ref.mine_ref = bf16[4,864,128]{2,1,0:T(8,128)(2,1)S(1)} all-to-all(bf16[4,864,128]{2,1,0:T(8,128)(2,1)S(1)} %shard_map.90), channel_id=1, replica_groups=mesh['x'=4,'y'=4,'z'=16,'c'=2] {'y'}, dimensions={0} | all-to-all | bytes 1769472 | tf_op jit(solution)/shard_map/all_to_all | solution.py:319
  158.4 7.2 %collective-permute-start.5 = (bf16[4,864,128]{2,1,0:T(8,128)(2,1)S(1)}, bf16[4,864,128]{2,1,0:T(8,128)(2,1)S(1)}, u32[]{:S(2)}, u32[]{:S(2)}) collective-permute-start(bf16[4,864,128]{2,1,0:T(8,128)(2,1)S(1)} %all_to_all.32.all_ref.mine_ref), channel_id=1, source_target_pairs={{0,1},{1,0},{2,3},{3,2},{4,5},{5,4},{6,7},{7,6},{8,9},{9,8},{10,11... | collective-permute-start | bytes 2654216 | tf_op jit(solution)/shard_map/ppermute | solution.py:350
  165.6 0.0 copy-done
  165.6 0.0 copy-done.1
  165.6 1.8 %shard_map.91 = (bf16[128,384]{1,0:T(8,128)(2,1)}, bf16[128,768]{1,0:T(8,128)(2,1)}) custom-call(s32[2]{0:T(128)S(1)} %pad_add_fusion.place_ref, bf16[4,864,128]{2,1,0:T(8,128)(2,1)S(1)} %all_to_all.32.all_ref.mine_ref, bf16[768,384]{1,0:T(8,128)(2,1)S(1)} %copy-done, bf16[768,384]{1,0:T(8,128)(2,1)S(1)} %copy-done.1), custom_call_target="tpu_custom_call" | custom-call | tf_op jit(solution)/shard_map/pallas_call | solution.py:304
  167.3 0.2 collective-permute-done.5.other_ref
  167.6 1.7 %shard_map.92 = (bf16[768,384]{1,0:T(8,128)(2,1)}, bf16[768,384]{1,0:T(8,128)(2,1)}) custom-call(s32[2]{0:T(128)S(1)} %pad_add_fusion.place_ref, bf16[4,864,128]{2,1,0:T(8,128)(2,1)S(1)} %all_to_all.32.all_ref.mine_ref, bf16[4,864,128]{2,1,0:T(8,128)(2,1)S(1)} %collective-permute-done.5.other_ref), custom_call_target="tpu_custom_call" | custom-call | tf_op jit(solution)/shard_map/pallas_call | solution.py:304
  (3 shorter events, 0.1 us)
Async XLA Ops:
  3.8 55.1 %all-to-all-start = ((bf16[128,9,2,128]{3,2,1,0:T(2,128)(2,1)}), bf16[128,9,2,128]{3,2,1,0:T(2,128)(2,1)S(1)}, u32[]{:S(2)}, u32[]{:S(2)}) async-start(bf16[128,9,2,128]{3,2,1,0:T(2,128)(2,1)} %get-tuple-element.22), calls=%async_computation | async-start | bytes 1179648 | tf_op jit(solution)/shard_map/all_to_all | solution.py:319
  24.4 3.9 %collective-permute-start = (bf16[144,768]{1,0:T(8,128)(2,1)S(1)}, bf16[144,768]{1,0:T(8,128)(2,1)S(1)}, u32[]{:S(2)}, u32[]{:S(2)}) collective-permute-start(bf16[144,768]{1,0:T(8,128)(2,1)S(1)} %get-tuple-element.23), channel_id=1, source_target_pairs={{0,1},{1,0},{2,3},{3,2},{4,5},{5,4},{6,7},{7,6},{8,9},{9,8},{10,11... | collective-permute-start | bytes 663560 | tf_op jit(solution)/shard_map/ppermute | solution.py:350
  28.3 17.4 %collective-permute-start.1 = (bf16[2,144,768]{2,1,0:T(8,128)(2,1)S(1)}, bf16[2,144,768]{2,1,0:T(8,128)(2,1)S(1)}, u32[]{:S(2)}, u32[]{:S(2)}) collective-permute-start(bf16[2,144,768]{2,1,0:T(8,128)(2,1)S(1)} %pad_maximum_fusion.refs_0_), channel_id=1, source_target_pairs={{0,32},{32,64},{64,96},{96,0},{1,33},{33,65},{65,97},{97,1},{2,34}... | collective-permute-start | bytes 1327112 | tf_op jit(solution)/shard_map/ppermute | solution.py:347
  31.3 15.7 %collective-permute-start.2 = (bf16[2,144,768]{2,1,0:T(8,128)(2,1)S(1)}, bf16[2,144,768]{2,1,0:T(8,128)(2,1)S(1)}, u32[]{:S(2)}, u32[]{:S(2)}) collective-permute-start(bf16[2,144,768]{2,1,0:T(8,128)(2,1)S(1)} %pad_maximum_fusion.refs_0_), channel_id=1, source_target_pairs={{0,96},{32,0},{64,32},{96,64},{1,97},{33,1},{65,33},{97,65},{2,98}... | collective-permute-start | bytes 1327112 | tf_op jit(solution)/shard_map/ppermute | solution.py:347
  63.6 42.7 %all-to-all-start.1 = ((bf16[128,9,2,128]{3,2,1,0:T(2,128)(2,1)}), bf16[128,9,2,128]{3,2,1,0:T(2,128)(2,1)S(1)}, u32[]{:S(2)}, u32[]{:S(2)}) async-start(bf16[128,9,2,128]{3,2,1,0:T(2,128)(2,1)} %shard_map.85), calls=%async_computation.1 | async-start | bytes 1179648 | tf_op jit(solution)/shard_map/all_to_all | solution.py:319
  71.8 17.2 %collective-permute-start.3 = (bf16[2,144,768]{2,1,0:T(8,128)(2,1)S(1)}, bf16[2,144,768]{2,1,0:T(8,128)(2,1)S(1)}, u32[]{:S(2)}, u32[]{:S(2)}) collective-permute-start(bf16[2,144,768]{2,1,0:T(8,128)(2,1)S(1)} %pad_maximum_fusion.refs_0_), channel_id=1, source_target_pairs={{0,64},{32,96},{64,0},{96,32},{1,65},{33,97},{65,1},{97,33},{2,66}... | collective-permute-start | bytes 1327112 | tf_op jit(solution)/shard_map/ppermute | solution.py:347
  108.9 13.8 %all-to-all-start.2 = ((bf16[16,40,128]{2,1,0:T(8,128)(2,1)}), bf16[16,40,128]{2,1,0:T(8,128)(2,1)S(1)}, u32[]{:S(2)}, u32[]{:S(2)}) async-start(bf16[16,40,128]{2,1,0:T(8,128)(2,1)} %get-tuple-element.29), calls=%async_computation.2 | async-start | bytes 327680 | tf_op jit(solution)/shard_map/all_to_all | solution.py:319
  118.9 3.7 %collective-permute-start.4 = (bf16[4,144,128]{2,1,0:T(8,128)(2,1)S(1)}, bf16[4,144,128]{2,1,0:T(8,128)(2,1)S(1)}, u32[]{:S(2)}, u32[]{:S(2)}) collective-permute-start(bf16[4,144,128]{2,1,0:T(8,128)(2,1)S(1)} %get-tuple-element.32), channel_id=1, source_target_pairs={{0,1},{1,0},{2,3},{3,2},{4,5},{5,4},{6,7},{7,6},{8,9},{9,8},{10,11... | collective-permute-start | bytes 442376 | tf_op jit(solution)/shard_map/ppermute | solution.py:350
  146.8 18.8 %copy-start = (bf16[768,384]{1,0:T(8,128)(2,1)S(1)}, bf16[768,384]{1,0:T(8,128)(2,1)}, u32[]{:S(2)}) copy-start(bf16[768,384]{1,0:T(8,128)(2,1)} %ws_ref.1) | copy-start | bytes 1769476
  146.8 18.8 %copy-start.1 = (bf16[768,384]{1,0:T(8,128)(2,1)S(1)}, bf16[768,384]{1,0:T(8,128)(2,1)}, u32[]{:S(2)}) copy-start(bf16[768,384]{1,0:T(8,128)(2,1)} %wv_ref.1) | copy-start | bytes 1769476
  158.4 9.2 %collective-permute-start.5 = (bf16[4,864,128]{2,1,0:T(8,128)(2,1)S(1)}, bf16[4,864,128]{2,1,0:T(8,128)(2,1)S(1)}, u32[]{:S(2)}, u32[]{:S(2)}) collective-permute-start(bf16[4,864,128]{2,1,0:T(8,128)(2,1)S(1)} %all_to_all.32.all_ref.mine_ref), channel_id=1, source_target_pairs={{0,1},{1,0},{2,3},{3,2},{4,5},{5,4},{6,7},{7,6},{8,9},{9,8},{10,11... | collective-permute-start | bytes 2654216 | tf_op jit(solution)/shard_map/ppermute | solution.py:350

commit v9 on v8

--- a/solution.py
+++ b/solution.py
@@ -27,7 +27,7 @@
 SLOT = 40
 BLOCK = 16
 WHOLE = 576
-MESSAGE = 144
+MESSAGE = 96
 
 
 def iota(shape, dim):
@@ -165,19 +165,19 @@
         if h % 2 == 0:
             pending = both
         else:
-            lane = iota((ROWS, LOCAL), 1) < HEAD
-            joined = jnp.where(lane, pltpu.roll(pending, HEAD, 1), both)
-            for m, part in enumerate(spread(joined, slot)):
-                n = h // 2 * 8 + m
-                out_ref[n // 3 * 16 : (n // 3 + 1) * 16, 6 + n % 3] = part.astype(BF16).reshape(16, 2, LOCAL)
+            k = HEADS + h // 2
+            joined = jnp.where(head_lanes, pltpu.roll(pending, HEAD, 1), both).astype(BF16)
+            out_ref[:, k] = joined.reshape(LOCAL, 2, LOCAL)
 
 
 def index_of(place_ref, dy, dc):
     return lax.rem(place_ref[0] + dy, 4) * 2 + lax.rem(place_ref[1] + dc, 2)
 
 
-def gather_columns(place_ref, in_ref, base, count, exts, dests, out_ref, first):
-    j = place_ref[0] * 2 + place_ref[1]
+def partial_kernel(place_ref, in_ref, *refs):
+    exts, (out_ref, keep_ref, give_ref), (dests, cols, scratch) = refs[:4], refs[4:7], refs[7:]
+    here = place_ref[1]
+    j = place_ref[0] * 2 + here
     head = (j * 3 // 4, (j * 6 + 5) // 8)
     lane_slot = iota((ROWS, LOCAL), 1) >> 4
     sub_rows = iota((ROWS, LOCAL), 0).astype(F32)
@@ -186,48 +186,48 @@
         for i in range(2):
             lanes = pl.ds(pl.multiple_of(head[i] * LOCAL, LOCAL), LOCAL)
             dests[i, source] = exts[n // 2][n % 2, LOCAL:, lanes].astype(F32)[:8]
-    turned = [in_ref[:, base + b].reshape(ROWS, LOCAL).astype(F32) for b in range(count)]
+    turned = [in_ref[:, b].reshape(ROWS, LOCAL).astype(F32) for b in range(6)]
     turned = [pltpu.roll(rows, BLOCK * b, 1) if b else rows for b, rows in enumerate(turned)]
     limit = lax.rem(j, 4)
-    limit = jnp.where(limit == 1, 1, jnp.where(limit == 2, 2, 3)) * count
+    limit = jnp.where(limit == 1, 2, jnp.where(limit == 2, 4, 6))
     for p in range(8):
         rows = turned[0]
-        for b in range(1, count):
+        for b in range(1, 6):
             rows = jnp.where(lane_slot == (b + p) % 8, turned[b], rows)
-        rows = rows.astype(BF16)
         routes = [(sub_rows == dests[i, p, :1]).astype(BF16) for i in range(2)]
-        found = dot(rows, jnp.concatenate(routes, axis=1), ((0,), (0,)))
-        found = [found[:, :LOCAL], found[:, LOCAL:]]
+        found = dot(rows.astype(BF16), jnp.concatenate(routes, axis=1), ((0,), (0,)))
         blocks = []
-        for b in range(count):
+        for b in range(6):
             cut = slice((b + p) % 8 * BLOCK, ((b + p) % 8 + 1) * BLOCK)
-            blocks.append(jnp.where(b * 3 < limit, found[0][cut], found[1][cut]))
-        out_ref[p, first : first + count * BLOCK, :] = jnp.concatenate(blocks, axis=0).astype(BF16)
-
-
-def partial_kernel(place_ref, in_ref, *refs):
-    exts, (out_ref, cols_ref), (dests, scratch) = refs[:4], refs[4:6], refs[6:]
-    gather_columns(place_ref, in_ref, 0, 6, exts, dests, cols_ref, 0)
+            blocks.append(jnp.where(b < limit, found[cut, :LOCAL], found[cut, LOCAL:]))
+        cols[p] = jnp.concatenate(blocks, axis=0).astype(BF16)
     total = None
     for n, (dy, dc) in enumerate(STEPS):
         source = index_of(place_ref, 4 - dy, dc)
-        term = dot(cols_ref[source], exts[n // 2][n % 2, :LOCAL, :])
+        term = dot(cols[source], exts[n // 2][n % 2, :LOCAL, :])
         total = term if total is None else total + term
     for k in range(WIDTH // LOCAL):
         scratch[k * COLUMNS : (k + 1) * COLUMNS, :] = total[:, k * LOCAL : (k + 1) * LOCAL]
     scratch[16 * PIECE :, :] = jnp.zeros((8, LOCAL), F32)
     for i in range(16):
         out_ref[i] = scratch[i * PIECE : i * PIECE + SLOT, :].astype(BF16)
-
-
-def forward_kernel(place_ref, in_ref, cols_ref, *refs):
-    exts, (keep_ref, give_ref), (dests, scratch) = refs[:4], refs[4:6], refs[6:]
-    gather_columns(place_ref, in_ref, 6, 3, exts, dests, scratch, 0)
-    here = place_ref[1]
     for y in range(4):
-        for ref, c in ((keep_ref, here), (give_ref, 1 - here)):
-            ref[y, :COLUMNS, :] = cols_ref[y * 2 + c]
-            ref[y, COLUMNS:, :] = scratch[y * 2 + c]
+        keep_ref[y] = cols[y * 2 + here]
+        give_ref[y] = cols[y * 2 + 1 - here]
+
+
+def output_kernel(in_ref, ext_ref, att_ref):
+    sub_rows = iota((ROWS, LOCAL), 0).astype(F32)
+    head_lanes = iota((LOCAL, LOCAL), 1) < HEAD
+    dests = ext_ref[0, LOCAL:, :].astype(F32)[:1]
+    for k in range(HEADS // 2):
+        rows = in_ref[:, HEADS + k].reshape(ROWS, LOCAL)
+        found = []
+        for h in (2 * k, 2 * k + 1):
+            route = (sub_rows == dests[:, h * LOCAL : (h + 1) * LOCAL]).astype(BF16)
+            found.append(dot(route, rows, ((0,), (0,))))
+        both = jnp.where(head_lanes, found[0], found[1])
+        att_ref[:, k * LOCAL : (k + 1) * LOCAL] = both.astype(BF16)
 
 
 def pack_kernel(block_ref, keep_ref, got_ref, out_ref, scratch):
@@ -240,22 +240,22 @@
         out_ref[y, WHOLE + MESSAGE :, :] = got_ref[y]
 
 
-def return_kernel(place_ref, all_ref, ws_ref, wv_ref, att_ref, grad_ref, held):
+def return_kernel(place_ref, all_ref, ws_ref, wv_ref, grad_ref, held):
     here = place_ref[1]
     for y in range(4):
         held[y * 2 + here] = all_ref[y, WHOLE : WHOLE + MESSAGE, :]
         held[y * 2 + 1 - here] = all_ref[y, WHOLE + MESSAGE :, :]
 
-    def columns(blocks, per, first):
+    def columns(first):
         rows = [
-            held[n // per, first + n % per * BLOCK : first + (n % per + 1) * BLOCK, :]
-            for n in blocks
+            held[n // 6, n % 6 * BLOCK : (n % 6 + 1) * BLOCK, :]
+            for h in range(HEADS)
+            for n in range(h * 8 + first, h * 8 + first + 4)
         ]
         return jnp.concatenate(rows, axis=0).astype(F32).T.astype(BF16)
 
-    left = columns([h * 8 + m for h in range(HEADS) for m in range(4)], 6, 0)
-    right = columns([h * 8 + 4 + m for h in range(HEADS) for m in range(4)], 6, 0)
-    att_ref[...] = columns(range(24), 3, COLUMNS)
+    left = columns(0)
+    right = columns(4)
     total = dot(left, ws_ref[...], ((1,), (1,))) + dot(right, wv_ref[...], ((1,), (1,)))
     grad_ref[...] = total.astype(BF16)
 
@@ -295,17 +295,19 @@
         copy.wait()
 
 
-def call(kernel, out, *args, scratch=(), scalars=0, held=False, far=False):
-    space = pl.ANY if held else pltpu.VMEM
+def call(kernel, out, *args, scratch=(), scalars=0, held=False, far=()):
     if held:
         args = [pltpu.with_memory_space_constraint(arg, pltpu.HBM) for arg in args]
     specs = [pl.BlockSpec(memory_space=pltpu.SMEM)] * scalars
-    specs += [pl.BlockSpec(memory_space=space)] * (len(args) - scalars)
+    specs += [pl.BlockSpec(memory_space=pl.ANY if held else pltpu.VMEM)] * (len(args) - scalars)
+    outs = [
+        pl.BlockSpec(memory_space=pl.ANY if n in far else pltpu.VMEM) for n in range(len(out))
+    ]
     return pl.pallas_call(
         kernel,
         out_shape=out,
         in_specs=specs,
-        out_specs=jax.tree.map(lambda _: pl.BlockSpec(memory_space=pl.ANY if far else pltpu.VMEM), out),
+        out_specs=outs,
         scratch_shapes=scratch,
         compiler_params=pltpu.CompilerParams(vmem_limit_bytes=48 * 1024 * 1024),
     )(*args)
@@ -355,46 +357,43 @@
     arrived, pair, near, place = lax.optimization_barrier((arrived, pair, near, place))
     exts = [pair, near[0], shift(pair, 2), near[1]]
     arrived = arrived.transpose(1, 0, 2, 3).reshape(9, ROWS, LOCAL)
-    worked = call(attend_kernel, shape(LOCAL, 9, 2, LOCAL), arrived)
+    (worked,) = call(
+        attend_kernel,
+        [shape(LOCAL, 9, 2, LOCAL)],
+        arrived,
+    )
     back = swap(worked, OWNERS)
-    part, cols = call(
+    part, keep, give = call(
         partial_kernel,
-        (shape(16, SLOT, LOCAL), shape(8, COLUMNS, LOCAL)),
+        [shape(16, SLOT, LOCAL), shape(4, MESSAGE, LOCAL), shape(4, MESSAGE, LOCAL)],
         place,
         back,
         *exts,
-        scratch=[pltpu.VMEM((2, 8, 8, LOCAL), F32), pltpu.VMEM((16 * PIECE + 8, LOCAL), F32)],
+        scratch=[
+            pltpu.VMEM((2, 8, 8, LOCAL), F32),
+            pltpu.VMEM((8, COLUMNS, LOCAL), BF16),
+            pltpu.VMEM((16 * PIECE + 8, LOCAL), F32),
+        ],
         scalars=1,
     )
-    keep, give = call(
-        forward_kernel,
-        (shape(4, MESSAGE, LOCAL), shape(4, MESSAGE, LOCAL)),
-        place,
-        back,
-        cols,
-        *exts,
-        scratch=[pltpu.VMEM((2, 8, 8, LOCAL), F32), pltpu.VMEM((8, COLUMNS // 2, LOCAL), BF16)],
-        scalars=1,
-    )
-    got = flip(give)
+    (attention,) = call(output_kernel, [shape(LOCAL, PROJ)], back, pair)
     part = swap(part, ("x", "z"), NEAR)
-    part, keep, got = lax.optimization_barrier((part, keep, got))
-    part = call(sum_kernel, shape(4, SLOT, LOCAL), part)
-    block = call(sum_kernel, shape(16, SLOT, LOCAL), swap(part, "z", FAR))
-    block = swap(block, ("x", "z"), NEAR)
-    block = call(
+    part, keep, got, attention = lax.optimization_barrier((part, keep, flip(give), attention))
+    (part,) = call(sum_kernel, [shape(4, SLOT, LOCAL)], part)
+    (block,) = call(sum_kernel, [shape(16, SLOT, LOCAL)], swap(part, "z", FAR))
+    (block,) = call(
         pack_kernel,
-        shape(4, WHOLE + 2 * MESSAGE, LOCAL),
-        block,
+        [shape(4, WHOLE + 2 * MESSAGE, LOCAL)],
+        swap(block, ("x", "z"), NEAR),
         keep,
         got,
         scratch=[pltpu.VMEM((WHOLE, LOCAL), F32)],
     )
     block = swap(block, "y")
     other = flip(block)
-    attention, grad_tokens = call(
+    (grad_tokens,) = call(
         return_kernel,
-        (shape(LOCAL, PROJ), shape(LOCAL, WIDTH)),
+        [shape(LOCAL, WIDTH)],
         place,
         block,
         w_shared,
@@ -413,7 +412,7 @@
             pltpu.SemaphoreType.DMA((2, WIDTH // LOCAL)),
         ],
         scalars=1,
-        far=True,
+        far=(0, 1),
     )
     return (attention[None], grad_tokens[None], grad_shared, grad_value)
 

time: 170 us -> 169 us (level)
  transfers between devices with their start and end apart: 9 -> 9, of which waited for: 9 -> 8; matrix products, arithmetic and copies ran while one was open for 0% -> 0% of each run, Pallas kernels for 2% -> 2%
where the time goes in v9:
time: 169 us; the launch traced here: 168 us
  starting transfers between devices  62.1 us (37%)
  waiting for transfers between devices  55.8 us (33%)
  blocking collectives  34.7 us (21%)
  Pallas kernels  14.5 us (9%)
    all_to_all x3, starting transfers between devices, swap(): lax.all_to_all(rows, axes, split_axis=0, concat_axis=0, tiled=True, axis_...  37.6 us
    all_to_all x3, blocking collectives, swap(): lax.all_to_all(rows, axes, split_axis=0, concat_axis=0, tiled=True, axis_...  34.7 us
    all_to_all x3, waiting for transfers between devices, swap(): lax.all_to_all(rows, axes, split_axis=0, concat_axis=0, tiled=True, axis_...  30.5 us
    ppermute x3, waiting for transfers between devices, shift(): return lax.ppermute(pair, 'y', [(y, (y + dy) % 4) for y in range(4)])  24.1 us
    pallas_call x9, Pallas kernels, call(): pl.pallas_call(kernel, out_shape=out, in_specs=specs, out_specs=outs, scr...  14.5 us
    ppermute x3, starting transfers between devices, flip(): return lax.ppermute(part, 'c', [(0, 1), (1, 0)])  12.8 us
    ppermute x3, starting transfers between devices, shift(): return lax.ppermute(pair, 'y', [(y, (y + dy) % 4) for y in range(4)])  11.7 us
  transfers between devices with their start and end apart: 9, of which 8 were waited for; matrix products, arithmetic and copies ran while one was open for 0% of the time, Pallas kernels for 2%

profile of v9, /device:TPU:1, one launch (start us, length us, event | category | flops | bytes accessed | tf_op | source)
XLA Modules:
  0.0 168.4 jit_solution(4423957273200074533)
XLA Ops:
  0.6 3.2 %shard_map.84 = (bf16[128,9,2,128]{3,2,1,0:T(2,128)(2,1)}, bf16[144,768]{1,0:T(8,128)(2,1)S(1)}) custom-call(s32[6,1,128]{2,1,0:T(1,128)} %bitcast.19, bf16[128,768]{1,0:T(8,128)(2,1)} %bitcast.15, bf16[768,384]{1,0:T(8,128)(2,1)} %ws_ref.1, bf16[768,384]{1,0:T(8,128)(2,1)} %wv_ref.1, bf16[128,384]{1,0:T(8,128)(2,1)} %bitcast.17), custom_call_target="tpu_custom_call" | custom-call | tf_op jit(solution)/shard_map/pallas_call | solution.py:306
  3.8 20.6 %all-to-all-start = ((bf16[128,9,2,128]{3,2,1,0:T(2,128)(2,1)}), bf16[128,9,2,128]{3,2,1,0:T(2,128)(2,1)S(1)}, u32[]{:S(2)}, u32[]{:S(2)}) async-start(bf16[128,9,2,128]{3,2,1,0:T(2,128)(2,1)} %get-tuple-element.20), calls=%async_computation | async-start | bytes 1179648 | tf_op jit(solution)/shard_map/all_to_all | solution.py:321
  24.4 2.8 %collective-permute-start = (bf16[144,768]{1,0:T(8,128)(2,1)S(1)}, bf16[144,768]{1,0:T(8,128)(2,1)S(1)}, u32[]{:S(2)}, u32[]{:S(2)}) collective-permute-start(bf16[144,768]{1,0:T(8,128)(2,1)S(1)} %get-tuple-element.21), channel_id=1, source_target_pairs={{0,1},{1,0},{2,3},{3,2},{4,5},{5,4},{6,7},{7,6},{8,9},{9,8},{10,11... | collective-permute-start | bytes 663560 | tf_op jit(solution)/shard_map/ppermute | solution.py:352
  27.2 1.1 collective-permute-done
  28.3 2.9 %collective-permute-start.1 = (bf16[2,144,768]{2,1,0:T(8,128)(2,1)S(1)}, bf16[2,144,768]{2,1,0:T(8,128)(2,1)S(1)}, u32[]{:S(2)}, u32[]{:S(2)}) collective-permute-start(bf16[2,144,768]{2,1,0:T(8,128)(2,1)S(1)} %pad_maximum_fusion.refs_0_.ext_ref), channel_id=1, source_target_pairs={{0,32},{32,64},{64,96},{96,0},{1,33},{33,65},{65,97},{97,1},{2,34}... | collective-permute-start | bytes 1327112 | tf_op jit(solution)/shard_map/ppermute | solution.py:349
  31.3 3.6 %collective-permute-start.2 = (bf16[2,144,768]{2,1,0:T(8,128)(2,1)S(1)}, bf16[2,144,768]{2,1,0:T(8,128)(2,1)S(1)}, u32[]{:S(2)}, u32[]{:S(2)}) collective-permute-start(bf16[2,144,768]{2,1,0:T(8,128)(2,1)S(1)} %pad_maximum_fusion.refs_0_.ext_ref), channel_id=1, source_target_pairs={{0,96},{32,0},{64,32},{96,64},{1,97},{33,1},{65,33},{97,65},{2,98}... | collective-permute-start | bytes 1327112 | tf_op jit(solution)/shard_map/ppermute | solution.py:349
  34.9 0.1 pad_add_fusion.place_ref
  35.0 10.8 %collective-permute-done.1.refs_1_ = bf16[2,144,768]{2,1,0:T(8,128)(2,1)S(1)} collective-permute-done((bf16[2,144,768]{2,1,0:T(8,128)(2,1)S(1)}, bf16[2,144,768]{2,1,0:T(8,128)(2,1)S(1)}, u32[]{:S(2)}, u32[]{:S(2)}) %collective-permute-start.1) | collective-permute-done | bytes 442400 | tf_op jit(solution)/shard_map/ppermute | solution.py:349
  45.7 1.3 collective-permute-done.2.refs_3_
  47.0 11.9 %all-to-all-done = bf16[128,9,2,128]{3,2,1,0:T(2,128)(2,1)S(1)} async-done(((bf16[128,9,2,128]{3,2,1,0:T(2,128)(2,1)}), bf16[128,9,2,128]{3,2,1,0:T(2,128)(2,1)S(1)}, u32[]{:S(2)}, u32[]{:S(2)}) %all-to-all-start) | async-done | bytes 589856 | tf_op jit(solution)/shard_map/all_to_all | solution.py:321
  58.9 0.5 copy.9
  59.4 4.1 %shard_map.85 = bf16[128,9,2,128]{3,2,1,0:T(2,128)(2,1)} custom-call(bf16[9,256,128]{2,1,0:T(8,128)(2,1)S(1)} %bitcast.11), custom_call_target="tpu_custom_call" | custom-call | tf_op jit(solution)/shard_map/pallas_call | solution.py:306
  63.5 8.2 %all-to-all-start.1 = ((bf16[128,9,2,128]{3,2,1,0:T(2,128)(2,1)}), bf16[128,9,2,128]{3,2,1,0:T(2,128)(2,1)S(1)}, u32[]{:S(2)}, u32[]{:S(2)}) async-start(bf16[128,9,2,128]{3,2,1,0:T(2,128)(2,1)} %shard_map.85), calls=%async_computation.1 | async-start | bytes 1179648 | tf_op jit(solution)/shard_map/all_to_all | solution.py:321
  71.7 5.2 %collective-permute-start.3 = (bf16[2,144,768]{2,1,0:T(8,128)(2,1)S(1)}, bf16[2,144,768]{2,1,0:T(8,128)(2,1)S(1)}, u32[]{:S(2)}, u32[]{:S(2)}) collective-permute-start(bf16[2,144,768]{2,1,0:T(8,128)(2,1)S(1)} %pad_maximum_fusion.refs_0_.ext_ref), channel_id=1, source_target_pairs={{0,64},{32,96},{64,0},{96,32},{1,65},{33,97},{65,1},{97,33},{2,66}... | collective-permute-start | bytes 1327112 | tf_op jit(solution)/shard_map/ppermute | solution.py:349
  76.9 12.1 %collective-permute-done.3.refs_2_ = bf16[2,144,768]{2,1,0:T(8,128)(2,1)S(1)} collective-permute-done((bf16[2,144,768]{2,1,0:T(8,128)(2,1)S(1)}, bf16[2,144,768]{2,1,0:T(8,128)(2,1)S(1)}, u32[]{:S(2)}, u32[]{:S(2)}) %collective-permute-start.3) | collective-permute-done | bytes 442400 | tf_op jit(solution)/shard_map/ppermute | solution.py:349
  89.0 17.3 %all-to-all-done.1.in_ref = bf16[128,9,2,128]{3,2,1,0:T(2,128)(2,1)S(1)} async-done(((bf16[128,9,2,128]{3,2,1,0:T(2,128)(2,1)}), bf16[128,9,2,128]{3,2,1,0:T(2,128)(2,1)S(1)}, u32[]{:S(2)}, u32[]{:S(2)}) %all-to-all-start.1) | async-done | bytes 589856 | tf_op jit(solution)/shard_map/all_to_all | solution.py:321
  106.3 2.6 %shard_map.86 = (bf16[16,40,128]{2,1,0:T(8,128)(2,1)}, bf16[4,96,128]{2,1,0:T(8,128)(2,1)S(1)}, bf16[4,96,128]{2,1,0:T(8,128)(2,1)S(1)}) custom-call(s32[2]{0:T(128)S(1)} %pad_add_fusion.place_ref, bf16[128,9,2,128]{3,2,1,0:T(2,128)(2,1)S(1)} %all-to-all-done.1.in_ref, bf16[2,144,768]{2,1,0:T(8,128)(2,1)S(1)} %pad_maximum_fusion.refs_0_.ext_ref, ...), custom_call_target="tpu_custom_call" | custom-call | tf_op jit(solution)/shard_map/pallas_call | solution.py:306
  108.9 8.8 %all-to-all-start.2 = ((bf16[16,40,128]{2,1,0:T(8,128)(2,1)}), bf16[16,40,128]{2,1,0:T(8,128)(2,1)S(1)}, u32[]{:S(2)}, u32[]{:S(2)}) async-start(bf16[16,40,128]{2,1,0:T(8,128)(2,1)} %get-tuple-element.27), calls=%async_computation.2 | async-start | bytes 327680 | tf_op jit(solution)/shard_map/all_to_all | solution.py:321
  117.7 2.7 %collective-permute-start.4 = (bf16[4,96,128]{2,1,0:T(8,128)(2,1)S(1)}, bf16[4,96,128]{2,1,0:T(8,128)(2,1)S(1)}, u32[]{:S(2)}, u32[]{:S(2)}) collective-permute-start(bf16[4,96,128]{2,1,0:T(8,128)(2,1)S(1)} %get-tuple-element.29), channel_id=1, source_target_pairs={{0,1},{1,0},{2,3},{3,2},{4,5},{5,4},{6,7},{7,6},{8,9},{9,8},{10,11... | collective-permute-start | bytes 294920 | tf_op jit(solution)/shard_map/ppermute | solution.py:352
  120.4 1.0 shard_map.87
  121.4 0.0 collective-permute-done.4.got_ref
  121.4 1.3 all-to-all-done.2.in_ref
  122.7 12.6 %all_to_all.30.in_ref = bf16[4,40,128]{2,1,0:T(8,128)(2,1)S(1)} all-to-all(bf16[4,40,128]{2,1,0:T(8,128)(2,1)S(1)} %shard_map.88), channel_id=1, replica_groups={{6,8,18,28},{4,14,16,26},{2,12,22,24},{0,10,20,30},{7,9,19,29},{5,15,17..., dimensions={0} | all-to-all | bytes 81920 | tf_op jit(solution)/shard_map/all_to_all | solution.py:321
  135.4 11.1 %all_to_all.31.block_ref = bf16[16,40,128]{2,1,0:T(8,128)(2,1)S(1)} all-to-all(bf16[16,40,128]{2,1,0:T(8,128)(2,1)S(1)} %shard_map.89), channel_id=1, replica_groups={{6,4,2,0,134,132,130,128,262,260,258,256,390,388,386,384},{8,14,12,10,1..., dimensions={0} | all-to-all | bytes 327680 | tf_op jit(solution)/shard_map/all_to_all | solution.py:321
  146.5 0.1 shard_map.90
  146.6 0.0 copy-start
  146.6 0.0 copy-start.1
  146.6 10.9 %all_to_all.32.all_ref.mine_ref = bf16[4,768,128]{2,1,0:T(8,128)(2,1)S(1)} all-to-all(bf16[4,768,128]{2,1,0:T(8,128)(2,1)S(1)} %shard_map.90), channel_id=1, replica_groups=mesh['x'=4,'y'=4,'z'=16,'c'=2] {'y'}, dimensions={0} | all-to-all | bytes 1572864 | tf_op jit(solution)/shard_map/all_to_all | solution.py:321
  157.5 7.3 %collective-permute-start.5 = (bf16[4,768,128]{2,1,0:T(8,128)(2,1)S(1)}, bf16[4,768,128]{2,1,0:T(8,128)(2,1)S(1)}, u32[]{:S(2)}, u32[]{:S(2)}) collective-permute-start(bf16[4,768,128]{2,1,0:T(8,128)(2,1)S(1)} %all_to_all.32.all_ref.mine_ref), channel_id=1, source_target_pairs={{0,1},{1,0},{2,3},{3,2},{4,5},{5,4},{6,7},{7,6},{8,9},{9,8},{10,11... | collective-permute-start | bytes 2359304 | tf_op jit(solution)/shard_map/ppermute | solution.py:352
  164.8 0.0 copy-done
  164.8 0.0 copy-done.1
  164.8 1.8 %shard_map.91 = bf16[128,768]{1,0:T(8,128)(2,1)} custom-call(s32[2]{0:T(128)S(1)} %pad_add_fusion.place_ref, bf16[4,768,128]{2,1,0:T(8,128)(2,1)S(1)} %all_to_all.32.all_ref.mine_ref, bf16[768,384]{1,0:T(8,128)(2,1)S(1)} %copy-done, bf16[768,384]{1,0:T(8,128)(2,1)S(1)} %copy-done.1), custom_call_target="tpu_custom_call" | custom-call | tf_op jit(solution)/shard_map/pallas_call | solution.py:306
  166.6 0.1 collective-permute-done.5.other_ref
  166.7 1.7 %shard_map.92 = (bf16[768,384]{1,0:T(8,128)(2,1)}, bf16[768,384]{1,0:T(8,128)(2,1)}) custom-call(s32[2]{0:T(128)S(1)} %pad_add_fusion.place_ref, bf16[4,768,128]{2,1,0:T(8,128)(2,1)S(1)} %all_to_all.32.all_ref.mine_ref, bf16[4,768,128]{2,1,0:T(8,128)(2,1)S(1)} %collective-permute-done.5.other_ref), custom_call_target="tpu_custom_call" | custom-call | tf_op jit(solution)/shard_map/pallas_call | solution.py:306
  (3 shorter events, 0.1 us)
Async XLA Ops:
  3.8 55.1 %all-to-all-start = ((bf16[128,9,2,128]{3,2,1,0:T(2,128)(2,1)}), bf16[128,9,2,128]{3,2,1,0:T(2,128)(2,1)S(1)}, u32[]{:S(2)}, u32[]{:S(2)}) async-start(bf16[128,9,2,128]{3,2,1,0:T(2,128)(2,1)} %get-tuple-element.20), calls=%async_computation | async-start | bytes 1179648 | tf_op jit(solution)/shard_map/all_to_all | solution.py:321
  24.4 3.9 %collective-permute-start = (bf16[144,768]{1,0:T(8,128)(2,1)S(1)}, bf16[144,768]{1,0:T(8,128)(2,1)S(1)}, u32[]{:S(2)}, u32[]{:S(2)}) collective-permute-start(bf16[144,768]{1,0:T(8,128)(2,1)S(1)} %get-tuple-element.21), channel_id=1, source_target_pairs={{0,1},{1,0},{2,3},{3,2},{4,5},{5,4},{6,7},{7,6},{8,9},{9,8},{10,11... | collective-permute-start | bytes 663560 | tf_op jit(solution)/shard_map/ppermute | solution.py:352
  28.3 17.4 %collective-permute-start.1 = (bf16[2,144,768]{2,1,0:T(8,128)(2,1)S(1)}, bf16[2,144,768]{2,1,0:T(8,128)(2,1)S(1)}, u32[]{:S(2)}, u32[]{:S(2)}) collective-permute-start(bf16[2,144,768]{2,1,0:T(8,128)(2,1)S(1)} %pad_maximum_fusion.refs_0_.ext_ref), channel_id=1, source_target_pairs={{0,32},{32,64},{64,96},{96,0},{1,33},{33,65},{65,97},{97,1},{2,34}... | collective-permute-start | bytes 1327112 | tf_op jit(solution)/shard_map/ppermute | solution.py:349
  31.3 15.7 %collective-permute-start.2 = (bf16[2,144,768]{2,1,0:T(8,128)(2,1)S(1)}, bf16[2,144,768]{2,1,0:T(8,128)(2,1)S(1)}, u32[]{:S(2)}, u32[]{:S(2)}) collective-permute-start(bf16[2,144,768]{2,1,0:T(8,128)(2,1)S(1)} %pad_maximum_fusion.refs_0_.ext_ref), channel_id=1, source_target_pairs={{0,96},{32,0},{64,32},{96,64},{1,97},{33,1},{65,33},{97,65},{2,98}... | collective-permute-start | bytes 1327112 | tf_op jit(solution)/shard_map/ppermute | solution.py:349
  63.5 42.7 %all-to-all-start.1 = ((bf16[128,9,2,128]{3,2,1,0:T(2,128)(2,1)}), bf16[128,9,2,128]{3,2,1,0:T(2,128)(2,1)S(1)}, u32[]{:S(2)}, u32[]{:S(2)}) async-start(bf16[128,9,2,128]{3,2,1,0:T(2,128)(2,1)} %shard_map.85), calls=%async_computation.1 | async-start | bytes 1179648 | tf_op jit(solution)/shard_map/all_to_all | solution.py:321
  71.7 17.2 %collective-permute-start.3 = (bf16[2,144,768]{2,1,0:T(8,128)(2,1)S(1)}, bf16[2,144,768]{2,1,0:T(8,128)(2,1)S(1)}, u32[]{:S(2)}, u32[]{:S(2)}) collective-permute-start(bf16[2,144,768]{2,1,0:T(8,128)(2,1)S(1)} %pad_maximum_fusion.refs_0_.ext_ref), channel_id=1, source_target_pairs={{0,64},{32,96},{64,0},{96,32},{1,65},{33,97},{65,1},{97,33},{2,66}... | collective-permute-start | bytes 1327112 | tf_op jit(solution)/shard_map/ppermute | solution.py:349
  108.9 13.8 %all-to-all-start.2 = ((bf16[16,40,128]{2,1,0:T(8,128)(2,1)}), bf16[16,40,128]{2,1,0:T(8,128)(2,1)S(1)}, u32[]{:S(2)}, u32[]{:S(2)}) async-start(bf16[16,40,128]{2,1,0:T(8,128)(2,1)} %get-tuple-element.27), calls=%async_computation.2 | async-start | bytes 327680 | tf_op jit(solution)/shard_map/all_to_all | solution.py:321
  117.7 3.7 %collective-permute-start.4 = (bf16[4,96,128]{2,1,0:T(8,128)(2,1)S(1)}, bf16[4,96,128]{2,1,0:T(8,128)(2,1)S(1)}, u32[]{:S(2)}, u32[]{:S(2)}) collective-permute-start(bf16[4,96,128]{2,1,0:T(8,128)(2,1)S(1)} %get-tuple-element.29), channel_id=1, source_target_pairs={{0,1},{1,0},{2,3},{3,2},{4,5},{5,4},{6,7},{7,6},{8,9},{9,8},{10,11... | collective-permute-start | bytes 294920 | tf_op jit(solution)/shard_map/ppermute | solution.py:352
  146.6 18.2 %copy-start = (bf16[768,384]{1,0:T(8,128)(2,1)S(1)}, bf16[768,384]{1,0:T(8,128)(2,1)}, u32[]{:S(2)}) copy-start(bf16[768,384]{1,0:T(8,128)(2,1)} %ws_ref.1) | copy-start | bytes 1769476
  146.6 18.2 %copy-start.1 = (bf16[768,384]{1,0:T(8,128)(2,1)S(1)}, bf16[768,384]{1,0:T(8,128)(2,1)}, u32[]{:S(2)}) copy-start(bf16[768,384]{1,0:T(8,128)(2,1)} %wv_ref.1) | copy-start | bytes 1769476
  157.5 9.2 %collective-permute-start.5 = (bf16[4,768,128]{2,1,0:T(8,128)(2,1)S(1)}, bf16[4,768,128]{2,1,0:T(8,128)(2,1)S(1)}, u32[]{:S(2)}, u32[]{:S(2)}) collective-permute-start(bf16[4,768,128]{2,1,0:T(8,128)(2,1)S(1)} %all_to_all.32.all_ref.mine_ref), channel_id=1, source_target_pairs={{0,1},{1,0},{2,3},{3,2},{4,5},{5,4},{6,7},{7,6},{8,9},{9,8},{10,11... | collective-permute-start | bytes 2359304 | tf_op jit(solution)/shard_map/ppermute | solution.py:352

commit v10 on v9

--- a/solution.py
+++ b/solution.py
@@ -120,54 +120,65 @@
     slot = iota((ROWS // 8, LOCAL), 1) >> 4
     hidden = jnp.zeros((half, half), BF16)
     pending = None
-    for h in range(HEADS):
-        block = in_ref[h].astype(F32)
-        empty = block[:, :1] > 32768.0
-        block = jnp.where(empty & first, 0.0, block)
-        query = jnp.where(head_lanes, block * 0.125, jnp.where(bias_lane, 1.0, 0.0)).astype(BF16)
-        key = jnp.where(
-            head_lanes, block, jnp.where(bias_lane & empty, -1e30, 0.0)
-        ).astype(BF16)
-        block = block.astype(BF16)
-        shared = block[:, :HEAD]
-        value = block[:, HEAD:]
-        pair = in_ref[HEADS + h // 2]
-        cot = pair[:, :HEAD] if h % 2 == 0 else pair[:, HEAD:]
-        probs = []
-        d_scores = []
-        for rows, cols, causal in (
+    for start in range(0, HEADS, 3):
+        group = range(start, start + 3)
+        blocks, keys, queries, cots = {}, {}, {}, {}
+        for h in group:
+            block = in_ref[h].astype(F32)
+            empty = block[:, :1] > 32768.0
+            block = jnp.where(empty & first, 0.0, block)
+            query = jnp.where(head_lanes, block * 0.125, jnp.where(bias_lane, 1.0, 0.0))
+            queries[h] = query.astype(BF16)
+            keys[h] = jnp.where(
+                head_lanes, block, jnp.where(bias_lane & empty, -1e30, 0.0)
+            ).astype(BF16)
+            blocks[h] = block.astype(BF16)
+            pair = in_ref[HEADS + h // 2]
+            cots[h] = pair[:, :HEAD] if h % 2 == 0 else pair[:, HEAD:]
+        tiles = (
             (slice(0, half), slice(0, half), left_causal),
             (slice(0, ROWS), slice(half, ROWS), right_causal),
-        ):
-            scores = dot(key[rows], query[cols], ((1,), (1,)))
-            scores = jnp.where(causal, scores, -1e30)
-            weights = jnp.exp(scores - jnp.max(scores, axis=0, keepdims=True))
-            scale = 1.0 / jnp.sum(weights, axis=0, keepdims=True)
-            prob = (weights * scale).astype(BF16)
-            d_prob = dot(value[rows], cot[cols], ((1,), (1,)))
-            wide = prob.astype(F32)
-            delta = jnp.sum(wide * d_prob, axis=0, keepdims=True)
-            probs.append(prob)
-            d_scores.append((wide * (d_prob - delta)).astype(BF16))
-        probs = jnp.concatenate([jnp.concatenate([probs[0], hidden], axis=0), probs[1]], axis=1)
-        d_scores = jnp.concatenate(
-            [jnp.concatenate([d_scores[0], hidden], axis=0), d_scores[1]], axis=1
         )
-        turned = block.T
-        above = dot(turned[:HEAD], d_scores)
-        out = dot(turned[HEAD:], probs)
-        both = jnp.concatenate([above, out], axis=0).T
-        d_shared = (dot(d_scores, shared) + both[:, :HEAD]) * 0.125
-        d_value = dot(probs, cot)
-        for m, part in enumerate(spread(jnp.concatenate([d_shared, d_value], axis=1), slot)):
-            n = h * 8 + m
-            out_ref[n // 6 * 16 : (n // 6 + 1) * 16, n % 6] = part.astype(BF16).reshape(16, 2, LOCAL)
-        if h % 2 == 0:
-            pending = both
-        else:
-            k = HEADS + h // 2
-            joined = jnp.where(head_lanes, pltpu.roll(pending, HEAD, 1), both).astype(BF16)
-            out_ref[:, k] = joined.reshape(LOCAL, 2, LOCAL)
+        scores, d_probs = {}, {}
+        for h in group:
+            scores[h] = dot(keys[h], queries[h], ((1,), (1,)))
+            d_probs[h] = dot(blocks[h][:, HEAD:], cots[h], ((1,), (1,)))
+        probs, d_scores = {}, {}
+        for h in group:
+            parts = []
+            for rows, cols, causal in tiles:
+                tile = jnp.where(causal, scores[h][rows, cols], -1e30)
+                weights = jnp.exp(tile - jnp.max(tile, axis=0, keepdims=True))
+                scale = 1.0 / jnp.sum(weights, axis=0, keepdims=True)
+                parts.append((weights * scale).astype(BF16))
+            lower = [
+                (parts[n].astype(F32), d_probs[h][rows, cols])
+                for n, (rows, cols, causal) in enumerate(tiles)
+            ]
+            slopes = [
+                (wide * (d_prob - jnp.sum(wide * d_prob, axis=0, keepdims=True))).astype(BF16)
+                for wide, d_prob in lower
+            ]
+            for held, done in ((probs, parts), (d_scores, slopes)):
+                left = jnp.concatenate([done[0], hidden], axis=0)
+                held[h] = jnp.concatenate([left, done[1]], axis=1)
+        for h in group:
+            turned = blocks[h].T
+            above = dot(turned[:HEAD], d_scores[h])
+            above = above + dot(turned[:HEAD], d_scores[h], ((1,), (1,)))
+            out = dot(turned[HEAD:], probs[h])
+            d_value = dot(cots[h].T, probs[h], ((1,), (1,)))
+            grads = jnp.concatenate([above * 0.125, d_value], axis=0).T
+            for m, part in enumerate(spread(grads, slot)):
+                n = h * 8 + m
+                part = part.astype(BF16).reshape(16, 2, LOCAL)
+                out_ref[n // 6 * 16 : (n // 6 + 1) * 16, n % 6] = part
+            if h % 2 == 0:
+                pending = out
+            else:
+                k = HEADS + h // 2
+                joined = jnp.concatenate([pending, out], axis=0).T.astype(BF16)
+                out_ref[:, k] = joined.reshape(LOCAL, 2, LOCAL)
 
 
 def index_of(place_ref, dy, dc):
@@ -186,8 +197,8 @@
         for i in range(2):
             lanes = pl.ds(pl.multiple_of(head[i] * LOCAL, LOCAL), LOCAL)
             dests[i, source] = exts[n // 2][n % 2, LOCAL:, lanes].astype(F32)[:8]
-    turned = [in_ref[:, b].reshape(ROWS, LOCAL).astype(F32) for b in range(6)]
-    turned = [pltpu.roll(rows, BLOCK * b, 1) if b else rows for b, rows in enumerate(turned)]
+    turned = [in_ref[:, b].reshape(ROWS, LOCAL) for b in range(6)]
+    turned = [pltpu.roll(rows.astype(F32), BLOCK * b, 1).astype(BF16) if b else rows for b, rows in enumerate(turned)]
     limit = lax.rem(j, 4)
     limit = jnp.where(limit == 1, 2, jnp.where(limit == 2, 4, 6))
     for p in range(8):
@@ -195,16 +206,17 @@
         for b in range(1, 6):
             rows = jnp.where(lane_slot == (b + p) % 8, turned[b], rows)
         routes = [(sub_rows == dests[i, p, :1]).astype(BF16) for i in range(2)]
-        found = dot(rows.astype(BF16), jnp.concatenate(routes, axis=1), ((0,), (0,)))
+        found = dot(rows, jnp.concatenate(routes, axis=1), ((0,), (0,)))
         blocks = []
         for b in range(6):
             cut = slice((b + p) % 8 * BLOCK, ((b + p) % 8 + 1) * BLOCK)
             blocks.append(jnp.where(b < limit, found[cut, :LOCAL], found[cut, LOCAL:]))
         cols[p] = jnp.concatenate(blocks, axis=0).astype(BF16)
     total = None
-    for n, (dy, dc) in enumerate(STEPS):
-        source = index_of(place_ref, 4 - dy, dc)
-        term = dot(cols[source], exts[n // 2][n % 2, :LOCAL, :])
+    for dy in range(4):
+        near = [cols[index_of(place_ref, 4 - dy, dc)] for dc in range(2)]
+        rows = exts[dy][:, :LOCAL, :].reshape(2 * LOCAL, WIDTH)
+        term = dot(jnp.concatenate(near, axis=1), rows)
         total = term if total is None else total + term
     for k in range(WIDTH // LOCAL):
         scratch[k * COLUMNS : (k + 1) * COLUMNS, :] = total[:, k * LOCAL : (k + 1) * LOCAL]

time: 169 us -> 168 us (level)
  no operation moved by 1% of the time
where the time goes in v10:
time: 168 us; the launch traced here: 167 us
  starting transfers between devices  62 us (37%)
  waiting for transfers between devices  55.8 us (33%)
  blocking collectives  34.7 us (21%)
  Pallas kernels  13.3 us (8%)
    all_to_all x3, starting transfers between devices, swap(): lax.all_to_all(rows, axes, split_axis=0, concat_axis=0, tiled=True, axis_...  37.6 us
    all_to_all x3, blocking collectives, swap(): lax.all_to_all(rows, axes, split_axis=0, concat_axis=0, tiled=True, axis_...  34.7 us
    all_to_all x3, waiting for transfers between devices, swap(): lax.all_to_all(rows, axes, split_axis=0, concat_axis=0, tiled=True, axis_...  30.5 us
    ppermute x3, waiting for transfers between devices, shift(): return lax.ppermute(pair, 'y', [(y, (y + dy) % 4) for y in range(4)])  24.1 us
    pallas_call x9, Pallas kernels, call(): pl.pallas_call(kernel, out_shape=out, in_specs=specs, out_specs=outs, scr...  13.3 us
    ppermute x3, starting transfers between devices, flip(): return lax.ppermute(part, 'c', [(0, 1), (1, 0)])  12.7 us
    ppermute x3, starting transfers between devices, shift(): return lax.ppermute(pair, 'y', [(y, (y + dy) % 4) for y in range(4)])  11.7 us
  transfers between devices with their start and end apart: 9, of which 8 were waited for; matrix products, arithmetic and copies ran while one was open for 0% of the time, Pallas kernels for 2%

profile of v10, /device:TPU:1, one launch (start us, length us, event | category | flops | bytes accessed | tf_op | source)
XLA Modules:
  0.0 167.2 jit_solution(10247114197063852413)
XLA Ops:
  0.6 3.2 %shard_map.84 = (bf16[128,9,2,128]{3,2,1,0:T(2,128)(2,1)}, bf16[144,768]{1,0:T(8,128)(2,1)S(1)}) custom-call(s32[6,1,128]{2,1,0:T(1,128)} %bitcast.19, bf16[128,768]{1,0:T(8,128)(2,1)} %bitcast.15, bf16[768,384]{1,0:T(8,128)(2,1)} %ws_ref.1, bf16[768,384]{1,0:T(8,128)(2,1)} %wv_ref.1, bf16[128,384]{1,0:T(8,128)(2,1)} %bitcast.17), custom_call_target="tpu_custom_call" | custom-call | tf_op jit(solution)/shard_map/pallas_call | solution.py:318
  3.8 20.6 %all-to-all-start = ((bf16[128,9,2,128]{3,2,1,0:T(2,128)(2,1)}), bf16[128,9,2,128]{3,2,1,0:T(2,128)(2,1)S(1)}, u32[]{:S(2)}, u32[]{:S(2)}) async-start(bf16[128,9,2,128]{3,2,1,0:T(2,128)(2,1)} %get-tuple-element.20), calls=%async_computation | async-start | bytes 1179648 | tf_op jit(solution)/shard_map/all_to_all | solution.py:333
  24.4 2.8 %collective-permute-start = (bf16[144,768]{1,0:T(8,128)(2,1)S(1)}, bf16[144,768]{1,0:T(8,128)(2,1)S(1)}, u32[]{:S(2)}, u32[]{:S(2)}) collective-permute-start(bf16[144,768]{1,0:T(8,128)(2,1)S(1)} %get-tuple-element.21), channel_id=1, source_target_pairs={{0,1},{1,0},{2,3},{3,2},{4,5},{5,4},{6,7},{7,6},{8,9},{9,8},{10,11... | collective-permute-start | bytes 663560 | tf_op jit(solution)/shard_map/ppermute | solution.py:364
  27.2 1.1 collective-permute-done
  28.3 2.9 %collective-permute-start.1 = (bf16[2,144,768]{2,1,0:T(8,128)(2,1)S(1)}, bf16[2,144,768]{2,1,0:T(8,128)(2,1)S(1)}, u32[]{:S(2)}, u32[]{:S(2)}) collective-permute-start(bf16[2,144,768]{2,1,0:T(8,128)(2,1)S(1)} %pad_maximum_fusion.refs_0_.ext_ref), channel_id=1, source_target_pairs={{0,32},{32,64},{64,96},{96,0},{1,33},{33,65},{65,97},{97,1},{2,34}... | collective-permute-start | bytes 1327112 | tf_op jit(solution)/shard_map/ppermute | solution.py:361
  31.3 3.6 %collective-permute-start.2 = (bf16[2,144,768]{2,1,0:T(8,128)(2,1)S(1)}, bf16[2,144,768]{2,1,0:T(8,128)(2,1)S(1)}, u32[]{:S(2)}, u32[]{:S(2)}) collective-permute-start(bf16[2,144,768]{2,1,0:T(8,128)(2,1)S(1)} %pad_maximum_fusion.refs_0_.ext_ref), channel_id=1, source_target_pairs={{0,96},{32,0},{64,32},{96,64},{1,97},{33,1},{65,33},{97,65},{2,98}... | collective-permute-start | bytes 1327112 | tf_op jit(solution)/shard_map/ppermute | solution.py:361
  34.9 0.1 pad_add_fusion.place_ref
  35.0 10.8 %collective-permute-done.1.refs_1_ = bf16[2,144,768]{2,1,0:T(8,128)(2,1)S(1)} collective-permute-done((bf16[2,144,768]{2,1,0:T(8,128)(2,1)S(1)}, bf16[2,144,768]{2,1,0:T(8,128)(2,1)S(1)}, u32[]{:S(2)}, u32[]{:S(2)}) %collective-permute-start.1) | collective-permute-done | bytes 442400 | tf_op jit(solution)/shard_map/ppermute | solution.py:361
  45.7 1.3 collective-permute-done.2.refs_3_
  47.0 11.9 %all-to-all-done = bf16[128,9,2,128]{3,2,1,0:T(2,128)(2,1)S(1)} async-done(((bf16[128,9,2,128]{3,2,1,0:T(2,128)(2,1)}), bf16[128,9,2,128]{3,2,1,0:T(2,128)(2,1)S(1)}, u32[]{:S(2)}, u32[]{:S(2)}) %all-to-all-start) | async-done | bytes 589856 | tf_op jit(solution)/shard_map/all_to_all | solution.py:333
  58.9 0.5 copy.9
  59.4 3.2 %shard_map.85 = bf16[128,9,2,128]{3,2,1,0:T(2,128)(2,1)} custom-call(bf16[9,256,128]{2,1,0:T(8,128)(2,1)S(1)} %bitcast.11), custom_call_target="tpu_custom_call" | custom-call | tf_op jit(solution)/shard_map/pallas_call | solution.py:318
  62.6 8.2 %all-to-all-start.1 = ((bf16[128,9,2,128]{3,2,1,0:T(2,128)(2,1)}), bf16[128,9,2,128]{3,2,1,0:T(2,128)(2,1)S(1)}, u32[]{:S(2)}, u32[]{:S(2)}) async-start(bf16[128,9,2,128]{3,2,1,0:T(2,128)(2,1)} %shard_map.85), calls=%async_computation.1 | async-start | bytes 1179648 | tf_op jit(solution)/shard_map/all_to_all | solution.py:333
  70.8 5.2 %collective-permute-start.3 = (bf16[2,144,768]{2,1,0:T(8,128)(2,1)S(1)}, bf16[2,144,768]{2,1,0:T(8,128)(2,1)S(1)}, u32[]{:S(2)}, u32[]{:S(2)}) collective-permute-start(bf16[2,144,768]{2,1,0:T(8,128)(2,1)S(1)} %pad_maximum_fusion.refs_0_.ext_ref), channel_id=1, source_target_pairs={{0,64},{32,96},{64,0},{96,32},{1,65},{33,97},{65,1},{97,33},{2,66}... | collective-permute-start | bytes 1327112 | tf_op jit(solution)/shard_map/ppermute | solution.py:361
  76.0 12.1 %collective-permute-done.3.refs_2_ = bf16[2,144,768]{2,1,0:T(8,128)(2,1)S(1)} collective-permute-done((bf16[2,144,768]{2,1,0:T(8,128)(2,1)S(1)}, bf16[2,144,768]{2,1,0:T(8,128)(2,1)S(1)}, u32[]{:S(2)}, u32[]{:S(2)}) %collective-permute-start.3) | collective-permute-done | bytes 442400 | tf_op jit(solution)/shard_map/ppermute | solution.py:361
  88.0 17.3 %all-to-all-done.1.in_ref = bf16[128,9,2,128]{3,2,1,0:T(2,128)(2,1)S(1)} async-done(((bf16[128,9,2,128]{3,2,1,0:T(2,128)(2,1)}), bf16[128,9,2,128]{3,2,1,0:T(2,128)(2,1)S(1)}, u32[]{:S(2)}, u32[]{:S(2)}) %all-to-all-start.1) | async-done | bytes 589856 | tf_op jit(solution)/shard_map/all_to_all | solution.py:333
  105.3 2.3 %shard_map.86 = (bf16[16,40,128]{2,1,0:T(8,128)(2,1)}, bf16[4,96,128]{2,1,0:T(8,128)(2,1)S(1)}, bf16[4,96,128]{2,1,0:T(8,128)(2,1)S(1)}) custom-call(s32[2]{0:T(128)S(1)} %pad_add_fusion.place_ref, bf16[128,9,2,128]{3,2,1,0:T(2,128)(2,1)S(1)} %all-to-all-done.1.in_ref, bf16[2,144,768]{2,1,0:T(8,128)(2,1)S(1)} %pad_maximum_fusion.refs_0_.ext_ref, ...), custom_call_target="tpu_custom_call" | custom-call | tf_op jit(solution)/shard_map/pallas_call | solution.py:318
  107.7 8.8 %all-to-all-start.2 = ((bf16[16,40,128]{2,1,0:T(8,128)(2,1)}), bf16[16,40,128]{2,1,0:T(8,128)(2,1)S(1)}, u32[]{:S(2)}, u32[]{:S(2)}) async-start(bf16[16,40,128]{2,1,0:T(8,128)(2,1)} %get-tuple-element.27), calls=%async_computation.2 | async-start | bytes 327680 | tf_op jit(solution)/shard_map/all_to_all | solution.py:333
  116.5 2.7 %collective-permute-start.4 = (bf16[4,96,128]{2,1,0:T(8,128)(2,1)S(1)}, bf16[4,96,128]{2,1,0:T(8,128)(2,1)S(1)}, u32[]{:S(2)}, u32[]{:S(2)}) collective-permute-start(bf16[4,96,128]{2,1,0:T(8,128)(2,1)S(1)} %get-tuple-element.29), channel_id=1, source_target_pairs={{0,1},{1,0},{2,3},{3,2},{4,5},{5,4},{6,7},{7,6},{8,9},{9,8},{10,11... | collective-permute-start | bytes 294920 | tf_op jit(solution)/shard_map/ppermute | solution.py:364
  119.2 1.0 shard_map.87
  120.2 0.0 collective-permute-done.4.got_ref
  120.2 1.2 all-to-all-done.2.in_ref
  121.5 12.6 %all_to_all.30.in_ref = bf16[4,40,128]{2,1,0:T(8,128)(2,1)S(1)} all-to-all(bf16[4,40,128]{2,1,0:T(8,128)(2,1)S(1)} %shard_map.88), channel_id=1, replica_groups={{6,8,18,28},{4,14,16,26},{2,12,22,24},{0,10,20,30},{7,9,19,29},{5,15,17..., dimensions={0} | all-to-all | bytes 81920 | tf_op jit(solution)/shard_map/all_to_all | solution.py:333
  134.1 11.1 %all_to_all.31.block_ref = bf16[16,40,128]{2,1,0:T(8,128)(2,1)S(1)} all-to-all(bf16[16,40,128]{2,1,0:T(8,128)(2,1)S(1)} %shard_map.89), channel_id=1, replica_groups={{6,4,2,0,134,132,130,128,262,260,258,256,390,388,386,384},{8,14,12,10,1..., dimensions={0} | all-to-all | bytes 327680 | tf_op jit(solution)/shard_map/all_to_all | solution.py:333
  145.2 0.1 shard_map.90
  145.3 0.0 copy-start
  145.3 0.0 copy-start.1
  145.3 11.0 %all_to_all.32.all_ref.mine_ref = bf16[4,768,128]{2,1,0:T(8,128)(2,1)S(1)} all-to-all(bf16[4,768,128]{2,1,0:T(8,128)(2,1)S(1)} %shard_map.90), channel_id=1, replica_groups=mesh['x'=4,'y'=4,'z'=16,'c'=2] {'y'}, dimensions={0} | all-to-all | bytes 1572864 | tf_op jit(solution)/shard_map/all_to_all | solution.py:333
  156.3 7.2 %collective-permute-start.5 = (bf16[4,768,128]{2,1,0:T(8,128)(2,1)S(1)}, bf16[4,768,128]{2,1,0:T(8,128)(2,1)S(1)}, u32[]{:S(2)}, u32[]{:S(2)}) collective-permute-start(bf16[4,768,128]{2,1,0:T(8,128)(2,1)S(1)} %all_to_all.32.all_ref.mine_ref), channel_id=1, source_target_pairs={{0,1},{1,0},{2,3},{3,2},{4,5},{5,4},{6,7},{7,6},{8,9},{9,8},{10,11... | collective-permute-start | bytes 2359304 | tf_op jit(solution)/shard_map/ppermute | solution.py:364
  163.6 0.0 copy-done
  163.6 0.0 copy-done.1
  163.6 1.8 %shard_map.91 = bf16[128,768]{1,0:T(8,128)(2,1)} custom-call(s32[2]{0:T(128)S(1)} %pad_add_fusion.place_ref, bf16[4,768,128]{2,1,0:T(8,128)(2,1)S(1)} %all_to_all.32.all_ref.mine_ref, bf16[768,384]{1,0:T(8,128)(2,1)S(1)} %copy-done, bf16[768,384]{1,0:T(8,128)(2,1)S(1)} %copy-done.1), custom_call_target="tpu_custom_call" | custom-call | tf_op jit(solution)/shard_map/pallas_call | solution.py:318
  165.3 0.1 collective-permute-done.5.other_ref
  165.4 1.7 %shard_map.92 = (bf16[768,384]{1,0:T(8,128)(2,1)}, bf16[768,384]{1,0:T(8,128)(2,1)}) custom-call(s32[2]{0:T(128)S(1)} %pad_add_fusion.place_ref, bf16[4,768,128]{2,1,0:T(8,128)(2,1)S(1)} %all_to_all.32.all_ref.mine_ref, bf16[4,768,128]{2,1,0:T(8,128)(2,1)S(1)} %collective-permute-done.5.other_ref), custom_call_target="tpu_custom_call" | custom-call | tf_op jit(solution)/shard_map/pallas_call | solution.py:318
  (3 shorter events, 0.1 us)
Async XLA Ops:
  3.8 55.1 %all-to-all-start = ((bf16[128,9,2,128]{3,2,1,0:T(2,128)(2,1)}), bf16[128,9,2,128]{3,2,1,0:T(2,128)(2,1)S(1)}, u32[]{:S(2)}, u32[]{:S(2)}) async-start(bf16[128,9,2,128]{3,2,1,0:T(2,128)(2,1)} %get-tuple-element.20), calls=%async_computation | async-start | bytes 1179648 | tf_op jit(solution)/shard_map/all_to_all | solution.py:333
  24.4 3.9 %collective-permute-start = (bf16[144,768]{1,0:T(8,128)(2,1)S(1)}, bf16[144,768]{1,0:T(8,128)(2,1)S(1)}, u32[]{:S(2)}, u32[]{:S(2)}) collective-permute-start(bf16[144,768]{1,0:T(8,128)(2,1)S(1)} %get-tuple-element.21), channel_id=1, source_target_pairs={{0,1},{1,0},{2,3},{3,2},{4,5},{5,4},{6,7},{7,6},{8,9},{9,8},{10,11... | collective-permute-start | bytes 663560 | tf_op jit(solution)/shard_map/ppermute | solution.py:364
  28.3 17.4 %collective-permute-start.1 = (bf16[2,144,768]{2,1,0:T(8,128)(2,1)S(1)}, bf16[2,144,768]{2,1,0:T(8,128)(2,1)S(1)}, u32[]{:S(2)}, u32[]{:S(2)}) collective-permute-start(bf16[2,144,768]{2,1,0:T(8,128)(2,1)S(1)} %pad_maximum_fusion.refs_0_.ext_ref), channel_id=1, source_target_pairs={{0,32},{32,64},{64,96},{96,0},{1,33},{33,65},{65,97},{97,1},{2,34}... | collective-permute-start | bytes 1327112 | tf_op jit(solution)/shard_map/ppermute | solution.py:361
  31.3 15.7 %collective-permute-start.2 = (bf16[2,144,768]{2,1,0:T(8,128)(2,1)S(1)}, bf16[2,144,768]{2,1,0:T(8,128)(2,1)S(1)}, u32[]{:S(2)}, u32[]{:S(2)}) collective-permute-start(bf16[2,144,768]{2,1,0:T(8,128)(2,1)S(1)} %pad_maximum_fusion.refs_0_.ext_ref), channel_id=1, source_target_pairs={{0,96},{32,0},{64,32},{96,64},{1,97},{33,1},{65,33},{97,65},{2,98}... | collective-permute-start | bytes 1327112 | tf_op jit(solution)/shard_map/ppermute | solution.py:361
  62.6 42.7 %all-to-all-start.1 = ((bf16[128,9,2,128]{3,2,1,0:T(2,128)(2,1)}), bf16[128,9,2,128]{3,2,1,0:T(2,128)(2,1)S(1)}, u32[]{:S(2)}, u32[]{:S(2)}) async-start(bf16[128,9,2,128]{3,2,1,0:T(2,128)(2,1)} %shard_map.85), calls=%async_computation.1 | async-start | bytes 1179648 | tf_op jit(solution)/shard_map/all_to_all | solution.py:333
  70.8 17.2 %collective-permute-start.3 = (bf16[2,144,768]{2,1,0:T(8,128)(2,1)S(1)}, bf16[2,144,768]{2,1,0:T(8,128)(2,1)S(1)}, u32[]{:S(2)}, u32[]{:S(2)}) collective-permute-start(bf16[2,144,768]{2,1,0:T(8,128)(2,1)S(1)} %pad_maximum_fusion.refs_0_.ext_ref), channel_id=1, source_target_pairs={{0,64},{32,96},{64,0},{96,32},{1,65},{33,97},{65,1},{97,33},{2,66}... | collective-permute-start | bytes 1327112 | tf_op jit(solution)/shard_map/ppermute | solution.py:361
  107.7 13.8 %all-to-all-start.2 = ((bf16[16,40,128]{2,1,0:T(8,128)(2,1)}), bf16[16,40,128]{2,1,0:T(8,128)(2,1)S(1)}, u32[]{:S(2)}, u32[]{:S(2)}) async-start(bf16[16,40,128]{2,1,0:T(8,128)(2,1)} %get-tuple-element.27), calls=%async_computation.2 | async-start | bytes 327680 | tf_op jit(solution)/shard_map/all_to_all | solution.py:333
  116.5 3.7 %collective-permute-start.4 = (bf16[4,96,128]{2,1,0:T(8,128)(2,1)S(1)}, bf16[4,96,128]{2,1,0:T(8,128)(2,1)S(1)}, u32[]{:S(2)}, u32[]{:S(2)}) collective-permute-start(bf16[4,96,128]{2,1,0:T(8,128)(2,1)S(1)} %get-tuple-element.29), channel_id=1, source_target_pairs={{0,1},{1,0},{2,3},{3,2},{4,5},{5,4},{6,7},{7,6},{8,9},{9,8},{10,11... | collective-permute-start | bytes 294920 | tf_op jit(solution)/shard_map/ppermute | solution.py:364
  145.3 18.2 %copy-start = (bf16[768,384]{1,0:T(8,128)(2,1)S(1)}, bf16[768,384]{1,0:T(8,128)(2,1)}, u32[]{:S(2)}) copy-start(bf16[768,384]{1,0:T(8,128)(2,1)} %ws_ref.1) | copy-start | bytes 1769476
  145.3 18.2 %copy-start.1 = (bf16[768,384]{1,0:T(8,128)(2,1)S(1)}, bf16[768,384]{1,0:T(8,128)(2,1)}, u32[]{:S(2)}) copy-start(bf16[768,384]{1,0:T(8,128)(2,1)} %wv_ref.1) | copy-start | bytes 1769476
  156.3 9.1 %collective-permute-start.5 = (bf16[4,768,128]{2,1,0:T(8,128)(2,1)S(1)}, bf16[4,768,128]{2,1,0:T(8,128)(2,1)S(1)}, u32[]{:S(2)}, u32[]{:S(2)}) collective-permute-start(bf16[4,768,128]{2,1,0:T(8,128)(2,1)S(1)} %all_to_all.32.all_ref.mine_ref), channel_id=1, source_target_pairs={{0,1},{1,0},{2,3},{3,2},{4,5},{5,4},{6,7},{7,6},{8,9},{9,8},{10,11... | collective-permute-start | bytes 2359304 | tf_op jit(solution)/shard_map/ppermute | solution.py:364

commit v11 on v10

--- a/solution.py
+++ b/solution.py
@@ -20,6 +20,7 @@
 OWNERS = ("y", "c", "z")
 RING = [(3, 4, 9, 14), (2, 7, 8, 13), (1, 6, 11, 12), (0, 5, 10, 15)]
 FAR = [list(group) for group in RING]
+QUARTER = [[group[b] for group in RING] for b in range(4)]
 NEAR = [[x * 16 + RING[n][b] for x in range(4) for n in range(4)] for b in range(4)]
 STEPS = [(dy, dc) for dy in range(4) for dc in range(2)]
 COLUMNS = 96
@@ -27,7 +28,6 @@
 SLOT = 40
 BLOCK = 16
 WHOLE = 576
-MESSAGE = 96
 
 
 def iota(shape, dim):
@@ -223,9 +223,9 @@
     scratch[16 * PIECE :, :] = jnp.zeros((8, LOCAL), F32)
     for i in range(16):
         out_ref[i] = scratch[i * PIECE : i * PIECE + SLOT, :].astype(BF16)
-    for y in range(4):
-        keep_ref[y] = cols[y * 2 + here]
-        give_ref[y] = cols[y * 2 + 1 - here]
+    for dy in range(4):
+        keep_ref[dy] = cols[index_of(place_ref, dy, 0)]
+        give_ref[dy] = cols[index_of(place_ref, dy, 1)]
 
 
 def output_kernel(in_ref, ext_ref, att_ref):
@@ -242,21 +242,25 @@
         att_ref[:, k * LOCAL : (k + 1) * LOCAL] = both.astype(BF16)
 
 
-def pack_kernel(block_ref, keep_ref, got_ref, out_ref, scratch):
+def message_kernel(keep_ref, got_ref, *outs):
+    for dy, out_ref in enumerate(outs):
+        out_ref[0] = keep_ref[dy]
+        out_ref[1] = got_ref[dy]
+
+
+def repeat_kernel(in_ref, out_ref, scratch):
+    for i in range(4):
+        scratch[i * PIECE : (i + 1) * PIECE, :] = in_ref[i].astype(F32)[:PIECE]
+    block = scratch[...].astype(BF16)
     for i in range(16):
-        scratch[i * PIECE : (i + 1) * PIECE, :] = block_ref[i].astype(F32)[:PIECE]
-    block = scratch[...].astype(BF16)
-    for y in range(4):
-        out_ref[y, :WHOLE, :] = block
-        out_ref[y, WHOLE : WHOLE + MESSAGE, :] = keep_ref[y]
-        out_ref[y, WHOLE + MESSAGE :, :] = got_ref[y]
-
-
-def return_kernel(place_ref, all_ref, ws_ref, wv_ref, grad_ref, held):
-    here = place_ref[1]
-    for y in range(4):
-        held[y * 2 + here] = all_ref[y, WHOLE : WHOLE + MESSAGE, :]
-        held[y * 2 + 1 - here] = all_ref[y, WHOLE + MESSAGE :, :]
+        out_ref[i] = block
+
+
+def return_kernel(place_ref, *refs):
+    parts, (ws_ref, wv_ref, grad_ref, held) = refs[:4], refs[4:]
+    for dy in range(4):
+        for dc in range(2):
+            held[index_of(place_ref, 4 - dy, dc)] = parts[dy][dc]
 
     def columns(first):
         rows = [
@@ -377,7 +381,7 @@
     back = swap(worked, OWNERS)
     part, keep, give = call(
         partial_kernel,
-        [shape(16, SLOT, LOCAL), shape(4, MESSAGE, LOCAL), shape(4, MESSAGE, LOCAL)],
+        [shape(16, SLOT, LOCAL), shape(4, COLUMNS, LOCAL), shape(4, COLUMNS, LOCAL)],
         place,
         back,
         *exts,
@@ -391,28 +395,33 @@
     (attention,) = call(output_kernel, [shape(LOCAL, PROJ)], back, pair)
     part = swap(part, ("x", "z"), NEAR)
     part, keep, got, attention = lax.optimization_barrier((part, keep, flip(give), attention))
+    parts = call(message_kernel, [shape(2, COLUMNS, LOCAL)] * 4, keep, got)
     (part,) = call(sum_kernel, [shape(4, SLOT, LOCAL)], part)
-    (block,) = call(sum_kernel, [shape(16, SLOT, LOCAL)], swap(part, "z", FAR))
+    part, parts = lax.optimization_barrier((part, parts))
+    moved = [shift(parts[dy], dy) for dy in range(1, 4)]
+    part, moved = lax.optimization_barrier((swap(part, "z", FAR), moved))
+    (block,) = call(sum_kernel, [shape(4, SLOT, LOCAL)], part)
     (block,) = call(
-        pack_kernel,
-        [shape(4, WHOLE + 2 * MESSAGE, LOCAL)],
-        swap(block, ("x", "z"), NEAR),
-        keep,
-        got,
-        scratch=[pltpu.VMEM((WHOLE, LOCAL), F32)],
-    )
-    block = swap(block, "y")
-    other = flip(block)
+        repeat_kernel,
+        [shape(16, 4 * PIECE, LOCAL)],
+        swap(block, "z", QUARTER),
+        scratch=[pltpu.VMEM((4 * PIECE, LOCAL), F32)],
+    )
     (grad_tokens,) = call(
         return_kernel,
         [shape(LOCAL, WIDTH)],
         place,
-        block,
+        parts[0],
+        *moved,
         w_shared,
         w_value,
-        scratch=[pltpu.VMEM((8, MESSAGE, LOCAL), BF16)],
+        scratch=[pltpu.VMEM((8, COLUMNS, LOCAL), BF16)],
         scalars=1,
     )
+    block = swap(block, ("y", "x"))
+    block, grad_tokens = lax.optimization_barrier((block, grad_tokens))
+    block = block.reshape(4, WHOLE, LOCAL)
+    other = flip(block)
     grad_shared, grad_value = call(
         finish_kernel,
         (shape(WIDTH, PROJ), shape(WIDTH, PROJ)),

time: 168 us -> 170 us (1.012)
  blocking collectives: 34.7 us -> 7.19 us
  starting transfers between devices: 62 us -> 79.7 us
  waiting for transfers between devices: 55.8 us -> 66.1 us
    all_to_all x3 -> x1, blocking collectives: 34.7 us -> 7.19 us  [swap(): lax.all_to_all(rows, axes, split_axis=0, concat_axis=0, tiled=True, axis_...]
    ppermute x3 -> x6, starting transfers between devices: 11.7 us -> 21.9 us  [shift(): return lax.ppermute(pair, 'y', [(y, (y + dy) % 4) for y in range(4)])]
    all_to_all x3 -> x5, starting transfers between devices: 37.6 us -> 45.7 us  [swap(): lax.all_to_all(rows, axes, split_axis=0, concat_axis=0, tiled=True, axis_...]
    all_to_all x3 -> x5, waiting for transfers between devices: 30.5 us -> 38 us  [swap(): lax.all_to_all(rows, axes, split_axis=0, concat_axis=0, tiled=True, axis_...]
    pallas_call x9 -> x10, Pallas kernels: 13.3 us -> 14.7 us  [call(): pl.pallas_call(kernel, out_shape=out, in_specs=specs, out_specs=outs, scr...]
    ppermute x3 -> x6, waiting for transfers between devices: 24.1 us -> 25.4 us  [shift(): return lax.ppermute(pair, 'y', [(y, (y + dy) % 4) for y in range(4)])]
  transfers between devices with their start and end apart: 9 -> 14, of which waited for: 8 -> 10; matrix products, arithmetic and copies ran while one was open for 0% -> 0% of each run, Pallas kernels for 2% -> 2%
where the time goes in v11:
time: 170 us; the launch traced here: 169 us
  starting transfers between devices  79.7 us (47%)
  waiting for transfers between devices  66.1 us (39%)
  Pallas kernels  14.7 us (9%)
  blocking collectives  7.19 us (4%)
    all_to_all x5, starting transfers between devices, swap(): lax.all_to_all(rows, axes, split_axis=0, concat_axis=0, tiled=True, axis_...  45.7 us
    all_to_all x5, waiting for transfers between devices, swap(): lax.all_to_all(rows, axes, split_axis=0, concat_axis=0, tiled=True, axis_...  38 us
    ppermute x6, waiting for transfers between devices, shift(): return lax.ppermute(pair, 'y', [(y, (y + dy) % 4) for y in range(4)])  25.4 us
    ppermute x6, starting transfers between devices, shift(): return lax.ppermute(pair, 'y', [(y, (y + dy) % 4) for y in range(4)])  21.9 us
    pallas_call x10, Pallas kernels, call(): pl.pallas_call(kernel, out_shape=out, in_specs=specs, out_specs=outs, scr...  14.7 us
    ppermute x3, starting transfers between devices, flip(): return lax.ppermute(part, 'c', [(0, 1), (1, 0)])  12 us
    all_to_all x1, blocking collectives, swap(): lax.all_to_all(rows, axes, split_axis=0, concat_axis=0, tiled=True, axis_...  7.19 us
  transfers between devices with their start and end apart: 14, of which 10 were waited for; matrix products, arithmetic and copies ran while one was open for 0% of the time, Pallas kernels for 2%

profile of v11, /device:TPU:1, one launch (start us, length us, event | category | flops | bytes accessed | tf_op | source)
XLA Modules:
  0.0 169.1 jit_solution(7022160906461730127)
XLA Ops:
  0.6 3.2 %shard_map.84 = (bf16[128,9,2,128]{3,2,1,0:T(2,128)(2,1)}, bf16[144,768]{1,0:T(8,128)(2,1)S(1)}) custom-call(s32[6,1,128]{2,1,0:T(1,128)} %bitcast.22, bf16[128,768]{1,0:T(8,128)(2,1)} %bitcast.18, bf16[768,384]{1,0:T(8,128)(2,1)} %refs_4_.1, bf16[768,384]{1,0:T(8,128)(2,1)} %refs_5_.1, bf16[128,384]{1,0:T(8,128)(2,1)} %bitcast.20), custom_call_target="tpu_custom_call" | custom-call | tf_op jit(solution)/shard_map/pallas_call | solution.py:322
  3.8 20.6 %all-to-all-start = ((bf16[128,9,2,128]{3,2,1,0:T(2,128)(2,1)}), bf16[128,9,2,128]{3,2,1,0:T(2,128)(2,1)S(1)}, u32[]{:S(2)}, u32[]{:S(2)}) async-start(bf16[128,9,2,128]{3,2,1,0:T(2,128)(2,1)} %get-tuple-element.35), calls=%async_computation | async-start | bytes 1179648 | tf_op jit(solution)/shard_map/all_to_all | solution.py:337
  24.4 2.8 %collective-permute-start = (bf16[144,768]{1,0:T(8,128)(2,1)S(1)}, bf16[144,768]{1,0:T(8,128)(2,1)S(1)}, u32[]{:S(2)}, u32[]{:S(2)}) collective-permute-start(bf16[144,768]{1,0:T(8,128)(2,1)S(1)} %get-tuple-element.36), channel_id=1, source_target_pairs={{0,1},{1,0},{2,3},{3,2},{4,5},{5,4},{6,7},{7,6},{8,9},{9,8},{10,11... | collective-permute-start | bytes 663560 | tf_op jit(solution)/shard_map/ppermute | solution.py:368
  27.2 1.1 collective-permute-done
  28.3 2.9 %collective-permute-start.1 = (bf16[2,144,768]{2,1,0:T(8,128)(2,1)S(1)}, bf16[2,144,768]{2,1,0:T(8,128)(2,1)S(1)}, u32[]{:S(2)}, u32[]{:S(2)}) collective-permute-start(bf16[2,144,768]{2,1,0:T(8,128)(2,1)S(1)} %pad_maximum_fusion.refs_0_.ext_ref), channel_id=1, source_target_pairs={{0,32},{32,64},{64,96},{96,0},{1,33},{33,65},{65,97},{97,1},{2,34}... | collective-permute-start | bytes 1327112 | tf_op jit(solution)/shard_map/ppermute | solution.py:365
  31.3 3.6 %collective-permute-start.2 = (bf16[2,144,768]{2,1,0:T(8,128)(2,1)S(1)}, bf16[2,144,768]{2,1,0:T(8,128)(2,1)S(1)}, u32[]{:S(2)}, u32[]{:S(2)}) collective-permute-start(bf16[2,144,768]{2,1,0:T(8,128)(2,1)S(1)} %pad_maximum_fusion.refs_0_.ext_ref), channel_id=1, source_target_pairs={{0,96},{32,0},{64,32},{96,64},{1,97},{33,1},{65,33},{97,65},{2,98}... | collective-permute-start | bytes 1327112 | tf_op jit(solution)/shard_map/ppermute | solution.py:365
  34.9 0.1 pad_add_fusion.place_ref
  35.0 10.8 %collective-permute-done.1.refs_1_ = bf16[2,144,768]{2,1,0:T(8,128)(2,1)S(1)} collective-permute-done((bf16[2,144,768]{2,1,0:T(8,128)(2,1)S(1)}, bf16[2,144,768]{2,1,0:T(8,128)(2,1)S(1)}, u32[]{:S(2)}, u32[]{:S(2)}) %collective-permute-start.1) | collective-permute-done | bytes 442400 | tf_op jit(solution)/shard_map/ppermute | solution.py:365
  45.7 1.3 collective-permute-done.2.refs_3_
  47.0 11.9 %all-to-all-done = bf16[128,9,2,128]{3,2,1,0:T(2,128)(2,1)S(1)} async-done(((bf16[128,9,2,128]{3,2,1,0:T(2,128)(2,1)}), bf16[128,9,2,128]{3,2,1,0:T(2,128)(2,1)S(1)}, u32[]{:S(2)}, u32[]{:S(2)}) %all-to-all-start) | async-done | bytes 589856 | tf_op jit(solution)/shard_map/all_to_all | solution.py:337
  58.9 0.5 copy.9
  59.4 3.2 %shard_map.85 = bf16[128,9,2,128]{3,2,1,0:T(2,128)(2,1)} custom-call(bf16[9,256,128]{2,1,0:T(8,128)(2,1)S(1)} %bitcast.14), custom_call_target="tpu_custom_call" | custom-call | tf_op jit(solution)/shard_map/pallas_call | solution.py:322
  62.6 8.2 %all-to-all-start.1 = ((bf16[128,9,2,128]{3,2,1,0:T(2,128)(2,1)}), bf16[128,9,2,128]{3,2,1,0:T(2,128)(2,1)S(1)}, u32[]{:S(2)}, u32[]{:S(2)}) async-start(bf16[128,9,2,128]{3,2,1,0:T(2,128)(2,1)} %shard_map.85), calls=%async_computation.1 | async-start | bytes 1179648 | tf_op jit(solution)/shard_map/all_to_all | solution.py:337
  70.8 5.2 %collective-permute-start.3 = (bf16[2,144,768]{2,1,0:T(8,128)(2,1)S(1)}, bf16[2,144,768]{2,1,0:T(8,128)(2,1)S(1)}, u32[]{:S(2)}, u32[]{:S(2)}) collective-permute-start(bf16[2,144,768]{2,1,0:T(8,128)(2,1)S(1)} %pad_maximum_fusion.refs_0_.ext_ref), channel_id=1, source_target_pairs={{0,64},{32,96},{64,0},{96,32},{1,65},{33,97},{65,1},{97,33},{2,66}... | collective-permute-start | bytes 1327112 | tf_op jit(solution)/shard_map/ppermute | solution.py:365
  76.0 12.1 %collective-permute-done.3.refs_2_ = bf16[2,144,768]{2,1,0:T(8,128)(2,1)S(1)} collective-permute-done((bf16[2,144,768]{2,1,0:T(8,128)(2,1)S(1)}, bf16[2,144,768]{2,1,0:T(8,128)(2,1)S(1)}, u32[]{:S(2)}, u32[]{:S(2)}) %collective-permute-start.3) | collective-permute-done | bytes 442400 | tf_op jit(solution)/shard_map/ppermute | solution.py:365
  88.0 17.3 %all-to-all-done.1.in_ref = bf16[128,9,2,128]{3,2,1,0:T(2,128)(2,1)S(1)} async-done(((bf16[128,9,2,128]{3,2,1,0:T(2,128)(2,1)}), bf16[128,9,2,128]{3,2,1,0:T(2,128)(2,1)S(1)}, u32[]{:S(2)}, u32[]{:S(2)}) %all-to-all-start.1) | async-done | bytes 589856 | tf_op jit(solution)/shard_map/all_to_all | solution.py:337
  105.3 2.3 %shard_map.86 = (bf16[16,40,128]{2,1,0:T(8,128)(2,1)}, bf16[4,96,128]{2,1,0:T(8,128)(2,1)S(1)}, bf16[4,96,128]{2,1,0:T(8,128)(2,1)S(1)}) custom-call(s32[2]{0:T(128)S(1)} %pad_add_fusion.place_ref, bf16[128,9,2,128]{3,2,1,0:T(2,128)(2,1)S(1)} %all-to-all-done.1.in_ref, bf16[2,144,768]{2,1,0:T(8,128)(2,1)S(1)} %pad_maximum_fusion.refs_0_.ext_ref, ...), custom_call_target="tpu_custom_call" | custom-call | tf_op jit(solution)/shard_map/pallas_call | solution.py:322
  107.7 8.8 %all-to-all-start.2 = ((bf16[16,40,128]{2,1,0:T(8,128)(2,1)}), bf16[16,40,128]{2,1,0:T(8,128)(2,1)S(1)}, u32[]{:S(2)}, u32[]{:S(2)}) async-start(bf16[16,40,128]{2,1,0:T(8,128)(2,1)} %get-tuple-element.42), calls=%async_computation.2 | async-start | bytes 327680 | tf_op jit(solution)/shard_map/all_to_all | solution.py:337
  116.5 2.7 %collective-permute-start.4 = (bf16[4,96,128]{2,1,0:T(8,128)(2,1)S(1)}, bf16[4,96,128]{2,1,0:T(8,128)(2,1)S(1)}, u32[]{:S(2)}, u32[]{:S(2)}) collective-permute-start(bf16[4,96,128]{2,1,0:T(8,128)(2,1)S(1)} %get-tuple-element.44), channel_id=1, source_target_pairs={{0,1},{1,0},{2,3},{3,2},{4,5},{5,4},{6,7},{7,6},{8,9},{9,8},{10,11... | collective-permute-start | bytes 294920 | tf_op jit(solution)/shard_map/ppermute | solution.py:368
  119.2 1.0 shard_map.87
  120.2 0.0 collective-permute-done.4.got_ref
  120.2 1.2 all-to-all-done.2.in_ref
  121.4 0.6 shard_map.88
  122.1 3.3 %all-to-all-start.3 = ((bf16[4,40,128]{2,1,0:T(8,128)(2,1)}), bf16[4,40,128]{2,1,0:T(8,128)(2,1)S(1)}, u32[]{:S(2)}, u32[]{:S(2)}) async-start(bf16[4,40,128]{2,1,0:T(8,128)(2,1)} %shard_map.88), calls=%async_computation.3 | async-start | bytes 81920 | tf_op jit(solution)/shard_map/all_to_all | solution.py:337
  125.4 2.2 %collective-permute-start.5 = (bf16[2,96,128]{2,1,0:T(8,128)(2,1)S(1)}, bf16[2,96,128]{2,1,0:T(8,128)(2,1)S(1)}, u32[]{:S(2)}, u32[]{:S(2)}) collective-permute-start(bf16[2,96,128]{2,1,0:T(8,128)(2,1)S(1)} %get-tuple-element.54), channel_id=1, source_target_pairs={{0,32},{32,64},{64,96},{96,0},{1,33},{33,65},{65,97},{97,1},{2,34}... | collective-permute-start | bytes 147464 | tf_op jit(solution)/shard_map/ppermute | solution.py:365
  127.6 4.0 %collective-permute-start.6 = (bf16[2,96,128]{2,1,0:T(8,128)(2,1)S(1)}, bf16[2,96,128]{2,1,0:T(8,128)(2,1)S(1)}, u32[]{:S(2)}, u32[]{:S(2)}) collective-permute-start(bf16[2,96,128]{2,1,0:T(8,128)(2,1)S(1)} %get-tuple-element.55), channel_id=1, source_target_pairs={{0,64},{32,96},{64,0},{96,32},{1,65},{33,97},{65,1},{97,33},{2,66}... | collective-permute-start | bytes 147464 | tf_op jit(solution)/shard_map/ppermute | solution.py:365
  131.6 4.0 %collective-permute-start.7 = (bf16[2,96,128]{2,1,0:T(8,128)(2,1)S(1)}, bf16[2,96,128]{2,1,0:T(8,128)(2,1)S(1)}, u32[]{:S(2)}, u32[]{:S(2)}) collective-permute-start(bf16[2,96,128]{2,1,0:T(8,128)(2,1)S(1)} %get-tuple-element.56), channel_id=1, source_target_pairs={{0,96},{32,0},{64,32},{96,64},{1,97},{33,1},{65,33},{97,65},{2,98}... | collective-permute-start | bytes 147464 | tf_op jit(solution)/shard_map/ppermute | solution.py:365
  135.6 0.0 collective-permute-done.5.refs_1_
  135.6 0.0 collective-permute-done.6.refs_2_
  135.6 1.3 collective-permute-done.7.refs_3_
  137.0 0.0 all-to-all-done.3.in_ref
  137.0 7.2 %all_to_all.30.in_ref = bf16[4,40,128]{2,1,0:T(8,128)(2,1)S(1)} all-to-all(bf16[4,40,128]{2,1,0:T(8,128)(2,1)S(1)} %shard_map.90), channel_id=1, replica_groups={{6,4,2,0},{8,14,12,10},{18,16,22,20},{28,26,24,30},{7,5,3,1},{9,15,13,1..., dimensions={0} | all-to-all | bytes 81920 | tf_op jit(solution)/shard_map/all_to_all | solution.py:337
  144.2 0.9 shard_map.91
  145.0 0.0 copy-start
  145.0 0.0 copy-start.1
  145.0 4.8 %all-to-all-start.5 = ((bf16[16,144,128]{2,1,0:T(8,128)(2,1)}), bf16[16,144,128]{2,1,0:T(8,128)(2,1)S(1)}, u32[]{:S(2)}, u32[]{:S(2)}) async-start(bf16[16,144,128]{2,1,0:T(8,128)(2,1)} %shard_map.91), calls=%async_computation.5 | async-start | bytes 1179648 | tf_op jit(solution)/shard_map/all_to_all | solution.py:337
  149.9 0.0 copy-done
  149.9 0.0 copy-done.1
  149.9 1.8 %shard_map.92 = bf16[128,768]{1,0:T(8,128)(2,1)} custom-call(s32[2]{0:T(128)S(1)} %pad_add_fusion.place_ref, bf16[2,96,128]{2,1,0:T(8,128)(2,1)S(1)} %get-tuple-element.58.refs_0_, bf16[2,96,128]{2,1,0:T(8,128)(2,1)S(1)} %collective-permute-done.5.refs_1_, bf16[2,96,128]{2,1,0:T(8,128)(2,1)S(1)} %collective-permute-done.6.refs_2_, ...), custom_call_target="tpu_custom_call" | custom-call | tf_op jit(solution)/shard_map/pallas_call | solution.py:322
  151.7 7.5 %all-to-all-done.5 = bf16[16,144,128]{2,1,0:T(8,128)(2,1)S(1)} async-done(((bf16[16,144,128]{2,1,0:T(8,128)(2,1)}), bf16[16,144,128]{2,1,0:T(8,128)(2,1)S(1)}, u32[]{:S(2)}, u32[]{:S(2)}) %all-to-all-start.5) | async-done | bytes 589856 | tf_op jit(solution)/shard_map/all_to_all | solution.py:337
  159.2 6.5 %collective-permute-start.8 = (bf16[4,576,128]{2,1,0:T(8,128)(2,1)S(1)}, bf16[4,576,128]{2,1,0:T(8,128)(2,1)S(1)}, u32[]{:S(2)}, u32[]{:S(2)}) collective-permute-start(bf16[4,576,128]{2,1,0:T(8,128)(2,1)S(1)} %bitcast.12), channel_id=1, source_target_pairs={{0,1},{1,0},{2,3},{3,2},{4,5},{5,4},{6,7},{7,6},{8,9},{9,8},{10,11... | collective-permute-start | bytes 1769480 | tf_op jit(solution)/shard_map/ppermute | solution.py:368
  165.7 1.6 collective-permute-done.8.other_ref
  167.3 1.7 %shard_map.93 = (bf16[768,384]{1,0:T(8,128)(2,1)}, bf16[768,384]{1,0:T(8,128)(2,1)}) custom-call(s32[2]{0:T(128)S(1)} %pad_add_fusion.place_ref, bf16[4,576,128]{2,1,0:T(8,128)(2,1)S(1)} %bitcast.13, bf16[4,576,128]{2,1,0:T(8,128)(2,1)S(1)} %collective-permute-done.8.other_ref), custom_call_target="tpu_custom_call" | custom-call | tf_op jit(solution)/shard_map/pallas_call | solution.py:322
  (3 shorter events, 0.1 us)
Async XLA Ops:
  3.8 55.1 %all-to-all-start = ((bf16[128,9,2,128]{3,2,1,0:T(2,128)(2,1)}), bf16[128,9,2,128]{3,2,1,0:T(2,128)(2,1)S(1)}, u32[]{:S(2)}, u32[]{:S(2)}) async-start(bf16[128,9,2,128]{3,2,1,0:T(2,128)(2,1)} %get-tuple-element.35), calls=%async_computation | async-start | bytes 1179648 | tf_op jit(solution)/shard_map/all_to_all | solution.py:337
  24.4 3.9 %collective-permute-start = (bf16[144,768]{1,0:T(8,128)(2,1)S(1)}, bf16[144,768]{1,0:T(8,128)(2,1)S(1)}, u32[]{:S(2)}, u32[]{:S(2)}) collective-permute-start(bf16[144,768]{1,0:T(8,128)(2,1)S(1)} %get-tuple-element.36), channel_id=1, source_target_pairs={{0,1},{1,0},{2,3},{3,2},{4,5},{5,4},{6,7},{7,6},{8,9},{9,8},{10,11... | collective-permute-start | bytes 663560 | tf_op jit(solution)/shard_map/ppermute | solution.py:368
  28.3 17.4 %collective-permute-start.1 = (bf16[2,144,768]{2,1,0:T(8,128)(2,1)S(1)}, bf16[2,144,768]{2,1,0:T(8,128)(2,1)S(1)}, u32[]{:S(2)}, u32[]{:S(2)}) collective-permute-start(bf16[2,144,768]{2,1,0:T(8,128)(2,1)S(1)} %pad_maximum_fusion.refs_0_.ext_ref), channel_id=1, source_target_pairs={{0,32},{32,64},{64,96},{96,0},{1,33},{33,65},{65,97},{97,1},{2,34}... | collective-permute-start | bytes 1327112 | tf_op jit(solution)/shard_map/ppermute | solution.py:365
  31.3 15.7 %collective-permute-start.2 = (bf16[2,144,768]{2,1,0:T(8,128)(2,1)S(1)}, bf16[2,144,768]{2,1,0:T(8,128)(2,1)S(1)}, u32[]{:S(2)}, u32[]{:S(2)}) collective-permute-start(bf16[2,144,768]{2,1,0:T(8,128)(2,1)S(1)} %pad_maximum_fusion.refs_0_.ext_ref), channel_id=1, source_target_pairs={{0,96},{32,0},{64,32},{96,64},{1,97},{33,1},{65,33},{97,65},{2,98}... | collective-permute-start | bytes 1327112 | tf_op jit(solution)/shard_map/ppermute | solution.py:365
  62.6 42.7 %all-to-all-start.1 = ((bf16[128,9,2,128]{3,2,1,0:T(2,128)(2,1)}), bf16[128,9,2,128]{3,2,1,0:T(2,128)(2,1)S(1)}, u32[]{:S(2)}, u32[]{:S(2)}) async-start(bf16[128,9,2,128]{3,2,1,0:T(2,128)(2,1)} %shard_map.85), calls=%async_computation.1 | async-start | bytes 1179648 | tf_op jit(solution)/shard_map/all_to_all | solution.py:337
  70.8 17.2 %collective-permute-start.3 = (bf16[2,144,768]{2,1,0:T(8,128)(2,1)S(1)}, bf16[2,144,768]{2,1,0:T(8,128)(2,1)S(1)}, u32[]{:S(2)}, u32[]{:S(2)}) collective-permute-start(bf16[2,144,768]{2,1,0:T(8,128)(2,1)S(1)} %pad_maximum_fusion.refs_0_.ext_ref), channel_id=1, source_target_pairs={{0,64},{32,96},{64,0},{96,32},{1,65},{33,97},{65,1},{97,33},{2,66}... | collective-permute-start | bytes 1327112 | tf_op jit(solution)/shard_map/ppermute | solution.py:365
  107.7 13.8 %all-to-all-start.2 = ((bf16[16,40,128]{2,1,0:T(8,128)(2,1)}), bf16[16,40,128]{2,1,0:T(8,128)(2,1)S(1)}, u32[]{:S(2)}, u32[]{:S(2)}) async-start(bf16[16,40,128]{2,1,0:T(8,128)(2,1)} %get-tuple-element.42), calls=%async_computation.2 | async-start | bytes 327680 | tf_op jit(solution)/shard_map/all_to_all | solution.py:337
  116.5 3.7 %collective-permute-start.4 = (bf16[4,96,128]{2,1,0:T(8,128)(2,1)S(1)}, bf16[4,96,128]{2,1,0:T(8,128)(2,1)S(1)}, u32[]{:S(2)}, u32[]{:S(2)}) collective-permute-start(bf16[4,96,128]{2,1,0:T(8,128)(2,1)S(1)} %get-tuple-element.44), channel_id=1, source_target_pairs={{0,1},{1,0},{2,3},{3,2},{4,5},{5,4},{6,7},{7,6},{8,9},{9,8},{10,11... | collective-permute-start | bytes 294920 | tf_op jit(solution)/shard_map/ppermute | solution.py:368
  122.1 14.9 %all-to-all-start.3 = ((bf16[4,40,128]{2,1,0:T(8,128)(2,1)}), bf16[4,40,128]{2,1,0:T(8,128)(2,1)S(1)}, u32[]{:S(2)}, u32[]{:S(2)}) async-start(bf16[4,40,128]{2,1,0:T(8,128)(2,1)} %shard_map.88), calls=%async_computation.3 | async-start | bytes 81920 | tf_op jit(solution)/shard_map/all_to_all | solution.py:337
  125.4 10.2 %collective-permute-start.5 = (bf16[2,96,128]{2,1,0:T(8,128)(2,1)S(1)}, bf16[2,96,128]{2,1,0:T(8,128)(2,1)S(1)}, u32[]{:S(2)}, u32[]{:S(2)}) collective-permute-start(bf16[2,96,128]{2,1,0:T(8,128)(2,1)S(1)} %get-tuple-element.54), channel_id=1, source_target_pairs={{0,32},{32,64},{64,96},{96,0},{1,33},{33,65},{65,97},{97,1},{2,34}... | collective-permute-start | bytes 147464 | tf_op jit(solution)/shard_map/ppermute | solution.py:365
  127.6 8.0 %collective-permute-start.6 = (bf16[2,96,128]{2,1,0:T(8,128)(2,1)S(1)}, bf16[2,96,128]{2,1,0:T(8,128)(2,1)S(1)}, u32[]{:S(2)}, u32[]{:S(2)}) collective-permute-start(bf16[2,96,128]{2,1,0:T(8,128)(2,1)S(1)} %get-tuple-element.55), channel_id=1, source_target_pairs={{0,64},{32,96},{64,0},{96,32},{1,65},{33,97},{65,1},{97,33},{2,66}... | collective-permute-start | bytes 147464 | tf_op jit(solution)/shard_map/ppermute | solution.py:365
  131.6 5.3 %collective-permute-start.7 = (bf16[2,96,128]{2,1,0:T(8,128)(2,1)S(1)}, bf16[2,96,128]{2,1,0:T(8,128)(2,1)S(1)}, u32[]{:S(2)}, u32[]{:S(2)}) collective-permute-start(bf16[2,96,128]{2,1,0:T(8,128)(2,1)S(1)} %get-tuple-element.56), channel_id=1, source_target_pairs={{0,96},{32,0},{64,32},{96,64},{1,97},{33,1},{65,33},{97,65},{2,98}... | collective-permute-start | bytes 147464 | tf_op jit(solution)/shard_map/ppermute | solution.py:365
  145.0 4.8 %copy-start = (bf16[768,384]{1,0:T(8,128)(2,1)S(1)}, bf16[768,384]{1,0:T(8,128)(2,1)}, u32[]{:S(2)}) copy-start(bf16[768,384]{1,0:T(8,128)(2,1)} %refs_4_.1) | copy-start | bytes 1769476
  145.0 4.8 %copy-start.1 = (bf16[768,384]{1,0:T(8,128)(2,1)S(1)}, bf16[768,384]{1,0:T(8,128)(2,1)}, u32[]{:S(2)}) copy-start(bf16[768,384]{1,0:T(8,128)(2,1)} %refs_5_.1) | copy-start | bytes 1769476
  145.0 14.2 %all-to-all-start.5 = ((bf16[16,144,128]{2,1,0:T(8,128)(2,1)}), bf16[16,144,128]{2,1,0:T(8,128)(2,1)S(1)}, u32[]{:S(2)}, u32[]{:S(2)}) async-start(bf16[16,144,128]{2,1,0:T(8,128)(2,1)} %shard_map.91), calls=%async_computation.5 | async-start | bytes 1179648 | tf_op jit(solution)/shard_map/all_to_all | solution.py:337
  159.2 8.1 %collective-permute-start.8 = (bf16[4,576,128]{2,1,0:T(8,128)(2,1)S(1)}, bf16[4,576,128]{2,1,0:T(8,128)(2,1)S(1)}, u32[]{:S(2)}, u32[]{:S(2)}) collective-permute-start(bf16[4,576,128]{2,1,0:T(8,128)(2,1)S(1)} %bitcast.12), channel_id=1, source_target_pairs={{0,1},{1,0},{2,3},{3,2},{4,5},{5,4},{6,7},{7,6},{8,9},{9,8},{10,11... | collective-permute-start | bytes 1769480 | tf_op jit(solution)/shard_map/ppermute | solution.py:368

commit v12 on v10

--- a/solution.py
+++ b/solution.py
@@ -365,15 +365,14 @@
 
     arrived = swap(sent, OWNERS)
     pair = jnp.stack([ext, flip(ext)])
-    near = (shift(pair, 1), shift(pair, 3))
-    arrived, pair, near, place = lax.optimization_barrier((arrived, pair, near, place))
-    exts = [pair, near[0], shift(pair, 2), near[1]]
+    exts = [pair, shift(pair, 1), shift(pair, 2), shift(pair, 3)]
     arrived = arrived.transpose(1, 0, 2, 3).reshape(9, ROWS, LOCAL)
     (worked,) = call(
         attend_kernel,
         [shape(LOCAL, 9, 2, LOCAL)],
         arrived,
     )
+    worked, exts, place = lax.optimization_barrier((worked, exts, place))
     back = swap(worked, OWNERS)
     part, keep, give = call(
         partial_kernel,

time: 168 us -> 172 us (1.024)
  blocking collectives: 34.7 us -> 82 us
  waiting for transfers between devices: 55.8 us -> 22.4 us
  starting transfers between devices: 62 us -> 52.7 us
    all_to_all x3 -> x4, blocking collectives: 34.7 us -> 82 us  [swap(): lax.all_to_all(rows, axes, split_axis=0, concat_axis=0, tiled=True, axis_...]
    ppermute x3, waiting for transfers between devices: 24.1 us -> 0.01 us  [shift(): return lax.ppermute(pair, 'y', [(y, (y + dy) % 4) for y in range(4)])]
    all_to_all x3 -> x2, waiting for transfers between devices: 30.5 us -> 21.2 us  [swap(): lax.all_to_all(rows, axes, split_axis=0, concat_axis=0, tiled=True, axis_...]
    all_to_all x3 -> x2, starting transfers between devices: 37.6 us -> 29.4 us  [swap(): lax.all_to_all(rows, axes, split_axis=0, concat_axis=0, tiled=True, axis_...]
  transfers between devices with their start and end apart: 9 -> 8, of which waited for: 8 -> 4; matrix products, arithmetic and copies ran while one was open for 0% -> 0% of each run, Pallas kernels for 2% -> 3%
where the time goes in v12:
time: 172 us; the launch traced here: 171 us
  blocking collectives  82 us (48%)
  starting transfers between devices  52.7 us (31%)
  waiting for transfers between devices  22.4 us (13%)
  Pallas kernels  12.5 us (7%)
    all_to_all x4, blocking collectives, swap(): lax.all_to_all(rows, axes, split_axis=0, concat_axis=0, tiled=True, axis_...  82 us
    all_to_all x2, starting transfers between devices, swap(): lax.all_to_all(rows, axes, split_axis=0, concat_axis=0, tiled=True, axis_...  29.4 us
    all_to_all x2, waiting for transfers between devices, swap(): lax.all_to_all(rows, axes, split_axis=0, concat_axis=0, tiled=True, axis_...  21.2 us
    ppermute x3, starting transfers between devices, flip(): return lax.ppermute(part, 'c', [(0, 1), (1, 0)])  12.7 us
    pallas_call x9, Pallas kernels, call(): pl.pallas_call(kernel, out_shape=out, in_specs=specs, out_specs=outs, scr...  12.5 us
    ppermute x3, starting transfers between devices, shift(): return lax.ppermute(pair, 'y', [(y, (y + dy) % 4) for y in range(4)])  10.6 us
  transfers between devices with their start and end apart: 8, of which 4 were waited for; matrix products, arithmetic and copies ran while one was open for 0% of the time, Pallas kernels for 3%

profile of v12, /device:TPU:1, one launch (start us, length us, event | category | flops | bytes accessed | tf_op | source)
XLA Modules:
  0.0 171.0 jit_solution(12671067441192800642)
XLA Ops:
  0.6 3.2 %shard_map.84 = (bf16[128,9,2,128]{3,2,1,0:T(2,128)(2,1)}, bf16[144,768]{1,0:T(8,128)(2,1)S(1)}) custom-call(s32[6,1,128]{2,1,0:T(1,128)} %bitcast.19, bf16[128,768]{1,0:T(8,128)(2,1)} %bitcast.15, bf16[768,384]{1,0:T(8,128)(2,1)} %ws_ref.1, bf16[768,384]{1,0:T(8,128)(2,1)} %wv_ref.1, bf16[128,384]{1,0:T(8,128)(2,1)} %bitcast.17), custom_call_target="tpu_custom_call" | custom-call | tf_op jit(solution)/shard_map/pallas_call | solution.py:318
  3.8 20.6 %all-to-all-start = ((bf16[128,9,2,128]{3,2,1,0:T(2,128)(2,1)}), bf16[128,9,2,128]{3,2,1,0:T(2,128)(2,1)S(1)}, u32[]{:S(2)}, u32[]{:S(2)}) async-start(bf16[128,9,2,128]{3,2,1,0:T(2,128)(2,1)} %get-tuple-element.21), calls=%async_computation | async-start | bytes 1179648 | tf_op jit(solution)/shard_map/all_to_all | solution.py:333
  24.4 2.8 %collective-permute-start = (bf16[144,768]{1,0:T(8,128)(2,1)S(1)}, bf16[144,768]{1,0:T(8,128)(2,1)S(1)}, u32[]{:S(2)}, u32[]{:S(2)}) collective-permute-start(bf16[144,768]{1,0:T(8,128)(2,1)S(1)} %get-tuple-element.22), channel_id=1, source_target_pairs={{0,1},{1,0},{2,3},{3,2},{4,5},{5,4},{6,7},{7,6},{8,9},{9,8},{10,11... | collective-permute-start | bytes 663560 | tf_op jit(solution)/shard_map/ppermute | solution.py:364
  27.2 1.1 collective-permute-done
  28.3 2.9 %collective-permute-start.1 = (bf16[2,144,768]{2,1,0:T(8,128)(2,1)S(1)}, bf16[2,144,768]{2,1,0:T(8,128)(2,1)S(1)}, u32[]{:S(2)}, u32[]{:S(2)}) collective-permute-start(bf16[2,144,768]{2,1,0:T(8,128)(2,1)S(1)} %pad_maximum_fusion.refs_0_.ext_ref), channel_id=1, source_target_pairs={{0,32},{32,64},{64,96},{96,0},{1,33},{33,65},{65,97},{97,1},{2,34}... | collective-permute-start | bytes 1327112 | tf_op jit(solution)/shard_map/ppermute | solution.py:361
  31.3 4.7 %collective-permute-start.2 = (bf16[2,144,768]{2,1,0:T(8,128)(2,1)S(1)}, bf16[2,144,768]{2,1,0:T(8,128)(2,1)S(1)}, u32[]{:S(2)}, u32[]{:S(2)}) collective-permute-start(bf16[2,144,768]{2,1,0:T(8,128)(2,1)S(1)} %pad_maximum_fusion.refs_0_.ext_ref), channel_id=1, source_target_pairs={{0,64},{32,96},{64,0},{96,32},{1,65},{33,97},{65,1},{97,33},{2,66}... | collective-permute-start | bytes 1327112 | tf_op jit(solution)/shard_map/ppermute | solution.py:361
  36.0 2.9 %collective-permute-start.3 = (bf16[2,144,768]{2,1,0:T(8,128)(2,1)S(1)}, bf16[2,144,768]{2,1,0:T(8,128)(2,1)S(1)}, u32[]{:S(2)}, u32[]{:S(2)}) collective-permute-start(bf16[2,144,768]{2,1,0:T(8,128)(2,1)S(1)} %pad_maximum_fusion.refs_0_.ext_ref), channel_id=1, source_target_pairs={{0,96},{32,0},{64,32},{96,64},{1,97},{33,1},{65,33},{97,65},{2,98}... | collective-permute-start | bytes 1327112 | tf_op jit(solution)/shard_map/ppermute | solution.py:361
  38.9 0.1 pad_add_fusion.place_ref
  39.0 20.0 %all-to-all-done = bf16[128,9,2,128]{3,2,1,0:T(2,128)(2,1)S(1)} async-done(((bf16[128,9,2,128]{3,2,1,0:T(2,128)(2,1)}), bf16[128,9,2,128]{3,2,1,0:T(2,128)(2,1)S(1)}, u32[]{:S(2)}, u32[]{:S(2)}) %all-to-all-start) | async-done | bytes 589856 | tf_op jit(solution)/shard_map/all_to_all | solution.py:333
  59.0 0.5 copy.9
  59.4 2.4 %shard_map.85 = bf16[128,9,2,128]{3,2,1,0:T(2,128)(2,1)S(1)} custom-call(bf16[9,256,128]{2,1,0:T(8,128)(2,1)S(1)} %bitcast.11), custom_call_target="tpu_custom_call" | custom-call | tf_op jit(solution)/shard_map/pallas_call | solution.py:318
  61.8 0.0 collective-permute-done.1.refs_1_
  61.8 0.0 collective-permute-done.2.refs_2_
  61.8 0.0 collective-permute-done.3.refs_3_
  61.8 47.3 %all_to_all.30.in_ref = bf16[128,9,2,128]{3,2,1,0:T(2,128)(2,1)S(1)} all-to-all(bf16[128,9,2,128]{3,2,1,0:T(2,128)(2,1)S(1)} %shard_map.85), channel_id=1, replica_groups=mesh['x'=4,'y'=4,'z'=16,'c'=2] {'y','c','z'}, dimensions={0} | all-to-all | bytes 1179648 | tf_op jit(solution)/shard_map/all_to_all | solution.py:333
  109.2 2.3 %shard_map.86 = (bf16[16,40,128]{2,1,0:T(8,128)(2,1)}, bf16[4,96,128]{2,1,0:T(8,128)(2,1)S(1)}, bf16[4,96,128]{2,1,0:T(8,128)(2,1)S(1)}) custom-call(s32[2]{0:T(128)S(1)} %pad_add_fusion.place_ref, bf16[128,9,2,128]{3,2,1,0:T(2,128)(2,1)S(1)} %all_to_all.30.in_ref, bf16[2,144,768]{2,1,0:T(8,128)(2,1)S(1)} %pad_maximum_fusion.refs_0_.ext_ref, ...), custom_call_target="tpu_custom_call" | custom-call | tf_op jit(solution)/shard_map/pallas_call | solution.py:318
  111.5 8.8 %all-to-all-start.2 = ((bf16[16,40,128]{2,1,0:T(8,128)(2,1)}), bf16[16,40,128]{2,1,0:T(8,128)(2,1)S(1)}, u32[]{:S(2)}, u32[]{:S(2)}) async-start(bf16[16,40,128]{2,1,0:T(8,128)(2,1)} %get-tuple-element.29), calls=%async_computation.2 | async-start | bytes 327680 | tf_op jit(solution)/shard_map/all_to_all | solution.py:333
  120.3 2.7 %collective-permute-start.4 = (bf16[4,96,128]{2,1,0:T(8,128)(2,1)S(1)}, bf16[4,96,128]{2,1,0:T(8,128)(2,1)S(1)}, u32[]{:S(2)}, u32[]{:S(2)}) collective-permute-start(bf16[4,96,128]{2,1,0:T(8,128)(2,1)S(1)} %get-tuple-element.31), channel_id=1, source_target_pairs={{0,1},{1,0},{2,3},{3,2},{4,5},{5,4},{6,7},{7,6},{8,9},{9,8},{10,11... | collective-permute-start | bytes 294920 | tf_op jit(solution)/shard_map/ppermute | solution.py:364
  123.1 1.0 shard_map.87
  124.0 0.0 collective-permute-done.4.got_ref
  124.1 1.2 all-to-all-done.2.in_ref
  125.3 12.6 %all_to_all.31.in_ref = bf16[4,40,128]{2,1,0:T(8,128)(2,1)S(1)} all-to-all(bf16[4,40,128]{2,1,0:T(8,128)(2,1)S(1)} %shard_map.88), channel_id=1, replica_groups={{6,8,18,28},{4,14,16,26},{2,12,22,24},{0,10,20,30},{7,9,19,29},{5,15,17..., dimensions={0} | all-to-all | bytes 81920 | tf_op jit(solution)/shard_map/all_to_all | solution.py:333
  138.0 11.1 %all_to_all.32.block_ref = bf16[16,40,128]{2,1,0:T(8,128)(2,1)S(1)} all-to-all(bf16[16,40,128]{2,1,0:T(8,128)(2,1)S(1)} %shard_map.89), channel_id=1, replica_groups={{6,4,2,0,134,132,130,128,262,260,258,256,390,388,386,384},{8,14,12,10,1..., dimensions={0} | all-to-all | bytes 327680 | tf_op jit(solution)/shard_map/all_to_all | solution.py:333
  149.1 0.1 shard_map.90
  149.2 0.0 copy-start
  149.2 0.0 copy-start.1
  149.2 11.0 %all_to_all.33.all_ref.mine_ref = bf16[4,768,128]{2,1,0:T(8,128)(2,1)S(1)} all-to-all(bf16[4,768,128]{2,1,0:T(8,128)(2,1)S(1)} %shard_map.90), channel_id=1, replica_groups=mesh['x'=4,'y'=4,'z'=16,'c'=2] {'y'}, dimensions={0} | all-to-all | bytes 1572864 | tf_op jit(solution)/shard_map/all_to_all | solution.py:333
  160.2 7.2 %collective-permute-start.5 = (bf16[4,768,128]{2,1,0:T(8,128)(2,1)S(1)}, bf16[4,768,128]{2,1,0:T(8,128)(2,1)S(1)}, u32[]{:S(2)}, u32[]{:S(2)}) collective-permute-start(bf16[4,768,128]{2,1,0:T(8,128)(2,1)S(1)} %all_to_all.33.all_ref.mine_ref), channel_id=1, source_target_pairs={{0,1},{1,0},{2,3},{3,2},{4,5},{5,4},{6,7},{7,6},{8,9},{9,8},{10,11... | collective-permute-start | bytes 2359304 | tf_op jit(solution)/shard_map/ppermute | solution.py:364
  167.4 0.0 copy-done
  167.4 0.0 copy-done.1
  167.4 1.8 %shard_map.91 = bf16[128,768]{1,0:T(8,128)(2,1)} custom-call(s32[2]{0:T(128)S(1)} %pad_add_fusion.place_ref, bf16[4,768,128]{2,1,0:T(8,128)(2,1)S(1)} %all_to_all.33.all_ref.mine_ref, bf16[768,384]{1,0:T(8,128)(2,1)S(1)} %copy-done, bf16[768,384]{1,0:T(8,128)(2,1)S(1)} %copy-done.1), custom_call_target="tpu_custom_call" | custom-call | tf_op jit(solution)/shard_map/pallas_call | solution.py:318
  169.2 0.1 collective-permute-done.5.other_ref
  169.3 1.7 %shard_map.92 = (bf16[768,384]{1,0:T(8,128)(2,1)}, bf16[768,384]{1,0:T(8,128)(2,1)}) custom-call(s32[2]{0:T(128)S(1)} %pad_add_fusion.place_ref, bf16[4,768,128]{2,1,0:T(8,128)(2,1)S(1)} %all_to_all.33.all_ref.mine_ref, bf16[4,768,128]{2,1,0:T(8,128)(2,1)S(1)} %collective-permute-done.5.other_ref), custom_call_target="tpu_custom_call" | custom-call | tf_op jit(solution)/shard_map/pallas_call | solution.py:318
  (3 shorter events, 0.1 us)
Async XLA Ops:
  3.8 55.1 %all-to-all-start = ((bf16[128,9,2,128]{3,2,1,0:T(2,128)(2,1)}), bf16[128,9,2,128]{3,2,1,0:T(2,128)(2,1)S(1)}, u32[]{:S(2)}, u32[]{:S(2)}) async-start(bf16[128,9,2,128]{3,2,1,0:T(2,128)(2,1)} %get-tuple-element.21), calls=%async_computation | async-start | bytes 1179648 | tf_op jit(solution)/shard_map/all_to_all | solution.py:333
  24.4 3.9 %collective-permute-start = (bf16[144,768]{1,0:T(8,128)(2,1)S(1)}, bf16[144,768]{1,0:T(8,128)(2,1)S(1)}, u32[]{:S(2)}, u32[]{:S(2)}) collective-permute-start(bf16[144,768]{1,0:T(8,128)(2,1)S(1)} %get-tuple-element.22), channel_id=1, source_target_pairs={{0,1},{1,0},{2,3},{3,2},{4,5},{5,4},{6,7},{7,6},{8,9},{9,8},{10,11... | collective-permute-start | bytes 663560 | tf_op jit(solution)/shard_map/ppermute | solution.py:364
  28.3 33.5 %collective-permute-start.1 = (bf16[2,144,768]{2,1,0:T(8,128)(2,1)S(1)}, bf16[2,144,768]{2,1,0:T(8,128)(2,1)S(1)}, u32[]{:S(2)}, u32[]{:S(2)}) collective-permute-start(bf16[2,144,768]{2,1,0:T(8,128)(2,1)S(1)} %pad_maximum_fusion.refs_0_.ext_ref), channel_id=1, source_target_pairs={{0,32},{32,64},{64,96},{96,0},{1,33},{33,65},{65,97},{97,1},{2,34}... | collective-permute-start | bytes 1327112 | tf_op jit(solution)/shard_map/ppermute | solution.py:361
  31.3 30.5 %collective-permute-start.2 = (bf16[2,144,768]{2,1,0:T(8,128)(2,1)S(1)}, bf16[2,144,768]{2,1,0:T(8,128)(2,1)S(1)}, u32[]{:S(2)}, u32[]{:S(2)}) collective-permute-start(bf16[2,144,768]{2,1,0:T(8,128)(2,1)S(1)} %pad_maximum_fusion.refs_0_.ext_ref), channel_id=1, source_target_pairs={{0,64},{32,96},{64,0},{96,32},{1,65},{33,97},{65,1},{97,33},{2,66}... | collective-permute-start | bytes 1327112 | tf_op jit(solution)/shard_map/ppermute | solution.py:361
  36.0 25.8 %collective-permute-start.3 = (bf16[2,144,768]{2,1,0:T(8,128)(2,1)S(1)}, bf16[2,144,768]{2,1,0:T(8,128)(2,1)S(1)}, u32[]{:S(2)}, u32[]{:S(2)}) collective-permute-start(bf16[2,144,768]{2,1,0:T(8,128)(2,1)S(1)} %pad_maximum_fusion.refs_0_.ext_ref), channel_id=1, source_target_pairs={{0,96},{32,0},{64,32},{96,64},{1,97},{33,1},{65,33},{97,65},{2,98}... | collective-permute-start | bytes 1327112 | tf_op jit(solution)/shard_map/ppermute | solution.py:361
  111.5 13.8 %all-to-all-start.2 = ((bf16[16,40,128]{2,1,0:T(8,128)(2,1)}), bf16[16,40,128]{2,1,0:T(8,128)(2,1)S(1)}, u32[]{:S(2)}, u32[]{:S(2)}) async-start(bf16[16,40,128]{2,1,0:T(8,128)(2,1)} %get-tuple-element.29), calls=%async_computation.2 | async-start | bytes 327680 | tf_op jit(solution)/shard_map/all_to_all | solution.py:333
  120.3 3.7 %collective-permute-start.4 = (bf16[4,96,128]{2,1,0:T(8,128)(2,1)S(1)}, bf16[4,96,128]{2,1,0:T(8,128)(2,1)S(1)}, u32[]{:S(2)}, u32[]{:S(2)}) collective-permute-start(bf16[4,96,128]{2,1,0:T(8,128)(2,1)S(1)} %get-tuple-element.31), channel_id=1, source_target_pairs={{0,1},{1,0},{2,3},{3,2},{4,5},{5,4},{6,7},{7,6},{8,9},{9,8},{10,11... | collective-permute-start | bytes 294920 | tf_op jit(solution)/shard_map/ppermute | solution.py:364
  149.2 18.2 %copy-start = (bf16[768,384]{1,0:T(8,128)(2,1)S(1)}, bf16[768,384]{1,0:T(8,128)(2,1)}, u32[]{:S(2)}) copy-start(bf16[768,384]{1,0:T(8,128)(2,1)} %ws_ref.1) | copy-start | bytes 1769476
  149.2 18.2 %copy-start.1 = (bf16[768,384]{1,0:T(8,128)(2,1)S(1)}, bf16[768,384]{1,0:T(8,128)(2,1)}, u32[]{:S(2)}) copy-start(bf16[768,384]{1,0:T(8,128)(2,1)} %wv_ref.1) | copy-start | bytes 1769476
  160.2 9.1 %collective-permute-start.5 = (bf16[4,768,128]{2,1,0:T(8,128)(2,1)S(1)}, bf16[4,768,128]{2,1,0:T(8,128)(2,1)S(1)}, u32[]{:S(2)}, u32[]{:S(2)}) collective-permute-start(bf16[4,768,128]{2,1,0:T(8,128)(2,1)S(1)} %all_to_all.33.all_ref.mine_ref), channel_id=1, source_target_pairs={{0,1},{1,0},{2,3},{3,2},{4,5},{5,4},{6,7},{7,6},{8,9},{9,8},{10,11... | collective-permute-start | bytes 2359304 | tf_op jit(solution)/shard_map/ppermute | solution.py:364

commit v13 on v10

--- a/solution.py
+++ b/solution.py
@@ -388,11 +388,13 @@
         ],
         scalars=1,
     )
+    part = swap(part, ("x", "z"), NEAR)
+    part, back, give = lax.optimization_barrier((part, back, give))
     (attention,) = call(output_kernel, [shape(LOCAL, PROJ)], back, pair)
-    part = swap(part, ("x", "z"), NEAR)
-    part, keep, got, attention = lax.optimization_barrier((part, keep, flip(give), attention))
     (part,) = call(sum_kernel, [shape(4, SLOT, LOCAL)], part)
-    (block,) = call(sum_kernel, [shape(16, SLOT, LOCAL)], swap(part, "z", FAR))
+    part = swap(part, "z", FAR)
+    part, got, attention = lax.optimization_barrier((part, flip(give), attention))
+    (block,) = call(sum_kernel, [shape(16, SLOT, LOCAL)], part)
     (block,) = call(
         pack_kernel,
         [shape(4, WHOLE + 2 * MESSAGE, LOCAL)],

time: 168 us -> 168 us (level)
  starting transfers between devices: 62 us -> 57.9 us
  waiting for transfers between devices: 55.8 us -> 58.9 us
    all_to_all x3, starting transfers between devices: 37.6 us -> 32 us  [swap(): lax.all_to_all(rows, axes, split_axis=0, concat_axis=0, tiled=True, axis_...]
    all_to_all x3, waiting for transfers between devices: 30.5 us -> 33.6 us  [swap(): lax.all_to_all(rows, axes, split_axis=0, concat_axis=0, tiled=True, axis_...]
where the time goes in v13:
time: 168 us
  waiting for transfers between devices  58.9 us (35%)
  starting transfers between devices  57.9 us (34%)
  blocking collectives  36.2 us (22%)
  Pallas kernels  13.3 us (8%)
    all_to_all x3, blocking collectives, swap(): lax.all_to_all(rows, axes, split_axis=0, concat_axis=0, tiled=True, axis_...  36.2 us
    all_to_all x3, waiting for transfers between devices, swap(): lax.all_to_all(rows, axes, split_axis=0, concat_axis=0, tiled=True, axis_...  33.6 us
    all_to_all x3, starting transfers between devices, swap(): lax.all_to_all(rows, axes, split_axis=0, concat_axis=0, tiled=True, axis_...  32 us
    ppermute x3, waiting for transfers between devices, shift(): return lax.ppermute(pair, 'y', [(y, (y + dy) % 4) for y in range(4)])  24.1 us
    ppermute x3, starting transfers between devices, flip(): return lax.ppermute(part, 'c', [(0, 1), (1, 0)])  14.1 us
    pallas_call x9, Pallas kernels, call(): pl.pallas_call(kernel, out_shape=out, in_specs=specs, out_specs=outs, scr...  13.3 us
    ppermute x3, starting transfers between devices, shift(): return lax.ppermute(pair, 'y', [(y, (y + dy) % 4) for y in range(4)])  11.7 us
  transfers between devices with their start and end apart: 9, of which 8 were waited for; matrix products, arithmetic and copies ran while one was open for 0% of the time, Pallas kernels for 2%

profile of v13, /device:TPU:1, one launch (start us, length us, event | category | flops | bytes accessed | tf_op | source)
XLA Modules:
  0.0 167.6 jit_solution(1284282403450168358)
XLA Ops:
  0.6 3.2 %shard_map.84 = (bf16[128,9,2,128]{3,2,1,0:T(2,128)(2,1)}, bf16[144,768]{1,0:T(8,128)(2,1)S(1)}) custom-call(s32[6,1,128]{2,1,0:T(1,128)} %bitcast.19, bf16[128,768]{1,0:T(8,128)(2,1)} %bitcast.15, bf16[768,384]{1,0:T(8,128)(2,1)} %ws_ref.1, bf16[768,384]{1,0:T(8,128)(2,1)} %wv_ref.1, bf16[128,384]{1,0:T(8,128)(2,1)} %bitcast.17), custom_call_target="tpu_custom_call" | custom-call | tf_op jit(solution)/shard_map/pallas_call | solution.py:318
  3.8 20.6 %all-to-all-start = ((bf16[128,9,2,128]{3,2,1,0:T(2,128)(2,1)}), bf16[128,9,2,128]{3,2,1,0:T(2,128)(2,1)S(1)}, u32[]{:S(2)}, u32[]{:S(2)}) async-start(bf16[128,9,2,128]{3,2,1,0:T(2,128)(2,1)} %get-tuple-element.22), calls=%async_computation | async-start | bytes 1179648 | tf_op jit(solution)/shard_map/all_to_all | solution.py:333
  24.4 2.8 %collective-permute-start = (bf16[144,768]{1,0:T(8,128)(2,1)S(1)}, bf16[144,768]{1,0:T(8,128)(2,1)S(1)}, u32[]{:S(2)}, u32[]{:S(2)}) collective-permute-start(bf16[144,768]{1,0:T(8,128)(2,1)S(1)} %get-tuple-element.23), channel_id=1, source_target_pairs={{0,1},{1,0},{2,3},{3,2},{4,5},{5,4},{6,7},{7,6},{8,9},{9,8},{10,11... | collective-permute-start | bytes 663560 | tf_op jit(solution)/shard_map/ppermute | solution.py:364
  27.2 1.1 collective-permute-done
  28.3 2.9 %collective-permute-start.1 = (bf16[2,144,768]{2,1,0:T(8,128)(2,1)S(1)}, bf16[2,144,768]{2,1,0:T(8,128)(2,1)S(1)}, u32[]{:S(2)}, u32[]{:S(2)}) collective-permute-start(bf16[2,144,768]{2,1,0:T(8,128)(2,1)S(1)} %pad_maximum_fusion.refs_0_.ext_ref), channel_id=1, source_target_pairs={{0,32},{32,64},{64,96},{96,0},{1,33},{33,65},{65,97},{97,1},{2,34}... | collective-permute-start | bytes 1327112 | tf_op jit(solution)/shard_map/ppermute | solution.py:361
  31.3 3.6 %collective-permute-start.2 = (bf16[2,144,768]{2,1,0:T(8,128)(2,1)S(1)}, bf16[2,144,768]{2,1,0:T(8,128)(2,1)S(1)}, u32[]{:S(2)}, u32[]{:S(2)}) collective-permute-start(bf16[2,144,768]{2,1,0:T(8,128)(2,1)S(1)} %pad_maximum_fusion.refs_0_.ext_ref), channel_id=1, source_target_pairs={{0,96},{32,0},{64,32},{96,64},{1,97},{33,1},{65,33},{97,65},{2,98}... | collective-permute-start | bytes 1327112 | tf_op jit(solution)/shard_map/ppermute | solution.py:361
  34.9 0.1 pad_add_fusion.place_ref
  35.0 10.8 %collective-permute-done.1.refs_1_ = bf16[2,144,768]{2,1,0:T(8,128)(2,1)S(1)} collective-permute-done((bf16[2,144,768]{2,1,0:T(8,128)(2,1)S(1)}, bf16[2,144,768]{2,1,0:T(8,128)(2,1)S(1)}, u32[]{:S(2)}, u32[]{:S(2)}) %collective-permute-start.1) | collective-permute-done | bytes 442400 | tf_op jit(solution)/shard_map/ppermute | solution.py:361
  45.7 1.3 collective-permute-done.2.refs_3_
  47.0 11.9 %all-to-all-done = bf16[128,9,2,128]{3,2,1,0:T(2,128)(2,1)S(1)} async-done(((bf16[128,9,2,128]{3,2,1,0:T(2,128)(2,1)}), bf16[128,9,2,128]{3,2,1,0:T(2,128)(2,1)S(1)}, u32[]{:S(2)}, u32[]{:S(2)}) %all-to-all-start) | async-done | bytes 589856 | tf_op jit(solution)/shard_map/all_to_all | solution.py:333
  58.9 0.5 copy.9
  59.4 3.2 %shard_map.85 = bf16[128,9,2,128]{3,2,1,0:T(2,128)(2,1)} custom-call(bf16[9,256,128]{2,1,0:T(8,128)(2,1)S(1)} %bitcast.11), custom_call_target="tpu_custom_call" | custom-call | tf_op jit(solution)/shard_map/pallas_call | solution.py:318
  62.6 8.2 %all-to-all-start.1 = ((bf16[128,9,2,128]{3,2,1,0:T(2,128)(2,1)}), bf16[128,9,2,128]{3,2,1,0:T(2,128)(2,1)S(1)}, u32[]{:S(2)}, u32[]{:S(2)}) async-start(bf16[128,9,2,128]{3,2,1,0:T(2,128)(2,1)} %shard_map.85), calls=%async_computation.1 | async-start | bytes 1179648 | tf_op jit(solution)/shard_map/all_to_all | solution.py:333
  70.8 5.2 %collective-permute-start.3 = (bf16[2,144,768]{2,1,0:T(8,128)(2,1)S(1)}, bf16[2,144,768]{2,1,0:T(8,128)(2,1)S(1)}, u32[]{:S(2)}, u32[]{:S(2)}) collective-permute-start(bf16[2,144,768]{2,1,0:T(8,128)(2,1)S(1)} %pad_maximum_fusion.refs_0_.ext_ref), channel_id=1, source_target_pairs={{0,64},{32,96},{64,0},{96,32},{1,65},{33,97},{65,1},{97,33},{2,66}... | collective-permute-start | bytes 1327112 | tf_op jit(solution)/shard_map/ppermute | solution.py:361
  76.0 12.1 %collective-permute-done.3.refs_2_ = bf16[2,144,768]{2,1,0:T(8,128)(2,1)S(1)} collective-permute-done((bf16[2,144,768]{2,1,0:T(8,128)(2,1)S(1)}, bf16[2,144,768]{2,1,0:T(8,128)(2,1)S(1)}, u32[]{:S(2)}, u32[]{:S(2)}) %collective-permute-start.3) | collective-permute-done | bytes 442400 | tf_op jit(solution)/shard_map/ppermute | solution.py:361
  88.0 17.3 %all-to-all-done.1.in_ref = bf16[128,9,2,128]{3,2,1,0:T(2,128)(2,1)S(1)} async-done(((bf16[128,9,2,128]{3,2,1,0:T(2,128)(2,1)}), bf16[128,9,2,128]{3,2,1,0:T(2,128)(2,1)S(1)}, u32[]{:S(2)}, u32[]{:S(2)}) %all-to-all-start.1) | async-done | bytes 589856 | tf_op jit(solution)/shard_map/all_to_all | solution.py:333
  105.3 1.7 shard_map.86
  107.0 13.6 %all_to_all.30.in_ref = bf16[16,40,128]{2,1,0:T(8,128)(2,1)S(1)} all-to-all(bf16[16,40,128]{2,1,0:T(8,128)(2,1)S(1)} %get-tuple-element.29), channel_id=1, replica_groups={{6,4,2,0,134,132,130,128,262,260,258,256,390,388,386,384},{8,14,12,10,1..., dimensions={0} | all-to-all | bytes 327680 | tf_op jit(solution)/shard_map/all_to_all | solution.py:333
  120.6 0.6 shard_map.87
  121.2 3.3 %all-to-all-start.3 = ((bf16[4,40,128]{2,1,0:T(8,128)(2,1)}), bf16[4,40,128]{2,1,0:T(8,128)(2,1)S(1)}, u32[]{:S(2)}, u32[]{:S(2)}) async-start(bf16[4,40,128]{2,1,0:T(8,128)(2,1)} %shard_map.87), calls=%async_computation.3 | async-start | bytes 81920 | tf_op jit(solution)/shard_map/all_to_all | solution.py:333
  124.5 4.4 %collective-permute-start.4 = (bf16[4,96,128]{2,1,0:T(8,128)(2,1)S(1)}, bf16[4,96,128]{2,1,0:T(8,128)(2,1)S(1)}, u32[]{:S(2)}, u32[]{:S(2)}) collective-permute-start(bf16[4,96,128]{2,1,0:T(8,128)(2,1)S(1)} %get-tuple-element.32), channel_id=1, source_target_pairs={{0,1},{1,0},{2,3},{3,2},{4,5},{5,4},{6,7},{7,6},{8,9},{9,8},{10,11... | collective-permute-start | bytes 294920 | tf_op jit(solution)/shard_map/ppermute | solution.py:364
  128.9 1.0 shard_map.88
  129.9 0.0 collective-permute-done.4.got_ref
  129.9 4.3 %all-to-all-done.3.in_ref = bf16[4,40,128]{2,1,0:T(8,128)(2,1)S(1)} async-done(((bf16[4,40,128]{2,1,0:T(8,128)(2,1)}), bf16[4,40,128]{2,1,0:T(8,128)(2,1)S(1)}, u32[]{:S(2)}, u32[]{:S(2)}) %all-to-all-start.3) | async-done | bytes 40992 | tf_op jit(solution)/shard_map/all_to_all | solution.py:333
  134.2 11.6 %all_to_all.31.block_ref = bf16[16,40,128]{2,1,0:T(8,128)(2,1)S(1)} all-to-all(bf16[16,40,128]{2,1,0:T(8,128)(2,1)S(1)} %shard_map.89), channel_id=1, replica_groups={{6,4,2,0,134,132,130,128,262,260,258,256,390,388,386,384},{8,14,12,10,1..., dimensions={0} | all-to-all | bytes 327680 | tf_op jit(solution)/shard_map/all_to_all | solution.py:333
  145.9 0.1 shard_map.90
  146.0 0.0 copy-start
  146.0 0.0 copy-start.1
  146.0 11.0 %all_to_all.32.all_ref.mine_ref = bf16[4,768,128]{2,1,0:T(8,128)(2,1)S(1)} all-to-all(bf16[4,768,128]{2,1,0:T(8,128)(2,1)S(1)} %shard_map.90), channel_id=1, replica_groups=mesh['x'=4,'y'=4,'z'=16,'c'=2] {'y'}, dimensions={0} | all-to-all | bytes 1572864 | tf_op jit(solution)/shard_map/all_to_all | solution.py:333
  157.0 6.9 %collective-permute-start.5 = (bf16[4,768,128]{2,1,0:T(8,128)(2,1)S(1)}, bf16[4,768,128]{2,1,0:T(8,128)(2,1)S(1)}, u32[]{:S(2)}, u32[]{:S(2)}) collective-permute-start(bf16[4,768,128]{2,1,0:T(8,128)(2,1)S(1)} %all_to_all.32.all_ref.mine_ref), channel_id=1, source_target_pairs={{0,1},{1,0},{2,3},{3,2},{4,5},{5,4},{6,7},{7,6},{8,9},{9,8},{10,11... | collective-permute-start | bytes 2359304 | tf_op jit(solution)/shard_map/ppermute | solution.py:364
  163.9 0.0 copy-done
  163.9 0.0 copy-done.1
  163.9 1.8 %shard_map.91 = bf16[128,768]{1,0:T(8,128)(2,1)} custom-call(s32[2]{0:T(128)S(1)} %pad_add_fusion.place_ref, bf16[4,768,128]{2,1,0:T(8,128)(2,1)S(1)} %all_to_all.32.all_ref.mine_ref, bf16[768,384]{1,0:T(8,128)(2,1)S(1)} %copy-done, bf16[768,384]{1,0:T(8,128)(2,1)S(1)} %copy-done.1), custom_call_target="tpu_custom_call" | custom-call | tf_op jit(solution)/shard_map/pallas_call | solution.py:318
  165.7 0.1 collective-permute-done.5.other_ref
  165.8 1.7 %shard_map.92 = (bf16[768,384]{1,0:T(8,128)(2,1)}, bf16[768,384]{1,0:T(8,128)(2,1)}) custom-call(s32[2]{0:T(128)S(1)} %pad_add_fusion.place_ref, bf16[4,768,128]{2,1,0:T(8,128)(2,1)S(1)} %all_to_all.32.all_ref.mine_ref, bf16[4,768,128]{2,1,0:T(8,128)(2,1)S(1)} %collective-permute-done.5.other_ref), custom_call_target="tpu_custom_call" | custom-call | tf_op jit(solution)/shard_map/pallas_call | solution.py:318
  (2 shorter events, 0.1 us)
Async XLA Ops:
  3.8 55.1 %all-to-all-start = ((bf16[128,9,2,128]{3,2,1,0:T(2,128)(2,1)}), bf16[128,9,2,128]{3,2,1,0:T(2,128)(2,1)S(1)}, u32[]{:S(2)}, u32[]{:S(2)}) async-start(bf16[128,9,2,128]{3,2,1,0:T(2,128)(2,1)} %get-tuple-element.22), calls=%async_computation | async-start | bytes 1179648 | tf_op jit(solution)/shard_map/all_to_all | solution.py:333
  24.4 3.9 %collective-permute-start = (bf16[144,768]{1,0:T(8,128)(2,1)S(1)}, bf16[144,768]{1,0:T(8,128)(2,1)S(1)}, u32[]{:S(2)}, u32[]{:S(2)}) collective-permute-start(bf16[144,768]{1,0:T(8,128)(2,1)S(1)} %get-tuple-element.23), channel_id=1, source_target_pairs={{0,1},{1,0},{2,3},{3,2},{4,5},{5,4},{6,7},{7,6},{8,9},{9,8},{10,11... | collective-permute-start | bytes 663560 | tf_op jit(solution)/shard_map/ppermute | solution.py:364
  28.3 17.4 %collective-permute-start.1 = (bf16[2,144,768]{2,1,0:T(8,128)(2,1)S(1)}, bf16[2,144,768]{2,1,0:T(8,128)(2,1)S(1)}, u32[]{:S(2)}, u32[]{:S(2)}) collective-permute-start(bf16[2,144,768]{2,1,0:T(8,128)(2,1)S(1)} %pad_maximum_fusion.refs_0_.ext_ref), channel_id=1, source_target_pairs={{0,32},{32,64},{64,96},{96,0},{1,33},{33,65},{65,97},{97,1},{2,34}... | collective-permute-start | bytes 1327112 | tf_op jit(solution)/shard_map/ppermute | solution.py:361
  31.3 15.7 %collective-permute-start.2 = (bf16[2,144,768]{2,1,0:T(8,128)(2,1)S(1)}, bf16[2,144,768]{2,1,0:T(8,128)(2,1)S(1)}, u32[]{:S(2)}, u32[]{:S(2)}) collective-permute-start(bf16[2,144,768]{2,1,0:T(8,128)(2,1)S(1)} %pad_maximum_fusion.refs_0_.ext_ref), channel_id=1, source_target_pairs={{0,96},{32,0},{64,32},{96,64},{1,97},{33,1},{65,33},{97,65},{2,98}... | collective-permute-start | bytes 1327112 | tf_op jit(solution)/shard_map/ppermute | solution.py:361
  62.6 42.7 %all-to-all-start.1 = ((bf16[128,9,2,128]{3,2,1,0:T(2,128)(2,1)}), bf16[128,9,2,128]{3,2,1,0:T(2,128)(2,1)S(1)}, u32[]{:S(2)}, u32[]{:S(2)}) async-start(bf16[128,9,2,128]{3,2,1,0:T(2,128)(2,1)} %shard_map.85), calls=%async_computation.1 | async-start | bytes 1179648 | tf_op jit(solution)/shard_map/all_to_all | solution.py:333
  70.8 17.2 %collective-permute-start.3 = (bf16[2,144,768]{2,1,0:T(8,128)(2,1)S(1)}, bf16[2,144,768]{2,1,0:T(8,128)(2,1)S(1)}, u32[]{:S(2)}, u32[]{:S(2)}) collective-permute-start(bf16[2,144,768]{2,1,0:T(8,128)(2,1)S(1)} %pad_maximum_fusion.refs_0_.ext_ref), channel_id=1, source_target_pairs={{0,64},{32,96},{64,0},{96,32},{1,65},{33,97},{65,1},{97,33},{2,66}... | collective-permute-start | bytes 1327112 | tf_op jit(solution)/shard_map/ppermute | solution.py:361
  121.2 13.0 %all-to-all-start.3 = ((bf16[4,40,128]{2,1,0:T(8,128)(2,1)}), bf16[4,40,128]{2,1,0:T(8,128)(2,1)S(1)}, u32[]{:S(2)}, u32[]{:S(2)}) async-start(bf16[4,40,128]{2,1,0:T(8,128)(2,1)} %shard_map.87), calls=%async_computation.3 | async-start | bytes 81920 | tf_op jit(solution)/shard_map/all_to_all | solution.py:333
  124.5 5.4 %collective-permute-start.4 = (bf16[4,96,128]{2,1,0:T(8,128)(2,1)S(1)}, bf16[4,96,128]{2,1,0:T(8,128)(2,1)S(1)}, u32[]{:S(2)}, u32[]{:S(2)}) collective-permute-start(bf16[4,96,128]{2,1,0:T(8,128)(2,1)S(1)} %get-tuple-element.32), channel_id=1, source_target_pairs={{0,1},{1,0},{2,3},{3,2},{4,5},{5,4},{6,7},{7,6},{8,9},{9,8},{10,11... | collective-permute-start | bytes 294920 | tf_op jit(solution)/shard_map/ppermute | solution.py:364
  146.0 18.0 %copy-start = (bf16[768,384]{1,0:T(8,128)(2,1)S(1)}, bf16[768,384]{1,0:T(8,128)(2,1)}, u32[]{:S(2)}) copy-start(bf16[768,384]{1,0:T(8,128)(2,1)} %ws_ref.1) | copy-start | bytes 1769476
  146.0 18.0 %copy-start.1 = (bf16[768,384]{1,0:T(8,128)(2,1)S(1)}, bf16[768,384]{1,0:T(8,128)(2,1)}, u32[]{:S(2)}) copy-start(bf16[768,384]{1,0:T(8,128)(2,1)} %wv_ref.1) | copy-start | bytes 1769476
  157.0 8.8 %collective-permute-start.5 = (bf16[4,768,128]{2,1,0:T(8,128)(2,1)S(1)}, bf16[4,768,128]{2,1,0:T(8,128)(2,1)S(1)}, u32[]{:S(2)}, u32[]{:S(2)}) collective-permute-start(bf16[4,768,128]{2,1,0:T(8,128)(2,1)S(1)} %all_to_all.32.all_ref.mine_ref), channel_id=1, source_target_pairs={{0,1},{1,0},{2,3},{3,2},{4,5},{5,4},{6,7},{7,6},{8,9},{9,8},{10,11... | collective-permute-start | bytes 2359304 | tf_op jit(solution)/shard_map/ppermute | solution.py:364

commit v14 on v13

--- a/solution.py
+++ b/solution.py
@@ -364,10 +364,9 @@
         return lax.ppermute(part, "c", [(0, 1), (1, 0)])
 
     arrived = swap(sent, OWNERS)
+    arrived, ext = lax.optimization_barrier((arrived, ext))
     pair = jnp.stack([ext, flip(ext)])
-    near = (shift(pair, 1), shift(pair, 3))
-    arrived, pair, near, place = lax.optimization_barrier((arrived, pair, near, place))
-    exts = [pair, near[0], shift(pair, 2), near[1]]
+    exts = [pair] + [shift(pair, dy) for dy in range(1, 4)]
     arrived = arrived.transpose(1, 0, 2, 3).reshape(9, ROWS, LOCAL)
     (worked,) = call(
         attend_kernel,

time: 168 us -> 172 us (1.024)
  blocking collectives: 36.2 us -> 90.7 us
  waiting for transfers between devices: 58.9 us -> 25.8 us
  starting transfers between devices: 57.9 us -> 41.6 us
    all_to_all x3 -> x4, blocking collectives: 36.2 us -> 90.7 us  [swap(): lax.all_to_all(rows, axes, split_axis=0, concat_axis=0, tiled=True, axis_...]
    all_to_all x3 -> x2, waiting for transfers between devices: 33.6 us -> 4.37 us  [swap(): lax.all_to_all(rows, axes, split_axis=0, concat_axis=0, tiled=True, axis_...]
    all_to_all x3 -> x2, starting transfers between devices: 32 us -> 15.4 us  [swap(): lax.all_to_all(rows, axes, split_axis=0, concat_axis=0, tiled=True, axis_...]
    ppermute x3, waiting for transfers between devices: 24.1 us -> 20.2 us  [shift(): return lax.ppermute(pair, 'y', [(y, (y + dy) % 4) for y in range(4)])]
  transfers between devices with their start and end apart: 9 -> 8, of which waited for: 8 -> 6; matrix products, arithmetic and copies ran while one was open for 0% -> 0% of each run, Pallas kernels for 2% -> 2%
where the time goes in v14:
time: 172 us
  blocking collectives  90.7 us (53%)
  starting transfers between devices  41.6 us (24%)
  waiting for transfers between devices  25.8 us (15%)
  Pallas kernels  12.5 us (7%)
    all_to_all x4, blocking collectives, swap(): lax.all_to_all(rows, axes, split_axis=0, concat_axis=0, tiled=True, axis_...  90.7 us
    ppermute x3, waiting for transfers between devices, shift(): return lax.ppermute(pair, 'y', [(y, (y + dy) % 4) for y in range(4)])  20.2 us
    ppermute x3, starting transfers between devices, flip(): return lax.ppermute(part, 'c', [(0, 1), (1, 0)])  15.7 us
    all_to_all x2, starting transfers between devices, swap(): lax.all_to_all(rows, axes, split_axis=0, concat_axis=0, tiled=True, axis_...  15.4 us
    pallas_call x9, Pallas kernels, call(): pl.pallas_call(kernel, out_shape=out, in_specs=specs, out_specs=outs, scr...  12.5 us
    ppermute x3, starting transfers between devices, shift(): return lax.ppermute(pair, 'y', [(y, (y + dy) % 4) for y in range(4)])  10.6 us
    all_to_all x2, waiting for transfers between devices, swap(): lax.all_to_all(rows, axes, split_axis=0, concat_axis=0, tiled=True, axis_...  4.37 us
  transfers between devices with their start and end apart: 8, of which 6 were waited for; matrix products, arithmetic and copies ran while one was open for 0% of the time, Pallas kernels for 2%

profile of v14, /device:TPU:1, one launch (start us, length us, event | category | flops | bytes accessed | tf_op | source)
XLA Modules:
  0.0 171.9 jit_solution(5268000922051461709)
XLA Ops:
  0.6 2.4 %shard_map.84 = (bf16[128,9,2,128]{3,2,1,0:T(2,128)(2,1)S(1)}, bf16[144,768]{1,0:T(8,128)(2,1)S(1)}) custom-call(s32[6,1,128]{2,1,0:T(1,128)} %bitcast.19, bf16[128,768]{1,0:T(8,128)(2,1)} %bitcast.15, bf16[768,384]{1,0:T(8,128)(2,1)} %ws_ref.1, bf16[768,384]{1,0:T(8,128)(2,1)} %wv_ref.1, bf16[128,384]{1,0:T(8,128)(2,1)} %bitcast.17), custom_call_target="tpu_custom_call" | custom-call | tf_op jit(solution)/shard_map/pallas_call | solution.py:318
  3.0 54.9 %all_to_all.30 = bf16[128,9,2,128]{3,2,1,0:T(2,128)(2,1)S(1)} all-to-all(bf16[128,9,2,128]{3,2,1,0:T(2,128)(2,1)S(1)} %get-tuple-element.19), channel_id=1, replica_groups=mesh['x'=4,'y'=4,'z'=16,'c'=2] {'y','c','z'}, dimensions={0} | all-to-all | bytes 1179648 | tf_op jit(solution)/shard_map/all_to_all | solution.py:333
  57.9 0.5 copy.9
  58.4 3.2 %shard_map.85 = bf16[128,9,2,128]{3,2,1,0:T(2,128)(2,1)} custom-call(bf16[9,256,128]{2,1,0:T(8,128)(2,1)S(1)} %bitcast.11), custom_call_target="tpu_custom_call" | custom-call | tf_op jit(solution)/shard_map/pallas_call | solution.py:318
  61.6 8.2 %all-to-all-start.1 = ((bf16[128,9,2,128]{3,2,1,0:T(2,128)(2,1)}), bf16[128,9,2,128]{3,2,1,0:T(2,128)(2,1)S(1)}, u32[]{:S(2)}, u32[]{:S(2)}) async-start(bf16[128,9,2,128]{3,2,1,0:T(2,128)(2,1)} %shard_map.85), calls=%async_computation.1 | async-start | bytes 1179648 | tf_op jit(solution)/shard_map/all_to_all | solution.py:333
  69.8 2.8 %collective-permute-start = (bf16[144,768]{1,0:T(8,128)(2,1)S(1)}, bf16[144,768]{1,0:T(8,128)(2,1)S(1)}, u32[]{:S(2)}, u32[]{:S(2)}) collective-permute-start(bf16[144,768]{1,0:T(8,128)(2,1)S(1)} %get-tuple-element.22), channel_id=1, source_target_pairs={{0,1},{1,0},{2,3},{3,2},{4,5},{5,4},{6,7},{7,6},{8,9},{9,8},{10,11... | collective-permute-start | bytes 663560 | tf_op jit(solution)/shard_map/ppermute | solution.py:364
  72.6 1.1 collective-permute-done
  73.7 2.9 %collective-permute-start.1 = (bf16[2,144,768]{2,1,0:T(8,128)(2,1)S(1)}, bf16[2,144,768]{2,1,0:T(8,128)(2,1)S(1)}, u32[]{:S(2)}, u32[]{:S(2)}) collective-permute-start(bf16[2,144,768]{2,1,0:T(8,128)(2,1)S(1)} %pad_maximum_fusion.refs_0_.ext_ref), channel_id=1, source_target_pairs={{0,32},{32,64},{64,96},{96,0},{1,33},{33,65},{65,97},{97,1},{2,34}... | collective-permute-start | bytes 1327112 | tf_op jit(solution)/shard_map/ppermute | solution.py:361
  76.7 4.7 %collective-permute-start.2 = (bf16[2,144,768]{2,1,0:T(8,128)(2,1)S(1)}, bf16[2,144,768]{2,1,0:T(8,128)(2,1)S(1)}, u32[]{:S(2)}, u32[]{:S(2)}) collective-permute-start(bf16[2,144,768]{2,1,0:T(8,128)(2,1)S(1)} %pad_maximum_fusion.refs_0_.ext_ref), channel_id=1, source_target_pairs={{0,64},{32,96},{64,0},{96,32},{1,65},{33,97},{65,1},{97,33},{2,66}... | collective-permute-start | bytes 1327112 | tf_op jit(solution)/shard_map/ppermute | solution.py:361
  81.4 2.9 %collective-permute-start.3 = (bf16[2,144,768]{2,1,0:T(8,128)(2,1)S(1)}, bf16[2,144,768]{2,1,0:T(8,128)(2,1)S(1)}, u32[]{:S(2)}, u32[]{:S(2)}) collective-permute-start(bf16[2,144,768]{2,1,0:T(8,128)(2,1)S(1)} %pad_maximum_fusion.refs_0_.ext_ref), channel_id=1, source_target_pairs={{0,96},{32,0},{64,32},{96,64},{1,97},{33,1},{65,33},{97,65},{2,98}... | collective-permute-start | bytes 1327112 | tf_op jit(solution)/shard_map/ppermute | solution.py:361
  84.3 0.1 pad_add_fusion.place_ref
  84.4 6.7 %collective-permute-done.1.refs_1_ = bf16[2,144,768]{2,1,0:T(8,128)(2,1)S(1)} collective-permute-done((bf16[2,144,768]{2,1,0:T(8,128)(2,1)S(1)}, bf16[2,144,768]{2,1,0:T(8,128)(2,1)S(1)}, u32[]{:S(2)}, u32[]{:S(2)}) %collective-permute-start.1) | collective-permute-done | bytes 442400 | tf_op jit(solution)/shard_map/ppermute | solution.py:361
  91.1 12.9 %collective-permute-done.2.refs_2_ = bf16[2,144,768]{2,1,0:T(8,128)(2,1)S(1)} collective-permute-done((bf16[2,144,768]{2,1,0:T(8,128)(2,1)S(1)}, bf16[2,144,768]{2,1,0:T(8,128)(2,1)S(1)}, u32[]{:S(2)}, u32[]{:S(2)}) %collective-permute-start.2) | collective-permute-done | bytes 442400 | tf_op jit(solution)/shard_map/ppermute | solution.py:361
  104.0 0.6 collective-permute-done.3.refs_3_
  104.6 0.0 all-to-all-done.1.in_ref
  104.6 1.7 shard_map.86
  106.3 13.2 %all_to_all.31.in_ref = bf16[16,40,128]{2,1,0:T(8,128)(2,1)S(1)} all-to-all(bf16[16,40,128]{2,1,0:T(8,128)(2,1)S(1)} %get-tuple-element.23), channel_id=1, replica_groups={{6,4,2,0,134,132,130,128,262,260,258,256,390,388,386,384},{8,14,12,10,1..., dimensions={0} | all-to-all | bytes 327680 | tf_op jit(solution)/shard_map/all_to_all | solution.py:333
  119.5 0.6 shard_map.87
  120.2 7.2 %all-to-all-start.3 = ((bf16[4,40,128]{2,1,0:T(8,128)(2,1)}), bf16[4,40,128]{2,1,0:T(8,128)(2,1)S(1)}, u32[]{:S(2)}, u32[]{:S(2)}) async-start(bf16[4,40,128]{2,1,0:T(8,128)(2,1)} %shard_map.87), calls=%async_computation.3 | async-start | bytes 81920 | tf_op jit(solution)/shard_map/all_to_all | solution.py:333
  127.4 4.4 %collective-permute-start.4 = (bf16[4,96,128]{2,1,0:T(8,128)(2,1)S(1)}, bf16[4,96,128]{2,1,0:T(8,128)(2,1)S(1)}, u32[]{:S(2)}, u32[]{:S(2)}) collective-permute-start(bf16[4,96,128]{2,1,0:T(8,128)(2,1)S(1)} %get-tuple-element.26), channel_id=1, source_target_pairs={{0,1},{1,0},{2,3},{3,2},{4,5},{5,4},{6,7},{7,6},{8,9},{9,8},{10,11... | collective-permute-start | bytes 294920 | tf_op jit(solution)/shard_map/ppermute | solution.py:364
  131.8 1.0 shard_map.88
  132.8 0.0 collective-permute-done.4.got_ref
  132.8 4.4 %all-to-all-done.3.in_ref = bf16[4,40,128]{2,1,0:T(8,128)(2,1)S(1)} async-done(((bf16[4,40,128]{2,1,0:T(8,128)(2,1)}), bf16[4,40,128]{2,1,0:T(8,128)(2,1)S(1)}, u32[]{:S(2)}, u32[]{:S(2)}) %all-to-all-start.3) | async-done | bytes 40992 | tf_op jit(solution)/shard_map/all_to_all | solution.py:333
  137.2 10.3 %all_to_all.32.block_ref = bf16[16,40,128]{2,1,0:T(8,128)(2,1)S(1)} all-to-all(bf16[16,40,128]{2,1,0:T(8,128)(2,1)S(1)} %shard_map.89), channel_id=1, replica_groups={{6,4,2,0,134,132,130,128,262,260,258,256,390,388,386,384},{8,14,12,10,1..., dimensions={0} | all-to-all | bytes 327680 | tf_op jit(solution)/shard_map/all_to_all | solution.py:333
  147.4 0.1 shard_map.90
  147.5 0.0 copy-start
  147.5 0.0 copy-start.1
  147.5 12.3 %all_to_all.33.all_ref.mine_ref = bf16[4,768,128]{2,1,0:T(8,128)(2,1)S(1)} all-to-all(bf16[4,768,128]{2,1,0:T(8,128)(2,1)S(1)} %shard_map.90), channel_id=1, replica_groups=mesh['x'=4,'y'=4,'z'=16,'c'=2] {'y'}, dimensions={0} | all-to-all | bytes 1572864 | tf_op jit(solution)/shard_map/all_to_all | solution.py:333
  159.8 8.5 %collective-permute-start.5 = (bf16[4,768,128]{2,1,0:T(8,128)(2,1)S(1)}, bf16[4,768,128]{2,1,0:T(8,128)(2,1)S(1)}, u32[]{:S(2)}, u32[]{:S(2)}) collective-permute-start(bf16[4,768,128]{2,1,0:T(8,128)(2,1)S(1)} %all_to_all.33.all_ref.mine_ref), channel_id=1, source_target_pairs={{0,1},{1,0},{2,3},{3,2},{4,5},{5,4},{6,7},{7,6},{8,9},{9,8},{10,11... | collective-permute-start | bytes 2359304 | tf_op jit(solution)/shard_map/ppermute | solution.py:364
  168.3 0.0 copy-done
  168.3 0.0 copy-done.1
  168.3 1.8 %shard_map.91 = bf16[128,768]{1,0:T(8,128)(2,1)} custom-call(s32[2]{0:T(128)S(1)} %pad_add_fusion.place_ref, bf16[4,768,128]{2,1,0:T(8,128)(2,1)S(1)} %all_to_all.33.all_ref.mine_ref, bf16[768,384]{1,0:T(8,128)(2,1)S(1)} %copy-done, bf16[768,384]{1,0:T(8,128)(2,1)S(1)} %copy-done.1), custom_call_target="tpu_custom_call" | custom-call | tf_op jit(solution)/shard_map/pallas_call | solution.py:318
  170.1 0.1 collective-permute-done.5.other_ref
  170.2 1.7 %shard_map.92 = (bf16[768,384]{1,0:T(8,128)(2,1)}, bf16[768,384]{1,0:T(8,128)(2,1)}) custom-call(s32[2]{0:T(128)S(1)} %pad_add_fusion.place_ref, bf16[4,768,128]{2,1,0:T(8,128)(2,1)S(1)} %all_to_all.33.all_ref.mine_ref, bf16[4,768,128]{2,1,0:T(8,128)(2,1)S(1)} %collective-permute-done.5.other_ref), custom_call_target="tpu_custom_call" | custom-call | tf_op jit(solution)/shard_map/pallas_call | solution.py:318
  (2 shorter events, 0.1 us)
Async XLA Ops:
  61.6 43.0 %all-to-all-start.1 = ((bf16[128,9,2,128]{3,2,1,0:T(2,128)(2,1)}), bf16[128,9,2,128]{3,2,1,0:T(2,128)(2,1)S(1)}, u32[]{:S(2)}, u32[]{:S(2)}) async-start(bf16[128,9,2,128]{3,2,1,0:T(2,128)(2,1)} %shard_map.85), calls=%async_computation.1 | async-start | bytes 1179648 | tf_op jit(solution)/shard_map/all_to_all | solution.py:333
  69.8 3.9 %collective-permute-start = (bf16[144,768]{1,0:T(8,128)(2,1)S(1)}, bf16[144,768]{1,0:T(8,128)(2,1)S(1)}, u32[]{:S(2)}, u32[]{:S(2)}) collective-permute-start(bf16[144,768]{1,0:T(8,128)(2,1)S(1)} %get-tuple-element.22), channel_id=1, source_target_pairs={{0,1},{1,0},{2,3},{3,2},{4,5},{5,4},{6,7},{7,6},{8,9},{9,8},{10,11... | collective-permute-start | bytes 663560 | tf_op jit(solution)/shard_map/ppermute | solution.py:364
  73.7 17.4 %collective-permute-start.1 = (bf16[2,144,768]{2,1,0:T(8,128)(2,1)S(1)}, bf16[2,144,768]{2,1,0:T(8,128)(2,1)S(1)}, u32[]{:S(2)}, u32[]{:S(2)}) collective-permute-start(bf16[2,144,768]{2,1,0:T(8,128)(2,1)S(1)} %pad_maximum_fusion.refs_0_.ext_ref), channel_id=1, source_target_pairs={{0,32},{32,64},{64,96},{96,0},{1,33},{33,65},{65,97},{97,1},{2,34}... | collective-permute-start | bytes 1327112 | tf_op jit(solution)/shard_map/ppermute | solution.py:361
  76.7 27.4 %collective-permute-start.2 = (bf16[2,144,768]{2,1,0:T(8,128)(2,1)S(1)}, bf16[2,144,768]{2,1,0:T(8,128)(2,1)S(1)}, u32[]{:S(2)}, u32[]{:S(2)}) collective-permute-start(bf16[2,144,768]{2,1,0:T(8,128)(2,1)S(1)} %pad_maximum_fusion.refs_0_.ext_ref), channel_id=1, source_target_pairs={{0,64},{32,96},{64,0},{96,32},{1,65},{33,97},{65,1},{97,33},{2,66}... | collective-permute-start | bytes 1327112 | tf_op jit(solution)/shard_map/ppermute | solution.py:361
  81.4 23.2 %collective-permute-start.3 = (bf16[2,144,768]{2,1,0:T(8,128)(2,1)S(1)}, bf16[2,144,768]{2,1,0:T(8,128)(2,1)S(1)}, u32[]{:S(2)}, u32[]{:S(2)}) collective-permute-start(bf16[2,144,768]{2,1,0:T(8,128)(2,1)S(1)} %pad_maximum_fusion.refs_0_.ext_ref), channel_id=1, source_target_pairs={{0,96},{32,0},{64,32},{96,64},{1,97},{33,1},{65,33},{97,65},{2,98}... | collective-permute-start | bytes 1327112 | tf_op jit(solution)/shard_map/ppermute | solution.py:361
  120.2 16.9 %all-to-all-start.3 = ((bf16[4,40,128]{2,1,0:T(8,128)(2,1)}), bf16[4,40,128]{2,1,0:T(8,128)(2,1)S(1)}, u32[]{:S(2)}, u32[]{:S(2)}) async-start(bf16[4,40,128]{2,1,0:T(8,128)(2,1)} %shard_map.87), calls=%async_computation.3 | async-start | bytes 81920 | tf_op jit(solution)/shard_map/all_to_all | solution.py:333
  127.4 5.4 %collective-permute-start.4 = (bf16[4,96,128]{2,1,0:T(8,128)(2,1)S(1)}, bf16[4,96,128]{2,1,0:T(8,128)(2,1)S(1)}, u32[]{:S(2)}, u32[]{:S(2)}) collective-permute-start(bf16[4,96,128]{2,1,0:T(8,128)(2,1)S(1)} %get-tuple-element.26), channel_id=1, source_target_pairs={{0,1},{1,0},{2,3},{3,2},{4,5},{5,4},{6,7},{7,6},{8,9},{9,8},{10,11... | collective-permute-start | bytes 294920 | tf_op jit(solution)/shard_map/ppermute | solution.py:364
  147.5 20.8 %copy-start = (bf16[768,384]{1,0:T(8,128)(2,1)S(1)}, bf16[768,384]{1,0:T(8,128)(2,1)}, u32[]{:S(2)}) copy-start(bf16[768,384]{1,0:T(8,128)(2,1)} %ws_ref.1) | copy-start | bytes 1769476
  147.5 20.8 %copy-start.1 = (bf16[768,384]{1,0:T(8,128)(2,1)S(1)}, bf16[768,384]{1,0:T(8,128)(2,1)}, u32[]{:S(2)}) copy-start(bf16[768,384]{1,0:T(8,128)(2,1)} %wv_ref.1) | copy-start | bytes 1769476
  159.8 10.4 %collective-permute-start.5 = (bf16[4,768,128]{2,1,0:T(8,128)(2,1)S(1)}, bf16[4,768,128]{2,1,0:T(8,128)(2,1)S(1)}, u32[]{:S(2)}, u32[]{:S(2)}) collective-permute-start(bf16[4,768,128]{2,1,0:T(8,128)(2,1)S(1)} %all_to_all.33.all_ref.mine_ref), channel_id=1, source_target_pairs={{0,1},{1,0},{2,3},{3,2},{4,5},{5,4},{6,7},{7,6},{8,9},{9,8},{10,11... | collective-permute-start | bytes 2359304 | tf_op jit(solution)/shard_map/ppermute | solution.py:364

commit v15 on v14

--- a/solution.py
+++ b/solution.py
@@ -186,7 +186,7 @@
 
 
 def partial_kernel(place_ref, in_ref, *refs):
-    exts, (out_ref, keep_ref, give_ref), (dests, cols, scratch) = refs[:4], refs[4:7], refs[7:]
+    exts, (out_ref, keep_ref, give_ref), (dests, cols, scratch) = refs[:2], refs[2:5], refs[5:]
     here = place_ref[1]
     j = place_ref[0] * 2 + here
     head = (j * 3 // 4, (j * 6 + 5) // 8)
@@ -196,7 +196,7 @@
         source = index_of(place_ref, 4 - dy, dc)
         for i in range(2):
             lanes = pl.ds(pl.multiple_of(head[i] * LOCAL, LOCAL), LOCAL)
-            dests[i, source] = exts[n // 2][n % 2, LOCAL:, lanes].astype(F32)[:8]
+            dests[i, source] = exts[dc][dy, LOCAL:, lanes].astype(F32)[:8]
     turned = [in_ref[:, b].reshape(ROWS, LOCAL) for b in range(6)]
     turned = [pltpu.roll(rows.astype(F32), BLOCK * b, 1).astype(BF16) if b else rows for b, rows in enumerate(turned)]
     limit = lax.rem(j, 4)
@@ -215,7 +215,7 @@
     total = None
     for dy in range(4):
         near = [cols[index_of(place_ref, 4 - dy, dc)] for dc in range(2)]
-        rows = exts[dy][:, :LOCAL, :].reshape(2 * LOCAL, WIDTH)
+        rows = jnp.concatenate([exts[dc][dy, :LOCAL, :] for dc in range(2)], axis=0)
         term = dot(jnp.concatenate(near, axis=1), rows)
         total = term if total is None else total + term
     for k in range(WIDTH // LOCAL):
@@ -365,8 +365,8 @@
 
     arrived = swap(sent, OWNERS)
     arrived, ext = lax.optimization_barrier((arrived, ext))
-    pair = jnp.stack([ext, flip(ext)])
-    exts = [pair] + [shift(pair, dy) for dy in range(1, 4)]
+    mine = jnp.stack([ext] + [shift(ext, dy) for dy in range(1, 4)])
+    exts = [mine, flip(mine)]
     arrived = arrived.transpose(1, 0, 2, 3).reshape(9, ROWS, LOCAL)
     (worked,) = call(
         attend_kernel,
@@ -389,7 +389,7 @@
     )
     part = swap(part, ("x", "z"), NEAR)
     part, back, give = lax.optimization_barrier((part, back, give))
-    (attention,) = call(output_kernel, [shape(LOCAL, PROJ)], back, pair)
+    (attention,) = call(output_kernel, [shape(LOCAL, PROJ)], back, mine)
     (part,) = call(sum_kernel, [shape(4, SLOT, LOCAL)], part)
     part = swap(part, "z", FAR)
     part, got, attention = lax.optimization_barrier((part, flip(give), attention))

time: 172 us -> 167 us (0.971)
  starting transfers between devices: 41.6 us -> 36.6 us
    ppermute x3, waiting for transfers between devices: 20.2 us -> 11.9 us  [shift(): return lax.ppermute(pair, 'y', [(y, (y + dy) % 4) for y in range(4)])]
    all_to_all x2, waiting for transfers between devices: 4.37 us -> 11.1 us  [swap(): lax.all_to_all(rows, axes, split_axis=0, concat_axis=0, tiled=True, axis_...]
    all_to_all x2, starting transfers between devices: 15.4 us -> 11.5 us  [swap(): lax.all_to_all(rows, axes, split_axis=0, concat_axis=0, tiled=True, axis_...]
where the time goes in v15:
time: 167 us
  blocking collectives  91.1 us (55%)
  starting transfers between devices  36.6 us (22%)
  waiting for transfers between devices  25 us (15%)
  Pallas kernels  12.4 us (7%)
    all_to_all x4, blocking collectives, swap(): lax.all_to_all(rows, axes, split_axis=0, concat_axis=0, tiled=True, axis_...  91.1 us
    ppermute x3, starting transfers between devices, flip(): return lax.ppermute(part, 'c', [(0, 1), (1, 0)])  14.6 us
    pallas_call x9, Pallas kernels, call(): pl.pallas_call(kernel, out_shape=out, in_specs=specs, out_specs=outs, scr...  12.4 us
    ppermute x3, waiting for transfers between devices, shift(): return lax.ppermute(pair, 'y', [(y, (y + dy) % 4) for y in range(4)])  11.9 us
    all_to_all x2, starting transfers between devices, swap(): lax.all_to_all(rows, axes, split_axis=0, concat_axis=0, tiled=True, axis_...  11.5 us
    all_to_all x2, waiting for transfers between devices, swap(): lax.all_to_all(rows, axes, split_axis=0, concat_axis=0, tiled=True, axis_...  11.1 us
    ppermute x3, starting transfers between devices, shift(): return lax.ppermute(pair, 'y', [(y, (y + dy) % 4) for y in range(4)])  10.5 us
  transfers between devices with their start and end apart: 8, of which 6 were waited for; matrix products, arithmetic and copies ran while one was open for 0% of the time, Pallas kernels for 2%

profile of v15, /device:TPU:1, one launch (start us, length us, event | category | flops | bytes accessed | tf_op | source)
XLA Modules:
  0.0 166.5 jit_solution(1919513680708222021)
XLA Ops:
  0.6 2.4 %shard_map.84 = (bf16[128,9,2,128]{3,2,1,0:T(2,128)(2,1)S(1)}, bf16[144,768]{1,0:T(8,128)(2,1)S(1)}) custom-call(s32[6,1,128]{2,1,0:T(1,128)} %bitcast.23, bf16[128,768]{1,0:T(8,128)(2,1)} %bitcast.19, bf16[768,384]{1,0:T(8,128)(2,1)} %ws_ref.1, bf16[768,384]{1,0:T(8,128)(2,1)} %wv_ref.1, bf16[128,384]{1,0:T(8,128)(2,1)} %bitcast.21), custom_call_target="tpu_custom_call" | custom-call | tf_op jit(solution)/shard_map/pallas_call | solution.py:318
  3.0 54.9 %all_to_all.30 = bf16[128,9,2,128]{3,2,1,0:T(2,128)(2,1)S(1)} all-to-all(bf16[128,9,2,128]{3,2,1,0:T(2,128)(2,1)S(1)} %get-tuple-element.19), channel_id=1, replica_groups=mesh['x'=4,'y'=4,'z'=16,'c'=2] {'y','c','z'}, dimensions={0} | all-to-all | bytes 1179648 | tf_op jit(solution)/shard_map/all_to_all | solution.py:333
  57.9 0.5 copy.9
  58.4 3.2 %shard_map.85 = bf16[128,9,2,128]{3,2,1,0:T(2,128)(2,1)} custom-call(bf16[9,256,128]{2,1,0:T(8,128)(2,1)S(1)} %bitcast.13), custom_call_target="tpu_custom_call" | custom-call | tf_op jit(solution)/shard_map/pallas_call | solution.py:318
  61.6 8.2 %all-to-all-start.1 = ((bf16[128,9,2,128]{3,2,1,0:T(2,128)(2,1)}), bf16[128,9,2,128]{3,2,1,0:T(2,128)(2,1)S(1)}, u32[]{:S(2)}, u32[]{:S(2)}) async-start(bf16[128,9,2,128]{3,2,1,0:T(2,128)(2,1)} %shard_map.85), calls=%async_computation.1 | async-start | bytes 1179648 | tf_op jit(solution)/shard_map/all_to_all | solution.py:333
  69.8 5.1 %collective-permute-start.2 = (bf16[144,768]{1,0:T(8,128)(2,1)S(1)}, bf16[144,768]{1,0:T(8,128)(2,1)S(1)}, u32[]{:S(2)}, u32[]{:S(2)}) collective-permute-start(bf16[144,768]{1,0:T(8,128)(2,1)S(1)} %get-tuple-element.22), channel_id=1, source_target_pairs={{0,96},{32,0},{64,32},{96,64},{1,97},{33,1},{65,33},{97,65},{2,98}... | collective-permute-start | bytes 663560 | tf_op jit(solution)/shard_map/ppermute | solution.py:361
  74.9 1.9 %collective-permute-start = (bf16[144,768]{1,0:T(8,128)(2,1)S(1)}, bf16[144,768]{1,0:T(8,128)(2,1)S(1)}, u32[]{:S(2)}, u32[]{:S(2)}) collective-permute-start(bf16[144,768]{1,0:T(8,128)(2,1)S(1)} %get-tuple-element.22), channel_id=1, source_target_pairs={{0,32},{32,64},{64,96},{96,0},{1,33},{33,65},{65,97},{97,1},{2,34}... | collective-permute-start | bytes 663560 | tf_op jit(solution)/shard_map/ppermute | solution.py:361
  76.8 3.4 %collective-permute-start.1 = (bf16[144,768]{1,0:T(8,128)(2,1)S(1)}, bf16[144,768]{1,0:T(8,128)(2,1)S(1)}, u32[]{:S(2)}, u32[]{:S(2)}) collective-permute-start(bf16[144,768]{1,0:T(8,128)(2,1)S(1)} %get-tuple-element.22), channel_id=1, source_target_pairs={{0,64},{32,96},{64,0},{96,32},{1,65},{33,97},{65,1},{97,33},{2,66}... | collective-permute-start | bytes 663560 | tf_op jit(solution)/shard_map/ppermute | solution.py:361
  80.3 0.3 collective-permute-done.2
  80.5 11.6 %collective-permute-done = bf16[144,768]{1,0:T(8,128)(2,1)S(1)} collective-permute-done((bf16[144,768]{1,0:T(8,128)(2,1)S(1)}, bf16[144,768]{1,0:T(8,128)(2,1)S(1)}, u32[]{:S(2)}, u32[]{:S(2)}) %collective-permute-start) | collective-permute-done | bytes 221216 | tf_op jit(solution)/shard_map/ppermute | solution.py:361
  92.1 0.0 collective-permute-done.1
  92.1 0.1 pad_maximum_fusion.refs_0_.ext_ref
  92.2 3.3 %collective-permute-start.3 = (bf16[4,144,768]{2,1,0:T(8,128)(2,1)S(1)}, bf16[4,144,768]{2,1,0:T(8,128)(2,1)S(1)}, u32[]{:S(2)}, u32[]{:S(2)}) collective-permute-start(bf16[4,144,768]{2,1,0:T(8,128)(2,1)S(1)} %pad_maximum_fusion.refs_0_.ext_ref), channel_id=1, source_target_pairs={{0,1},{1,0},{2,3},{3,2},{4,5},{5,4},{6,7},{7,6},{8,9},{9,8},{10,11... | collective-permute-start | bytes 2654216 | tf_op jit(solution)/shard_map/ppermute | solution.py:364
  95.6 0.1 pad_add_fusion.place_ref
  95.6 1.9 %collective-permute-done.3.refs_1_ = bf16[4,144,768]{2,1,0:T(8,128)(2,1)S(1)} collective-permute-done((bf16[4,144,768]{2,1,0:T(8,128)(2,1)S(1)}, bf16[4,144,768]{2,1,0:T(8,128)(2,1)S(1)}, u32[]{:S(2)}, u32[]{:S(2)}) %collective-permute-start.3) | collective-permute-done | bytes 884768 | tf_op jit(solution)/shard_map/ppermute | solution.py:364
  97.6 6.7 %all-to-all-done.1.in_ref = bf16[128,9,2,128]{3,2,1,0:T(2,128)(2,1)S(1)} async-done(((bf16[128,9,2,128]{3,2,1,0:T(2,128)(2,1)}), bf16[128,9,2,128]{3,2,1,0:T(2,128)(2,1)S(1)}, u32[]{:S(2)}, u32[]{:S(2)}) %all-to-all-start.1) | async-done | bytes 589856 | tf_op jit(solution)/shard_map/all_to_all | solution.py:333
  104.3 1.7 %shard_map.86 = (bf16[16,40,128]{2,1,0:T(8,128)(2,1)S(1)}, bf16[4,96,128]{2,1,0:T(8,128)(2,1)S(1)}, bf16[4,96,128]{2,1,0:T(8,128)(2,1)S(1)}) custom-call(s32[2]{0:T(128)S(1)} %pad_add_fusion.place_ref, bf16[128,9,2,128]{3,2,1,0:T(2,128)(2,1)S(1)} %all-to-all-done.1.in_ref, bf16[4,144,768]{2,1,0:T(8,128)(2,1)S(1)} %pad_maximum_fusion.refs_0_.ext_ref, ...), custom_call_target="tpu_custom_call" | custom-call | tf_op jit(solution)/shard_map/pallas_call | solution.py:318
  106.0 13.6 %all_to_all.31.in_ref = bf16[16,40,128]{2,1,0:T(8,128)(2,1)S(1)} all-to-all(bf16[16,40,128]{2,1,0:T(8,128)(2,1)S(1)} %get-tuple-element.23), channel_id=1, replica_groups={{6,4,2,0,134,132,130,128,262,260,258,256,390,388,386,384},{8,14,12,10,1..., dimensions={0} | all-to-all | bytes 327680 | tf_op jit(solution)/shard_map/all_to_all | solution.py:333
  119.5 0.6 shard_map.87
  120.2 3.3 %all-to-all-start.3 = ((bf16[4,40,128]{2,1,0:T(8,128)(2,1)}), bf16[4,40,128]{2,1,0:T(8,128)(2,1)S(1)}, u32[]{:S(2)}, u32[]{:S(2)}) async-start(bf16[4,40,128]{2,1,0:T(8,128)(2,1)} %shard_map.87), calls=%async_computation.3 | async-start | bytes 81920 | tf_op jit(solution)/shard_map/all_to_all | solution.py:333
  123.5 4.4 %collective-permute-start.4 = (bf16[4,96,128]{2,1,0:T(8,128)(2,1)S(1)}, bf16[4,96,128]{2,1,0:T(8,128)(2,1)S(1)}, u32[]{:S(2)}, u32[]{:S(2)}) collective-permute-start(bf16[4,96,128]{2,1,0:T(8,128)(2,1)S(1)} %get-tuple-element.26), channel_id=1, source_target_pairs={{0,1},{1,0},{2,3},{3,2},{4,5},{5,4},{6,7},{7,6},{8,9},{9,8},{10,11... | collective-permute-start | bytes 294920 | tf_op jit(solution)/shard_map/ppermute | solution.py:364
  127.9 1.0 shard_map.88
  128.8 0.0 collective-permute-done.4.got_ref
  128.8 4.3 %all-to-all-done.3.in_ref = bf16[4,40,128]{2,1,0:T(8,128)(2,1)S(1)} async-done(((bf16[4,40,128]{2,1,0:T(8,128)(2,1)}), bf16[4,40,128]{2,1,0:T(8,128)(2,1)S(1)}, u32[]{:S(2)}, u32[]{:S(2)}) %all-to-all-start.3) | async-done | bytes 40992 | tf_op jit(solution)/shard_map/all_to_all | solution.py:333
  133.2 11.6 %all_to_all.32.block_ref = bf16[16,40,128]{2,1,0:T(8,128)(2,1)S(1)} all-to-all(bf16[16,40,128]{2,1,0:T(8,128)(2,1)S(1)} %shard_map.89), channel_id=1, replica_groups={{6,4,2,0,134,132,130,128,262,260,258,256,390,388,386,384},{8,14,12,10,1..., dimensions={0} | all-to-all | bytes 327680 | tf_op jit(solution)/shard_map/all_to_all | solution.py:333
  144.9 0.1 shard_map.90
  144.9 0.0 copy-start
  144.9 0.0 copy-start.1
  145.0 11.0 %all_to_all.33.all_ref.mine_ref = bf16[4,768,128]{2,1,0:T(8,128)(2,1)S(1)} all-to-all(bf16[4,768,128]{2,1,0:T(8,128)(2,1)S(1)} %shard_map.90), channel_id=1, replica_groups=mesh['x'=4,'y'=4,'z'=16,'c'=2] {'y'}, dimensions={0} | all-to-all | bytes 1572864 | tf_op jit(solution)/shard_map/all_to_all | solution.py:333
  155.9 6.9 %collective-permute-start.5 = (bf16[4,768,128]{2,1,0:T(8,128)(2,1)S(1)}, bf16[4,768,128]{2,1,0:T(8,128)(2,1)S(1)}, u32[]{:S(2)}, u32[]{:S(2)}) collective-permute-start(bf16[4,768,128]{2,1,0:T(8,128)(2,1)S(1)} %all_to_all.33.all_ref.mine_ref), channel_id=1, source_target_pairs={{0,1},{1,0},{2,3},{3,2},{4,5},{5,4},{6,7},{7,6},{8,9},{9,8},{10,11... | collective-permute-start | bytes 2359304 | tf_op jit(solution)/shard_map/ppermute | solution.py:364
  162.9 0.0 copy-done
  162.9 0.0 copy-done.1
  162.9 1.8 %shard_map.91 = bf16[128,768]{1,0:T(8,128)(2,1)} custom-call(s32[2]{0:T(128)S(1)} %pad_add_fusion.place_ref, bf16[4,768,128]{2,1,0:T(8,128)(2,1)S(1)} %all_to_all.33.all_ref.mine_ref, bf16[768,384]{1,0:T(8,128)(2,1)S(1)} %copy-done, bf16[768,384]{1,0:T(8,128)(2,1)S(1)} %copy-done.1), custom_call_target="tpu_custom_call" | custom-call | tf_op jit(solution)/shard_map/pallas_call | solution.py:318
  164.7 0.1 collective-permute-done.5.other_ref
  164.8 1.7 %shard_map.92 = (bf16[768,384]{1,0:T(8,128)(2,1)}, bf16[768,384]{1,0:T(8,128)(2,1)}) custom-call(s32[2]{0:T(128)S(1)} %pad_add_fusion.place_ref, bf16[4,768,128]{2,1,0:T(8,128)(2,1)S(1)} %all_to_all.33.all_ref.mine_ref, bf16[4,768,128]{2,1,0:T(8,128)(2,1)S(1)} %collective-permute-done.5.other_ref), custom_call_target="tpu_custom_call" | custom-call | tf_op jit(solution)/shard_map/pallas_call | solution.py:318
  (1 shorter events, 0.0 us)
Async XLA Ops:
  61.6 42.7 %all-to-all-start.1 = ((bf16[128,9,2,128]{3,2,1,0:T(2,128)(2,1)}), bf16[128,9,2,128]{3,2,1,0:T(2,128)(2,1)S(1)}, u32[]{:S(2)}, u32[]{:S(2)}) async-start(bf16[128,9,2,128]{3,2,1,0:T(2,128)(2,1)} %shard_map.85), calls=%async_computation.1 | async-start | bytes 1179648 | tf_op jit(solution)/shard_map/all_to_all | solution.py:333
  69.8 10.7 %collective-permute-start.2 = (bf16[144,768]{1,0:T(8,128)(2,1)S(1)}, bf16[144,768]{1,0:T(8,128)(2,1)S(1)}, u32[]{:S(2)}, u32[]{:S(2)}) collective-permute-start(bf16[144,768]{1,0:T(8,128)(2,1)S(1)} %get-tuple-element.22), channel_id=1, source_target_pairs={{0,96},{32,0},{64,32},{96,64},{1,97},{33,1},{65,33},{97,65},{2,98}... | collective-permute-start | bytes 663560 | tf_op jit(solution)/shard_map/ppermute | solution.py:361
  74.9 17.2 %collective-permute-start = (bf16[144,768]{1,0:T(8,128)(2,1)S(1)}, bf16[144,768]{1,0:T(8,128)(2,1)S(1)}, u32[]{:S(2)}, u32[]{:S(2)}) collective-permute-start(bf16[144,768]{1,0:T(8,128)(2,1)S(1)} %get-tuple-element.22), channel_id=1, source_target_pairs={{0,32},{32,64},{64,96},{96,0},{1,33},{33,65},{65,97},{97,1},{2,34}... | collective-permute-start | bytes 663560 | tf_op jit(solution)/shard_map/ppermute | solution.py:361
  76.8 15.3 %collective-permute-start.1 = (bf16[144,768]{1,0:T(8,128)(2,1)S(1)}, bf16[144,768]{1,0:T(8,128)(2,1)S(1)}, u32[]{:S(2)}, u32[]{:S(2)}) collective-permute-start(bf16[144,768]{1,0:T(8,128)(2,1)S(1)} %get-tuple-element.22), channel_id=1, source_target_pairs={{0,64},{32,96},{64,0},{96,32},{1,65},{33,97},{65,1},{97,33},{2,66}... | collective-permute-start | bytes 663560 | tf_op jit(solution)/shard_map/ppermute | solution.py:361
  92.2 5.3 %collective-permute-start.3 = (bf16[4,144,768]{2,1,0:T(8,128)(2,1)S(1)}, bf16[4,144,768]{2,1,0:T(8,128)(2,1)S(1)}, u32[]{:S(2)}, u32[]{:S(2)}) collective-permute-start(bf16[4,144,768]{2,1,0:T(8,128)(2,1)S(1)} %pad_maximum_fusion.refs_0_.ext_ref), channel_id=1, source_target_pairs={{0,1},{1,0},{2,3},{3,2},{4,5},{5,4},{6,7},{7,6},{8,9},{9,8},{10,11... | collective-permute-start | bytes 2654216 | tf_op jit(solution)/shard_map/ppermute | solution.py:364
  120.2 13.0 %all-to-all-start.3 = ((bf16[4,40,128]{2,1,0:T(8,128)(2,1)}), bf16[4,40,128]{2,1,0:T(8,128)(2,1)S(1)}, u32[]{:S(2)}, u32[]{:S(2)}) async-start(bf16[4,40,128]{2,1,0:T(8,128)(2,1)} %shard_map.87), calls=%async_computation.3 | async-start | bytes 81920 | tf_op jit(solution)/shard_map/all_to_all | solution.py:333
  123.5 5.4 %collective-permute-start.4 = (bf16[4,96,128]{2,1,0:T(8,128)(2,1)S(1)}, bf16[4,96,128]{2,1,0:T(8,128)(2,1)S(1)}, u32[]{:S(2)}, u32[]{:S(2)}) collective-permute-start(bf16[4,96,128]{2,1,0:T(8,128)(2,1)S(1)} %get-tuple-element.26), channel_id=1, source_target_pairs={{0,1},{1,0},{2,3},{3,2},{4,5},{5,4},{6,7},{7,6},{8,9},{9,8},{10,11... | collective-permute-start | bytes 294920 | tf_op jit(solution)/shard_map/ppermute | solution.py:364
  144.9 18.0 %copy-start = (bf16[768,384]{1,0:T(8,128)(2,1)S(1)}, bf16[768,384]{1,0:T(8,128)(2,1)}, u32[]{:S(2)}) copy-start(bf16[768,384]{1,0:T(8,128)(2,1)} %ws_ref.1) | copy-start | bytes 1769476
  144.9 18.0 %copy-start.1 = (bf16[768,384]{1,0:T(8,128)(2,1)S(1)}, bf16[768,384]{1,0:T(8,128)(2,1)}, u32[]{:S(2)}) copy-start(bf16[768,384]{1,0:T(8,128)(2,1)} %wv_ref.1) | copy-start | bytes 1769476
  155.9 8.8 %collective-permute-start.5 = (bf16[4,768,128]{2,1,0:T(8,128)(2,1)S(1)}, bf16[4,768,128]{2,1,0:T(8,128)(2,1)S(1)}, u32[]{:S(2)}, u32[]{:S(2)}) collective-permute-start(bf16[4,768,128]{2,1,0:T(8,128)(2,1)S(1)} %all_to_all.33.all_ref.mine_ref), channel_id=1, source_target_pairs={{0,1},{1,0},{2,3},{3,2},{4,5},{5,4},{6,7},{7,6},{8,9},{9,8},{10,11... | collective-permute-start | bytes 2359304 | tf_op jit(solution)/shard_map/ppermute | solution.py:364

commit v16 on v15

--- a/solution.py
+++ b/solution.py
@@ -39,14 +39,15 @@
 
 
 def send_kernel(*refs):
-    sources, (out_ref, ext_ref), targets, sems = refs[:5], refs[5:7], refs[7:12], refs[12]
+    sources, (out_ref, ext_ref), targets, sems = refs[:5], refs[5:7], refs[7:11], refs[11]
+    places = [targets[0], targets[1], targets[2].at[:, :PROJ], targets[2].at[:, PROJ:], targets[3]]
     copies = [
-        pltpu.make_async_copy(source, target, sems.at[n])
-        for n, (source, target) in enumerate(zip(sources, targets))
+        pltpu.make_async_copy(source, place, sems.at[n])
+        for n, (source, place) in enumerate(zip(sources, places))
     ]
     for copy in copies:
         copy.start()
-    cluster_ref, tok_ref, ws_ref, wv_ref, cot_ref = targets
+    cluster_ref, tok_ref, both_ref, cot_ref = targets
     sub = iota((LOCAL, LOCAL), 0)
     lane = iota((LOCAL, LOCAL), 1)
     sub_rows = iota((ROWS, LOCAL), 0)
@@ -72,22 +73,22 @@
         copy.wait()
     tokens = tok_ref[...]
     ext_ref[:LOCAL, :] = tokens
-    shared = dot(tokens, ws_ref[...]).astype(BF16)
-    value = dot(tokens, wv_ref[...]).astype(BF16)
+    both = dot(tokens, both_ref[...]).astype(BF16)
+    shared, value = both[:, :PROJ], both[:, PROJ:]
     cot = cot_ref[...]
     blank = jnp.zeros((LOCAL, HEAD), BF16)
-    pending = None
+    moved = []
     for h in range(HEADS):
         cols = slice(h * HEAD, (h + 1) * HEAD)
         tail = [cot[:, cols], blank] if h % 2 == 0 else [blank, cot[:, cols]]
         packed = jnp.concatenate([shared[:, cols], value[:, cols]] + tail, axis=1)
-        moved = dot(hits[h], packed)
-        out_ref[:, h] = (moved[:, :LOCAL] + marks[h]).astype(BF16).reshape(LOCAL, 2, LOCAL)
-        if h % 2 == 0:
-            pending = moved[:, LOCAL:]
-        else:
-            packed = (pending + moved[:, LOCAL:]).astype(BF16)
-            out_ref[:, HEADS + h // 2] = packed.reshape(LOCAL, 2, LOCAL)
+        moved.append(dot(hits[h], packed))
+    for h in range(HEADS):
+        rows = (moved[h][:, :LOCAL] + marks[h]).astype(BF16)
+        out_ref[:, h] = rows.reshape(LOCAL, 2, LOCAL)
+    for k in range(HEADS // 2):
+        rows = (moved[2 * k][:, LOCAL:] + moved[2 * k + 1][:, LOCAL:]).astype(BF16)
+        out_ref[:, HEADS + k] = rows.reshape(LOCAL, 2, LOCAL)
 
 
 def position(row):
@@ -349,8 +350,7 @@
         scratch=[
             pltpu.VMEM((HEADS, 1, LOCAL), jnp.int32),
             pltpu.VMEM((LOCAL, WIDTH), BF16),
-            pltpu.VMEM((WIDTH, PROJ), BF16),
-            pltpu.VMEM((WIDTH, PROJ), BF16),
+            pltpu.VMEM((WIDTH, 2 * PROJ), BF16),
             pltpu.VMEM((LOCAL, PROJ), BF16),
             pltpu.SemaphoreType.DMA((5,)),
         ],

time: 167 us -> 167 us (level)
  no operation moved by 1% of the time
where the time goes in v16:
time: 167 us; the launch traced here: 166 us
  blocking collectives  91.1 us (55%)
  starting transfers between devices  36.6 us (22%)
  waiting for transfers between devices  25 us (15%)
  Pallas kernels  12.4 us (7%)
    all_to_all x4, blocking collectives, swap(): lax.all_to_all(rows, axes, split_axis=0, concat_axis=0, tiled=True, axis_...  91.1 us
    ppermute x3, starting transfers between devices, flip(): return lax.ppermute(part, 'c', [(0, 1), (1, 0)])  14.6 us
    pallas_call x9, Pallas kernels, call(): pl.pallas_call(kernel, out_shape=out, in_specs=specs, out_specs=outs, scr...  12.4 us
    ppermute x3, waiting for transfers between devices, shift(): return lax.ppermute(pair, 'y', [(y, (y + dy) % 4) for y in range(4)])  11.9 us
    all_to_all x2, starting transfers between devices, swap(): lax.all_to_all(rows, axes, split_axis=0, concat_axis=0, tiled=True, axis_...  11.5 us
    all_to_all x2, waiting for transfers between devices, swap(): lax.all_to_all(rows, axes, split_axis=0, concat_axis=0, tiled=True, axis_...  11.1 us
    ppermute x3, starting transfers between devices, shift(): return lax.ppermute(pair, 'y', [(y, (y + dy) % 4) for y in range(4)])  10.5 us
  transfers between devices with their start and end apart: 8, of which 6 were waited for; matrix products, arithmetic and copies ran while one was open for 0% of the time, Pallas kernels for 2%

profile of v16, /device:TPU:1, one launch (start us, length us, event | category | flops | bytes accessed | tf_op | source)
XLA Modules:
  0.0 166.5 jit_solution(9585921084449497025)
XLA Ops:
  0.6 2.3 %shard_map.84 = (bf16[128,9,2,128]{3,2,1,0:T(2,128)(2,1)S(1)}, bf16[144,768]{1,0:T(8,128)(2,1)S(1)}) custom-call(s32[6,1,128]{2,1,0:T(1,128)} %bitcast.23, bf16[128,768]{1,0:T(8,128)(2,1)} %bitcast.19, bf16[768,384]{1,0:T(8,128)(2,1)} %ws_ref.1, bf16[768,384]{1,0:T(8,128)(2,1)} %wv_ref.1, bf16[128,384]{1,0:T(8,128)(2,1)} %bitcast.21), custom_call_target="tpu_custom_call" | custom-call | tf_op jit(solution)/shard_map/pallas_call | solution.py:319
  2.9 54.9 %all_to_all.30 = bf16[128,9,2,128]{3,2,1,0:T(2,128)(2,1)S(1)} all-to-all(bf16[128,9,2,128]{3,2,1,0:T(2,128)(2,1)S(1)} %get-tuple-element.19), channel_id=1, replica_groups=mesh['x'=4,'y'=4,'z'=16,'c'=2] {'y','c','z'}, dimensions={0} | all-to-all | bytes 1179648 | tf_op jit(solution)/shard_map/all_to_all | solution.py:334
  57.9 0.5 copy.9
  58.3 3.2 %shard_map.85 = bf16[128,9,2,128]{3,2,1,0:T(2,128)(2,1)} custom-call(bf16[9,256,128]{2,1,0:T(8,128)(2,1)S(1)} %bitcast.13), custom_call_target="tpu_custom_call" | custom-call | tf_op jit(solution)/shard_map/pallas_call | solution.py:319
  61.5 8.2 %all-to-all-start.1 = ((bf16[128,9,2,128]{3,2,1,0:T(2,128)(2,1)}), bf16[128,9,2,128]{3,2,1,0:T(2,128)(2,1)S(1)}, u32[]{:S(2)}, u32[]{:S(2)}) async-start(bf16[128,9,2,128]{3,2,1,0:T(2,128)(2,1)} %shard_map.85), calls=%async_computation.1 | async-start | bytes 1179648 | tf_op jit(solution)/shard_map/all_to_all | solution.py:334
  69.7 5.1 %collective-permute-start.2 = (bf16[144,768]{1,0:T(8,128)(2,1)S(1)}, bf16[144,768]{1,0:T(8,128)(2,1)S(1)}, u32[]{:S(2)}, u32[]{:S(2)}) collective-permute-start(bf16[144,768]{1,0:T(8,128)(2,1)S(1)} %get-tuple-element.22), channel_id=1, source_target_pairs={{0,96},{32,0},{64,32},{96,64},{1,97},{33,1},{65,33},{97,65},{2,98}... | collective-permute-start | bytes 663560 | tf_op jit(solution)/shard_map/ppermute | solution.py:361
  74.8 1.9 %collective-permute-start = (bf16[144,768]{1,0:T(8,128)(2,1)S(1)}, bf16[144,768]{1,0:T(8,128)(2,1)S(1)}, u32[]{:S(2)}, u32[]{:S(2)}) collective-permute-start(bf16[144,768]{1,0:T(8,128)(2,1)S(1)} %get-tuple-element.22), channel_id=1, source_target_pairs={{0,32},{32,64},{64,96},{96,0},{1,33},{33,65},{65,97},{97,1},{2,34}... | collective-permute-start | bytes 663560 | tf_op jit(solution)/shard_map/ppermute | solution.py:361
  76.8 3.4 %collective-permute-start.1 = (bf16[144,768]{1,0:T(8,128)(2,1)S(1)}, bf16[144,768]{1,0:T(8,128)(2,1)S(1)}, u32[]{:S(2)}, u32[]{:S(2)}) collective-permute-start(bf16[144,768]{1,0:T(8,128)(2,1)S(1)} %get-tuple-element.22), channel_id=1, source_target_pairs={{0,64},{32,96},{64,0},{96,32},{1,65},{33,97},{65,1},{97,33},{2,66}... | collective-permute-start | bytes 663560 | tf_op jit(solution)/shard_map/ppermute | solution.py:361
  80.2 0.3 collective-permute-done.2
  80.5 11.6 %collective-permute-done = bf16[144,768]{1,0:T(8,128)(2,1)S(1)} collective-permute-done((bf16[144,768]{1,0:T(8,128)(2,1)S(1)}, bf16[144,768]{1,0:T(8,128)(2,1)S(1)}, u32[]{:S(2)}, u32[]{:S(2)}) %collective-permute-start) | collective-permute-done | bytes 221216 | tf_op jit(solution)/shard_map/ppermute | solution.py:361
  92.1 0.0 collective-permute-done.1
  92.1 0.1 pad_maximum_fusion.refs_0_.ext_ref
  92.2 3.3 %collective-permute-start.3 = (bf16[4,144,768]{2,1,0:T(8,128)(2,1)S(1)}, bf16[4,144,768]{2,1,0:T(8,128)(2,1)S(1)}, u32[]{:S(2)}, u32[]{:S(2)}) collective-permute-start(bf16[4,144,768]{2,1,0:T(8,128)(2,1)S(1)} %pad_maximum_fusion.refs_0_.ext_ref), channel_id=1, source_target_pairs={{0,1},{1,0},{2,3},{3,2},{4,5},{5,4},{6,7},{7,6},{8,9},{9,8},{10,11... | collective-permute-start | bytes 2654216 | tf_op jit(solution)/shard_map/ppermute | solution.py:364
  95.5 0.1 pad_add_fusion.place_ref
  95.6 1.9 %collective-permute-done.3.refs_1_ = bf16[4,144,768]{2,1,0:T(8,128)(2,1)S(1)} collective-permute-done((bf16[4,144,768]{2,1,0:T(8,128)(2,1)S(1)}, bf16[4,144,768]{2,1,0:T(8,128)(2,1)S(1)}, u32[]{:S(2)}, u32[]{:S(2)}) %collective-permute-start.3) | collective-permute-done | bytes 884768 | tf_op jit(solution)/shard_map/ppermute | solution.py:364
  97.5 6.7 %all-to-all-done.1.in_ref = bf16[128,9,2,128]{3,2,1,0:T(2,128)(2,1)S(1)} async-done(((bf16[128,9,2,128]{3,2,1,0:T(2,128)(2,1)}), bf16[128,9,2,128]{3,2,1,0:T(2,128)(2,1)S(1)}, u32[]{:S(2)}, u32[]{:S(2)}) %all-to-all-start.1) | async-done | bytes 589856 | tf_op jit(solution)/shard_map/all_to_all | solution.py:334
  104.2 1.7 %shard_map.86 = (bf16[16,40,128]{2,1,0:T(8,128)(2,1)S(1)}, bf16[4,96,128]{2,1,0:T(8,128)(2,1)S(1)}, bf16[4,96,128]{2,1,0:T(8,128)(2,1)S(1)}) custom-call(s32[2]{0:T(128)S(1)} %pad_add_fusion.place_ref, bf16[128,9,2,128]{3,2,1,0:T(2,128)(2,1)S(1)} %all-to-all-done.1.in_ref, bf16[4,144,768]{2,1,0:T(8,128)(2,1)S(1)} %pad_maximum_fusion.refs_0_.ext_ref, ...), custom_call_target="tpu_custom_call" | custom-call | tf_op jit(solution)/shard_map/pallas_call | solution.py:319
  105.9 13.6 %all_to_all.31.in_ref = bf16[16,40,128]{2,1,0:T(8,128)(2,1)S(1)} all-to-all(bf16[16,40,128]{2,1,0:T(8,128)(2,1)S(1)} %get-tuple-element.23), channel_id=1, replica_groups={{6,4,2,0,134,132,130,128,262,260,258,256,390,388,386,384},{8,14,12,10,1..., dimensions={0} | all-to-all | bytes 327680 | tf_op jit(solution)/shard_map/all_to_all | solution.py:334
  119.5 0.6 shard_map.87
  120.1 3.3 %all-to-all-start.3 = ((bf16[4,40,128]{2,1,0:T(8,128)(2,1)}), bf16[4,40,128]{2,1,0:T(8,128)(2,1)S(1)}, u32[]{:S(2)}, u32[]{:S(2)}) async-start(bf16[4,40,128]{2,1,0:T(8,128)(2,1)} %shard_map.87), calls=%async_computation.3 | async-start | bytes 81920 | tf_op jit(solution)/shard_map/all_to_all | solution.py:334
  123.4 4.4 %collective-permute-start.4 = (bf16[4,96,128]{2,1,0:T(8,128)(2,1)S(1)}, bf16[4,96,128]{2,1,0:T(8,128)(2,1)S(1)}, u32[]{:S(2)}, u32[]{:S(2)}) collective-permute-start(bf16[4,96,128]{2,1,0:T(8,128)(2,1)S(1)} %get-tuple-element.26), channel_id=1, source_target_pairs={{0,1},{1,0},{2,3},{3,2},{4,5},{5,4},{6,7},{7,6},{8,9},{9,8},{10,11... | collective-permute-start | bytes 294920 | tf_op jit(solution)/shard_map/ppermute | solution.py:364
  127.8 1.0 shard_map.88
  128.8 0.0 collective-permute-done.4.got_ref
  128.8 4.3 %all-to-all-done.3.in_ref = bf16[4,40,128]{2,1,0:T(8,128)(2,1)S(1)} async-done(((bf16[4,40,128]{2,1,0:T(8,128)(2,1)}), bf16[4,40,128]{2,1,0:T(8,128)(2,1)S(1)}, u32[]{:S(2)}, u32[]{:S(2)}) %all-to-all-start.3) | async-done | bytes 40992 | tf_op jit(solution)/shard_map/all_to_all | solution.py:334
  133.1 11.6 %all_to_all.32.block_ref = bf16[16,40,128]{2,1,0:T(8,128)(2,1)S(1)} all-to-all(bf16[16,40,128]{2,1,0:T(8,128)(2,1)S(1)} %shard_map.89), channel_id=1, replica_groups={{6,4,2,0,134,132,130,128,262,260,258,256,390,388,386,384},{8,14,12,10,1..., dimensions={0} | all-to-all | bytes 327680 | tf_op jit(solution)/shard_map/all_to_all | solution.py:334
  144.8 0.1 shard_map.90
  144.9 0.0 copy-start
  144.9 0.0 copy-start.1
  144.9 11.0 %all_to_all.33.all_ref.mine_ref = bf16[4,768,128]{2,1,0:T(8,128)(2,1)S(1)} all-to-all(bf16[4,768,128]{2,1,0:T(8,128)(2,1)S(1)} %shard_map.90), channel_id=1, replica_groups=mesh['x'=4,'y'=4,'z'=16,'c'=2] {'y'}, dimensions={0} | all-to-all | bytes 1572864 | tf_op jit(solution)/shard_map/all_to_all | solution.py:334
  155.9 7.0 %collective-permute-start.5 = (bf16[4,768,128]{2,1,0:T(8,128)(2,1)S(1)}, bf16[4,768,128]{2,1,0:T(8,128)(2,1)S(1)}, u32[]{:S(2)}, u32[]{:S(2)}) collective-permute-start(bf16[4,768,128]{2,1,0:T(8,128)(2,1)S(1)} %all_to_all.33.all_ref.mine_ref), channel_id=1, source_target_pairs={{0,1},{1,0},{2,3},{3,2},{4,5},{5,4},{6,7},{7,6},{8,9},{9,8},{10,11... | collective-permute-start | bytes 2359304 | tf_op jit(solution)/shard_map/ppermute | solution.py:364
  162.8 0.0 copy-done
  162.8 0.0 copy-done.1
  162.9 1.8 %shard_map.91 = bf16[128,768]{1,0:T(8,128)(2,1)} custom-call(s32[2]{0:T(128)S(1)} %pad_add_fusion.place_ref, bf16[4,768,128]{2,1,0:T(8,128)(2,1)S(1)} %all_to_all.33.all_ref.mine_ref, bf16[768,384]{1,0:T(8,128)(2,1)S(1)} %copy-done, bf16[768,384]{1,0:T(8,128)(2,1)S(1)} %copy-done.1), custom_call_target="tpu_custom_call" | custom-call | tf_op jit(solution)/shard_map/pallas_call | solution.py:319
  164.6 0.1 collective-permute-done.5.other_ref
  164.7 1.7 %shard_map.92 = (bf16[768,384]{1,0:T(8,128)(2,1)}, bf16[768,384]{1,0:T(8,128)(2,1)}) custom-call(s32[2]{0:T(128)S(1)} %pad_add_fusion.place_ref, bf16[4,768,128]{2,1,0:T(8,128)(2,1)S(1)} %all_to_all.33.all_ref.mine_ref, bf16[4,768,128]{2,1,0:T(8,128)(2,1)S(1)} %collective-permute-done.5.other_ref), custom_call_target="tpu_custom_call" | custom-call | tf_op jit(solution)/shard_map/pallas_call | solution.py:319
  (1 shorter events, 0.0 us)
Async XLA Ops:
  61.5 42.7 %all-to-all-start.1 = ((bf16[128,9,2,128]{3,2,1,0:T(2,128)(2,1)}), bf16[128,9,2,128]{3,2,1,0:T(2,128)(2,1)S(1)}, u32[]{:S(2)}, u32[]{:S(2)}) async-start(bf16[128,9,2,128]{3,2,1,0:T(2,128)(2,1)} %shard_map.85), calls=%async_computation.1 | async-start | bytes 1179648 | tf_op jit(solution)/shard_map/all_to_all | solution.py:334
  69.7 10.7 %collective-permute-start.2 = (bf16[144,768]{1,0:T(8,128)(2,1)S(1)}, bf16[144,768]{1,0:T(8,128)(2,1)S(1)}, u32[]{:S(2)}, u32[]{:S(2)}) collective-permute-start(bf16[144,768]{1,0:T(8,128)(2,1)S(1)} %get-tuple-element.22), channel_id=1, source_target_pairs={{0,96},{32,0},{64,32},{96,64},{1,97},{33,1},{65,33},{97,65},{2,98}... | collective-permute-start | bytes 663560 | tf_op jit(solution)/shard_map/ppermute | solution.py:361
  74.8 17.2 %collective-permute-start = (bf16[144,768]{1,0:T(8,128)(2,1)S(1)}, bf16[144,768]{1,0:T(8,128)(2,1)S(1)}, u32[]{:S(2)}, u32[]{:S(2)}) collective-permute-start(bf16[144,768]{1,0:T(8,128)(2,1)S(1)} %get-tuple-element.22), channel_id=1, source_target_pairs={{0,32},{32,64},{64,96},{96,0},{1,33},{33,65},{65,97},{97,1},{2,34}... | collective-permute-start | bytes 663560 | tf_op jit(solution)/shard_map/ppermute | solution.py:361
  76.8 15.3 %collective-permute-start.1 = (bf16[144,768]{1,0:T(8,128)(2,1)S(1)}, bf16[144,768]{1,0:T(8,128)(2,1)S(1)}, u32[]{:S(2)}, u32[]{:S(2)}) collective-permute-start(bf16[144,768]{1,0:T(8,128)(2,1)S(1)} %get-tuple-element.22), channel_id=1, source_target_pairs={{0,64},{32,96},{64,0},{96,32},{1,65},{33,97},{65,1},{97,33},{2,66}... | collective-permute-start | bytes 663560 | tf_op jit(solution)/shard_map/ppermute | solution.py:361
  92.2 5.3 %collective-permute-start.3 = (bf16[4,144,768]{2,1,0:T(8,128)(2,1)S(1)}, bf16[4,144,768]{2,1,0:T(8,128)(2,1)S(1)}, u32[]{:S(2)}, u32[]{:S(2)}) collective-permute-start(bf16[4,144,768]{2,1,0:T(8,128)(2,1)S(1)} %pad_maximum_fusion.refs_0_.ext_ref), channel_id=1, source_target_pairs={{0,1},{1,0},{2,3},{3,2},{4,5},{5,4},{6,7},{7,6},{8,9},{9,8},{10,11... | collective-permute-start | bytes 2654216 | tf_op jit(solution)/shard_map/ppermute | solution.py:364
  120.1 13.0 %all-to-all-start.3 = ((bf16[4,40,128]{2,1,0:T(8,128)(2,1)}), bf16[4,40,128]{2,1,0:T(8,128)(2,1)S(1)}, u32[]{:S(2)}, u32[]{:S(2)}) async-start(bf16[4,40,128]{2,1,0:T(8,128)(2,1)} %shard_map.87), calls=%async_computation.3 | async-start | bytes 81920 | tf_op jit(solution)/shard_map/all_to_all | solution.py:334
  123.4 5.4 %collective-permute-start.4 = (bf16[4,96,128]{2,1,0:T(8,128)(2,1)S(1)}, bf16[4,96,128]{2,1,0:T(8,128)(2,1)S(1)}, u32[]{:S(2)}, u32[]{:S(2)}) collective-permute-start(bf16[4,96,128]{2,1,0:T(8,128)(2,1)S(1)} %get-tuple-element.26), channel_id=1, source_target_pairs={{0,1},{1,0},{2,3},{3,2},{4,5},{5,4},{6,7},{7,6},{8,9},{9,8},{10,11... | collective-permute-start | bytes 294920 | tf_op jit(solution)/shard_map/ppermute | solution.py:364
  144.9 18.0 %copy-start = (bf16[768,384]{1,0:T(8,128)(2,1)S(1)}, bf16[768,384]{1,0:T(8,128)(2,1)}, u32[]{:S(2)}) copy-start(bf16[768,384]{1,0:T(8,128)(2,1)} %ws_ref.1) | copy-start | bytes 1769476
  144.9 18.0 %copy-start.1 = (bf16[768,384]{1,0:T(8,128)(2,1)S(1)}, bf16[768,384]{1,0:T(8,128)(2,1)}, u32[]{:S(2)}) copy-start(bf16[768,384]{1,0:T(8,128)(2,1)} %wv_ref.1) | copy-start | bytes 1769476
  155.9 8.9 %collective-permute-start.5 = (bf16[4,768,128]{2,1,0:T(8,128)(2,1)S(1)}, bf16[4,768,128]{2,1,0:T(8,128)(2,1)S(1)}, u32[]{:S(2)}, u32[]{:S(2)}) collective-permute-start(bf16[4,768,128]{2,1,0:T(8,128)(2,1)S(1)} %all_to_all.33.all_ref.mine_ref), channel_id=1, source_target_pairs={{0,1},{1,0},{2,3},{3,2},{4,5},{5,4},{6,7},{7,6},{8,9},{9,8},{10,11... | collective-permute-start | bytes 2359304 | tf_op jit(solution)/shard_map/ppermute | solution.py:364

commit v17 on v15

--- a/solution.py
+++ b/solution.py
@@ -364,7 +364,6 @@
         return lax.ppermute(part, "c", [(0, 1), (1, 0)])
 
     arrived = swap(sent, OWNERS)
-    arrived, ext = lax.optimization_barrier((arrived, ext))
     mine = jnp.stack([ext] + [shift(ext, dy) for dy in range(1, 4)])
     exts = [mine, flip(mine)]
     arrived = arrived.transpose(1, 0, 2, 3).reshape(9, ROWS, LOCAL)
@@ -373,6 +372,7 @@
         [shape(LOCAL, 9, 2, LOCAL)],
         arrived,
     )
+    worked, mine, exts, place = lax.optimization_barrier((worked, mine, exts, place))
     back = swap(worked, OWNERS)
     part, keep, give = call(
         partial_kernel,

time: 167 us -> 167 us (level)
  starting transfers between devices: 36.6 us -> 49.6 us
  blocking collectives: 91.1 us -> 78.7 us
    all_to_all x4, blocking collectives: 91.1 us -> 78.7 us  [swap(): lax.all_to_all(rows, axes, split_axis=0, concat_axis=0, tiled=True, axis_...]
    all_to_all x2, starting transfers between devices: 11.5 us -> 23.9 us  [swap(): lax.all_to_all(rows, axes, split_axis=0, concat_axis=0, tiled=True, axis_...]
    all_to_all x2, waiting for transfers between devices: 11.1 us -> 15.1 us  [swap(): lax.all_to_all(rows, axes, split_axis=0, concat_axis=0, tiled=True, axis_...]
    ppermute x3, waiting for transfers between devices: 11.9 us -> 9.23 us  [shift(): return lax.ppermute(pair, 'y', [(y, (y + dy) % 4) for y in range(4)])]
    ppermute x3, waiting for transfers between devices: 2.06 us -> 0.11 us  [flip(): return lax.ppermute(part, 'c', [(0, 1), (1, 0)])]
  transfers between devices with their start and end apart: 8 -> 8, of which waited for: 6 -> 6; matrix products, arithmetic and copies ran while one was open for 0% -> 0% of each run, Pallas kernels for 2% -> 3%
where the time goes in v17:
time: 167 us
  blocking collectives  78.7 us (47%)
  starting transfers between devices  49.6 us (30%)
  waiting for transfers between devices  24.4 us (15%)
  Pallas kernels  12.5 us (7%)
    all_to_all x4, blocking collectives, swap(): lax.all_to_all(rows, axes, split_axis=0, concat_axis=0, tiled=True, axis_...  78.7 us
    all_to_all x2, starting transfers between devices, swap(): lax.all_to_all(rows, axes, split_axis=0, concat_axis=0, tiled=True, axis_...  23.9 us
    all_to_all x2, waiting for transfers between devices, swap(): lax.all_to_all(rows, axes, split_axis=0, concat_axis=0, tiled=True, axis_...  15.1 us
    ppermute x3, starting transfers between devices, flip(): return lax.ppermute(part, 'c', [(0, 1), (1, 0)])  14.6 us
    pallas_call x9, Pallas kernels, call(): pl.pallas_call(kernel, out_shape=out, in_specs=specs, out_specs=outs, scr...  12.5 us
    ppermute x3, starting transfers between devices, shift(): return lax.ppermute(pair, 'y', [(y, (y + dy) % 4) for y in range(4)])  11.1 us
    ppermute x3, waiting for transfers between devices, shift(): return lax.ppermute(pair, 'y', [(y, (y + dy) % 4) for y in range(4)])  9.23 us
  transfers between devices with their start and end apart: 8, of which 6 were waited for; matrix products, arithmetic and copies ran while one was open for 0% of the time, Pallas kernels for 3%

profile of v17, /device:TPU:1, one launch (start us, length us, event | category | flops | bytes accessed | tf_op | source)
XLA Modules:
  0.0 166.6 jit_solution(416194906700919077)
XLA Ops:
  0.6 3.2 %shard_map.84 = (bf16[128,9,2,128]{3,2,1,0:T(2,128)(2,1)}, bf16[144,768]{1,0:T(8,128)(2,1)S(1)}) custom-call(s32[6,1,128]{2,1,0:T(1,128)} %bitcast.23, bf16[128,768]{1,0:T(8,128)(2,1)} %bitcast.19, bf16[768,384]{1,0:T(8,128)(2,1)} %ws_ref.1, bf16[768,384]{1,0:T(8,128)(2,1)} %wv_ref.1, bf16[128,384]{1,0:T(8,128)(2,1)} %bitcast.21), custom_call_target="tpu_custom_call" | custom-call | tf_op jit(solution)/shard_map/pallas_call | solution.py:318
  3.8 20.6 %all-to-all-start = ((bf16[128,9,2,128]{3,2,1,0:T(2,128)(2,1)}), bf16[128,9,2,128]{3,2,1,0:T(2,128)(2,1)S(1)}, u32[]{:S(2)}, u32[]{:S(2)}) async-start(bf16[128,9,2,128]{3,2,1,0:T(2,128)(2,1)} %get-tuple-element.22), calls=%async_computation | async-start | bytes 1179648 | tf_op jit(solution)/shard_map/all_to_all | solution.py:333
  24.4 3.5 %collective-permute-start = (bf16[144,768]{1,0:T(8,128)(2,1)S(1)}, bf16[144,768]{1,0:T(8,128)(2,1)S(1)}, u32[]{:S(2)}, u32[]{:S(2)}) collective-permute-start(bf16[144,768]{1,0:T(8,128)(2,1)S(1)} %get-tuple-element.23), channel_id=1, source_target_pairs={{0,32},{32,64},{64,96},{96,0},{1,33},{33,65},{65,97},{97,1},{2,34}... | collective-permute-start | bytes 663560 | tf_op jit(solution)/shard_map/ppermute | solution.py:361
  27.9 4.7 %collective-permute-start.1 = (bf16[144,768]{1,0:T(8,128)(2,1)S(1)}, bf16[144,768]{1,0:T(8,128)(2,1)S(1)}, u32[]{:S(2)}, u32[]{:S(2)}) collective-permute-start(bf16[144,768]{1,0:T(8,128)(2,1)S(1)} %get-tuple-element.23), channel_id=1, source_target_pairs={{0,64},{32,96},{64,0},{96,32},{1,65},{33,97},{65,1},{97,33},{2,66}... | collective-permute-start | bytes 663560 | tf_op jit(solution)/shard_map/ppermute | solution.py:361
  32.6 2.9 %collective-permute-start.2 = (bf16[144,768]{1,0:T(8,128)(2,1)S(1)}, bf16[144,768]{1,0:T(8,128)(2,1)S(1)}, u32[]{:S(2)}, u32[]{:S(2)}) collective-permute-start(bf16[144,768]{1,0:T(8,128)(2,1)S(1)} %get-tuple-element.23), channel_id=1, source_target_pairs={{0,96},{32,0},{64,32},{96,64},{1,97},{33,1},{65,33},{97,65},{2,98}... | collective-permute-start | bytes 663560 | tf_op jit(solution)/shard_map/ppermute | solution.py:361
  35.5 0.1 collective-permute-done
  35.6 7.6 %collective-permute-done.1 = bf16[144,768]{1,0:T(8,128)(2,1)S(1)} collective-permute-done((bf16[144,768]{1,0:T(8,128)(2,1)S(1)}, bf16[144,768]{1,0:T(8,128)(2,1)S(1)}, u32[]{:S(2)}, u32[]{:S(2)}) %collective-permute-start.1) | collective-permute-done | bytes 221216 | tf_op jit(solution)/shard_map/ppermute | solution.py:361
  43.2 1.5 collective-permute-done.2
  44.7 0.1 pad_maximum_fusion.refs_0_.ext_ref
  44.9 3.3 %collective-permute-start.3 = (bf16[4,144,768]{2,1,0:T(8,128)(2,1)S(1)}, bf16[4,144,768]{2,1,0:T(8,128)(2,1)S(1)}, u32[]{:S(2)}, u32[]{:S(2)}) collective-permute-start(bf16[4,144,768]{2,1,0:T(8,128)(2,1)S(1)} %pad_maximum_fusion.refs_0_.ext_ref), channel_id=1, source_target_pairs={{0,1},{1,0},{2,3},{3,2},{4,5},{5,4},{6,7},{7,6},{8,9},{9,8},{10,11... | collective-permute-start | bytes 2654216 | tf_op jit(solution)/shard_map/ppermute | solution.py:364
  48.2 0.1 pad_add_fusion.place_ref
  48.2 10.7 %all-to-all-done = bf16[128,9,2,128]{3,2,1,0:T(2,128)(2,1)S(1)} async-done(((bf16[128,9,2,128]{3,2,1,0:T(2,128)(2,1)}), bf16[128,9,2,128]{3,2,1,0:T(2,128)(2,1)S(1)}, u32[]{:S(2)}, u32[]{:S(2)}) %all-to-all-start) | async-done | bytes 589856 | tf_op jit(solution)/shard_map/all_to_all | solution.py:333
  58.9 0.5 copy.9
  59.4 2.4 %shard_map.85 = bf16[128,9,2,128]{3,2,1,0:T(2,128)(2,1)S(1)} custom-call(bf16[9,256,128]{2,1,0:T(8,128)(2,1)S(1)} %bitcast.13), custom_call_target="tpu_custom_call" | custom-call | tf_op jit(solution)/shard_map/pallas_call | solution.py:318
  61.8 0.0 collective-permute-done.3.refs_1_
  61.8 42.5 %all_to_all.30.in_ref = bf16[128,9,2,128]{3,2,1,0:T(2,128)(2,1)S(1)} all-to-all(bf16[128,9,2,128]{3,2,1,0:T(2,128)(2,1)S(1)} %shard_map.85), channel_id=1, replica_groups=mesh['x'=4,'y'=4,'z'=16,'c'=2] {'y','c','z'}, dimensions={0} | all-to-all | bytes 1179648 | tf_op jit(solution)/shard_map/all_to_all | solution.py:333
  104.3 1.7 %shard_map.86 = (bf16[16,40,128]{2,1,0:T(8,128)(2,1)S(1)}, bf16[4,96,128]{2,1,0:T(8,128)(2,1)S(1)}, bf16[4,96,128]{2,1,0:T(8,128)(2,1)S(1)}) custom-call(s32[2]{0:T(128)S(1)} %pad_add_fusion.place_ref, bf16[128,9,2,128]{3,2,1,0:T(2,128)(2,1)S(1)} %all_to_all.30.in_ref, bf16[4,144,768]{2,1,0:T(8,128)(2,1)S(1)} %pad_maximum_fusion.refs_0_.ext_ref, ...), custom_call_target="tpu_custom_call" | custom-call | tf_op jit(solution)/shard_map/pallas_call | solution.py:318
  106.0 13.6 %all_to_all.31.in_ref = bf16[16,40,128]{2,1,0:T(8,128)(2,1)S(1)} all-to-all(bf16[16,40,128]{2,1,0:T(8,128)(2,1)S(1)} %get-tuple-element.28), channel_id=1, replica_groups={{6,4,2,0,134,132,130,128,262,260,258,256,390,388,386,384},{8,14,12,10,1..., dimensions={0} | all-to-all | bytes 327680 | tf_op jit(solution)/shard_map/all_to_all | solution.py:333
  119.6 0.6 shard_map.87
  120.2 3.3 %all-to-all-start.3 = ((bf16[4,40,128]{2,1,0:T(8,128)(2,1)}), bf16[4,40,128]{2,1,0:T(8,128)(2,1)S(1)}, u32[]{:S(2)}, u32[]{:S(2)}) async-start(bf16[4,40,128]{2,1,0:T(8,128)(2,1)} %shard_map.87), calls=%async_computation.3 | async-start | bytes 81920 | tf_op jit(solution)/shard_map/all_to_all | solution.py:333
  123.5 4.4 %collective-permute-start.4 = (bf16[4,96,128]{2,1,0:T(8,128)(2,1)S(1)}, bf16[4,96,128]{2,1,0:T(8,128)(2,1)S(1)}, u32[]{:S(2)}, u32[]{:S(2)}) collective-permute-start(bf16[4,96,128]{2,1,0:T(8,128)(2,1)S(1)} %get-tuple-element.31), channel_id=1, source_target_pairs={{0,1},{1,0},{2,3},{3,2},{4,5},{5,4},{6,7},{7,6},{8,9},{9,8},{10,11... | collective-permute-start | bytes 294920 | tf_op jit(solution)/shard_map/ppermute | solution.py:364
  127.9 1.0 shard_map.88
  128.9 0.0 collective-permute-done.4.got_ref
  128.9 4.3 %all-to-all-done.3.in_ref = bf16[4,40,128]{2,1,0:T(8,128)(2,1)S(1)} async-done(((bf16[4,40,128]{2,1,0:T(8,128)(2,1)}), bf16[4,40,128]{2,1,0:T(8,128)(2,1)S(1)}, u32[]{:S(2)}, u32[]{:S(2)}) %all-to-all-start.3) | async-done | bytes 40992 | tf_op jit(solution)/shard_map/all_to_all | solution.py:333
  133.2 11.6 %all_to_all.32.block_ref = bf16[16,40,128]{2,1,0:T(8,128)(2,1)S(1)} all-to-all(bf16[16,40,128]{2,1,0:T(8,128)(2,1)S(1)} %shard_map.89), channel_id=1, replica_groups={{6,4,2,0,134,132,130,128,262,260,258,256,390,388,386,384},{8,14,12,10,1..., dimensions={0} | all-to-all | bytes 327680 | tf_op jit(solution)/shard_map/all_to_all | solution.py:333
  144.9 0.1 shard_map.90
  145.0 0.0 copy-start
  145.0 0.0 copy-start.1
  145.0 11.0 %all_to_all.33.all_ref.mine_ref = bf16[4,768,128]{2,1,0:T(8,128)(2,1)S(1)} all-to-all(bf16[4,768,128]{2,1,0:T(8,128)(2,1)S(1)} %shard_map.90), channel_id=1, replica_groups=mesh['x'=4,'y'=4,'z'=16,'c'=2] {'y'}, dimensions={0} | all-to-all | bytes 1572864 | tf_op jit(solution)/shard_map/all_to_all | solution.py:333
  156.0 7.0 %collective-permute-start.5 = (bf16[4,768,128]{2,1,0:T(8,128)(2,1)S(1)}, bf16[4,768,128]{2,1,0:T(8,128)(2,1)S(1)}, u32[]{:S(2)}, u32[]{:S(2)}) collective-permute-start(bf16[4,768,128]{2,1,0:T(8,128)(2,1)S(1)} %all_to_all.33.all_ref.mine_ref), channel_id=1, source_target_pairs={{0,1},{1,0},{2,3},{3,2},{4,5},{5,4},{6,7},{7,6},{8,9},{9,8},{10,11... | collective-permute-start | bytes 2359304 | tf_op jit(solution)/shard_map/ppermute | solution.py:364
  162.9 0.0 copy-done
  162.9 0.0 copy-done.1
  162.9 1.8 %shard_map.91 = bf16[128,768]{1,0:T(8,128)(2,1)} custom-call(s32[2]{0:T(128)S(1)} %pad_add_fusion.place_ref, bf16[4,768,128]{2,1,0:T(8,128)(2,1)S(1)} %all_to_all.33.all_ref.mine_ref, bf16[768,384]{1,0:T(8,128)(2,1)S(1)} %copy-done, bf16[768,384]{1,0:T(8,128)(2,1)S(1)} %copy-done.1), custom_call_target="tpu_custom_call" | custom-call | tf_op jit(solution)/shard_map/pallas_call | solution.py:318
  164.7 0.1 collective-permute-done.5.other_ref
  164.8 1.7 %shard_map.92 = (bf16[768,384]{1,0:T(8,128)(2,1)}, bf16[768,384]{1,0:T(8,128)(2,1)}) custom-call(s32[2]{0:T(128)S(1)} %pad_add_fusion.place_ref, bf16[4,768,128]{2,1,0:T(8,128)(2,1)S(1)} %all_to_all.33.all_ref.mine_ref, bf16[4,768,128]{2,1,0:T(8,128)(2,1)S(1)} %collective-permute-done.5.other_ref), custom_call_target="tpu_custom_call" | custom-call | tf_op jit(solution)/shard_map/pallas_call | solution.py:318
  (1 shorter events, 0.0 us)
Async XLA Ops:
  3.8 55.1 %all-to-all-start = ((bf16[128,9,2,128]{3,2,1,0:T(2,128)(2,1)}), bf16[128,9,2,128]{3,2,1,0:T(2,128)(2,1)S(1)}, u32[]{:S(2)}, u32[]{:S(2)}) async-start(bf16[128,9,2,128]{3,2,1,0:T(2,128)(2,1)} %get-tuple-element.22), calls=%async_computation | async-start | bytes 1179648 | tf_op jit(solution)/shard_map/all_to_all | solution.py:333
  24.4 11.2 %collective-permute-start = (bf16[144,768]{1,0:T(8,128)(2,1)S(1)}, bf16[144,768]{1,0:T(8,128)(2,1)S(1)}, u32[]{:S(2)}, u32[]{:S(2)}) collective-permute-start(bf16[144,768]{1,0:T(8,128)(2,1)S(1)} %get-tuple-element.23), channel_id=1, source_target_pairs={{0,32},{32,64},{64,96},{96,0},{1,33},{33,65},{65,97},{97,1},{2,34}... | collective-permute-start | bytes 663560 | tf_op jit(solution)/shard_map/ppermute | solution.py:361
  27.9 15.4 %collective-permute-start.1 = (bf16[144,768]{1,0:T(8,128)(2,1)S(1)}, bf16[144,768]{1,0:T(8,128)(2,1)S(1)}, u32[]{:S(2)}, u32[]{:S(2)}) collective-permute-start(bf16[144,768]{1,0:T(8,128)(2,1)S(1)} %get-tuple-element.23), channel_id=1, source_target_pairs={{0,64},{32,96},{64,0},{96,32},{1,65},{33,97},{65,1},{97,33},{2,66}... | collective-permute-start | bytes 663560 | tf_op jit(solution)/shard_map/ppermute | solution.py:361
  32.6 12.1 %collective-permute-start.2 = (bf16[144,768]{1,0:T(8,128)(2,1)S(1)}, bf16[144,768]{1,0:T(8,128)(2,1)S(1)}, u32[]{:S(2)}, u32[]{:S(2)}) collective-permute-start(bf16[144,768]{1,0:T(8,128)(2,1)S(1)} %get-tuple-element.23), channel_id=1, source_target_pairs={{0,96},{32,0},{64,32},{96,64},{1,97},{33,1},{65,33},{97,65},{2,98}... | collective-permute-start | bytes 663560 | tf_op jit(solution)/shard_map/ppermute | solution.py:361
  44.9 17.0 %collective-permute-start.3 = (bf16[4,144,768]{2,1,0:T(8,128)(2,1)S(1)}, bf16[4,144,768]{2,1,0:T(8,128)(2,1)S(1)}, u32[]{:S(2)}, u32[]{:S(2)}) collective-permute-start(bf16[4,144,768]{2,1,0:T(8,128)(2,1)S(1)} %pad_maximum_fusion.refs_0_.ext_ref), channel_id=1, source_target_pairs={{0,1},{1,0},{2,3},{3,2},{4,5},{5,4},{6,7},{7,6},{8,9},{9,8},{10,11... | collective-permute-start | bytes 2654216 | tf_op jit(solution)/shard_map/ppermute | solution.py:364
  120.2 13.0 %all-to-all-start.3 = ((bf16[4,40,128]{2,1,0:T(8,128)(2,1)}), bf16[4,40,128]{2,1,0:T(8,128)(2,1)S(1)}, u32[]{:S(2)}, u32[]{:S(2)}) async-start(bf16[4,40,128]{2,1,0:T(8,128)(2,1)} %shard_map.87), calls=%async_computation.3 | async-start | bytes 81920 | tf_op jit(solution)/shard_map/all_to_all | solution.py:333
  123.5 5.4 %collective-permute-start.4 = (bf16[4,96,128]{2,1,0:T(8,128)(2,1)S(1)}, bf16[4,96,128]{2,1,0:T(8,128)(2,1)S(1)}, u32[]{:S(2)}, u32[]{:S(2)}) collective-permute-start(bf16[4,96,128]{2,1,0:T(8,128)(2,1)S(1)} %get-tuple-element.31), channel_id=1, source_target_pairs={{0,1},{1,0},{2,3},{3,2},{4,5},{5,4},{6,7},{7,6},{8,9},{9,8},{10,11... | collective-permute-start | bytes 294920 | tf_op jit(solution)/shard_map/ppermute | solution.py:364
  145.0 18.0 %copy-start = (bf16[768,384]{1,0:T(8,128)(2,1)S(1)}, bf16[768,384]{1,0:T(8,128)(2,1)}, u32[]{:S(2)}) copy-start(bf16[768,384]{1,0:T(8,128)(2,1)} %ws_ref.1) | copy-start | bytes 1769476
  145.0 18.0 %copy-start.1 = (bf16[768,384]{1,0:T(8,128)(2,1)S(1)}, bf16[768,384]{1,0:T(8,128)(2,1)}, u32[]{:S(2)}) copy-start(bf16[768,384]{1,0:T(8,128)(2,1)} %wv_ref.1) | copy-start | bytes 1769476
  156.0 8.9 %collective-permute-start.5 = (bf16[4,768,128]{2,1,0:T(8,128)(2,1)S(1)}, bf16[4,768,128]{2,1,0:T(8,128)(2,1)S(1)}, u32[]{:S(2)}, u32[]{:S(2)}) collective-permute-start(bf16[4,768,128]{2,1,0:T(8,128)(2,1)S(1)} %all_to_all.33.all_ref.mine_ref), channel_id=1, source_target_pairs={{0,1},{1,0},{2,3},{3,2},{4,5},{5,4},{6,7},{7,6},{8,9},{9,8},{10,11... | collective-permute-start | bytes 2359304 | tf_op jit(solution)/shard_map/ppermute | solution.py:364
